TPU v7x, 32 devices: a whole 2x2x4 slice. The times are simulated.
32 devices in a mesh: parts: 2 (over y), expert: 8 (over z, x), replica: 2 (over core).
Axes of the slice: x: 2, y: 2, z: 4, core: 2. Of those that a mesh axis runs over, the one named last changes fastest.
Arguments:
- tokens: bfloat16 [4096, 1024], P(('parts', 'expert', 'replica')), parts along dimension 0, may hold values from -6 to 6
- cotangent: bfloat16 [4096, 1024], P(('parts', 'expert', 'replica')), parts along dimension 0, may hold values from -2 to 2
- expert_ids: int32 [4096, 8], P(('parts', 'expert', 'replica')), parts along dimension 0, may hold values from 0 to 7, as said below
- gate_values: bfloat16 [4096, 8], P(('parts', 'expert', 'replica')), parts along dimension 0, may hold values from 0.049804688 to 0.5
- replica_pick: int32 [4096, 8], P(('parts', 'expert', 'replica')), parts along dimension 0, may hold values from 0 to 2
- replica_plan: int32 [16], P('parts'), parts along dimension 0, may hold values from 0 to 7, as said below
- gate_proj: bfloat16 [8, 1024, 384], P('expert'), may hold values from -0.1875 to 0.1875
- up_proj: bfloat16 [8, 1024, 384], P('expert'), may hold values from -0.1875 to 0.1875
- down_proj: bfloat16 [8, 1024, 384], P('expert'), may hold values from -0.3125 to 0.3125
Outputs:
- token_grad: bfloat16 [4096, 1024], P(('parts', 'expert', 'replica')), parts along dimension 0
- gate_grad: bfloat16 [4096, 8], P(('parts', 'expert', 'replica')), parts along dimension 0
- grad_gate_proj: bfloat16 [16, 1024, 384], P(('parts', 'expert'), 'replica'), parts along dimension 0
- grad_up_proj: bfloat16 [16, 1024, 384], P(('parts', 'expert'), 'replica'), parts along dimension 0
- grad_down_proj: bfloat16 [16, 1024, 384], P(('parts', 'expert'), 'replica'), parts along dimension 0
There are 2 independent parts, one for each index of `parts`. A program takes and returns all parts, laid end to end along the dimension named above; an argument that names none is the same for every part. Nothing has to cross between parts.
Inputs may be any that keep to these rules, and one draw needn't show every extreme that they name: `expert_ids`: each row names 8 different experts. `replica_plan`: 4 different experts appear, each exactly 2 times.
All inputs are finite; a program needn't handle non-finite values.
Results may differ from a plain program's by a relative error of at most 0.0095.
Values may be sent and summed in bfloat16 or wider, within the bound.
No kernel may reach another device: no remote copies, remote signals or barrier semaphores. Data moves between devices by JAX's collectives and lax.ppermute only.
A program may use at most 128 MiB of HBM per device.

v0:
```python
import jax
import jax.numpy as jnp
from jax import lax
from jax.experimental import pallas as pl
from jax.experimental.pallas import tpu as pltpu
from jax.sharding import PartitionSpec as P

CAP = 6


def route_assignments(flat_ids, flat_pick, replica_plan, capacity):
    experts = replica_plan.shape[0]
    lane_ids = jnp.arange(experts, dtype=jnp.int32)
    same_plan = replica_plan[:, None] == replica_plan[None, :]
    earlier = lane_ids[None, :] < lane_ids[:, None]
    position = jnp.sum(jnp.logical_and(same_plan, earlier), axis=1)
    hot_mask = jnp.any(replica_plan[None, :] == lane_ids[:, None], axis=1)
    is_hot = jnp.any(
        jnp.logical_and(flat_ids[:, None] == lane_ids[None, :], hot_mask[None, :]), axis=1
    )
    use_copy = jnp.logical_and(is_hot, flat_pick >= 1)
    matches = jnp.logical_and(
        replica_plan[None, :] == flat_ids[:, None], position[None, :] == flat_pick[:, None] - 1
    )
    holder = jnp.sum(jnp.where(matches, lane_ids[None, :], 0), axis=1)
    target = jnp.where(use_copy, holder, flat_ids)
    copy_role = use_copy.astype(jnp.int32)
    bucket = target * 2 + copy_role
    sequence = jnp.arange(bucket.shape[0], dtype=jnp.int32)
    arrival = jnp.sum(
        jnp.logical_and(bucket[None, :] == bucket[:, None], sequence[None, :] < sequence[:, None]),
        axis=1,
    )
    kept_mask = arrival < capacity
    slot_index = target * (2 * capacity) + copy_role * capacity + jnp.minimum(arrival, capacity - 1)
    return (slot_index, kept_mask)


def fill_slots(slot_index, kept_mask, slot_count):
    slot_ids = jnp.arange(slot_count, dtype=jnp.int32)
    matches = jnp.logical_and(slot_index[None, :] == slot_ids[:, None], kept_mask[None, :])
    sequence = jnp.arange(slot_index.shape[0], dtype=jnp.int32)
    source = jnp.sum(jnp.where(matches, sequence[None, :], 0), axis=1)
    filled = jnp.any(matches, axis=1)
    return (source, filled)


def expert_backward(row_block, upstream, weight, gate_w, up_w, down_w):
    contract_cols = (((1,), (1,)), ((), ()))
    contract_rows = (((0,), (0,)), ((), ()))
    gate_pre = jnp.dot(row_block, gate_w, preferred_element_type=jnp.float32)
    up_pre = jnp.dot(row_block, up_w, preferred_element_type=jnp.float32)
    sigmoid_gate = jax.nn.sigmoid(gate_pre)
    activated = gate_pre * sigmoid_gate
    hidden = (activated * up_pre).astype(jnp.bfloat16)
    output_rows = lax.dot_general(hidden, down_w, contract_cols, preferred_element_type=jnp.float32)
    weight_col = weight.astype(jnp.float32)[:, None]
    upstream_f = upstream.astype(jnp.float32)
    gate_rows = jnp.sum(upstream_f * output_rows, axis=1)
    hidden_grad = weight_col * jnp.dot(upstream, down_w, preferred_element_type=jnp.float32)
    slope = sigmoid_gate * (1.0 + gate_pre * (1.0 - sigmoid_gate))
    gate_delta = (hidden_grad * up_pre * slope).astype(jnp.bfloat16)
    up_delta = (hidden_grad * activated).astype(jnp.bfloat16)
    input_grad = (
        lax.dot_general(gate_delta, gate_w, contract_cols, preferred_element_type=jnp.float32)
        + lax.dot_general(up_delta, up_w, contract_cols, preferred_element_type=jnp.float32)
    ).astype(jnp.bfloat16)
    scaled = (weight_col * upstream_f).astype(jnp.bfloat16)
    grad_set = (
        lax.dot_general(row_block, gate_delta, contract_rows, preferred_element_type=jnp.float32),
        lax.dot_general(row_block, up_delta, contract_rows, preferred_element_type=jnp.float32),
        lax.dot_general(scaled, hidden, contract_rows, preferred_element_type=jnp.float32),
    )
    return (input_grad, gate_rows, grad_set)


def per_device_moving_weights(
    tokens,
    cotangent,
    expert_ids,
    gate_values,
    replica_pick,
    replica_plan,
    gate_proj,
    up_proj,
    down_proj,
):
    experts = lax.axis_size("expert")
    capacity = CAP
    slot_total = 2 * capacity
    model_width = tokens.shape[1]
    topk = expert_ids.shape[1]
    token_count = tokens.shape[0]
    slot_index, kept_mask = route_assignments(
        expert_ids.reshape(-1), replica_pick.reshape(-1), replica_plan, capacity
    )
    source, filled = fill_slots(slot_index, kept_mask, experts * slot_total)
    token_of = source // topk
    zero_half = jnp.zeros((), jnp.bfloat16)
    send_rows = jnp.where(filled[:, None], jnp.take(tokens, token_of, axis=0), zero_half).reshape(
        experts, slot_total, model_width
    )
    send_upstream = jnp.where(
        filled[:, None], jnp.take(cotangent, token_of, axis=0), zero_half
    ).reshape(experts, slot_total, model_width)
    send_weight = jnp.where(filled, gate_values.reshape(-1)[source], zero_half).reshape(
        experts, slot_total
    )
    arrived = lax.all_to_all(send_rows, "expert", split_axis=0, concat_axis=0, tiled=True)
    own_gate = gate_proj[0]
    own_up = up_proj[0]
    own_down = down_proj[0]
    hidden_width = own_gate.shape[1]
    spread = (
        lax.all_to_all(
            own_gate.reshape(experts, -1), "expert", split_axis=0, concat_axis=0, tiled=True
        ),
        lax.all_to_all(
            own_up.reshape(experts, -1), "expert", split_axis=0, concat_axis=0, tiled=True
        ),
        lax.all_to_all(
            own_down.reshape(experts, -1), "expert", split_axis=0, concat_axis=0, tiled=True
        ),
    )
    chosen_gate = jnp.take(spread[0], replica_plan, axis=0)
    chosen_up = jnp.take(spread[1], replica_plan, axis=0)
    chosen_down = jnp.take(spread[2], replica_plan, axis=0)
    collected = (
        lax.all_to_all(chosen_gate, "expert", split_axis=0, concat_axis=0, tiled=True),
        lax.all_to_all(chosen_up, "expert", split_axis=0, concat_axis=0, tiled=True),
        lax.all_to_all(chosen_down, "expert", split_axis=0, concat_axis=0, tiled=True),
    )
    copy_gate = collected[0].reshape(model_width, hidden_width)
    copy_up = collected[1].reshape(model_width, hidden_width)
    copy_down = collected[2].reshape(model_width, hidden_width)
    arrived_up, arrived_weight = (
        lax.all_to_all(send_upstream, "expert", split_axis=0, concat_axis=0, tiled=True),
        lax.all_to_all(send_weight, "expert", split_axis=0, concat_axis=0, tiled=True),
    )
    owned_dx, owned_gate_rows, owned_grads = expert_backward(
        arrived[:, :capacity].reshape(-1, model_width),
        arrived_up[:, :capacity].reshape(-1, model_width),
        arrived_weight[:, :capacity].reshape(-1),
        own_gate,
        own_up,
        own_down,
    )
    copied_dx, copied_gate_rows, copied_grads = expert_backward(
        arrived[:, capacity:].reshape(-1, model_width),
        arrived_up[:, capacity:].reshape(-1, model_width),
        arrived_weight[:, capacity:].reshape(-1),
        copy_gate,
        copy_up,
        copy_down,
    )
    back_rows = jnp.concatenate(
        [
            owned_dx.reshape(experts, capacity, model_width),
            copied_dx.reshape(experts, capacity, model_width),
        ],
        axis=1,
    )
    back_gate = jnp.concatenate(
        [owned_gate_rows.reshape(experts, capacity), copied_gate_rows.reshape(experts, capacity)],
        axis=1,
    ).astype(jnp.bfloat16)
    returned, returned_gate = (
        lax.all_to_all(back_rows, "expert", split_axis=0, concat_axis=0, tiled=True),
        lax.all_to_all(back_gate, "expert", split_axis=0, concat_axis=0, tiled=True),
    )
    copy_pieces = (
        copied_grads[0].astype(jnp.bfloat16).reshape(experts, -1),
        copied_grads[1].astype(jnp.bfloat16).reshape(experts, -1),
        copied_grads[2].astype(jnp.bfloat16).reshape(experts, -1),
    )
    grad_spread = (
        lax.all_to_all(copy_pieces[0], "expert", split_axis=0, concat_axis=0, tiled=True),
        lax.all_to_all(copy_pieces[1], "expert", split_axis=0, concat_axis=0, tiled=True),
        lax.all_to_all(copy_pieces[2], "expert", split_axis=0, concat_axis=0, tiled=True),
    )
    lane_ids = jnp.arange(experts, dtype=jnp.int32)
    owner_map = (replica_plan[None, :] == lane_ids[:, None]).astype(jnp.bfloat16)
    summed_gate = jnp.dot(owner_map, grad_spread[0], preferred_element_type=jnp.float32).astype(
        jnp.bfloat16
    )
    summed_up = jnp.dot(owner_map, grad_spread[1], preferred_element_type=jnp.float32).astype(
        jnp.bfloat16
    )
    summed_down = jnp.dot(owner_map, grad_spread[2], preferred_element_type=jnp.float32).astype(
        jnp.bfloat16
    )
    grad_back = (
        lax.all_to_all(summed_gate, "expert", split_axis=0, concat_axis=0, tiled=True),
        lax.all_to_all(summed_up, "expert", split_axis=0, concat_axis=0, tiled=True),
        lax.all_to_all(summed_down, "expert", split_axis=0, concat_axis=0, tiled=True),
    )
    total_gate = owned_grads[0] + grad_back[0].reshape(model_width, hidden_width).astype(
        jnp.float32
    )
    total_up = owned_grads[1] + grad_back[1].reshape(model_width, hidden_width).astype(jnp.float32)
    total_down = owned_grads[2] + grad_back[2].reshape(model_width, hidden_width).astype(
        jnp.float32
    )
    shares = (
        lax.psum_scatter(
            total_gate.astype(jnp.bfloat16), "replica", scatter_dimension=0, tiled=True
        ).astype(jnp.float32),
        lax.psum_scatter(
            total_up.astype(jnp.bfloat16), "replica", scatter_dimension=0, tiled=True
        ).astype(jnp.float32),
        lax.psum_scatter(
            total_down.astype(jnp.bfloat16), "replica", scatter_dimension=0, tiled=True
        ).astype(jnp.float32),
    )
    flat_back = returned.reshape(experts * slot_total, model_width)
    picked_rows = jnp.take(flat_back, slot_index, axis=0)
    picked_rows = jnp.where(kept_mask[:, None], picked_rows, zero_half).astype(jnp.float32)
    token_grad = jnp.sum(picked_rows.reshape(token_count, topk, model_width), axis=1).astype(
        jnp.bfloat16
    )
    gate_grad = jnp.where(kept_mask, returned_gate.reshape(-1)[slot_index], zero_half).reshape(
        token_count, topk
    )
    return (
        token_grad,
        gate_grad,
        shares[0].astype(jnp.bfloat16)[None],
        shares[1].astype(jnp.bfloat16)[None],
        shares[2].astype(jnp.bfloat16)[None],
    )


BF = jnp.bfloat16
F32 = jnp.float32
CONTRACT_ROWS = (((0,), (0,)), ((), ()))
CONTRACT_COLS = (((1,), (1,)), ((), ()))
VMEM_LIMIT = 40 * 1024 * 1024

MAIN = 16
QUARTERS = 4
SEND_ROWS = 2 * QUARTERS * MAIN + 16
BACK_ROWS = QUARTERS * MAIN + 16


def copies_of(experts):
    return 2 if experts <= 8 else 8


def iota(shape, axis):
    return lax.broadcasted_iota(jnp.int32, shape, axis)


def flip(values, eye):
    return lax.dot_general(values.astype(BF), eye, CONTRACT_ROWS, preferred_element_type=F32)


def repeat_rows(table, times):
    width = table.shape[1]
    return jnp.concatenate(
        [jnp.broadcast_to(table[e : e + 1], (times, width)) for e in range(table.shape[0])], axis=0
    )


def route_kernel(plan_ref, ids_ref, pick_ref, gate_ref, tok_ref, cot_ref, send_ref, slot_ref, gates_ref):
    tokens, topk = ids_ref.shape
    experts = send_ref.shape[0]
    width = tok_ref.shape[1] // QUARTERS
    copies = copies_of(experts)
    eye = (iota((tokens, tokens), 0) == iota((tokens, tokens), 1)).astype(BF)
    before = (iota((tokens, tokens), 0) < iota((tokens, tokens), 1)).astype(BF)
    ids = flip(ids_ref[...].astype(F32), eye).astype(jnp.int32)
    pick = flip(pick_ref[...].astype(F32), eye).astype(jnp.int32)
    gate = flip(gate_ref[...], eye)
    expert_row = iota((experts, tokens), 0)
    named = jnp.zeros((experts, tokens), jnp.int32)
    gates = jnp.zeros((experts, tokens), F32)
    for k in range(topk):
        hit = ids[k : k + 1] == expert_row
        named = jnp.where(hit, pick[k : k + 1] + 1, named)
        gates = jnp.where(hit, gate[k : k + 1], gates)
    hot = jnp.zeros((experts, tokens), jnp.int32)
    for j in range(experts):
        hot = jnp.where(expert_row == plan_ref[j], 1, hot)
    chosen = jnp.where(named == 0, -1, jnp.where(hot > 0, named - 1, 0))
    masks = jnp.concatenate([(chosen == c).astype(F32) for c in range(copies + 1)], axis=0)
    rank = jnp.dot(masks.astype(BF), before, preferred_element_type=F32).astype(jnp.int32)
    slot = jnp.full((experts, tokens), -1, jnp.int32)
    for c in range(copies + 1):
        rank_c = rank[c * experts : (c + 1) * experts]
        keep = jnp.logical_and(chosen == c, rank_c < CAP)
        slot = jnp.where(keep, c * CAP + rank_c, slot)
    slot_ref[...] = slot
    gates_ref[...] = gates
    slot16 = repeat_rows(slot, MAIN)
    gate16 = repeat_rows(gates, MAIN)
    lane_row = jnp.bitwise_and(iota(slot16.shape, 0), MAIN - 1)
    onehot = (slot16 == lane_row).astype(F32)
    rows = jnp.dot(onehot.astype(BF), tok_ref[...], preferred_element_type=F32).astype(BF)
    scaled = jnp.dot(
        (onehot * gate16).astype(BF), cot_ref[...], preferred_element_type=F32
    ).astype(BF)
    for e in range(experts):
        for q in range(QUARTERS):
            here = slice(e * MAIN, (e + 1) * MAIN)
            cols = slice(q * width, (q + 1) * width)
            send_ref[e, q * MAIN : (q + 1) * MAIN, :] = rows[here, cols]
            send_ref[e, (QUARTERS + q) * MAIN : (QUARTERS + q + 1) * MAIN, :] = scaled[here, cols]
    wanted = MAIN + jnp.bitwise_and(jnp.right_shift(lane_row, 2), 1)
    is_scaled = lane_row >= 8
    last = (slot16 == wanted).astype(F32)
    last_rows = jnp.where(is_scaled, 0.0, last)
    last_scaled = jnp.where(is_scaled, last * gate16, 0.0)
    tail = jnp.zeros((experts * MAIN, width), F32)
    for q in range(QUARTERS):
        mine = jnp.bitwise_and(lane_row, 3) == q
        cols = slice(q * width, (q + 1) * width)
        tail += jnp.dot(
            jnp.where(mine, last_rows, 0.0).astype(BF), tok_ref[:, cols], preferred_element_type=F32
        )
        tail += jnp.dot(
            jnp.where(mine, last_scaled, 0.0).astype(BF),
            cot_ref[:, cols],
            preferred_element_type=F32,
        )
    tail = tail.astype(BF)
    for e in range(experts):
        send_ref[e, 2 * QUARTERS * MAIN :, :] = tail[e * MAIN : (e + 1) * MAIN]


def expert_kernel(
    recv_ref, gate_ref, up_ref, down_ref, back_ref, x_ref, s_ref, dg_ref, du_ref, hid_ref
):
    experts, unused, width = recv_ref.shape
    main_rows = experts * MAIN
    tail = jnp.concatenate([recv_ref[i, 2 * QUARTERS * MAIN :, :] for i in range(experts)], axis=0)
    row = iota((4 * experts, main_rows), 0)
    col = iota((4 * experts, main_rows), 1)
    kind = (row >= 2 * experts).astype(jnp.int32)
    sender = jnp.right_shift(row - kind * 2 * experts, 1)
    base = sender * MAIN + kind * 8 + jnp.bitwise_and(row, 1) * 4
    for q in range(QUARTERS):
        cols = slice(q * width, (q + 1) * width)
        picked = jnp.dot(
            (col == base + q).astype(F32).astype(BF), tail, preferred_element_type=F32
        ).astype(BF)
        x_ref[main_rows:, cols] = picked[: 2 * experts]
        s_ref[main_rows:, cols] = picked[2 * experts :]
        for i in range(experts):
            here = slice(i * MAIN, (i + 1) * MAIN)
            x_ref[here, cols] = recv_ref[i, q * MAIN : (q + 1) * MAIN, :]
            s_ref[here, cols] = recv_ref[i, (QUARTERS + q) * MAIN : (QUARTERS + q + 1) * MAIN, :]
    rows = x_ref[...]
    gate_pre = jnp.dot(rows, gate_ref[...], preferred_element_type=F32)
    up_pre = jnp.dot(rows, up_ref[...], preferred_element_type=F32)
    hidden_grad = jnp.dot(s_ref[...], down_ref[...], preferred_element_type=F32)
    sig = jax.nn.sigmoid(gate_pre)
    activated = gate_pre * sig
    hidden = (activated * up_pre).astype(BF)
    slope = sig * (1.0 + gate_pre * (1.0 - sig))
    gate_delta = (hidden_grad * up_pre * slope).astype(BF)
    up_delta = (hidden_grad * activated).astype(BF)
    hid_ref[...] = hidden
    dg_ref[...] = gate_delta
    du_ref[...] = up_delta
    grad = (
        lax.dot_general(gate_delta, gate_ref[...], CONTRACT_COLS, preferred_element_type=F32)
        + lax.dot_general(up_delta, up_ref[...], CONTRACT_COLS, preferred_element_type=F32)
    ).astype(BF)
    product = hidden.astype(F32) * hidden_grad
    product = jnp.concatenate(
        [product, jnp.zeros((width - product.shape[0], product.shape[1]), F32)], axis=0
    )
    gate_lanes = lax.dot_general(
        jnp.ones((8, product.shape[1]), F32),
        product,
        CONTRACT_COLS,
        preferred_element_type=F32,
        precision=lax.Precision.HIGHEST,
    )
    trow = iota((main_rows, 2 * experts), 0)
    tcol = iota((main_rows, 2 * experts), 1)
    inner = jnp.bitwise_and(trow, MAIN - 1)
    source = jnp.right_shift(trow, 4) * 2 + jnp.right_shift(inner, 2)
    spread = jnp.zeros((main_rows, width), F32)
    for q in range(QUARTERS):
        cols = slice(q * width, (q + 1) * width)
        mine = jnp.logical_and(jnp.bitwise_and(inner, 3) == q, inner < 8)
        place = jnp.logical_and(mine, tcol == source).astype(F32).astype(BF)
        spread += jnp.dot(place, grad[main_rows:, cols], preferred_element_type=F32)
        for i in range(experts):
            back_ref[i, q * MAIN : (q + 1) * MAIN, :] = grad[i * MAIN : (i + 1) * MAIN, cols]
    for i in range(experts):
        back_ref[i, QUARTERS * MAIN :, :] = jnp.concatenate(
            [spread[i * MAIN : i * MAIN + 8], gate_lanes], axis=0
        ).astype(BF)


def grads_of(half, x_ref, s_ref, dg_ref, du_ref, hid_ref):
    rows = x_ref.shape[1] // 2
    cols = pl.ds(pl.multiple_of(half * rows, rows), rows)
    x_half = x_ref[:, cols]
    s_half = s_ref[:, cols]
    return (
        lax.dot_general(x_half, dg_ref[...], CONTRACT_ROWS, preferred_element_type=F32),
        lax.dot_general(x_half, du_ref[...], CONTRACT_ROWS, preferred_element_type=F32),
        lax.dot_general(s_half, hid_ref[...], CONTRACT_ROWS, preferred_element_type=F32),
    )


def other_half_kernel(member_ref, x_ref, s_ref, dg_ref, du_ref, hid_ref, out_ref):
    parts = grads_of(1 - member_ref[0], x_ref, s_ref, dg_ref, du_ref, hid_ref)
    rows = parts[0].shape[0]
    for n in range(3):
        out_ref[n * rows : (n + 1) * rows, :] = parts[n].astype(BF)


def own_half_kernel(
    member_ref, x_ref, s_ref, dg_ref, du_ref, hid_ref, came_ref, gate_ref, up_ref, down_ref
):
    parts = grads_of(member_ref[0], x_ref, s_ref, dg_ref, du_ref, hid_ref)
    rows = parts[0].shape[0]
    for n, out_ref in enumerate((gate_ref, up_ref, down_ref)):
        came = came_ref[n * rows : (n + 1) * rows, :].astype(F32)
        out_ref[...] = (parts[n].astype(BF).astype(F32) + came).astype(BF)


def combine_kernel(me_ref, ids_ref, slot_ref, gates_ref, ret_ref, token_ref, grad_ref):
    tokens, topk = ids_ref.shape
    experts, unused, width = ret_ref.shape
    eye = (iota((tokens, tokens), 0) == iota((tokens, tokens), 1)).astype(BF)
    ids = flip(ids_ref[...].astype(F32), eye).astype(jnp.int32)
    slot = slot_ref[...]
    slot16 = repeat_rows(slot, MAIN)
    lane_row = jnp.bitwise_and(iota(slot16.shape, 0), MAIN - 1)
    onehot = (slot16 == lane_row).astype(F32).astype(BF)
    wanted = MAIN + jnp.right_shift(lane_row, 2)
    last = jnp.where(jnp.logical_and(slot16 == wanted, lane_row < 8), 1.0, 0.0)
    tail = jnp.concatenate([ret_ref[e, QUARTERS * MAIN :, :] for e in range(experts)], axis=0)
    for q in range(QUARTERS):
        cols = slice(q * width, (q + 1) * width)
        main = jnp.concatenate(
            [ret_ref[e, q * MAIN : (q + 1) * MAIN, :] for e in range(experts)], axis=0
        )
        mine = jnp.bitwise_and(lane_row, 3) == q
        place = jnp.where(mine, last, 0.0).astype(BF)
        total = lax.dot_general(onehot, main, CONTRACT_ROWS, preferred_element_type=F32)
        total += lax.dot_general(place, tail, CONTRACT_ROWS, preferred_element_type=F32)
        token_ref[:, cols] = total.astype(BF)
    me = me_ref[0]
    lane = jnp.where(slot < MAIN, me * MAIN + slot, experts * MAIN + 2 * me + slot - MAIN)
    lane = jnp.where(slot < 0, -1, lane)
    lane_index = iota((width, tokens), 0)
    found = []
    for e in range(experts):
        pick = (lane_index == lane[e : e + 1]).astype(F32).astype(BF)
        mine = jnp.dot(ret_ref[e, QUARTERS * MAIN :, :], pick, preferred_element_type=F32)
        found.append(mine[8:9])
    found = jnp.concatenate(found, axis=0)
    kept = slot >= 0
    grads = jnp.where(kept, found / jnp.where(kept, gates_ref[...], 1.0), 0.0)
    expert_row = iota((experts, tokens), 0)
    by_choice = [
        jnp.sum(jnp.where(expert_row == ids[k : k + 1], grads, 0.0), axis=0, keepdims=True)
        for k in range(topk)
    ]
    by_choice = jnp.concatenate(by_choice, axis=0).astype(BF)
    grad_ref[...] = lax.dot_general(
        eye, by_choice, CONTRACT_COLS, preferred_element_type=F32
    ).astype(BF)


def local_call(kernel, outs, scalars, arrays, name, flops, moved):
    smem = pl.BlockSpec(memory_space=pltpu.SMEM)
    vmem = pl.BlockSpec(memory_space=pltpu.VMEM)
    return pl.pallas_call(
        kernel,
        out_shape=[jax.ShapeDtypeStruct(shape, kind) for shape, kind in outs],
        in_specs=[smem] * len(scalars) + [vmem] * len(arrays),
        out_specs=[vmem] * len(outs),
        compiler_params=pltpu.CompilerParams(vmem_limit_bytes=VMEM_LIMIT),
        cost_estimate=pl.CostEstimate(flops=flops, bytes_accessed=moved, transcendentals=0),
        name=name,
    )(*scalars, *arrays)


def per_device_moving_rows(
    tokens,
    cotangent,
    expert_ids,
    gate_values,
    replica_pick,
    replica_plan,
    gate_proj,
    up_proj,
    down_proj,
):
    experts = lax.axis_size("expert")
    token_count, model_width = tokens.shape
    topk = expert_ids.shape[1]
    hidden_width = gate_proj.shape[2]
    width = model_width // QUARTERS
    served = experts * (MAIN + 2)
    me = lax.axis_index("expert").reshape(1).astype(jnp.int32)
    member = lax.axis_index("replica").reshape(1).astype(jnp.int32)
    send, slot, gates = local_call(
        route_kernel,
        [
            ((experts, SEND_ROWS, width), BF),
            ((experts, token_count), jnp.int32),
            ((experts, token_count), F32),
        ],
        [replica_plan],
        [expert_ids, replica_pick, gate_values, tokens, cotangent],
        "route",
        2 * 2 * served * token_count * model_width,
        2 * 2 * (token_count + served) * model_width,
    )
    recv = lax.all_to_all(send, "expert", split_axis=0, concat_axis=0, tiled=True)
    matmul = 2 * served * model_width * hidden_width
    back, x_rows, s_rows, gate_delta, up_delta, hidden = local_call(
        expert_kernel,
        [
            ((experts, BACK_ROWS, width), BF),
            ((served, model_width), BF),
            ((served, model_width), BF),
            ((served, hidden_width), BF),
            ((served, hidden_width), BF),
            ((served, hidden_width), BF),
        ],
        [],
        [recv, gate_proj[0], up_proj[0], down_proj[0]],
        "expert_rows",
        5 * matmul,
        2 * 3 * model_width * hidden_width,
    )
    returned = lax.all_to_all(back, "expert", split_axis=0, concat_axis=0, tiled=True)
    half = model_width // 2
    (leaving,) = local_call(
        other_half_kernel,
        [((3 * half, hidden_width), BF)],
        [member],
        [x_rows, s_rows, gate_delta, up_delta, hidden],
        "other_half",
        3 * matmul // 2,
        2 * 3 * half * hidden_width,
    )
    came = lax.ppermute(leaving, "replica", [(0, 1), (1, 0)])
    shares = local_call(
        own_half_kernel,
        [((half, hidden_width), BF)] * 3,
        [member],
        [x_rows, s_rows, gate_delta, up_delta, hidden, came],
        "own_half",
        3 * matmul // 2,
        2 * 2 * 3 * half * hidden_width,
    )
    token_grad, gate_grad = local_call(
        combine_kernel,
        [((token_count, model_width), BF), ((token_count, topk), BF)],
        [me],
        [expert_ids, slot, gates, returned],
        "combine",
        2 * served * token_count * model_width,
        2 * 2 * token_count * model_width,
    )
    return (token_grad, gate_grad, shares[0][None], shares[1][None], shares[2][None])


def per_device(tokens, cotangent, expert_ids, gate_values, replica_pick, replica_plan, *matrices):
    experts = lax.axis_size("expert")
    slots = (copies_of(experts) + 1) * CAP
    row_bytes = 3 * 2 * tokens.shape[1] * experts
    matrix_bytes = 4 * sum(2 * m[0].size for m in matrices)
    fits = slots == MAIN + 2 and experts == 8 and lax.axis_size("replica") == 2
    rows_cheaper = slots * row_bytes < 2 * CAP * row_bytes + matrix_bytes
    plan = per_device_moving_rows if fits and rows_cheaper else per_device_moving_weights
    return plan(
        tokens, cotangent, expert_ids, gate_values, replica_pick, replica_plan, *matrices
    )


def solution(mesh):
    placed = (
        P(("parts", "expert", "replica"), None),
        P(("parts", "expert", "replica"), None),
        P(("parts", "expert", "replica"), None),
        P(("parts", "expert", "replica"), None),
        P(("parts", "expert", "replica"), None),
        P("parts"),
        P("expert", None, None),
        P("expert", None, None),
        P("expert", None, None),
    )
    return jax.shard_map(
        per_device,
        mesh=mesh,
        in_specs=placed,
        out_specs=(
            P(("parts", "expert", "replica"), None),
            P(("parts", "expert", "replica"), None),
            P(("parts", "expert"), "replica", None),
            P(("parts", "expert"), "replica", None),
            P(("parts", "expert"), "replica", None),
        ),
        check_vma=False,
    )
```

profile of v0, /device:TPU:0, one launch (start us, length us, event | category | flops | bytes accessed | tf_op | source)
XLA Modules:
  0.0 54.1 jit_solution(15009259381801395045)
XLA Ops:
  0.6 0.0 copy-start.1
  0.6 0.0 copy-start
  0.7 0.9 %copy.16.gate_ref = bf16[128,8]{1,0:T(8,128)(2,1)S(1)} copy(bf16[128,8]{0,1:T(8,128)(2,1)} %param.12) | data formatting | bytes 4096 | tf_op args[3]
  1.6 0.8 %copy.17.ids_ref = s32[128,8]{1,0:T(8,128)S(1)} copy(s32[128,8]{0,1:T(8,128)} %param.11) | data formatting | bytes 8192 | tf_op args[2]
  2.4 0.0 copy-start.3
  2.4 0.8 %copy.15.pick_ref = s32[128,8]{1,0:T(8,128)S(1)} copy(s32[128,8]{0,1:T(8,128)} %param.13) | data formatting | bytes 8192 | tf_op args[4]
  3.2 0.0 copy-start.12
  3.2 0.9 %copy-done.12 = bf16[128,1024]{1,0:T(8,128)(2,1)S(1)} copy-done((bf16[128,1024]{1,0:T(8,128)(2,1)S(1)}, bf16[128,1024]{1,0:T(8,128)(2,1)}, u32[]{:S(2)}) %copy-start.12) | copy-done | bytes 262168
  4.1 0.0 copy-start.13
  4.1 0.9 %copy-done.13 = bf16[128,1024]{1,0:T(8,128)(2,1)S(1)} copy-done((bf16[128,1024]{1,0:T(8,128)(2,1)S(1)}, bf16[128,1024]{1,0:T(8,128)(2,1)}, u32[]{:S(2)}) %copy-start.13) | copy-done | bytes 262168
  5.1 0.0 copy-start.14
  5.1 0.7 %copy-done.14 = s32[8]{0:T(128)S(1)} copy-done((s32[8]{0:T(128)S(1)}, s32[8]{0:T(128)}, u32[]{:S(2)}) %copy-start.14) | copy-done | bytes 56
  5.7 2.1 %route.1 = (bf16[8,144,256]{2,1,0:T(8,128)(2,1)}, s32[8,128]{1,0:T(8,128)S(1)}, f32[8,128]{1,0:T(8,128)S(1)}) custom-call(s32[8]{0:T(128)S(1)} %copy-done.14, s32[128,8]{1,0:T(8,128)S(1)} %copy.17.ids_ref, s32[128,8]{1,0:T(8,128)S(1)} %copy.15.pick_ref, bf16[128,8]{1,0:T(8,128)(2,1)S(1)} %copy.16.gate_ref, bf16[128,1024]{1,0:T(8,128)(2,1)S(1)} %copy-done.12, ...), custom_call_target="tpu_custom_call" | custom-call | flops 75497472 | bytes 1114112 | tf_op jit(solution)/shard_map/route/pallas_call | solution.py:475
  7.8 0.0 copy-done.3
  7.8 7.3 %all-to-all-start = ((bf16[8,144,256]{2,1,0:T(8,128)(2,1)}), bf16[8,144,256]{2,1,0:T(8,128)(2,1)S(1)}, u32[]{:S(2)}, u32[]{:S(2)}) async-start(bf16[8,144,256]{2,1,0:T(8,128)(2,1)} %get-tuple-element.21), calls=%async_computation | async-start | bytes 1179648 | tf_op jit(solution)/shard_map/all_to_all | solution.py:518
  15.1 15.9 %all-to-all-done.recv_ref = bf16[8,144,256]{2,1,0:T(8,128)(2,1)S(1)} async-done(((bf16[8,144,256]{2,1,0:T(8,128)(2,1)}), bf16[8,144,256]{2,1,0:T(8,128)(2,1)S(1)}, u32[]{:S(2)}, u32[]{:S(2)}) %all-to-all-start) | async-done | bytes 589856 | tf_op jit(solution)/shard_map/all_to_all | solution.py:518
  31.0 0.0 copy-done.1
  31.0 0.0 copy-done
  31.0 0.0 copy-start.2
  31.0 1.1 %copy-done.2 = bf16[1,1024,384]{2,1,0:T(8,128)(2,1)S(1)} copy-done((bf16[1,1024,384]{2,1,0:T(8,128)(2,1)S(1)}, bf16[1,1024,384]{2,1,0:T(8,128)(2,1)}, u32[]{:S(2)}) %copy-start.2) | copy-done | bytes 786456
  32.1 1.6 %expert_rows.1 = (bf16[8,80,256]{2,1,0:T(8,128)(2,1)S(1)}, bf16[144,1024]{1,0:T(8,128)(2,1)S(1)}, bf16[144,1024]{1,0:T(8,128)(2,1)S(1)}, bf16[144,384]{1,0:T(8,1...) custom-call(bf16[8,144,256]{2,1,0:T(8,128)(2,1)S(1)} %all-to-all-done.recv_ref, ...), custom_call_target="tpu_custom_call" | custom-call | flops 566231040 | bytes 2359296 | tf_op jit(solution)/shard_map/expert_rows/pallas_call | solution.py:475
  33.7 0.0 copy-start.5
  33.7 0.0 copy-start.7
  33.7 0.0 copy-start.9
  33.7 0.0 copy-start.11
  33.8 0.0 copy-start.4
  33.8 0.6 %other_half.1 = bf16[1536,384]{1,0:T(8,128)(2,1)S(1)} custom-call(s32[1]{0:T(128)} %bitcast.4.member_ref, bf16[144,1024]{1,0:T(8,128)(2,1)S(1)} %get-tuple-element.25.x_ref, bf16[144,1024]{1,0:T(8,128)(2,1)S(1)} %get-tuple-element.26.s_ref, bf16[144,384]{1,0:T(8,128)(2,1)S(1)} %get-tuple-element.27.dg_ref, bf16[144,384]{1,0:T(8,128)(2,1)S(1)} %get-tuple-element.28.du_ref, ...), custom_call_target="tpu_custom_call" | custom-call | flops 169869312 | bytes 1179648 | tf_op jit(solution)/shard_map/other_half/pallas_call | solution.py:475
  34.4 0.1 collective-permute-start
  34.5 0.0 copy-done.5
  34.5 0.0 copy-done.7
  34.5 0.0 copy-done.9
  34.5 0.1 copy-done.11
  34.6 0.0 copy-start.6
  34.6 3.8 %all-to-all-start.1 = ((bf16[8,80,256]{2,1,0:T(8,128)(2,1)}), bf16[8,80,256]{2,1,0:T(8,128)(2,1)S(1)}, u32[]{:S(2)}, u32[]{:S(2)}) async-start(bf16[8,80,256]{2,1,0:T(8,128)(2,1)} %copy-done.11), calls=%async_computation.1 | async-start | bytes 655360 | tf_op jit(solution)/shard_map/all_to_all | solution.py:536
  38.3 10.9 %all-to-all-done.1.ret_ref = bf16[8,80,256]{2,1,0:T(8,128)(2,1)S(1)} async-done(((bf16[8,80,256]{2,1,0:T(8,128)(2,1)}), bf16[8,80,256]{2,1,0:T(8,128)(2,1)S(1)}, u32[]{:S(2)}, u32[]{:S(2)}) %all-to-all-start.1) | async-done | bytes 327712 | tf_op jit(solution)/shard_map/all_to_all | solution.py:536
  49.2 0.0 copy-done.4
  49.2 1.0 %combine.1 = (bf16[128,1024]{1,0:T(8,128)(2,1)}, bf16[128,8]{1,0:T(8,128)(2,1)S(1)}) custom-call(s32[1]{0:T(128)} %bitcast.me_ref, s32[128,8]{1,0:T(8,128)S(1)} %copy-done.4, s32[8,128]{1,0:T(8,128)S(1)} %get-tuple-element.19.slot_ref, f32[8,128]{1,0:T(8,128)S(1)} %get-tuple-element.20.gates_ref, bf16[8,80,256]{2,1,0:T(8,128)(2,1)S(1)} %all-to-all-done.1.ret_ref), custom_call_target="tpu_custom_call" | custom-call | flops 37748736 | bytes 524288 | tf_op jit(solution)/shard_map/combine/pallas_call | solution.py:475
  50.3 0.7 %copy.18 = bf16[128,8]{0,1:T(8,128)(2,1)} copy(bf16[128,8]{1,0:T(8,128)(2,1)S(1)} %get-tuple-element.34) | data formatting | bytes 4096
  50.9 0.0 collective-permute-done.came_ref
  50.9 0.0 copy-done.6
  50.9 0.0 copy-start.8
  50.9 0.9 %copy-done.8 = bf16[144,384]{1,0:T(8,128)(2,1)S(1)} copy-done((bf16[144,384]{1,0:T(8,128)(2,1)S(1)}, bf16[144,384]{1,0:T(8,128)(2,1)}, u32[]{:S(2)}) %copy-start.8) | copy-done | bytes 110616
  51.8 0.0 copy-start.10
  51.8 0.9 %copy-done.10 = bf16[144,384]{1,0:T(8,128)(2,1)S(1)} copy-done((bf16[144,384]{1,0:T(8,128)(2,1)S(1)}, bf16[144,384]{1,0:T(8,128)(2,1)}, u32[]{:S(2)}) %copy-start.10) | copy-done | bytes 110616
  52.7 1.4 %own_half.1 = (bf16[512,384]{1,0:T(8,128)(2,1)}, bf16[512,384]{1,0:T(8,128)(2,1)}, bf16[512,384]{1,0:T(8,128)(2,1)}) custom-call(s32[1]{0:T(128)} %bitcast.4.member_ref, bf16[144,1024]{1,0:T(8,128)(2,1)S(1)} %get-tuple-element.25.x_ref, bf16[144,1024]{1,0:T(8,128)(2,1)S(1)} %get-tuple-element.26.s_ref, bf16[144,384]{1,0:T(8,128)(2,1)S(1)} %copy-done.6, ...), custom_call_target="tpu_custom_call" | custom-call | flops 169869312 | bytes 2359296 | tf_op jit(solution)/shard_map/own_half/pallas_call | solution.py:475
Async XLA Ops:
  0.6 30.3 %copy-start.1 = (bf16[1,1024,384]{2,1,0:T(8,128)(2,1)S(1)}, bf16[1,1024,384]{2,1,0:T(8,128)(2,1)}, u32[]{:S(2)}) copy-start(bf16[1,1024,384]{2,1,0:T(8,128)(2,1)} %param.16) | copy-start | bytes 2359300
  0.6 30.3 %copy-start = (bf16[1,1024,384]{2,1,0:T(8,128)(2,1)S(1)}, bf16[1,1024,384]{2,1,0:T(8,128)(2,1)}, u32[]{:S(2)}) copy-start(bf16[1,1024,384]{2,1,0:T(8,128)(2,1)} %param.15) | copy-start | bytes 2359300
  2.4 5.5 %copy-start.3 = (s32[128,8]{1,0:T(8,128)}, s32[128,8]{1,0:T(8,128)S(1)}, u32[]{:S(2)}) copy-start(s32[128,8]{1,0:T(8,128)S(1)} %copy.17.ids_ref) | copy-start | bytes 12292
  3.2 0.9 %copy-start.12 = (bf16[128,1024]{1,0:T(8,128)(2,1)S(1)}, bf16[128,1024]{1,0:T(8,128)(2,1)}, u32[]{:S(2)}) copy-start(bf16[128,1024]{1,0:T(8,128)(2,1)} %tok_ref.1) | copy-start | bytes 786436
  4.1 0.9 %copy-start.13 = (bf16[128,1024]{1,0:T(8,128)(2,1)S(1)}, bf16[128,1024]{1,0:T(8,128)(2,1)}, u32[]{:S(2)}) copy-start(bf16[128,1024]{1,0:T(8,128)(2,1)} %cot_ref.1) | copy-start | bytes 786436
  5.1 0.7 %copy-start.14 = (s32[8]{0:T(128)S(1)}, s32[8]{0:T(128)}, u32[]{:S(2)}) copy-start(s32[8]{0:T(128)} %plan_ref.1) | copy-start | bytes 100
  7.8 23.1 %all-to-all-start = ((bf16[8,144,256]{2,1,0:T(8,128)(2,1)}), bf16[8,144,256]{2,1,0:T(8,128)(2,1)S(1)}, u32[]{:S(2)}, u32[]{:S(2)}) async-start(bf16[8,144,256]{2,1,0:T(8,128)(2,1)} %get-tuple-element.21), calls=%async_computation | async-start | bytes 1179648 | tf_op jit(solution)/shard_map/all_to_all | solution.py:518
  31.0 1.1 %copy-start.2 = (bf16[1,1024,384]{2,1,0:T(8,128)(2,1)S(1)}, bf16[1,1024,384]{2,1,0:T(8,128)(2,1)}, u32[]{:S(2)}) copy-start(bf16[1,1024,384]{2,1,0:T(8,128)(2,1)} %param.17) | copy-start | bytes 2359300
  33.7 0.8 %copy-start.5 = (bf16[144,384]{1,0:T(8,128)(2,1)}, bf16[144,384]{1,0:T(8,128)(2,1)S(1)}, u32[]{:S(2)}) copy-start(bf16[144,384]{1,0:T(8,128)(2,1)S(1)} %get-tuple-element.27.dg_ref) | copy-start | bytes 331780
  33.7 0.8 %copy-start.7 = (bf16[144,384]{1,0:T(8,128)(2,1)}, bf16[144,384]{1,0:T(8,128)(2,1)S(1)}, u32[]{:S(2)}) copy-start(bf16[144,384]{1,0:T(8,128)(2,1)S(1)} %get-tuple-element.28.du_ref) | copy-start | bytes 331780
  33.7 0.8 %copy-start.9 = (bf16[144,384]{1,0:T(8,128)(2,1)}, bf16[144,384]{1,0:T(8,128)(2,1)S(1)}, u32[]{:S(2)}) copy-start(bf16[144,384]{1,0:T(8,128)(2,1)S(1)} %get-tuple-element.29.hid_ref) | copy-start | bytes 331780
  33.7 0.8 %copy-start.11 = (bf16[8,80,256]{2,1,0:T(8,128)(2,1)}, bf16[8,80,256]{2,1,0:T(8,128)(2,1)S(1)}, u32[]{:S(2)}) copy-start(bf16[8,80,256]{2,1,0:T(8,128)(2,1)S(1)} %get-tuple-element.22) | copy-start | bytes 983044
  33.8 15.5 %copy-start.4 = (s32[128,8]{1,0:T(8,128)S(1)}, s32[128,8]{1,0:T(8,128)}, u32[]{:S(2)}) copy-start(s32[128,8]{1,0:T(8,128)} %copy-done.3) | copy-start | bytes 12292
  34.4 16.5 %collective-permute-start = (bf16[1536,384]{1,0:T(8,128)(2,1)S(1)}, bf16[1536,384]{1,0:T(8,128)(2,1)S(1)}, u32[]{:S(2)}, u32[]{:S(2)}) collective-permute-start(bf16[1536,384]{1,0:T(8,128)(2,1)S(1)} %other_half.1), channel_id=1, source_target_pairs={{0,1},{1,0},{2,3},{3,2},{4,5},{5,4},{6,7},{7,6},{8,9},{9,8},{10,11... | collective-permute-start | bytes 3538952 | tf_op jit(solution)/shard_map/ppermute | solution.py:547
  34.6 16.3 %copy-start.6 = (bf16[144,384]{1,0:T(8,128)(2,1)S(1)}, bf16[144,384]{1,0:T(8,128)(2,1)}, u32[]{:S(2)}) copy-start(bf16[144,384]{1,0:T(8,128)(2,1)} %copy-done.5) | copy-start | bytes 331780
  34.6 14.6 %all-to-all-start.1 = ((bf16[8,80,256]{2,1,0:T(8,128)(2,1)}), bf16[8,80,256]{2,1,0:T(8,128)(2,1)S(1)}, u32[]{:S(2)}, u32[]{:S(2)}) async-start(bf16[8,80,256]{2,1,0:T(8,128)(2,1)} %copy-done.11), calls=%async_computation.1 | async-start | bytes 655360 | tf_op jit(solution)/shard_map/all_to_all | solution.py:536
  50.9 0.9 %copy-start.8 = (bf16[144,384]{1,0:T(8,128)(2,1)S(1)}, bf16[144,384]{1,0:T(8,128)(2,1)}, u32[]{:S(2)}) copy-start(bf16[144,384]{1,0:T(8,128)(2,1)} %copy-done.7) | copy-start | bytes 331780
  51.8 0.9 %copy-start.10 = (bf16[144,384]{1,0:T(8,128)(2,1)S(1)}, bf16[144,384]{1,0:T(8,128)(2,1)}, u32[]{:S(2)}) copy-start(bf16[144,384]{1,0:T(8,128)(2,1)} %copy-done.9) | copy-start | bytes 331780
where the time goes:
time: 54.6 us; the launch traced here: 54.1 us
  waiting for transfers between devices  26.8 us (49%)
  starting transfers between devices  11.1 us (20%)
  local copies, waits for them, and re-layouts  8.75 us (16%)
  Pallas kernels  6.72 us (12%)
  between operations  0.74 us (1%)
    all_to_all x1, waiting for transfers between devices, per_device_moving_rows(): lax.all_to_all(send, 'expert', split_axis=0, concat_axis=0, tiled=True)  15.9 us
    all_to_all x1, waiting for transfers between devices, per_device_moving_rows(): lax.all_to_all(back, 'expert', split_axis=0, concat_axis=0, tiled=True)  10.9 us
    unnamed x34, local copies, waits for them, and re-layouts  8.75 us
    all_to_all x1, starting transfers between devices, per_device_moving_rows(): lax.all_to_all(send, 'expert', split_axis=0, concat_axis=0, tiled=True)  7.26 us
    pallas_call x5, Pallas kernels, local_call(): pl.pallas_call(kernel, out_shape=[jax.ShapeDtypeStruct(shape, kind) for s...  6.72 us
    all_to_all x1, starting transfers between devices, per_device_moving_rows(): lax.all_to_all(back, 'expert', split_axis=0, concat_axis=0, tiled=True)  3.77 us
  transfers between devices with their start and end apart: 3, of which 2 were waited for; matrix products, arithmetic and copies ran while one was open for 1% of the time, Pallas kernels for 2%

commit v1 on v0

--- a/solution.py
+++ b/solution.py
@@ -234,12 +234,13 @@
 F32 = jnp.float32
 CONTRACT_ROWS = (((0,), (0,)), ((), ()))
 CONTRACT_COLS = (((1,), (1,)), ((), ()))
-VMEM_LIMIT = 40 * 1024 * 1024
+MIB = 1024 * 1024
 
 MAIN = 16
 QUARTERS = 4
 SEND_ROWS = 2 * QUARTERS * MAIN + 16
 BACK_ROWS = QUARTERS * MAIN + 16
+FAR_FIRST = (4, 5, 6, 7, 1, 2, 3)
 
 
 def copies_of(experts):
@@ -250,8 +251,8 @@
     return lax.broadcasted_iota(jnp.int32, shape, axis)
 
 
-def flip(values, eye):
-    return lax.dot_general(values.astype(BF), eye, CONTRACT_ROWS, preferred_element_type=F32)
+def mask(condition):
+    return condition.astype(F32).astype(BF)
 
 
 def repeat_rows(table, times):
@@ -261,17 +262,38 @@
     )
 
 
-def route_kernel(plan_ref, ids_ref, pick_ref, gate_ref, tok_ref, cot_ref, send_ref, slot_ref, gates_ref):
-    tokens, topk = ids_ref.shape
-    experts = send_ref.shape[0]
+def route_kernel(plan_hbm, ids_hbm, pick_hbm, gate_hbm, tok_hbm, cot_hbm, *refs):
+    sems = refs[-1]
+    plan_ref, ids_ref, pick_ref, gate_ref, tok_ref, cot_ref = refs[-7:-1]
+    slot_ref, gates_ref = refs[-9:-7]
+    send_refs = refs[:-9]
+    topk, tokens = ids_ref.shape
+    experts = len(send_refs)
     width = tok_ref.shape[1] // QUARTERS
     copies = copies_of(experts)
-    eye = (iota((tokens, tokens), 0) == iota((tokens, tokens), 1)).astype(BF)
-    before = (iota((tokens, tokens), 0) < iota((tokens, tokens), 1)).astype(BF)
-    ids = flip(ids_ref[...].astype(F32), eye).astype(jnp.int32)
-    pick = flip(pick_ref[...].astype(F32), eye).astype(jnp.int32)
-    gate = flip(gate_ref[...], eye)
-    expert_row = iota((experts, tokens), 0)
+    loads = [
+        pltpu.make_async_copy(source, place, sems.at[n])
+        for n, (source, place) in enumerate(
+            (
+                (plan_hbm, plan_ref),
+                (ids_hbm, ids_ref),
+                (pick_hbm, pick_ref),
+                (gate_hbm, gate_ref),
+                (tok_hbm, tok_ref),
+                (cot_hbm, cot_ref),
+            )
+        )
+    ]
+    for load in loads:
+        load.start()
+    before = mask(iota((tokens, tokens), 0) < iota((tokens, tokens), 1))
+    me = lax.axis_index("expert")
+    expert_row = jnp.bitwise_xor(iota((experts, tokens), 0), me)
+    for load in loads[:4]:
+        load.wait()
+    ids = ids_ref[...]
+    pick = pick_ref[...]
+    gate = gate_ref[...].astype(F32)
     named = jnp.zeros((experts, tokens), jnp.int32)
     gates = jnp.zeros((experts, tokens), F32)
     for k in range(topk):
@@ -293,27 +315,23 @@
     gates_ref[...] = gates
     slot16 = repeat_rows(slot, MAIN)
     gate16 = repeat_rows(gates, MAIN)
-    lane_row = jnp.bitwise_and(iota(slot16.shape, 0), MAIN - 1)
-    onehot = (slot16 == lane_row).astype(F32)
+    inner = jnp.bitwise_and(iota(slot16.shape, 0), MAIN - 1)
+    onehot = (slot16 == inner).astype(F32)
+    wanted = MAIN + jnp.bitwise_and(jnp.right_shift(inner, 2), 1)
+    last = (slot16 == wanted).astype(F32)
+    last_rows = jnp.where(inner >= 8, 0.0, last)
+    last_scaled = jnp.where(inner >= 8, last * gate16, 0.0)
+    quarter = jnp.bitwise_and(inner, 3)
+    for load in loads[4:]:
+        load.wait()
     rows = jnp.dot(onehot.astype(BF), tok_ref[...], preferred_element_type=F32).astype(BF)
     scaled = jnp.dot(
         (onehot * gate16).astype(BF), cot_ref[...], preferred_element_type=F32
     ).astype(BF)
-    for e in range(experts):
-        for q in range(QUARTERS):
-            here = slice(e * MAIN, (e + 1) * MAIN)
-            cols = slice(q * width, (q + 1) * width)
-            send_ref[e, q * MAIN : (q + 1) * MAIN, :] = rows[here, cols]
-            send_ref[e, (QUARTERS + q) * MAIN : (QUARTERS + q + 1) * MAIN, :] = scaled[here, cols]
-    wanted = MAIN + jnp.bitwise_and(jnp.right_shift(lane_row, 2), 1)
-    is_scaled = lane_row >= 8
-    last = (slot16 == wanted).astype(F32)
-    last_rows = jnp.where(is_scaled, 0.0, last)
-    last_scaled = jnp.where(is_scaled, last * gate16, 0.0)
     tail = jnp.zeros((experts * MAIN, width), F32)
     for q in range(QUARTERS):
-        mine = jnp.bitwise_and(lane_row, 3) == q
         cols = slice(q * width, (q + 1) * width)
+        mine = quarter == q
         tail += jnp.dot(
             jnp.where(mine, last_rows, 0.0).astype(BF), tok_ref[:, cols], preferred_element_type=F32
         )
@@ -323,32 +341,39 @@
             preferred_element_type=F32,
         )
     tail = tail.astype(BF)
-    for e in range(experts):
-        send_ref[e, 2 * QUARTERS * MAIN :, :] = tail[e * MAIN : (e + 1) * MAIN]
-
-
-def expert_kernel(
-    recv_ref, gate_ref, up_ref, down_ref, back_ref, x_ref, s_ref, dg_ref, du_ref, hid_ref
-):
-    experts, unused, width = recv_ref.shape
+    for k in range(experts):
+        here = slice(k * MAIN, (k + 1) * MAIN)
+        for q in range(QUARTERS):
+            cols = slice(q * width, (q + 1) * width)
+            send_refs[k][q * MAIN : (q + 1) * MAIN, :] = rows[here, cols]
+            send_refs[k][(QUARTERS + q) * MAIN : (QUARTERS + q + 1) * MAIN, :] = scaled[here, cols]
+        send_refs[k][2 * QUARTERS * MAIN :, :] = tail[here]
+
+
+def expert_kernel(*refs):
+    back_count = len(refs) - 8
+    experts = back_count // 2
+    recv_refs = refs[:experts]
+    gate_ref, up_ref, down_ref = refs[experts : experts + 3]
+    back_refs = refs[experts + 3 : 2 * experts + 3]
+    x_ref, s_ref, dg_ref, du_ref, hid_ref = refs[2 * experts + 3 :]
+    width = recv_refs[0].shape[1]
     main_rows = experts * MAIN
-    tail = jnp.concatenate([recv_ref[i, 2 * QUARTERS * MAIN :, :] for i in range(experts)], axis=0)
+    tail = jnp.concatenate([ref[2 * QUARTERS * MAIN :, :] for ref in recv_refs], axis=0)
     row = iota((4 * experts, main_rows), 0)
     col = iota((4 * experts, main_rows), 1)
     kind = (row >= 2 * experts).astype(jnp.int32)
-    sender = jnp.right_shift(row - kind * 2 * experts, 1)
-    base = sender * MAIN + kind * 8 + jnp.bitwise_and(row, 1) * 4
+    chunk = jnp.right_shift(row - kind * 2 * experts, 1)
+    base = chunk * MAIN + kind * 8 + jnp.bitwise_and(row, 1) * 4
     for q in range(QUARTERS):
         cols = slice(q * width, (q + 1) * width)
-        picked = jnp.dot(
-            (col == base + q).astype(F32).astype(BF), tail, preferred_element_type=F32
-        ).astype(BF)
+        picked = jnp.dot(mask(col == base + q), tail, preferred_element_type=F32).astype(BF)
         x_ref[main_rows:, cols] = picked[: 2 * experts]
         s_ref[main_rows:, cols] = picked[2 * experts :]
-        for i in range(experts):
+        for i, ref in enumerate(recv_refs):
             here = slice(i * MAIN, (i + 1) * MAIN)
-            x_ref[here, cols] = recv_ref[i, q * MAIN : (q + 1) * MAIN, :]
-            s_ref[here, cols] = recv_ref[i, (QUARTERS + q) * MAIN : (QUARTERS + q + 1) * MAIN, :]
+            x_ref[here, cols] = ref[q * MAIN : (q + 1) * MAIN, :]
+            s_ref[here, cols] = ref[(QUARTERS + q) * MAIN : (QUARTERS + q + 1) * MAIN, :]
     rows = x_ref[...]
     gate_pre = jnp.dot(rows, gate_ref[...], preferred_element_type=F32)
     up_pre = jnp.dot(rows, up_ref[...], preferred_element_type=F32)
@@ -385,12 +410,12 @@
     for q in range(QUARTERS):
         cols = slice(q * width, (q + 1) * width)
         mine = jnp.logical_and(jnp.bitwise_and(inner, 3) == q, inner < 8)
-        place = jnp.logical_and(mine, tcol == source).astype(F32).astype(BF)
+        place = mask(jnp.logical_and(mine, tcol == source))
         spread += jnp.dot(place, grad[main_rows:, cols], preferred_element_type=F32)
-        for i in range(experts):
-            back_ref[i, q * MAIN : (q + 1) * MAIN, :] = grad[i * MAIN : (i + 1) * MAIN, cols]
-    for i in range(experts):
-        back_ref[i, QUARTERS * MAIN :, :] = jnp.concatenate(
+        for i, ref in enumerate(back_refs):
+            ref[q * MAIN : (q + 1) * MAIN, :] = grad[i * MAIN : (i + 1) * MAIN, cols]
+    for i, ref in enumerate(back_refs):
+        ref[QUARTERS * MAIN :, :] = jnp.concatenate(
             [spread[i * MAIN : i * MAIN + 8], gate_lanes], axis=0
         ).astype(BF)
 
@@ -407,80 +432,86 @@
     )
 
 
-def other_half_kernel(member_ref, x_ref, s_ref, dg_ref, du_ref, hid_ref, out_ref):
-    parts = grads_of(1 - member_ref[0], x_ref, s_ref, dg_ref, du_ref, hid_ref)
+def other_half_kernel(x_ref, s_ref, dg_ref, du_ref, hid_ref, out_ref):
+    half = 1 - lax.axis_index("replica")
+    parts = grads_of(half, x_ref, s_ref, dg_ref, du_ref, hid_ref)
     rows = parts[0].shape[0]
     for n in range(3):
         out_ref[n * rows : (n + 1) * rows, :] = parts[n].astype(BF)
 
 
 def own_half_kernel(
-    member_ref, x_ref, s_ref, dg_ref, du_ref, hid_ref, came_ref, gate_ref, up_ref, down_ref
+    x_ref, s_ref, dg_ref, du_ref, hid_ref, came_ref, gate_ref, up_ref, down_ref
 ):
-    parts = grads_of(member_ref[0], x_ref, s_ref, dg_ref, du_ref, hid_ref)
+    parts = grads_of(lax.axis_index("replica"), x_ref, s_ref, dg_ref, du_ref, hid_ref)
     rows = parts[0].shape[0]
     for n, out_ref in enumerate((gate_ref, up_ref, down_ref)):
         came = came_ref[n * rows : (n + 1) * rows, :].astype(F32)
         out_ref[...] = (parts[n].astype(BF).astype(F32) + came).astype(BF)
 
 
-def combine_kernel(me_ref, ids_ref, slot_ref, gates_ref, ret_ref, token_ref, grad_ref):
-    tokens, topk = ids_ref.shape
-    experts, unused, width = ret_ref.shape
-    eye = (iota((tokens, tokens), 0) == iota((tokens, tokens), 1)).astype(BF)
-    ids = flip(ids_ref[...].astype(F32), eye).astype(jnp.int32)
+def combine_kernel(ids_ref, slot_ref, gates_ref, *refs):
+    token_ref, grad_ref = refs[-2:]
+    ret_refs = refs[:-2]
+    topk, tokens = ids_ref.shape
+    experts = len(ret_refs)
+    width = ret_refs[0].shape[1]
+    ids = ids_ref[...]
     slot = slot_ref[...]
     slot16 = repeat_rows(slot, MAIN)
-    lane_row = jnp.bitwise_and(iota(slot16.shape, 0), MAIN - 1)
-    onehot = (slot16 == lane_row).astype(F32).astype(BF)
-    wanted = MAIN + jnp.right_shift(lane_row, 2)
-    last = jnp.where(jnp.logical_and(slot16 == wanted, lane_row < 8), 1.0, 0.0)
-    tail = jnp.concatenate([ret_ref[e, QUARTERS * MAIN :, :] for e in range(experts)], axis=0)
+    inner = jnp.bitwise_and(iota(slot16.shape, 0), MAIN - 1)
+    onehot = mask(slot16 == inner)
+    wanted = MAIN + jnp.right_shift(inner, 2)
+    last = jnp.where(jnp.logical_and(slot16 == wanted, inner < 8), 1.0, 0.0)
+    quarter = jnp.bitwise_and(inner, 3)
+    tail = jnp.concatenate([ref[QUARTERS * MAIN :, :] for ref in ret_refs], axis=0)
     for q in range(QUARTERS):
-        cols = slice(q * width, (q + 1) * width)
-        main = jnp.concatenate(
-            [ret_ref[e, q * MAIN : (q + 1) * MAIN, :] for e in range(experts)], axis=0
-        )
-        mine = jnp.bitwise_and(lane_row, 3) == q
-        place = jnp.where(mine, last, 0.0).astype(BF)
+        main = jnp.concatenate([ref[q * MAIN : (q + 1) * MAIN, :] for ref in ret_refs], axis=0)
+        place = jnp.where(quarter == q, last, 0.0).astype(BF)
         total = lax.dot_general(onehot, main, CONTRACT_ROWS, preferred_element_type=F32)
         total += lax.dot_general(place, tail, CONTRACT_ROWS, preferred_element_type=F32)
-        token_ref[:, cols] = total.astype(BF)
-    me = me_ref[0]
-    lane = jnp.where(slot < MAIN, me * MAIN + slot, experts * MAIN + 2 * me + slot - MAIN)
-    lane = jnp.where(slot < 0, -1, lane)
+        token_ref[:, q * width : (q + 1) * width] = total.astype(BF)
     lane_index = iota((width, tokens), 0)
     found = []
-    for e in range(experts):
-        pick = (lane_index == lane[e : e + 1]).astype(F32).astype(BF)
-        mine = jnp.dot(ret_ref[e, QUARTERS * MAIN :, :], pick, preferred_element_type=F32)
-        found.append(mine[8:9])
+    for k, ref in enumerate(ret_refs):
+        mine = slot[k : k + 1]
+        lane = jnp.where(mine < MAIN, k * MAIN + mine, experts * MAIN + 2 * k + mine - MAIN)
+        lane = jnp.where(mine < 0, -1, lane)
+        sums = jnp.dot(
+            ref[QUARTERS * MAIN :, :], mask(lane_index == lane), preferred_element_type=F32
+        )
+        found.append(sums[8:9])
     found = jnp.concatenate(found, axis=0)
     kept = slot >= 0
     grads = jnp.where(kept, found / jnp.where(kept, gates_ref[...], 1.0), 0.0)
-    expert_row = iota((experts, tokens), 0)
+    expert_row = jnp.bitwise_xor(iota((experts, tokens), 0), lax.axis_index("expert"))
     by_choice = [
         jnp.sum(jnp.where(expert_row == ids[k : k + 1], grads, 0.0), axis=0, keepdims=True)
         for k in range(topk)
     ]
-    by_choice = jnp.concatenate(by_choice, axis=0).astype(BF)
-    grad_ref[...] = lax.dot_general(
-        eye, by_choice, CONTRACT_COLS, preferred_element_type=F32
-    ).astype(BF)
-
-
-def local_call(kernel, outs, scalars, arrays, name, flops, moved):
-    smem = pl.BlockSpec(memory_space=pltpu.SMEM)
+    grad_ref[...] = jnp.concatenate(by_choice, axis=0).astype(BF)
+
+
+def local_call(kernel, outs, arrays, name, flops, moved, space=pltpu.VMEM, scratch=(), limit=16):
     vmem = pl.BlockSpec(memory_space=pltpu.VMEM)
     return pl.pallas_call(
         kernel,
         out_shape=[jax.ShapeDtypeStruct(shape, kind) for shape, kind in outs],
-        in_specs=[smem] * len(scalars) + [vmem] * len(arrays),
+        in_specs=[pl.BlockSpec(memory_space=space)] * len(arrays),
         out_specs=[vmem] * len(outs),
-        compiler_params=pltpu.CompilerParams(vmem_limit_bytes=VMEM_LIMIT),
+        scratch_shapes=list(scratch),
+        compiler_params=pltpu.CompilerParams(vmem_limit_bytes=limit * MIB),
         cost_estimate=pl.CostEstimate(flops=flops, bytes_accessed=moved, transcendentals=0),
         name=name,
-    )(*scalars, *arrays)
+    )(*arrays)
+
+
+def exchange(chunks):
+    count = len(chunks)
+    came = list(chunks)
+    for k in FAR_FIRST:
+        came[k] = lax.ppermute(chunks[k], "expert", [(i, i ^ k) for i in range(count)])
+    return came
 
 
 def per_device_moving_rows(
@@ -500,46 +531,47 @@
     hidden_width = gate_proj.shape[2]
     width = model_width // QUARTERS
     served = experts * (MAIN + 2)
-    me = lax.axis_index("expert").reshape(1).astype(jnp.int32)
-    member = lax.axis_index("replica").reshape(1).astype(jnp.int32)
-    send, slot, gates = local_call(
+    small = (topk, token_count)
+    routed = local_call(
         route_kernel,
-        [
-            ((experts, SEND_ROWS, width), BF),
-            ((experts, token_count), jnp.int32),
-            ((experts, token_count), F32),
-        ],
-        [replica_plan],
-        [expert_ids, replica_pick, gate_values, tokens, cotangent],
+        [((SEND_ROWS, width), BF)] * experts
+        + [((experts, token_count), jnp.int32), ((experts, token_count), F32)],
+        [replica_plan, expert_ids.T, replica_pick.T, gate_values.T, tokens, cotangent],
         "route",
         2 * 2 * served * token_count * model_width,
         2 * 2 * (token_count + served) * model_width,
-    )
-    recv = lax.all_to_all(send, "expert", split_axis=0, concat_axis=0, tiled=True)
+        space=pltpu.HBM,
+        limit=58,
+        scratch=[
+            pltpu.SMEM((experts,), jnp.int32),
+            pltpu.VMEM(small, jnp.int32),
+            pltpu.VMEM(small, jnp.int32),
+            pltpu.VMEM(small, BF),
+            pltpu.VMEM(tokens.shape, BF),
+            pltpu.VMEM(tokens.shape, BF),
+            pltpu.SemaphoreType.DMA((6,)),
+        ],
+    )
+    slot, gates = routed[experts:]
+    recv = exchange(routed[:experts])
     matmul = 2 * served * model_width * hidden_width
-    back, x_rows, s_rows, gate_delta, up_delta, hidden = local_call(
+    outs = local_call(
         expert_kernel,
-        [
-            ((experts, BACK_ROWS, width), BF),
-            ((served, model_width), BF),
-            ((served, model_width), BF),
-            ((served, hidden_width), BF),
-            ((served, hidden_width), BF),
-            ((served, hidden_width), BF),
-        ],
-        [],
-        [recv, gate_proj[0], up_proj[0], down_proj[0]],
+        [((BACK_ROWS, width), BF)] * experts
+        + [((served, model_width), BF)] * 2
+        + [((served, hidden_width), BF)] * 3,
+        [*recv, gate_proj[0], up_proj[0], down_proj[0]],
         "expert_rows",
         5 * matmul,
         2 * 3 * model_width * hidden_width,
     )
-    returned = lax.all_to_all(back, "expert", split_axis=0, concat_axis=0, tiled=True)
+    factors = outs[experts:]
+    returned = exchange(outs[:experts])
     half = model_width // 2
     (leaving,) = local_call(
         other_half_kernel,
         [((3 * half, hidden_width), BF)],
-        [member],
-        [x_rows, s_rows, gate_delta, up_delta, hidden],
+        factors,
         "other_half",
         3 * matmul // 2,
         2 * 3 * half * hidden_width,
@@ -548,22 +580,21 @@
     shares = local_call(
         own_half_kernel,
         [((half, hidden_width), BF)] * 3,
-        [member],
-        [x_rows, s_rows, gate_delta, up_delta, hidden, came],
+        [*factors, came],
         "own_half",
         3 * matmul // 2,
         2 * 2 * 3 * half * hidden_width,
     )
+    returned, shares = lax.optimization_barrier((returned, shares))
     token_grad, gate_grad = local_call(
         combine_kernel,
-        [((token_count, model_width), BF), ((token_count, topk), BF)],
-        [me],
-        [expert_ids, slot, gates, returned],
+        [((token_count, model_width), BF), ((topk, token_count), BF)],
+        [expert_ids.T, slot, gates, *returned],
         "combine",
         2 * served * token_count * model_width,
         2 * 2 * token_count * model_width,
     )
-    return (token_grad, gate_grad, shares[0][None], shares[1][None], shares[2][None])
+    return (token_grad, gate_grad.T, shares[0][None], shares[1][None], shares[2][None])
 
 
 def per_device(tokens, cotangent, expert_ids, gate_values, replica_pick, replica_plan, *matrices):

time: 54.6 us -> 47.5 us (0.87)
  waiting for transfers between devices: 26.8 us -> 9.78 us
  starting transfers between devices: 11.1 us -> 25.4 us
  local copies, waits for them, and re-layouts: 8.75 us -> 4.3 us
    all_to_all x2 -> x0, waiting for transfers between devices: 26.8 us -> none  [the longest x1 15.9 us: per_device_moving_rows(): lax.all_to_all(send, 'expert', split_axis=0, concat_axis=0, tiled=True)]
    ppermute x0 -> x14, starting transfers between devices: none -> 25.3 us  [exchange(): lax.ppermute(chunks[k], 'expert', [(i, i ^ k) for i in range(count)])]
    all_to_all x2 -> x0, starting transfers between devices: 11 us -> none  [the longest x1 7.26 us: per_device_moving_rows(): lax.all_to_all(send, 'expert', split_axis=0, concat_axis=0, tiled=True)]
    ppermute x0 -> x14, waiting for transfers between devices: none -> 9.77 us  [exchange(): lax.ppermute(chunks[k], 'expert', [(i, i ^ k) for i in range(count)])]
    unnamed x34 -> x14, local copies, waits for them, and re-layouts: 8.75 us -> 4.3 us
  transfers between devices with their start and end apart: 3 -> 15, of which waited for: 2 -> 3; matrix products, arithmetic and copies ran while one was open for 1% -> 0% of each run, Pallas kernels for 2% -> 3%
where the time goes in v1:
time: 47.5 us; the launch traced here: 47.2 us
  starting transfers between devices  25.4 us (53%)
  waiting for transfers between devices  9.78 us (21%)
  Pallas kernels  7.01 us (15%)
  local copies, waits for them, and re-layouts  4.3 us (9%)
  between operations  0.71 us (1%)
    ppermute x14, starting transfers between devices, exchange(): lax.ppermute(chunks[k], 'expert', [(i, i ^ k) for i in range(count)])  25.3 us
    ppermute x14, waiting for transfers between devices, exchange(): lax.ppermute(chunks[k], 'expert', [(i, i ^ k) for i in range(count)])  9.77 us
    pallas_call x5, Pallas kernels, local_call(): pl.pallas_call(kernel, out_shape=[jax.ShapeDtypeStruct(shape, kind) for s...  7.01 us
    unnamed x14, local copies, waits for them, and re-layouts  4.3 us
  transfers between devices with their start and end apart: 15, of which 3 were waited for; matrix products, arithmetic and copies ran while one was open for 0% of the time, Pallas kernels for 3%

profile of v1, /device:TPU:0, one launch (start us, length us, event | category | flops | bytes accessed | tf_op | source)
XLA Modules:
  0.0 47.2 jit_solution(7151114391031809520)
XLA Ops:
  0.6 2.3 %route.1 = (bf16[144,256]{1,0:T(8,128)(2,1)}, bf16[144,256]{1,0:T(8,128)(2,1)}, bf16[144,256]{1,0:T(8,128)(2,1)}, bf16[144,256]{1,0:T(8,128)(2,1)}, bf16[144,256...) custom-call(s32[8]{0:T(128)} %plan_hbm.1, ...), custom_call_target="tpu_custom_call" | custom-call | flops 75497472 | bytes 1114112 | tf_op jit(solution)/shard_map/route/pallas_call | solution.py:497
  3.0 3.0 %collective-permute-start = (bf16[144,256]{1,0:T(8,128)(2,1)}, bf16[144,256]{1,0:T(8,128)(2,1)S(1)}, u32[]{:S(2)}, u32[]{:S(2)}) collective-permute-start(bf16[144,256]{1,0:T(8,128)(2,1)} %get-tuple-element.47), channel_id=1, source_target_pairs={{0,2},{2,0},{4,6},{6,4},{8,10},{10,8},{12,14},{14,12},{1,3},{3,1},... | collective-permute-start | bytes 221192 | tf_op jit(solution)/shard_map/ppermute | solution.py:513
  6.0 1.6 %collective-permute-start.1 = (bf16[144,256]{1,0:T(8,128)(2,1)}, bf16[144,256]{1,0:T(8,128)(2,1)S(1)}, u32[]{:S(2)}, u32[]{:S(2)}) collective-permute-start(bf16[144,256]{1,0:T(8,128)(2,1)} %get-tuple-element.48), channel_id=1, source_target_pairs={{0,4},{2,6},{4,0},{6,2},{8,12},{10,14},{12,8},{14,10},{1,5},{3,7},... | collective-permute-start | bytes 221192 | tf_op jit(solution)/shard_map/ppermute | solution.py:513
  7.6 0.0 collective-permute-start.2
  7.6 3.0 %collective-permute-start.3 = (bf16[144,256]{1,0:T(8,128)(2,1)}, bf16[144,256]{1,0:T(8,128)(2,1)S(1)}, u32[]{:S(2)}, u32[]{:S(2)}) collective-permute-start(bf16[144,256]{1,0:T(8,128)(2,1)} %get-tuple-element.50), channel_id=1, source_target_pairs={{0,8},{2,10},{4,12},{6,14},{8,0},{10,2},{12,4},{14,6},{1,9},{3,11}... | collective-permute-start | bytes 221192 | tf_op jit(solution)/shard_map/ppermute | solution.py:513
  10.6 1.3 %collective-permute-start.4 = (bf16[144,256]{1,0:T(8,128)(2,1)}, bf16[144,256]{1,0:T(8,128)(2,1)S(1)}, u32[]{:S(2)}, u32[]{:S(2)}) collective-permute-start(bf16[144,256]{1,0:T(8,128)(2,1)} %get-tuple-element.51), channel_id=1, source_target_pairs={{0,10},{2,8},{4,14},{6,12},{8,2},{10,0},{12,6},{14,4},{1,11},{3,9}... | collective-permute-start | bytes 221192 | tf_op jit(solution)/shard_map/ppermute | solution.py:513
  11.8 0.0 collective-permute-done.refs_1_
  11.8 3.6 %collective-permute-start.5 = (bf16[144,256]{1,0:T(8,128)(2,1)}, bf16[144,256]{1,0:T(8,128)(2,1)S(1)}, u32[]{:S(2)}, u32[]{:S(2)}) collective-permute-start(bf16[144,256]{1,0:T(8,128)(2,1)} %get-tuple-element.52), channel_id=1, source_target_pairs={{0,12},{2,14},{4,8},{6,10},{8,4},{10,6},{12,0},{14,2},{1,13},{3,15... | collective-permute-start | bytes 221192 | tf_op jit(solution)/shard_map/ppermute | solution.py:513
  15.4 0.0 collective-permute-done.1.refs_2_
  15.4 0.0 collective-permute-start.6
  15.5 0.0 collective-permute-done.2.refs_3_
  15.5 0.0 collective-permute-done.3.refs_4_
  15.5 6.5 %collective-permute-done.4.refs_5_ = bf16[144,256]{1,0:T(8,128)(2,1)S(1)} collective-permute-done((bf16[144,256]{1,0:T(8,128)(2,1)}, bf16[144,256]{1,0:T(8,128)(2,1)S(1)}, u32[]{:S(2)}, u32[]{:S(2)}) %collective-permute-start.4) | collective-permute-done | bytes 73760 | tf_op jit(solution)/shard_map/ppermute | solution.py:513
  22.0 0.0 collective-permute-done.5.refs_6_
  22.0 0.8 %collective-permute-done.6.refs_7_ = bf16[144,256]{1,0:T(8,128)(2,1)S(1)} collective-permute-done((bf16[144,256]{1,0:T(8,128)(2,1)}, bf16[144,256]{1,0:T(8,128)(2,1)S(1)}, u32[]{:S(2)}, u32[]{:S(2)}) %collective-permute-start.6) | collective-permute-done | bytes 73760 | tf_op jit(solution)/shard_map/ppermute | solution.py:513
  22.8 0.0 copy-start
  22.8 1.1 %copy-done = bf16[1,1024,384]{2,1,0:T(8,128)(2,1)S(1)} copy-done((bf16[1,1024,384]{2,1,0:T(8,128)(2,1)S(1)}, bf16[1,1024,384]{2,1,0:T(8,128)(2,1)}, u32[]{:S(2)}) %copy-start) | copy-done | bytes 786456
  23.9 0.0 copy-start.1
  23.9 1.1 %copy-done.1 = bf16[1,1024,384]{2,1,0:T(8,128)(2,1)S(1)} copy-done((bf16[1,1024,384]{2,1,0:T(8,128)(2,1)S(1)}, bf16[1,1024,384]{2,1,0:T(8,128)(2,1)}, u32[]{:S(2)}) %copy-start.1) | copy-done | bytes 786456
  25.1 0.0 copy-start.2
  25.1 1.1 %copy-done.2 = bf16[1,1024,384]{2,1,0:T(8,128)(2,1)S(1)} copy-done((bf16[1,1024,384]{2,1,0:T(8,128)(2,1)S(1)}, bf16[1,1024,384]{2,1,0:T(8,128)(2,1)}, u32[]{:S(2)}) %copy-start.2) | copy-done | bytes 786456
  26.2 0.9 %copy-done.3 = bf16[144,256]{1,0:T(8,128)(2,1)S(1)} copy-done((bf16[144,256]{1,0:T(8,128)(2,1)S(1)}, bf16[144,256]{1,0:T(8,128)(2,1)}, u32[]{:S(2)}) %copy-start.3) | copy-done | bytes 73752
  27.1 1.6 %expert_rows.1 = (bf16[80,256]{1,0:T(8,128)(2,1)S(1)}, bf16[80,256]{1,0:T(8,128)(2,1)S(1)}, bf16[80,256]{1,0:T(8,128)(2,1)S(1)}, bf16[80,256]{1,0:T(8,128)(2,1)S...) custom-call(bf16[144,256]{1,0:T(8,128)(2,1)S(1)} %copy-done.3, ...), custom_call_target="tpu_custom_call" | custom-call | flops 566231040 | bytes 2359296 | tf_op jit(solution)/shard_map/expert_rows/pallas_call | solution.py:497
  28.7 0.6 %other_half.1 = bf16[1536,384]{1,0:T(8,128)(2,1)S(1)} custom-call(bf16[144,1024]{1,0:T(8,128)(2,1)S(1)} %get-tuple-element.62.x_ref, bf16[144,1024]{1,0:T(8,128)(2,1)S(1)} %get-tuple-element.63.s_ref, bf16[144,384]{1,0:T(8,128)(2,1)S(1)} %get-tuple-element.64.dg_ref, bf16[144,384]{1,0:T(8,128)(2,1)S(1)} %get-tuple-element.65.du_ref, ...), custom_call_target="tpu_custom_call" | custom-call | flops 169869312 | bytes 1179648 | tf_op jit(solution)/shard_map/other_half/pallas_call | solution.py:497
  29.4 0.0 copy-start.4
  29.4 0.0 copy-start.5
  29.4 0.0 copy-start.6
  29.4 0.1 collective-permute-start.14
  29.5 0.8 %collective-permute-start.7 = (bf16[80,256]{1,0:T(8,128)(2,1)S(1)}, bf16[80,256]{1,0:T(8,128)(2,1)S(1)}, u32[]{:S(2)}, u32[]{:S(2)}) collective-permute-start(bf16[80,256]{1,0:T(8,128)(2,1)S(1)} %get-tuple-element.55), channel_id=1, source_target_pairs={{0,2},{2,0},{4,6},{6,4},{8,10},{10,8},{12,14},{14,12},{1,3},{3,1},... | collective-permute-start | bytes 122888 | tf_op jit(solution)/shard_map/ppermute | solution.py:513
  30.3 3.0 %collective-permute-start.8 = (bf16[80,256]{1,0:T(8,128)(2,1)S(1)}, bf16[80,256]{1,0:T(8,128)(2,1)S(1)}, u32[]{:S(2)}, u32[]{:S(2)}) collective-permute-start(bf16[80,256]{1,0:T(8,128)(2,1)S(1)} %get-tuple-element.56), channel_id=1, source_target_pairs={{0,4},{2,6},{4,0},{6,2},{8,12},{10,14},{12,8},{14,10},{1,5},{3,7},... | collective-permute-start | bytes 122888 | tf_op jit(solution)/shard_map/ppermute | solution.py:513
  33.3 0.6 %collective-permute-start.9 = (bf16[80,256]{1,0:T(8,128)(2,1)S(1)}, bf16[80,256]{1,0:T(8,128)(2,1)S(1)}, u32[]{:S(2)}, u32[]{:S(2)}) collective-permute-start(bf16[80,256]{1,0:T(8,128)(2,1)S(1)} %get-tuple-element.57), channel_id=1, source_target_pairs={{0,6},{2,4},{4,2},{6,0},{8,14},{10,12},{12,10},{14,8},{1,7},{3,5},... | collective-permute-start | bytes 122888 | tf_op jit(solution)/shard_map/ppermute | solution.py:513
  33.9 3.1 %collective-permute-start.10 = (bf16[80,256]{1,0:T(8,128)(2,1)S(1)}, bf16[80,256]{1,0:T(8,128)(2,1)S(1)}, u32[]{:S(2)}, u32[]{:S(2)}) collective-permute-start(bf16[80,256]{1,0:T(8,128)(2,1)S(1)} %get-tuple-element.58), channel_id=1, source_target_pairs={{0,8},{2,10},{4,12},{6,14},{8,0},{10,2},{12,4},{14,6},{1,9},{3,11}... | collective-permute-start | bytes 122888 | tf_op jit(solution)/shard_map/ppermute | solution.py:513
  37.1 0.0 collective-permute-done.7.refs_1_
  37.1 0.5 %collective-permute-start.11 = (bf16[80,256]{1,0:T(8,128)(2,1)S(1)}, bf16[80,256]{1,0:T(8,128)(2,1)S(1)}, u32[]{:S(2)}, u32[]{:S(2)}) collective-permute-start(bf16[80,256]{1,0:T(8,128)(2,1)S(1)} %get-tuple-element.59), channel_id=1, source_target_pairs={{0,10},{2,8},{4,14},{6,12},{8,2},{10,0},{12,6},{14,4},{1,11},{3,9}... | collective-permute-start | bytes 122888 | tf_op jit(solution)/shard_map/ppermute | solution.py:513
  37.6 0.0 collective-permute-done.8.refs_2_
  37.6 1.9 %collective-permute-start.12 = (bf16[80,256]{1,0:T(8,128)(2,1)S(1)}, bf16[80,256]{1,0:T(8,128)(2,1)S(1)}, u32[]{:S(2)}, u32[]{:S(2)}) collective-permute-start(bf16[80,256]{1,0:T(8,128)(2,1)S(1)} %get-tuple-element.60), channel_id=1, source_target_pairs={{0,12},{2,14},{4,8},{6,10},{8,4},{10,6},{12,0},{14,2},{1,13},{3,15... | collective-permute-start | bytes 122888 | tf_op jit(solution)/shard_map/ppermute | solution.py:513
  39.5 0.0 collective-permute-done.14.came_ref
  39.5 2.9 %collective-permute-start.13 = (bf16[80,256]{1,0:T(8,128)(2,1)S(1)}, bf16[80,256]{1,0:T(8,128)(2,1)S(1)}, u32[]{:S(2)}, u32[]{:S(2)}) collective-permute-start(bf16[80,256]{1,0:T(8,128)(2,1)S(1)} %get-tuple-element.61), channel_id=1, source_target_pairs={{0,14},{2,12},{4,10},{6,8},{8,6},{10,4},{12,2},{14,0},{1,15},{3,13... | collective-permute-start | bytes 122888 | tf_op jit(solution)/shard_map/ppermute | solution.py:513
  42.3 1.4 %own_half.1 = (bf16[512,384]{1,0:T(8,128)(2,1)}, bf16[512,384]{1,0:T(8,128)(2,1)}, bf16[512,384]{1,0:T(8,128)(2,1)}) custom-call(bf16[144,1024]{1,0:T(8,128)(2,1)S(1)} %get-tuple-element.62.x_ref, bf16[144,1024]{1,0:T(8,128)(2,1)S(1)} %get-tuple-element.63.s_ref, bf16[144,384]{1,0:T(8,128)(2,1)S(1)} %get-tuple-element.64.dg_ref, ...), custom_call_target="tpu_custom_call" | custom-call | flops 169869312 | bytes 2359296 | tf_op jit(solution)/shard_map/own_half/pallas_call | solution.py:497
  43.7 0.0 collective-permute-done.9.refs_3_
  43.7 0.0 collective-permute-done.10.refs_4_
  43.7 0.0 collective-permute-done.11.refs_5_
  43.7 0.0 collective-permute-done.12.refs_6_
  43.7 2.4 %collective-permute-done.13.refs_7_ = bf16[80,256]{1,0:T(8,128)(2,1)S(1)} collective-permute-done((bf16[80,256]{1,0:T(8,128)(2,1)S(1)}, bf16[80,256]{1,0:T(8,128)(2,1)S(1)}, u32[]{:S(2)}, u32[]{:S(2)}) %collective-permute-start.13) | collective-permute-done | bytes 40992 | tf_op jit(solution)/shard_map/ppermute | solution.py:513
  46.2 0.0 copy-done.4
  46.2 0.0 copy-done.5
  46.2 0.0 copy-done.6
  46.2 1.0 %combine.1 = (bf16[128,1024]{1,0:T(8,128)(2,1)}, bf16[8,128]{1,0:T(8,128)(2,1)}) custom-call(s32[8,128]{1,0:T(8,128)S(1)} %bitcast.14, s32[8,128]{1,0:T(8,128)S(1)} %copy-done.5, f32[8,128]{1,0:T(8,128)S(1)} %copy-done.6, bf16[80,256]{1,0:T(8,128)(2,1)S(1)} %get-tuple-element.70.refs_0_, bf16[80,256]{1,0:T(8,128)(2,1)S(1)} %collective-permute-done.7.refs_1_, ...), custom_call_target="tpu_custom_call" | custom-call | flops 37748736 | bytes 524288 | tf_op jit(solution)/shard_map/combine/pallas_call | solution.py:497
  (1 shorter events, 0.0 us)
Async XLA Ops:
  3.0 8.9 %collective-permute-start = (bf16[144,256]{1,0:T(8,128)(2,1)}, bf16[144,256]{1,0:T(8,128)(2,1)S(1)}, u32[]{:S(2)}, u32[]{:S(2)}) collective-permute-start(bf16[144,256]{1,0:T(8,128)(2,1)} %get-tuple-element.47), channel_id=1, source_target_pairs={{0,2},{2,0},{4,6},{6,4},{8,10},{10,8},{12,14},{14,12},{1,3},{3,1},... | collective-permute-start | bytes 221192 | tf_op jit(solution)/shard_map/ppermute | solution.py:513
  6.0 9.5 %collective-permute-start.1 = (bf16[144,256]{1,0:T(8,128)(2,1)}, bf16[144,256]{1,0:T(8,128)(2,1)S(1)}, u32[]{:S(2)}, u32[]{:S(2)}) collective-permute-start(bf16[144,256]{1,0:T(8,128)(2,1)} %get-tuple-element.48), channel_id=1, source_target_pairs={{0,4},{2,6},{4,0},{6,2},{8,12},{10,14},{12,8},{14,10},{1,5},{3,7},... | collective-permute-start | bytes 221192 | tf_op jit(solution)/shard_map/ppermute | solution.py:513
  7.6 7.9 %collective-permute-start.2 = (bf16[144,256]{1,0:T(8,128)(2,1)}, bf16[144,256]{1,0:T(8,128)(2,1)S(1)}, u32[]{:S(2)}, u32[]{:S(2)}) collective-permute-start(bf16[144,256]{1,0:T(8,128)(2,1)} %get-tuple-element.49), channel_id=1, source_target_pairs={{0,6},{2,4},{4,2},{6,0},{8,14},{10,12},{12,10},{14,8},{1,7},{3,5},... | collective-permute-start | bytes 221192 | tf_op jit(solution)/shard_map/ppermute | solution.py:513
  7.6 7.9 %collective-permute-start.3 = (bf16[144,256]{1,0:T(8,128)(2,1)}, bf16[144,256]{1,0:T(8,128)(2,1)S(1)}, u32[]{:S(2)}, u32[]{:S(2)}) collective-permute-start(bf16[144,256]{1,0:T(8,128)(2,1)} %get-tuple-element.50), channel_id=1, source_target_pairs={{0,8},{2,10},{4,12},{6,14},{8,0},{10,2},{12,4},{14,6},{1,9},{3,11}... | collective-permute-start | bytes 221192 | tf_op jit(solution)/shard_map/ppermute | solution.py:513
  10.6 11.5 %collective-permute-start.4 = (bf16[144,256]{1,0:T(8,128)(2,1)}, bf16[144,256]{1,0:T(8,128)(2,1)S(1)}, u32[]{:S(2)}, u32[]{:S(2)}) collective-permute-start(bf16[144,256]{1,0:T(8,128)(2,1)} %get-tuple-element.51), channel_id=1, source_target_pairs={{0,10},{2,8},{4,14},{6,12},{8,2},{10,0},{12,6},{14,4},{1,11},{3,9}... | collective-permute-start | bytes 221192 | tf_op jit(solution)/shard_map/ppermute | solution.py:513
  11.8 10.2 %collective-permute-start.5 = (bf16[144,256]{1,0:T(8,128)(2,1)}, bf16[144,256]{1,0:T(8,128)(2,1)S(1)}, u32[]{:S(2)}, u32[]{:S(2)}) collective-permute-start(bf16[144,256]{1,0:T(8,128)(2,1)} %get-tuple-element.52), channel_id=1, source_target_pairs={{0,12},{2,14},{4,8},{6,10},{8,4},{10,6},{12,0},{14,2},{1,13},{3,15... | collective-permute-start | bytes 221192 | tf_op jit(solution)/shard_map/ppermute | solution.py:513
  15.4 7.4 %collective-permute-start.6 = (bf16[144,256]{1,0:T(8,128)(2,1)}, bf16[144,256]{1,0:T(8,128)(2,1)S(1)}, u32[]{:S(2)}, u32[]{:S(2)}) collective-permute-start(bf16[144,256]{1,0:T(8,128)(2,1)} %get-tuple-element.53), channel_id=1, source_target_pairs={{0,14},{2,12},{4,10},{6,8},{8,6},{10,4},{12,2},{14,0},{1,15},{3,13... | collective-permute-start | bytes 221192 | tf_op jit(solution)/shard_map/ppermute | solution.py:513
  22.8 1.1 %copy-start = (bf16[1,1024,384]{2,1,0:T(8,128)(2,1)S(1)}, bf16[1,1024,384]{2,1,0:T(8,128)(2,1)}, u32[]{:S(2)}) copy-start(bf16[1,1024,384]{2,1,0:T(8,128)(2,1)} %param.15) | copy-start | bytes 2359300
  23.9 1.1 %copy-start.1 = (bf16[1,1024,384]{2,1,0:T(8,128)(2,1)S(1)}, bf16[1,1024,384]{2,1,0:T(8,128)(2,1)}, u32[]{:S(2)}) copy-start(bf16[1,1024,384]{2,1,0:T(8,128)(2,1)} %param.16) | copy-start | bytes 2359300
  25.1 1.1 %copy-start.2 = (bf16[1,1024,384]{2,1,0:T(8,128)(2,1)S(1)}, bf16[1,1024,384]{2,1,0:T(8,128)(2,1)}, u32[]{:S(2)}) copy-start(bf16[1,1024,384]{2,1,0:T(8,128)(2,1)} %param.17) | copy-start | bytes 2359300
  26.2 0.9 %copy-start.3 = (bf16[144,256]{1,0:T(8,128)(2,1)S(1)}, bf16[144,256]{1,0:T(8,128)(2,1)}, u32[]{:S(2)}) copy-start(bf16[144,256]{1,0:T(8,128)(2,1)} %get-tuple-element.46.refs_0_) | copy-start | bytes 221188
  29.4 16.8 %copy-start.4 = (s32[128,8]{0,1:T(8,128)S(1)}, s32[128,8]{0,1:T(8,128)}, u32[]{:S(2)}) copy-start(s32[128,8]{0,1:T(8,128)} %param.11) | copy-start | bytes 12292
  29.4 16.8 %copy-start.5 = (s32[8,128]{1,0:T(8,128)S(1)}, s32[8,128]{1,0:T(8,128)}, u32[]{:S(2)}) copy-start(s32[8,128]{1,0:T(8,128)} %get-tuple-element.44.slot_ref) | copy-start | bytes 12292
  29.4 16.8 %copy-start.6 = (f32[8,128]{1,0:T(8,128)S(1)}, f32[8,128]{1,0:T(8,128)}, u32[]{:S(2)}) copy-start(f32[8,128]{1,0:T(8,128)} %get-tuple-element.45.gates_ref) | copy-start | bytes 12292
  29.4 10.1 %collective-permute-start.14 = (bf16[1536,384]{1,0:T(8,128)(2,1)S(1)}, bf16[1536,384]{1,0:T(8,128)(2,1)S(1)}, u32[]{:S(2)}, u32[]{:S(2)}) collective-permute-start(bf16[1536,384]{1,0:T(8,128)(2,1)S(1)} %other_half.1), channel_id=1, source_target_pairs={{0,1},{1,0},{2,3},{3,2},{4,5},{5,4},{6,7},{7,6},{8,9},{9,8},{10,11... | collective-permute-start | bytes 3538952 | tf_op jit(solution)/shard_map/ppermute | solution.py:579
  29.5 7.6 %collective-permute-start.7 = (bf16[80,256]{1,0:T(8,128)(2,1)S(1)}, bf16[80,256]{1,0:T(8,128)(2,1)S(1)}, u32[]{:S(2)}, u32[]{:S(2)}) collective-permute-start(bf16[80,256]{1,0:T(8,128)(2,1)S(1)} %get-tuple-element.55), channel_id=1, source_target_pairs={{0,2},{2,0},{4,6},{6,4},{8,10},{10,8},{12,14},{14,12},{1,3},{3,1},... | collective-permute-start | bytes 122888 | tf_op jit(solution)/shard_map/ppermute | solution.py:513
  30.3 7.3 %collective-permute-start.8 = (bf16[80,256]{1,0:T(8,128)(2,1)S(1)}, bf16[80,256]{1,0:T(8,128)(2,1)S(1)}, u32[]{:S(2)}, u32[]{:S(2)}) collective-permute-start(bf16[80,256]{1,0:T(8,128)(2,1)S(1)} %get-tuple-element.56), channel_id=1, source_target_pairs={{0,4},{2,6},{4,0},{6,2},{8,12},{10,14},{12,8},{14,10},{1,5},{3,7},... | collective-permute-start | bytes 122888 | tf_op jit(solution)/shard_map/ppermute | solution.py:513
  33.3 10.4 %collective-permute-start.9 = (bf16[80,256]{1,0:T(8,128)(2,1)S(1)}, bf16[80,256]{1,0:T(8,128)(2,1)S(1)}, u32[]{:S(2)}, u32[]{:S(2)}) collective-permute-start(bf16[80,256]{1,0:T(8,128)(2,1)S(1)} %get-tuple-element.57), channel_id=1, source_target_pairs={{0,6},{2,4},{4,2},{6,0},{8,14},{10,12},{12,10},{14,8},{1,7},{3,5},... | collective-permute-start | bytes 122888 | tf_op jit(solution)/shard_map/ppermute | solution.py:513
  33.9 9.8 %collective-permute-start.10 = (bf16[80,256]{1,0:T(8,128)(2,1)S(1)}, bf16[80,256]{1,0:T(8,128)(2,1)S(1)}, u32[]{:S(2)}, u32[]{:S(2)}) collective-permute-start(bf16[80,256]{1,0:T(8,128)(2,1)S(1)} %get-tuple-element.58), channel_id=1, source_target_pairs={{0,8},{2,10},{4,12},{6,14},{8,0},{10,2},{12,4},{14,6},{1,9},{3,11}... | collective-permute-start | bytes 122888 | tf_op jit(solution)/shard_map/ppermute | solution.py:513
  37.1 6.6 %collective-permute-start.11 = (bf16[80,256]{1,0:T(8,128)(2,1)S(1)}, bf16[80,256]{1,0:T(8,128)(2,1)S(1)}, u32[]{:S(2)}, u32[]{:S(2)}) collective-permute-start(bf16[80,256]{1,0:T(8,128)(2,1)S(1)} %get-tuple-element.59), channel_id=1, source_target_pairs={{0,10},{2,8},{4,14},{6,12},{8,2},{10,0},{12,6},{14,4},{1,11},{3,9}... | collective-permute-start | bytes 122888 | tf_op jit(solution)/shard_map/ppermute | solution.py:513
  37.6 6.1 %collective-permute-start.12 = (bf16[80,256]{1,0:T(8,128)(2,1)S(1)}, bf16[80,256]{1,0:T(8,128)(2,1)S(1)}, u32[]{:S(2)}, u32[]{:S(2)}) collective-permute-start(bf16[80,256]{1,0:T(8,128)(2,1)S(1)} %get-tuple-element.60), channel_id=1, source_target_pairs={{0,12},{2,14},{4,8},{6,10},{8,4},{10,6},{12,0},{14,2},{1,13},{3,15... | collective-permute-start | bytes 122888 | tf_op jit(solution)/shard_map/ppermute | solution.py:513
  39.5 6.7 %collective-permute-start.13 = (bf16[80,256]{1,0:T(8,128)(2,1)S(1)}, bf16[80,256]{1,0:T(8,128)(2,1)S(1)}, u32[]{:S(2)}, u32[]{:S(2)}) collective-permute-start(bf16[80,256]{1,0:T(8,128)(2,1)S(1)} %get-tuple-element.61), channel_id=1, source_target_pairs={{0,14},{2,12},{4,10},{6,8},{8,6},{10,4},{12,2},{14,0},{1,15},{3,13... | collective-permute-start | bytes 122888 | tf_op jit(solution)/shard_map/ppermute | solution.py:513

commit v2 on v1

--- a/solution.py
+++ b/solution.py
@@ -240,7 +240,7 @@
 QUARTERS = 4
 SEND_ROWS = 2 * QUARTERS * MAIN + 16
 BACK_ROWS = QUARTERS * MAIN + 16
-FAR_FIRST = (4, 5, 6, 7, 1, 2, 3)
+STEPS = (0, 1, 4, 5, 6, 7, 2, 3)
 
 
 def copies_of(experts):
@@ -249,6 +249,14 @@
 
 def iota(shape, axis):
     return lax.broadcasted_iota(jnp.int32, shape, axis)
+
+
+def partners(experts, tokens):
+    row = iota((experts, tokens), 0)
+    step = jnp.zeros((experts, tokens), jnp.int32)
+    for c in range(1, experts):
+        step = jnp.where(row == c, STEPS[c], step)
+    return jnp.bitwise_xor(step, lax.axis_index("expert"))
 
 
 def mask(condition):
@@ -287,8 +295,7 @@
     for load in loads:
         load.start()
     before = mask(iota((tokens, tokens), 0) < iota((tokens, tokens), 1))
-    me = lax.axis_index("expert")
-    expert_row = jnp.bitwise_xor(iota((experts, tokens), 0), me)
+    expert_row = partners(experts, tokens)
     for load in loads[:4]:
         load.wait()
     ids = ids_ref[...]
@@ -484,7 +491,7 @@
     found = jnp.concatenate(found, axis=0)
     kept = slot >= 0
     grads = jnp.where(kept, found / jnp.where(kept, gates_ref[...], 1.0), 0.0)
-    expert_row = jnp.bitwise_xor(iota((experts, tokens), 0), lax.axis_index("expert"))
+    expert_row = partners(experts, tokens)
     by_choice = [
         jnp.sum(jnp.where(expert_row == ids[k : k + 1], grads, 0.0), axis=0, keepdims=True)
         for k in range(topk)
@@ -508,10 +515,17 @@
 
 def exchange(chunks):
     count = len(chunks)
-    came = list(chunks)
-    for k in FAR_FIRST:
-        came[k] = lax.ppermute(chunks[k], "expert", [(i, i ^ k) for i in range(count)])
-    return came
+    moved = [
+        lax.ppermute(chunk, "expert", [(i, i ^ step) for i in range(count)])
+        for chunk, step in zip(chunks[1:], STEPS[1:])
+    ]
+    return [chunks[0], *moved]
+
+
+def hold_kernel(*refs):
+    count = len(refs) // 2
+    for source, place in zip(refs[:count], refs[count:]):
+        place[...] = source[...]
 
 
 def per_device_moving_rows(
@@ -554,19 +568,29 @@
     )
     slot, gates = routed[experts:]
     recv = exchange(routed[:experts])
+    held = [recv[0], gate_proj[0], up_proj[0], down_proj[0]]
+    held = local_call(
+        hold_kernel,
+        [(array.shape, BF) for array in held],
+        held,
+        "hold",
+        0,
+        4 * 3 * model_width * hidden_width,
+    )
     matmul = 2 * served * model_width * hidden_width
     outs = local_call(
         expert_kernel,
         [((BACK_ROWS, width), BF)] * experts
         + [((served, model_width), BF)] * 2
         + [((served, hidden_width), BF)] * 3,
-        [*recv, gate_proj[0], up_proj[0], down_proj[0]],
+        [held[0], *recv[1:], *held[1:]],
         "expert_rows",
         5 * matmul,
         2 * 3 * model_width * hidden_width,
     )
     factors = outs[experts:]
     returned = exchange(outs[:experts])
+    returned[1], factors = lax.optimization_barrier((returned[1], factors))
     half = model_width // 2
     (leaving,) = local_call(
         other_half_kernel,

time: 47.5 us -> 44 us (0.926)
  waiting for transfers between devices: 9.78 us -> 7.06 us
  starting transfers between devices: 25.4 us -> 24.4 us
    ppermute x14, waiting for transfers between devices: 9.77 us -> 7.06 us  [exchange(): lax.ppermute(chunk, 'expert', [(i, i ^ step) for i in range(count)])]
    ppermute x14, starting transfers between devices: 25.3 us -> 24.3 us  [exchange(): lax.ppermute(chunk, 'expert', [(i, i ^ step) for i in range(count)])]
    pallas_call x5 -> x6, Pallas kernels: 7.01 us -> 7.2 us  [local_call(): pl.pallas_call(kernel, out_shape=[jax.ShapeDtypeStruct(shape, kind) for s...]
  transfers between devices with their start and end apart: 15 -> 15, of which waited for: 3 -> 5; matrix products, arithmetic and copies ran while one was open for 0% -> 0% of each run, Pallas kernels for 3% -> 4%
where the time goes in v2:
time: 44 us; the launch traced here: 43.7 us
  starting transfers between devices  24.4 us (55%)
  Pallas kernels  7.2 us (16%)
  waiting for transfers between devices  7.06 us (16%)
  local copies, waits for them, and re-layouts  4.3 us (10%)
  between operations  0.74 us (2%)
    ppermute x14, starting transfers between devices, exchange(): lax.ppermute(chunk, 'expert', [(i, i ^ step) for i in range(count)])  24.3 us
    pallas_call x6, Pallas kernels, local_call(): pl.pallas_call(kernel, out_shape=[jax.ShapeDtypeStruct(shape, kind) for s...  7.2 us
    ppermute x14, waiting for transfers between devices, exchange(): lax.ppermute(chunk, 'expert', [(i, i ^ step) for i in range(count)])  7.06 us
    unnamed x14, local copies, waits for them, and re-layouts  4.3 us
  transfers between devices with their start and end apart: 15, of which 5 were waited for; matrix products, arithmetic and copies ran while one was open for 0% of the time, Pallas kernels for 4%

profile of v2, /device:TPU:0, one launch (start us, length us, event | category | flops | bytes accessed | tf_op | source)
XLA Modules:
  0.0 43.7 jit_solution(13377601104616027972)
XLA Ops:
  0.6 2.3 %route.1 = (bf16[144,256]{1,0:T(8,128)(2,1)}, bf16[144,256]{1,0:T(8,128)(2,1)}, bf16[144,256]{1,0:T(8,128)(2,1)}, bf16[144,256]{1,0:T(8,128)(2,1)}, bf16[144,256...) custom-call(s32[8]{0:T(128)} %plan_hbm.1, ...), custom_call_target="tpu_custom_call" | custom-call | flops 75497472 | bytes 1114112 | tf_op jit(solution)/shard_map/route/pallas_call | solution.py:504
  3.0 3.0 %collective-permute-start = (bf16[144,256]{1,0:T(8,128)(2,1)}, bf16[144,256]{1,0:T(8,128)(2,1)S(1)}, u32[]{:S(2)}, u32[]{:S(2)}) collective-permute-start(bf16[144,256]{1,0:T(8,128)(2,1)} %get-tuple-element.58), channel_id=1, source_target_pairs={{0,2},{2,0},{4,6},{6,4},{8,10},{10,8},{12,14},{14,12},{1,3},{3,1},... | collective-permute-start | bytes 221192 | tf_op jit(solution)/shard_map/ppermute | solution.py:519
  6.0 2.6 %collective-permute-start.1 = (bf16[144,256]{1,0:T(8,128)(2,1)}, bf16[144,256]{1,0:T(8,128)(2,1)S(1)}, u32[]{:S(2)}, u32[]{:S(2)}) collective-permute-start(bf16[144,256]{1,0:T(8,128)(2,1)} %get-tuple-element.59), channel_id=1, source_target_pairs={{0,8},{2,10},{4,12},{6,14},{8,0},{10,2},{12,4},{14,6},{1,9},{3,11}... | collective-permute-start | bytes 221192 | tf_op jit(solution)/shard_map/ppermute | solution.py:519
  8.6 0.0 collective-permute-start.2
  8.6 3.9 %collective-permute-start.3 = (bf16[144,256]{1,0:T(8,128)(2,1)}, bf16[144,256]{1,0:T(8,128)(2,1)S(1)}, u32[]{:S(2)}, u32[]{:S(2)}) collective-permute-start(bf16[144,256]{1,0:T(8,128)(2,1)} %get-tuple-element.61), channel_id=1, source_target_pairs={{0,12},{2,14},{4,8},{6,10},{8,4},{10,6},{12,0},{14,2},{1,13},{3,15... | collective-permute-start | bytes 221192 | tf_op jit(solution)/shard_map/ppermute | solution.py:519
  12.5 1.1 %collective-permute-start.4 = (bf16[144,256]{1,0:T(8,128)(2,1)}, bf16[144,256]{1,0:T(8,128)(2,1)S(1)}, u32[]{:S(2)}, u32[]{:S(2)}) collective-permute-start(bf16[144,256]{1,0:T(8,128)(2,1)} %get-tuple-element.62), channel_id=1, source_target_pairs={{0,14},{2,12},{4,10},{6,8},{8,6},{10,4},{12,2},{14,0},{1,15},{3,13... | collective-permute-start | bytes 221192 | tf_op jit(solution)/shard_map/ppermute | solution.py:519
  13.6 0.0 collective-permute-done.refs_1_
  13.6 0.0 collective-permute-start.5
  13.6 2.6 %collective-permute-done.1.refs_2_ = bf16[144,256]{1,0:T(8,128)(2,1)S(1)} collective-permute-done((bf16[144,256]{1,0:T(8,128)(2,1)}, bf16[144,256]{1,0:T(8,128)(2,1)S(1)}, u32[]{:S(2)}, u32[]{:S(2)}) %collective-permute-start.1) | collective-permute-done | bytes 73760 | tf_op jit(solution)/shard_map/ppermute | solution.py:519
  16.2 0.1 collective-permute-start.6
  16.3 0.0 copy-start
  16.4 1.1 %copy-done = bf16[1,1024,384]{2,1,0:T(8,128)(2,1)S(1)} copy-done((bf16[1,1024,384]{2,1,0:T(8,128)(2,1)S(1)}, bf16[1,1024,384]{2,1,0:T(8,128)(2,1)}, u32[]{:S(2)}) %copy-start) | copy-done | bytes 786456
  17.5 0.0 copy-start.1
  17.5 1.1 %copy-done.1 = bf16[1,1024,384]{2,1,0:T(8,128)(2,1)S(1)} copy-done((bf16[1,1024,384]{2,1,0:T(8,128)(2,1)S(1)}, bf16[1,1024,384]{2,1,0:T(8,128)(2,1)}, u32[]{:S(2)}) %copy-start.1) | copy-done | bytes 786456
  18.6 1.1 %copy-done.2 = bf16[1,1024,384]{2,1,0:T(8,128)(2,1)S(1)} copy-done((bf16[1,1024,384]{2,1,0:T(8,128)(2,1)S(1)}, bf16[1,1024,384]{2,1,0:T(8,128)(2,1)}, u32[]{:S(2)}) %copy-start.2) | copy-done | bytes 786456
  19.8 0.9 %copy-done.3 = bf16[144,256]{1,0:T(8,128)(2,1)S(1)} copy-done((bf16[144,256]{1,0:T(8,128)(2,1)S(1)}, bf16[144,256]{1,0:T(8,128)(2,1)}, u32[]{:S(2)}) %copy-start.3) | copy-done | bytes 73752
  20.6 0.2 hold.1
  20.8 0.0 collective-permute-done.2.refs_3_
  20.9 0.0 collective-permute-done.3.refs_4_
  20.9 0.0 collective-permute-done.4.refs_5_
  20.9 0.0 collective-permute-done.5.refs_6_
  20.9 0.8 %collective-permute-done.6.refs_7_ = bf16[144,256]{1,0:T(8,128)(2,1)S(1)} collective-permute-done((bf16[144,256]{1,0:T(8,128)(2,1)}, bf16[144,256]{1,0:T(8,128)(2,1)S(1)}, u32[]{:S(2)}, u32[]{:S(2)}) %collective-permute-start.6) | collective-permute-done | bytes 73760 | tf_op jit(solution)/shard_map/ppermute | solution.py:519
  21.7 1.6 %expert_rows.1 = (bf16[80,256]{1,0:T(8,128)(2,1)S(1)}, bf16[80,256]{1,0:T(8,128)(2,1)S(1)}, bf16[80,256]{1,0:T(8,128)(2,1)S(1)}, bf16[80,256]{1,0:T(8,128)(2,1)S...) custom-call(bf16[144,256]{1,0:T(8,128)(2,1)S(1)} %get-tuple-element., ...), custom_call_target="tpu_custom_call" | custom-call | flops 566231040 | bytes 2359296 | tf_op jit(solution)/shard_map/expert_rows/pallas_call | solution.py:504
  23.3 1.8 %collective-permute-start.7 = (bf16[80,256]{1,0:T(8,128)(2,1)S(1)}, bf16[80,256]{1,0:T(8,128)(2,1)S(1)}, u32[]{:S(2)}, u32[]{:S(2)}) collective-permute-start(bf16[80,256]{1,0:T(8,128)(2,1)S(1)} %get-tuple-element.69), channel_id=1, source_target_pairs={{0,2},{2,0},{4,6},{6,4},{8,10},{10,8},{12,14},{14,12},{1,3},{3,1},... | collective-permute-start | bytes 122888 | tf_op jit(solution)/shard_map/ppermute | solution.py:519
  25.1 2.2 %collective-permute-done.7.refs_1_ = bf16[80,256]{1,0:T(8,128)(2,1)S(1)} collective-permute-done((bf16[80,256]{1,0:T(8,128)(2,1)S(1)}, bf16[80,256]{1,0:T(8,128)(2,1)S(1)}, u32[]{:S(2)}, u32[]{:S(2)}) %collective-permute-start.7) | collective-permute-done | bytes 40992 | tf_op jit(solution)/shard_map/ppermute | solution.py:519
  27.3 0.6 %other_half.1 = bf16[1536,384]{1,0:T(8,128)(2,1)S(1)} custom-call(bf16[144,1024]{1,0:T(8,128)(2,1)S(1)} %get-tuple-element.82.x_ref, bf16[144,1024]{1,0:T(8,128)(2,1)S(1)} %get-tuple-element.83.s_ref, bf16[144,384]{1,0:T(8,128)(2,1)S(1)} %get-tuple-element.84.dg_ref, bf16[144,384]{1,0:T(8,128)(2,1)S(1)} %get-tuple-element.85.du_ref, ...), custom_call_target="tpu_custom_call" | custom-call | flops 169869312 | bytes 1179648 | tf_op jit(solution)/shard_map/other_half/pallas_call | solution.py:504
  27.9 0.0 copy-start.4
  28.0 0.0 copy-start.5
  28.0 0.0 copy-start.6
  28.0 0.1 collective-permute-start.14
  28.1 3.4 %collective-permute-start.8 = (bf16[80,256]{1,0:T(8,128)(2,1)S(1)}, bf16[80,256]{1,0:T(8,128)(2,1)S(1)}, u32[]{:S(2)}, u32[]{:S(2)}) collective-permute-start(bf16[80,256]{1,0:T(8,128)(2,1)S(1)} %get-tuple-element.76), channel_id=1, source_target_pairs={{0,8},{2,10},{4,12},{6,14},{8,0},{10,2},{12,4},{14,6},{1,9},{3,11}... | collective-permute-start | bytes 122888 | tf_op jit(solution)/shard_map/ppermute | solution.py:519
  31.5 1.5 %collective-permute-start.9 = (bf16[80,256]{1,0:T(8,128)(2,1)S(1)}, bf16[80,256]{1,0:T(8,128)(2,1)S(1)}, u32[]{:S(2)}, u32[]{:S(2)}) collective-permute-start(bf16[80,256]{1,0:T(8,128)(2,1)S(1)} %get-tuple-element.77), channel_id=1, source_target_pairs={{0,10},{2,8},{4,14},{6,12},{8,2},{10,0},{12,6},{14,4},{1,11},{3,9}... | collective-permute-start | bytes 122888 | tf_op jit(solution)/shard_map/ppermute | solution.py:519
  33.0 2.6 %collective-permute-start.10 = (bf16[80,256]{1,0:T(8,128)(2,1)S(1)}, bf16[80,256]{1,0:T(8,128)(2,1)S(1)}, u32[]{:S(2)}, u32[]{:S(2)}) collective-permute-start(bf16[80,256]{1,0:T(8,128)(2,1)S(1)} %get-tuple-element.78), channel_id=1, source_target_pairs={{0,12},{2,14},{4,8},{6,10},{8,4},{10,6},{12,0},{14,2},{1,13},{3,15... | collective-permute-start | bytes 122888 | tf_op jit(solution)/shard_map/ppermute | solution.py:519
  35.6 1.2 %collective-permute-start.11 = (bf16[80,256]{1,0:T(8,128)(2,1)S(1)}, bf16[80,256]{1,0:T(8,128)(2,1)S(1)}, u32[]{:S(2)}, u32[]{:S(2)}) collective-permute-start(bf16[80,256]{1,0:T(8,128)(2,1)S(1)} %get-tuple-element.79), channel_id=1, source_target_pairs={{0,14},{2,12},{4,10},{6,8},{8,6},{10,4},{12,2},{14,0},{1,15},{3,13... | collective-permute-start | bytes 122888 | tf_op jit(solution)/shard_map/ppermute | solution.py:519
  36.8 0.0 collective-permute-done.8.refs_2_
  36.8 0.0 collective-permute-start.12
  36.8 0.0 collective-permute-done.14.came_ref
  36.8 3.0 %collective-permute-start.13 = (bf16[80,256]{1,0:T(8,128)(2,1)S(1)}, bf16[80,256]{1,0:T(8,128)(2,1)S(1)}, u32[]{:S(2)}, u32[]{:S(2)}) collective-permute-start(bf16[80,256]{1,0:T(8,128)(2,1)S(1)} %get-tuple-element.81), channel_id=1, source_target_pairs={{0,6},{2,4},{4,2},{6,0},{8,14},{10,12},{12,10},{14,8},{1,7},{3,5},... | collective-permute-start | bytes 122888 | tf_op jit(solution)/shard_map/ppermute | solution.py:519
  39.8 1.4 %own_half.1 = (bf16[512,384]{1,0:T(8,128)(2,1)}, bf16[512,384]{1,0:T(8,128)(2,1)}, bf16[512,384]{1,0:T(8,128)(2,1)}) custom-call(bf16[144,1024]{1,0:T(8,128)(2,1)S(1)} %get-tuple-element.82.x_ref, bf16[144,1024]{1,0:T(8,128)(2,1)S(1)} %get-tuple-element.83.s_ref, bf16[144,384]{1,0:T(8,128)(2,1)S(1)} %get-tuple-element.84.dg_ref, ...), custom_call_target="tpu_custom_call" | custom-call | flops 169869312 | bytes 2359296 | tf_op jit(solution)/shard_map/own_half/pallas_call | solution.py:504
  41.2 0.0 collective-permute-done.9.refs_3_
  41.2 0.0 collective-permute-done.10.refs_4_
  41.2 1.2 %collective-permute-done.11.refs_5_ = bf16[80,256]{1,0:T(8,128)(2,1)S(1)} collective-permute-done((bf16[80,256]{1,0:T(8,128)(2,1)S(1)}, bf16[80,256]{1,0:T(8,128)(2,1)S(1)}, u32[]{:S(2)}, u32[]{:S(2)}) %collective-permute-start.11) | collective-permute-done | bytes 40992 | tf_op jit(solution)/shard_map/ppermute | solution.py:519
  42.4 0.0 collective-permute-done.12.refs_6_
  42.4 0.2 collective-permute-done.13.refs_7_
  42.6 0.0 copy-done.4
  42.6 0.0 copy-done.5
  42.6 0.0 copy-done.6
  42.6 1.0 %combine.1 = (bf16[128,1024]{1,0:T(8,128)(2,1)}, bf16[8,128]{1,0:T(8,128)(2,1)}) custom-call(s32[8,128]{1,0:T(8,128)S(1)} %bitcast.14, s32[8,128]{1,0:T(8,128)S(1)} %copy-done.5, f32[8,128]{1,0:T(8,128)S(1)} %copy-done.6, bf16[80,256]{1,0:T(8,128)(2,1)S(1)} %get-tuple-element.90.refs_0_, bf16[80,256]{1,0:T(8,128)(2,1)S(1)} %collective-permute-done.7.refs_1_, ...), custom_call_target="tpu_custom_call" | custom-call | flops 37748736 | bytes 524288 | tf_op jit(solution)/shard_map/combine/pallas_call | solution.py:504
  (2 shorter events, 0.0 us)
Async XLA Ops:
  3.0 10.7 %collective-permute-start = (bf16[144,256]{1,0:T(8,128)(2,1)}, bf16[144,256]{1,0:T(8,128)(2,1)S(1)}, u32[]{:S(2)}, u32[]{:S(2)}) collective-permute-start(bf16[144,256]{1,0:T(8,128)(2,1)} %get-tuple-element.58), channel_id=1, source_target_pairs={{0,2},{2,0},{4,6},{6,4},{8,10},{10,8},{12,14},{14,12},{1,3},{3,1},... | collective-permute-start | bytes 221192 | tf_op jit(solution)/shard_map/ppermute | solution.py:519
  6.0 10.2 %collective-permute-start.1 = (bf16[144,256]{1,0:T(8,128)(2,1)}, bf16[144,256]{1,0:T(8,128)(2,1)S(1)}, u32[]{:S(2)}, u32[]{:S(2)}) collective-permute-start(bf16[144,256]{1,0:T(8,128)(2,1)} %get-tuple-element.59), channel_id=1, source_target_pairs={{0,8},{2,10},{4,12},{6,14},{8,0},{10,2},{12,4},{14,6},{1,9},{3,11}... | collective-permute-start | bytes 221192 | tf_op jit(solution)/shard_map/ppermute | solution.py:519
  8.6 12.3 %collective-permute-start.2 = (bf16[144,256]{1,0:T(8,128)(2,1)}, bf16[144,256]{1,0:T(8,128)(2,1)S(1)}, u32[]{:S(2)}, u32[]{:S(2)}) collective-permute-start(bf16[144,256]{1,0:T(8,128)(2,1)} %get-tuple-element.60), channel_id=1, source_target_pairs={{0,10},{2,8},{4,14},{6,12},{8,2},{10,0},{12,6},{14,4},{1,11},{3,9}... | collective-permute-start | bytes 221192 | tf_op jit(solution)/shard_map/ppermute | solution.py:519
  8.6 12.3 %collective-permute-start.3 = (bf16[144,256]{1,0:T(8,128)(2,1)}, bf16[144,256]{1,0:T(8,128)(2,1)S(1)}, u32[]{:S(2)}, u32[]{:S(2)}) collective-permute-start(bf16[144,256]{1,0:T(8,128)(2,1)} %get-tuple-element.61), channel_id=1, source_target_pairs={{0,12},{2,14},{4,8},{6,10},{8,4},{10,6},{12,0},{14,2},{1,13},{3,15... | collective-permute-start | bytes 221192 | tf_op jit(solution)/shard_map/ppermute | solution.py:519
  12.5 8.4 %collective-permute-start.4 = (bf16[144,256]{1,0:T(8,128)(2,1)}, bf16[144,256]{1,0:T(8,128)(2,1)S(1)}, u32[]{:S(2)}, u32[]{:S(2)}) collective-permute-start(bf16[144,256]{1,0:T(8,128)(2,1)} %get-tuple-element.62), channel_id=1, source_target_pairs={{0,14},{2,12},{4,10},{6,8},{8,6},{10,4},{12,2},{14,0},{1,15},{3,13... | collective-permute-start | bytes 221192 | tf_op jit(solution)/shard_map/ppermute | solution.py:519
  13.6 7.3 %collective-permute-start.5 = (bf16[144,256]{1,0:T(8,128)(2,1)}, bf16[144,256]{1,0:T(8,128)(2,1)S(1)}, u32[]{:S(2)}, u32[]{:S(2)}) collective-permute-start(bf16[144,256]{1,0:T(8,128)(2,1)} %get-tuple-element.63), channel_id=1, source_target_pairs={{0,4},{2,6},{4,0},{6,2},{8,12},{10,14},{12,8},{14,10},{1,5},{3,7},... | collective-permute-start | bytes 221192 | tf_op jit(solution)/shard_map/ppermute | solution.py:519
  16.2 5.5 %collective-permute-start.6 = (bf16[144,256]{1,0:T(8,128)(2,1)}, bf16[144,256]{1,0:T(8,128)(2,1)S(1)}, u32[]{:S(2)}, u32[]{:S(2)}) collective-permute-start(bf16[144,256]{1,0:T(8,128)(2,1)} %get-tuple-element.64), channel_id=1, source_target_pairs={{0,6},{2,4},{4,2},{6,0},{8,14},{10,12},{12,10},{14,8},{1,7},{3,5},... | collective-permute-start | bytes 221192 | tf_op jit(solution)/shard_map/ppermute | solution.py:519
  16.3 1.1 %copy-start = (bf16[1,1024,384]{2,1,0:T(8,128)(2,1)S(1)}, bf16[1,1024,384]{2,1,0:T(8,128)(2,1)}, u32[]{:S(2)}) copy-start(bf16[1,1024,384]{2,1,0:T(8,128)(2,1)} %param.15) | copy-start | bytes 2359300
  17.5 1.1 %copy-start.1 = (bf16[1,1024,384]{2,1,0:T(8,128)(2,1)S(1)}, bf16[1,1024,384]{2,1,0:T(8,128)(2,1)}, u32[]{:S(2)}) copy-start(bf16[1,1024,384]{2,1,0:T(8,128)(2,1)} %param.16) | copy-start | bytes 2359300
  18.6 1.1 %copy-start.2 = (bf16[1,1024,384]{2,1,0:T(8,128)(2,1)S(1)}, bf16[1,1024,384]{2,1,0:T(8,128)(2,1)}, u32[]{:S(2)}) copy-start(bf16[1,1024,384]{2,1,0:T(8,128)(2,1)} %param.17) | copy-start | bytes 2359300
  19.7 0.9 %copy-start.3 = (bf16[144,256]{1,0:T(8,128)(2,1)S(1)}, bf16[144,256]{1,0:T(8,128)(2,1)}, u32[]{:S(2)}) copy-start(bf16[144,256]{1,0:T(8,128)(2,1)} %get-tuple-element.56.refs_0_) | copy-start | bytes 221188
  23.3 4.0 %collective-permute-start.7 = (bf16[80,256]{1,0:T(8,128)(2,1)S(1)}, bf16[80,256]{1,0:T(8,128)(2,1)S(1)}, u32[]{:S(2)}, u32[]{:S(2)}) collective-permute-start(bf16[80,256]{1,0:T(8,128)(2,1)S(1)} %get-tuple-element.69), channel_id=1, source_target_pairs={{0,2},{2,0},{4,6},{6,4},{8,10},{10,8},{12,14},{14,12},{1,3},{3,1},... | collective-permute-start | bytes 122888 | tf_op jit(solution)/shard_map/ppermute | solution.py:519
  27.9 14.7 %copy-start.4 = (s32[128,8]{0,1:T(8,128)S(1)}, s32[128,8]{0,1:T(8,128)}, u32[]{:S(2)}) copy-start(s32[128,8]{0,1:T(8,128)} %param.11) | copy-start | bytes 12292
  28.0 14.7 %copy-start.5 = (s32[8,128]{1,0:T(8,128)S(1)}, s32[8,128]{1,0:T(8,128)}, u32[]{:S(2)}) copy-start(s32[8,128]{1,0:T(8,128)} %get-tuple-element.54.slot_ref) | copy-start | bytes 12292
  28.0 14.7 %copy-start.6 = (f32[8,128]{1,0:T(8,128)S(1)}, f32[8,128]{1,0:T(8,128)}, u32[]{:S(2)}) copy-start(f32[8,128]{1,0:T(8,128)} %get-tuple-element.55.gates_ref) | copy-start | bytes 12292
  28.0 8.8 %collective-permute-start.14 = (bf16[1536,384]{1,0:T(8,128)(2,1)S(1)}, bf16[1536,384]{1,0:T(8,128)(2,1)S(1)}, u32[]{:S(2)}, u32[]{:S(2)}) collective-permute-start(bf16[1536,384]{1,0:T(8,128)(2,1)S(1)} %other_half.1), channel_id=1, source_target_pairs={{0,1},{1,0},{2,3},{3,2},{4,5},{5,4},{6,7},{7,6},{8,9},{9,8},{10,11... | collective-permute-start | bytes 3538952 | tf_op jit(solution)/shard_map/ppermute | solution.py:603
  28.1 8.7 %collective-permute-start.8 = (bf16[80,256]{1,0:T(8,128)(2,1)S(1)}, bf16[80,256]{1,0:T(8,128)(2,1)S(1)}, u32[]{:S(2)}, u32[]{:S(2)}) collective-permute-start(bf16[80,256]{1,0:T(8,128)(2,1)S(1)} %get-tuple-element.76), channel_id=1, source_target_pairs={{0,8},{2,10},{4,12},{6,14},{8,0},{10,2},{12,4},{14,6},{1,9},{3,11}... | collective-permute-start | bytes 122888 | tf_op jit(solution)/shard_map/ppermute | solution.py:519
  31.5 9.7 %collective-permute-start.9 = (bf16[80,256]{1,0:T(8,128)(2,1)S(1)}, bf16[80,256]{1,0:T(8,128)(2,1)S(1)}, u32[]{:S(2)}, u32[]{:S(2)}) collective-permute-start(bf16[80,256]{1,0:T(8,128)(2,1)S(1)} %get-tuple-element.77), channel_id=1, source_target_pairs={{0,10},{2,8},{4,14},{6,12},{8,2},{10,0},{12,6},{14,4},{1,11},{3,9}... | collective-permute-start | bytes 122888 | tf_op jit(solution)/shard_map/ppermute | solution.py:519
  33.0 8.1 %collective-permute-start.10 = (bf16[80,256]{1,0:T(8,128)(2,1)S(1)}, bf16[80,256]{1,0:T(8,128)(2,1)S(1)}, u32[]{:S(2)}, u32[]{:S(2)}) collective-permute-start(bf16[80,256]{1,0:T(8,128)(2,1)S(1)} %get-tuple-element.78), channel_id=1, source_target_pairs={{0,12},{2,14},{4,8},{6,10},{8,4},{10,6},{12,0},{14,2},{1,13},{3,15... | collective-permute-start | bytes 122888 | tf_op jit(solution)/shard_map/ppermute | solution.py:519
  35.6 6.8 %collective-permute-start.11 = (bf16[80,256]{1,0:T(8,128)(2,1)S(1)}, bf16[80,256]{1,0:T(8,128)(2,1)S(1)}, u32[]{:S(2)}, u32[]{:S(2)}) collective-permute-start(bf16[80,256]{1,0:T(8,128)(2,1)S(1)} %get-tuple-element.79), channel_id=1, source_target_pairs={{0,14},{2,12},{4,10},{6,8},{8,6},{10,4},{12,2},{14,0},{1,15},{3,13... | collective-permute-start | bytes 122888 | tf_op jit(solution)/shard_map/ppermute | solution.py:519
  36.8 5.6 %collective-permute-start.12 = (bf16[80,256]{1,0:T(8,128)(2,1)S(1)}, bf16[80,256]{1,0:T(8,128)(2,1)S(1)}, u32[]{:S(2)}, u32[]{:S(2)}) collective-permute-start(bf16[80,256]{1,0:T(8,128)(2,1)S(1)} %get-tuple-element.80), channel_id=1, source_target_pairs={{0,4},{2,6},{4,0},{6,2},{8,12},{10,14},{12,8},{14,10},{1,5},{3,7},... | collective-permute-start | bytes 122888 | tf_op jit(solution)/shard_map/ppermute | solution.py:519
  36.8 5.8 %collective-permute-start.13 = (bf16[80,256]{1,0:T(8,128)(2,1)S(1)}, bf16[80,256]{1,0:T(8,128)(2,1)S(1)}, u32[]{:S(2)}, u32[]{:S(2)}) collective-permute-start(bf16[80,256]{1,0:T(8,128)(2,1)S(1)} %get-tuple-element.81), channel_id=1, source_target_pairs={{0,6},{2,4},{4,2},{6,0},{8,14},{10,12},{12,10},{14,8},{1,7},{3,5},... | collective-permute-start | bytes 122888 | tf_op jit(solution)/shard_map/ppermute | solution.py:519

commit v3 on v2

--- a/solution.py
+++ b/solution.py
@@ -240,7 +240,9 @@
 QUARTERS = 4
 SEND_ROWS = 2 * QUARTERS * MAIN + 16
 BACK_ROWS = QUARTERS * MAIN + 16
-STEPS = (0, 1, 4, 5, 6, 7, 2, 3)
+STEPS = (4, 5, 6, 7, 0, 1, 2, 3)
+GROUP = 4
+GROUP_ROWS = GROUP * MAIN + 16
 
 
 def copies_of(experts):
@@ -254,7 +256,7 @@
 def partners(experts, tokens):
     row = iota((experts, tokens), 0)
     step = jnp.zeros((experts, tokens), jnp.int32)
-    for c in range(1, experts):
+    for c in range(experts):
         step = jnp.where(row == c, STEPS[c], step)
     return jnp.bitwise_xor(step, lax.axis_index("expert"))
 
@@ -358,25 +360,24 @@
 
 
 def expert_kernel(*refs):
-    back_count = len(refs) - 8
-    experts = back_count // 2
-    recv_refs = refs[:experts]
-    gate_ref, up_ref, down_ref = refs[experts : experts + 3]
-    back_refs = refs[experts + 3 : 2 * experts + 3]
-    x_ref, s_ref, dg_ref, du_ref, hid_ref = refs[2 * experts + 3 :]
+    recv_refs = refs[:GROUP]
+    gate_ref, up_ref, down_ref = refs[GROUP : GROUP + 3]
+    back_refs = refs[GROUP + 3 : 2 * GROUP + 3]
+    x_ref, s_ref, dg_ref, du_ref, hid_ref = refs[2 * GROUP + 3 :]
     width = recv_refs[0].shape[1]
-    main_rows = experts * MAIN
+    main_rows = GROUP * MAIN
     tail = jnp.concatenate([ref[2 * QUARTERS * MAIN :, :] for ref in recv_refs], axis=0)
-    row = iota((4 * experts, main_rows), 0)
-    col = iota((4 * experts, main_rows), 1)
-    kind = (row >= 2 * experts).astype(jnp.int32)
-    chunk = jnp.right_shift(row - kind * 2 * experts, 1)
-    base = chunk * MAIN + kind * 8 + jnp.bitwise_and(row, 1) * 4
+    row = iota((2 * MAIN, main_rows), 0)
+    col = iota((2 * MAIN, main_rows), 1)
+    inner = jnp.bitwise_and(row, MAIN - 1)
+    base = jnp.right_shift(inner, 1) * MAIN + (row - inner) // 2 + jnp.bitwise_and(row, 1) * 4
+    real = inner < 2 * GROUP
     for q in range(QUARTERS):
         cols = slice(q * width, (q + 1) * width)
-        picked = jnp.dot(mask(col == base + q), tail, preferred_element_type=F32).astype(BF)
-        x_ref[main_rows:, cols] = picked[: 2 * experts]
-        s_ref[main_rows:, cols] = picked[2 * experts :]
+        place = mask(jnp.logical_and(real, col == base + q))
+        picked = jnp.dot(place, tail, preferred_element_type=F32).astype(BF)
+        x_ref[main_rows:, cols] = picked[:MAIN]
+        s_ref[main_rows:, cols] = picked[MAIN:]
         for i, ref in enumerate(recv_refs):
             here = slice(i * MAIN, (i + 1) * MAIN)
             x_ref[here, cols] = ref[q * MAIN : (q + 1) * MAIN, :]
@@ -409,8 +410,8 @@
         preferred_element_type=F32,
         precision=lax.Precision.HIGHEST,
     )
-    trow = iota((main_rows, 2 * experts), 0)
-    tcol = iota((main_rows, 2 * experts), 1)
+    trow = iota((main_rows, MAIN), 0)
+    tcol = iota((main_rows, MAIN), 1)
     inner = jnp.bitwise_and(trow, MAIN - 1)
     source = jnp.right_shift(trow, 4) * 2 + jnp.right_shift(inner, 2)
     spread = jnp.zeros((main_rows, width), F32)
@@ -427,32 +428,32 @@
         ).astype(BF)
 
 
-def grads_of(half, x_ref, s_ref, dg_ref, du_ref, hid_ref):
-    rows = x_ref.shape[1] // 2
-    cols = pl.ds(pl.multiple_of(half * rows, rows), rows)
-    x_half = x_ref[:, cols]
-    s_half = s_ref[:, cols]
-    return (
-        lax.dot_general(x_half, dg_ref[...], CONTRACT_ROWS, preferred_element_type=F32),
-        lax.dot_general(x_half, du_ref[...], CONTRACT_ROWS, preferred_element_type=F32),
-        lax.dot_general(s_half, hid_ref[...], CONTRACT_ROWS, preferred_element_type=F32),
-    )
-
-
-def other_half_kernel(x_ref, s_ref, dg_ref, du_ref, hid_ref, out_ref):
-    half = 1 - lax.axis_index("replica")
-    parts = grads_of(half, x_ref, s_ref, dg_ref, du_ref, hid_ref)
+def grads_of(half, refs):
+    sums = [None] * 3
+    for first in range(0, len(refs), 5):
+        x_ref, s_ref, *right = refs[first : first + 5]
+        rows = x_ref.shape[1] // 2
+        cols = pl.ds(pl.multiple_of(half * rows, rows), rows)
+        x_half = x_ref[:, cols]
+        for n, left in enumerate((x_half, x_half, s_ref[:, cols])):
+            part = lax.dot_general(left, right[n][...], CONTRACT_ROWS, preferred_element_type=F32)
+            sums[n] = part if sums[n] is None else sums[n] + part
+    return sums
+
+
+def other_half_kernel(*refs):
+    out_ref = refs[-1]
+    parts = grads_of(1 - lax.axis_index("replica"), refs[:-1])
     rows = parts[0].shape[0]
     for n in range(3):
         out_ref[n * rows : (n + 1) * rows, :] = parts[n].astype(BF)
 
 
-def own_half_kernel(
-    x_ref, s_ref, dg_ref, du_ref, hid_ref, came_ref, gate_ref, up_ref, down_ref
-):
-    parts = grads_of(lax.axis_index("replica"), x_ref, s_ref, dg_ref, du_ref, hid_ref)
+def own_half_kernel(*refs):
+    came_ref = refs[-4]
+    parts = grads_of(lax.axis_index("replica"), refs[:-4])
     rows = parts[0].shape[0]
-    for n, out_ref in enumerate((gate_ref, up_ref, down_ref)):
+    for n, out_ref in enumerate(refs[-3:]):
         came = came_ref[n * rows : (n + 1) * rows, :].astype(F32)
         out_ref[...] = (parts[n].astype(BF).astype(F32) + came).astype(BF)
 
@@ -480,9 +481,10 @@
         token_ref[:, q * width : (q + 1) * width] = total.astype(BF)
     lane_index = iota((width, tokens), 0)
     found = []
-    for k, ref in enumerate(ret_refs):
-        mine = slot[k : k + 1]
-        lane = jnp.where(mine < MAIN, k * MAIN + mine, experts * MAIN + 2 * k + mine - MAIN)
+    for c, ref in enumerate(ret_refs):
+        mine = slot[c : c + 1]
+        place = c % GROUP
+        lane = jnp.where(mine < MAIN, place * MAIN + mine, GROUP * MAIN + 2 * place + mine - MAIN)
         lane = jnp.where(mine < 0, -1, lane)
         sums = jnp.dot(
             ref[QUARTERS * MAIN :, :], mask(lane_index == lane), preferred_element_type=F32
@@ -513,13 +515,12 @@
     )(*arrays)
 
 
-def exchange(chunks):
-    count = len(chunks)
-    moved = [
-        lax.ppermute(chunk, "expert", [(i, i ^ step) for i in range(count)])
-        for chunk, step in zip(chunks[1:], STEPS[1:])
+def exchange(chunks, steps):
+    experts = lax.axis_size("expert")
+    return [
+        lax.ppermute(chunk, "expert", [(i, i ^ step) for i in range(experts)]) if step else chunk
+        for chunk, step in zip(chunks, steps)
     ]
-    return [chunks[0], *moved]
 
 
 def hold_kernel(*refs):
@@ -567,38 +568,40 @@
         ],
     )
     slot, gates = routed[experts:]
-    recv = exchange(routed[:experts])
-    held = [recv[0], gate_proj[0], up_proj[0], down_proj[0]]
-    held = local_call(
+    recv = exchange(routed[:experts], STEPS)
+    matrices = [gate_proj[0], up_proj[0], down_proj[0]]
+    matrices = local_call(
         hold_kernel,
-        [(array.shape, BF) for array in held],
-        held,
+        [(array.shape, BF) for array in matrices],
+        matrices,
         "hold",
         0,
         4 * 3 * model_width * hidden_width,
     )
-    matmul = 2 * served * model_width * hidden_width
-    outs = local_call(
-        expert_kernel,
-        [((BACK_ROWS, width), BF)] * experts
-        + [((served, model_width), BF)] * 2
-        + [((served, hidden_width), BF)] * 3,
-        [held[0], *recv[1:], *held[1:]],
-        "expert_rows",
-        5 * matmul,
-        2 * 3 * model_width * hidden_width,
-    )
-    factors = outs[experts:]
-    returned = exchange(outs[:experts])
-    returned[1], factors = lax.optimization_barrier((returned[1], factors))
+    matmul = 2 * GROUP_ROWS * model_width * hidden_width
+    returned, factors = [], []
+    for first in range(0, experts, GROUP):
+        outs = local_call(
+            expert_kernel,
+            [((BACK_ROWS, width), BF)] * GROUP
+            + [((GROUP_ROWS, model_width), BF)] * 2
+            + [((GROUP_ROWS, hidden_width), BF)] * 3,
+            [*recv[first : first + GROUP], *matrices],
+            "expert_rows",
+            5 * matmul,
+            2 * 3 * model_width * hidden_width,
+        )
+        returned += exchange(outs[:GROUP], STEPS[first : first + GROUP])
+        factors += outs[GROUP:]
+    returned[:GROUP], factors = lax.optimization_barrier((returned[:GROUP], factors))
     half = model_width // 2
     (leaving,) = local_call(
         other_half_kernel,
         [((3 * half, hidden_width), BF)],
         factors,
         "other_half",
-        3 * matmul // 2,
-        2 * 3 * half * hidden_width,
+        1,
+        1,
     )
     came = lax.ppermute(leaving, "replica", [(0, 1), (1, 0)])
     shares = local_call(
@@ -606,8 +609,8 @@
         [((half, hidden_width), BF)] * 3,
         [*factors, came],
         "own_half",
-        3 * matmul // 2,
-        2 * 2 * 3 * half * hidden_width,
+        1,
+        1,
     )
     returned, shares = lax.optimization_barrier((returned, shares))
     token_grad, gate_grad = local_call(

time: 44 us -> 45.8 us (1.041)
  Pallas kernels: 7.2 us -> 8.57 us
  starting transfers between devices: 24.4 us -> 25.7 us
  local copies, waits for them, and re-layouts: 4.3 us -> 3.42 us
    pallas_call x6 -> x7, Pallas kernels: 7.2 us -> 8.57 us  [local_call(): pl.pallas_call(kernel, out_shape=[jax.ShapeDtypeStruct(shape, kind) for s...]
    ppermute x14, starting transfers between devices: 24.3 us -> 25.6 us  [exchange(): lax.ppermute(chunk, 'expert', [(i, i ^ step) for i in range(experts)])]
    unnamed x14, local copies, waits for them, and re-layouts: 4.3 us -> 3.42 us
  transfers between devices with their start and end apart: 15 -> 15, of which waited for: 5 -> 5; matrix products, arithmetic and copies ran while one was open for 0% -> 0% of each run, Pallas kernels for 4% -> 10%
where the time goes in v3:
time: 45.8 us; the launch traced here: 45.5 us
  starting transfers between devices  25.7 us (56%)
  Pallas kernels  8.57 us (19%)
  waiting for transfers between devices  7.08 us (15%)
  local copies, waits for them, and re-layouts  3.42 us (7%)
  between operations  0.76 us (2%)
    ppermute x14, starting transfers between devices, exchange(): lax.ppermute(chunk, 'expert', [(i, i ^ step) for i in range(experts)])  25.6 us
    pallas_call x7, Pallas kernels, local_call(): pl.pallas_call(kernel, out_shape=[jax.ShapeDtypeStruct(shape, kind) for s...  8.57 us
    ppermute x14, waiting for transfers between devices, exchange(): lax.ppermute(chunk, 'expert', [(i, i ^ step) for i in range(experts)])  7.07 us
    unnamed x14, local copies, waits for them, and re-layouts  3.42 us
  transfers between devices with their start and end apart: 15, of which 5 were waited for; matrix products, arithmetic and copies ran while one was open for 0% of the time, Pallas kernels for 10%

profile of v3, /device:TPU:0, one launch (start us, length us, event | category | flops | bytes accessed | tf_op | source)
XLA Modules:
  0.0 45.5 jit_solution(3865915940869822701)
XLA Ops:
  0.6 2.3 %route.1 = (bf16[144,256]{1,0:T(8,128)(2,1)}, bf16[144,256]{1,0:T(8,128)(2,1)}, bf16[144,256]{1,0:T(8,128)(2,1)}, bf16[144,256]{1,0:T(8,128)(2,1)}, bf16[144,256...) custom-call(s32[8]{0:T(128)} %plan_hbm.1, ...), custom_call_target="tpu_custom_call" | custom-call | flops 75497472 | bytes 1114112 | tf_op jit(solution)/shard_map/route/pallas_call | solution.py:506
  3.0 4.1 %collective-permute-start = (bf16[144,256]{1,0:T(8,128)(2,1)}, bf16[144,256]{1,0:T(8,128)(2,1)S(1)}, u32[]{:S(2)}, u32[]{:S(2)}) collective-permute-start(bf16[144,256]{1,0:T(8,128)(2,1)} %get-tuple-element.68), channel_id=1, source_target_pairs={{0,8},{2,10},{4,12},{6,14},{8,0},{10,2},{12,4},{14,6},{1,9},{3,11}... | collective-permute-start | bytes 221192 | tf_op jit(solution)/shard_map/ppermute | solution.py:521
  7.1 1.3 %collective-permute-start.1 = (bf16[144,256]{1,0:T(8,128)(2,1)}, bf16[144,256]{1,0:T(8,128)(2,1)S(1)}, u32[]{:S(2)}, u32[]{:S(2)}) collective-permute-start(bf16[144,256]{1,0:T(8,128)(2,1)} %get-tuple-element.69), channel_id=1, source_target_pairs={{0,10},{2,8},{4,14},{6,12},{8,2},{10,0},{12,6},{14,4},{1,11},{3,9}... | collective-permute-start | bytes 221192 | tf_op jit(solution)/shard_map/ppermute | solution.py:521
  8.3 3.6 %collective-permute-start.2 = (bf16[144,256]{1,0:T(8,128)(2,1)}, bf16[144,256]{1,0:T(8,128)(2,1)S(1)}, u32[]{:S(2)}, u32[]{:S(2)}) collective-permute-start(bf16[144,256]{1,0:T(8,128)(2,1)} %get-tuple-element.70), channel_id=1, source_target_pairs={{0,12},{2,14},{4,8},{6,10},{8,4},{10,6},{12,0},{14,2},{1,13},{3,15... | collective-permute-start | bytes 221192 | tf_op jit(solution)/shard_map/ppermute | solution.py:521
  11.9 0.0 collective-permute-start.3
  11.9 1.7 %collective-permute-start.8 = (bf16[144,256]{1,0:T(8,128)(2,1)}, bf16[144,256]{1,0:T(8,128)(2,1)S(1)}, u32[]{:S(2)}, u32[]{:S(2)}) collective-permute-start(bf16[144,256]{1,0:T(8,128)(2,1)} %get-tuple-element.85), channel_id=1, source_target_pairs={{0,2},{2,0},{4,6},{6,4},{8,10},{10,8},{12,14},{14,12},{1,3},{3,1},... | collective-permute-start | bytes 221192 | tf_op jit(solution)/shard_map/ppermute | solution.py:521
  13.6 0.0 collective-permute-done.refs_0_
  13.6 2.2 %collective-permute-start.9 = (bf16[144,256]{1,0:T(8,128)(2,1)}, bf16[144,256]{1,0:T(8,128)(2,1)S(1)}, u32[]{:S(2)}, u32[]{:S(2)}) collective-permute-start(bf16[144,256]{1,0:T(8,128)(2,1)} %get-tuple-element.86), channel_id=1, source_target_pairs={{0,4},{2,6},{4,0},{6,2},{8,12},{10,14},{12,8},{14,10},{1,5},{3,7},... | collective-permute-start | bytes 221192 | tf_op jit(solution)/shard_map/ppermute | solution.py:521
  15.8 2.5 %collective-permute-done.1.refs_1_ = bf16[144,256]{1,0:T(8,128)(2,1)S(1)} collective-permute-done((bf16[144,256]{1,0:T(8,128)(2,1)}, bf16[144,256]{1,0:T(8,128)(2,1)S(1)}, u32[]{:S(2)}, u32[]{:S(2)}) %collective-permute-start.1) | collective-permute-done | bytes 73760 | tf_op jit(solution)/shard_map/ppermute | solution.py:521
  18.3 1.0 %collective-permute-start.10 = (bf16[144,256]{1,0:T(8,128)(2,1)}, bf16[144,256]{1,0:T(8,128)(2,1)S(1)}, u32[]{:S(2)}, u32[]{:S(2)}) collective-permute-start(bf16[144,256]{1,0:T(8,128)(2,1)} %get-tuple-element.87), channel_id=1, source_target_pairs={{0,6},{2,4},{4,2},{6,0},{8,14},{10,12},{12,10},{14,8},{1,7},{3,5},... | collective-permute-start | bytes 221192 | tf_op jit(solution)/shard_map/ppermute | solution.py:521
  19.3 1.1 %copy-done = bf16[1,1024,384]{2,1,0:T(8,128)(2,1)S(1)} copy-done((bf16[1,1024,384]{2,1,0:T(8,128)(2,1)S(1)}, bf16[1,1024,384]{2,1,0:T(8,128)(2,1)}, u32[]{:S(2)}) %copy-start) | copy-done | bytes 786456
  20.4 1.1 %copy-done.1 = bf16[1,1024,384]{2,1,0:T(8,128)(2,1)S(1)} copy-done((bf16[1,1024,384]{2,1,0:T(8,128)(2,1)S(1)}, bf16[1,1024,384]{2,1,0:T(8,128)(2,1)}, u32[]{:S(2)}) %copy-start.1) | copy-done | bytes 786456
  21.6 1.1 %copy-done.2 = bf16[1,1024,384]{2,1,0:T(8,128)(2,1)S(1)} copy-done((bf16[1,1024,384]{2,1,0:T(8,128)(2,1)S(1)}, bf16[1,1024,384]{2,1,0:T(8,128)(2,1)}, u32[]{:S(2)}) %copy-start.2) | copy-done | bytes 786456
  22.7 0.2 hold.1
  22.9 0.0 collective-permute-done.2.refs_2_
  22.9 0.0 collective-permute-done.3.refs_3_
  22.9 0.0 copy-start.3
  22.9 1.3 %expert_rows.2 = (bf16[80,256]{1,0:T(8,128)(2,1)S(1)}, bf16[80,256]{1,0:T(8,128)(2,1)S(1)}, bf16[80,256]{1,0:T(8,128)(2,1)S(1)}, bf16[80,256]{1,0:T(8,128)(2,1)S...) custom-call(bf16[144,256]{1,0:T(8,128)(2,1)S(1)} %collective-permute, ...), custom_call_target="tpu_custom_call" | custom-call | flops 314572800 | bytes 2359296 | tf_op jit(solution)/shard_map/expert_rows/pallas_call | solution.py:506
  24.2 3.4 %collective-permute-start.4 = (bf16[80,256]{1,0:T(8,128)(2,1)S(1)}, bf16[80,256]{1,0:T(8,128)(2,1)S(1)}, u32[]{:S(2)}, u32[]{:S(2)}) collective-permute-start(bf16[80,256]{1,0:T(8,128)(2,1)S(1)} %get-tuple-element.75), channel_id=1, source_target_pairs={{0,8},{2,10},{4,12},{6,14},{8,0},{10,2},{12,4},{14,6},{1,9},{3,11}... | collective-permute-start | bytes 122888 | tf_op jit(solution)/shard_map/ppermute | solution.py:521
  27.7 0.9 %collective-permute-start.5 = (bf16[80,256]{1,0:T(8,128)(2,1)S(1)}, bf16[80,256]{1,0:T(8,128)(2,1)S(1)}, u32[]{:S(2)}, u32[]{:S(2)}) collective-permute-start(bf16[80,256]{1,0:T(8,128)(2,1)S(1)} %get-tuple-element.76), channel_id=1, source_target_pairs={{0,10},{2,8},{4,14},{6,12},{8,2},{10,0},{12,6},{14,4},{1,11},{3,9}... | collective-permute-start | bytes 122888 | tf_op jit(solution)/shard_map/ppermute | solution.py:521
  28.6 0.0 collective-permute-done.8.refs_1_
  28.6 1.5 %collective-permute-start.6 = (bf16[80,256]{1,0:T(8,128)(2,1)S(1)}, bf16[80,256]{1,0:T(8,128)(2,1)S(1)}, u32[]{:S(2)}, u32[]{:S(2)}) collective-permute-start(bf16[80,256]{1,0:T(8,128)(2,1)S(1)} %get-tuple-element.77), channel_id=1, source_target_pairs={{0,12},{2,14},{4,8},{6,10},{8,4},{10,6},{12,0},{14,2},{1,13},{3,15... | collective-permute-start | bytes 122888 | tf_op jit(solution)/shard_map/ppermute | solution.py:521
  30.0 0.0 collective-permute-done.9.refs_2_
  30.0 2.4 %collective-permute-start.7 = (bf16[80,256]{1,0:T(8,128)(2,1)S(1)}, bf16[80,256]{1,0:T(8,128)(2,1)S(1)}, u32[]{:S(2)}, u32[]{:S(2)}) collective-permute-start(bf16[80,256]{1,0:T(8,128)(2,1)S(1)} %get-tuple-element.78), channel_id=1, source_target_pairs={{0,14},{2,12},{4,10},{6,8},{8,6},{10,4},{12,2},{14,0},{1,15},{3,13... | collective-permute-start | bytes 122888 | tf_op jit(solution)/shard_map/ppermute | solution.py:521
  32.5 0.0 collective-permute-done.10.refs_3_
  32.5 0.0 copy-done.3
  32.5 1.3 %expert_rows.3 = (bf16[80,256]{1,0:T(8,128)(2,1)S(1)}, bf16[80,256]{1,0:T(8,128)(2,1)S(1)}, bf16[80,256]{1,0:T(8,128)(2,1)S(1)}, bf16[80,256]{1,0:T(8,128)(2,1)S...) custom-call(bf16[144,256]{1,0:T(8,128)(2,1)S(1)} %copy-done.3, ...), custom_call_target="tpu_custom_call" | custom-call | flops 314572800 | bytes 2359296 | tf_op jit(solution)/shard_map/expert_rows/pallas_call | solution.py:506
  33.8 0.0 collective-permute-done.4.refs_0_
  33.8 0.0 collective-permute-done.5.refs_1_
  33.8 0.8 %collective-permute-done.6.refs_2_ = bf16[80,256]{1,0:T(8,128)(2,1)S(1)} collective-permute-done((bf16[80,256]{1,0:T(8,128)(2,1)S(1)}, bf16[80,256]{1,0:T(8,128)(2,1)S(1)}, u32[]{:S(2)}, u32[]{:S(2)}) %collective-permute-start.6) | collective-permute-done | bytes 40992 | tf_op jit(solution)/shard_map/ppermute | solution.py:521
  34.6 2.2 %collective-permute-done.7.refs_3_ = bf16[80,256]{1,0:T(8,128)(2,1)S(1)} collective-permute-done((bf16[80,256]{1,0:T(8,128)(2,1)S(1)}, bf16[80,256]{1,0:T(8,128)(2,1)S(1)}, u32[]{:S(2)}, u32[]{:S(2)}) %collective-permute-start.7) | collective-permute-done | bytes 40992 | tf_op jit(solution)/shard_map/ppermute | solution.py:521
  36.8 0.8 %other_half.1 = bf16[1536,384]{1,0:T(8,128)(2,1)S(1)} custom-call(bf16[80,1024]{1,0:T(8,128)(2,1)S(1)} %get-tuple-element.101.refs_0_, bf16[80,1024]{1,0:T(8,128)(2,1)S(1)} %get-tuple-element.102.refs_1_, bf16[80,384]{1,0:T(8,128)(2,1)S(1)} %get-tuple-element.103.refs_2_, bf16[80,384]{1,0:T(8,128)(2,1)S(1)} %get-tuple-element.104.refs_3_, ...), custom_call_target="tpu_custom_call" | custom-call | flops 1 | bytes 1 | tf_op jit(solution)/shard_map/other_half/pallas_call | solution.py:506
  37.6 0.0 copy-start.4
  37.6 0.0 copy-start.5
  37.6 0.0 copy-start.6
  37.6 0.1 collective-permute-start.14
  37.7 1.9 %collective-permute-start.11 = (bf16[80,256]{1,0:T(8,128)(2,1)S(1)}, bf16[80,256]{1,0:T(8,128)(2,1)S(1)}, u32[]{:S(2)}, u32[]{:S(2)}) collective-permute-start(bf16[80,256]{1,0:T(8,128)(2,1)S(1)} %get-tuple-element.98), channel_id=1, source_target_pairs={{0,2},{2,0},{4,6},{6,4},{8,10},{10,8},{12,14},{14,12},{1,3},{3,1},... | collective-permute-start | bytes 122888 | tf_op jit(solution)/shard_map/ppermute | solution.py:521
  39.6 0.0 collective-permute-start.12
  39.6 1.7 %collective-permute-start.13 = (bf16[80,256]{1,0:T(8,128)(2,1)S(1)}, bf16[80,256]{1,0:T(8,128)(2,1)S(1)}, u32[]{:S(2)}, u32[]{:S(2)}) collective-permute-start(bf16[80,256]{1,0:T(8,128)(2,1)S(1)} %get-tuple-element.100), channel_id=1, source_target_pairs={{0,6},{2,4},{4,2},{6,0},{8,14},{10,12},{12,10},{14,8},{1,7},{3,5},... | collective-permute-start | bytes 122888 | tf_op jit(solution)/shard_map/ppermute | solution.py:521
  41.2 0.0 collective-permute-done.14.refs_10_
  41.2 1.6 %own_half.1 = (bf16[512,384]{1,0:T(8,128)(2,1)}, bf16[512,384]{1,0:T(8,128)(2,1)}, bf16[512,384]{1,0:T(8,128)(2,1)}) custom-call(bf16[80,1024]{1,0:T(8,128)(2,1)S(1)} %get-tuple-element.101.refs_0_, bf16[80,1024]{1,0:T(8,128)(2,1)S(1)} %get-tuple-element.102.refs_1_, bf16[80,384]{1,0:T(8,128)(2,1)S(1)} %get-tuple-element.103.refs_2_, ...), custom_call_target="tpu_custom_call" | custom-call | flops 1 | bytes 1 | tf_op jit(solution)/shard_map/own_half/pallas_call | solution.py:506
  42.8 0.0 collective-permute-done.11.refs_5_
  42.8 0.8 %collective-permute-done.12.refs_6_ = bf16[80,256]{1,0:T(8,128)(2,1)S(1)} collective-permute-done((bf16[80,256]{1,0:T(8,128)(2,1)S(1)}, bf16[80,256]{1,0:T(8,128)(2,1)S(1)}, u32[]{:S(2)}, u32[]{:S(2)}) %collective-permute-start.12) | collective-permute-done | bytes 40992 | tf_op jit(solution)/shard_map/ppermute | solution.py:521
  43.6 0.8 %collective-permute-done.13.refs_7_ = bf16[80,256]{1,0:T(8,128)(2,1)S(1)} collective-permute-done((bf16[80,256]{1,0:T(8,128)(2,1)S(1)}, bf16[80,256]{1,0:T(8,128)(2,1)S(1)}, u32[]{:S(2)}, u32[]{:S(2)}) %collective-permute-start.13) | collective-permute-done | bytes 40992 | tf_op jit(solution)/shard_map/ppermute | solution.py:521
  44.5 0.0 copy-done.4
  44.5 0.0 copy-done.5
  44.5 0.0 copy-done.6
  44.5 1.0 %combine.1 = (bf16[128,1024]{1,0:T(8,128)(2,1)}, bf16[8,128]{1,0:T(8,128)(2,1)}) custom-call(s32[8,128]{1,0:T(8,128)S(1)} %bitcast.14, s32[8,128]{1,0:T(8,128)S(1)} %copy-done.5, f32[8,128]{1,0:T(8,128)S(1)} %copy-done.6, bf16[80,256]{1,0:T(8,128)(2,1)S(1)} %collective-permute-done.4.refs_0_, bf16[80,256]{1,0:T(8,128)(2,1)S(1)} %collective-permute-done.5.refs_1_, ...), custom_call_target="tpu_custom_call" | custom-call | flops 37748736 | bytes 524288 | tf_op jit(solution)/shard_map/combine/pallas_call | solution.py:506
  (3 shorter events, 0.0 us)
Async XLA Ops:
  3.0 10.7 %collective-permute-start = (bf16[144,256]{1,0:T(8,128)(2,1)}, bf16[144,256]{1,0:T(8,128)(2,1)S(1)}, u32[]{:S(2)}, u32[]{:S(2)}) collective-permute-start(bf16[144,256]{1,0:T(8,128)(2,1)} %get-tuple-element.68), channel_id=1, source_target_pairs={{0,8},{2,10},{4,12},{6,14},{8,0},{10,2},{12,4},{14,6},{1,9},{3,11}... | collective-permute-start | bytes 221192 | tf_op jit(solution)/shard_map/ppermute | solution.py:521
  7.1 11.2 %collective-permute-start.1 = (bf16[144,256]{1,0:T(8,128)(2,1)}, bf16[144,256]{1,0:T(8,128)(2,1)S(1)}, u32[]{:S(2)}, u32[]{:S(2)}) collective-permute-start(bf16[144,256]{1,0:T(8,128)(2,1)} %get-tuple-element.69), channel_id=1, source_target_pairs={{0,10},{2,8},{4,14},{6,12},{8,2},{10,0},{12,6},{14,4},{1,11},{3,9}... | collective-permute-start | bytes 221192 | tf_op jit(solution)/shard_map/ppermute | solution.py:521
  8.3 14.6 %collective-permute-start.2 = (bf16[144,256]{1,0:T(8,128)(2,1)}, bf16[144,256]{1,0:T(8,128)(2,1)S(1)}, u32[]{:S(2)}, u32[]{:S(2)}) collective-permute-start(bf16[144,256]{1,0:T(8,128)(2,1)} %get-tuple-element.70), channel_id=1, source_target_pairs={{0,12},{2,14},{4,8},{6,10},{8,4},{10,6},{12,0},{14,2},{1,13},{3,15... | collective-permute-start | bytes 221192 | tf_op jit(solution)/shard_map/ppermute | solution.py:521
  11.9 11.0 %collective-permute-start.3 = (bf16[144,256]{1,0:T(8,128)(2,1)}, bf16[144,256]{1,0:T(8,128)(2,1)S(1)}, u32[]{:S(2)}, u32[]{:S(2)}) collective-permute-start(bf16[144,256]{1,0:T(8,128)(2,1)} %get-tuple-element.71), channel_id=1, source_target_pairs={{0,14},{2,12},{4,10},{6,8},{8,6},{10,4},{12,2},{14,0},{1,15},{3,13... | collective-permute-start | bytes 221192 | tf_op jit(solution)/shard_map/ppermute | solution.py:521
  11.9 16.6 %collective-permute-start.8 = (bf16[144,256]{1,0:T(8,128)(2,1)}, bf16[144,256]{1,0:T(8,128)(2,1)S(1)}, u32[]{:S(2)}, u32[]{:S(2)}) collective-permute-start(bf16[144,256]{1,0:T(8,128)(2,1)} %get-tuple-element.85), channel_id=1, source_target_pairs={{0,2},{2,0},{4,6},{6,4},{8,10},{10,8},{12,14},{14,12},{1,3},{3,1},... | collective-permute-start | bytes 221192 | tf_op jit(solution)/shard_map/ppermute | solution.py:521
  13.6 16.4 %collective-permute-start.9 = (bf16[144,256]{1,0:T(8,128)(2,1)}, bf16[144,256]{1,0:T(8,128)(2,1)S(1)}, u32[]{:S(2)}, u32[]{:S(2)}) collective-permute-start(bf16[144,256]{1,0:T(8,128)(2,1)} %get-tuple-element.86), channel_id=1, source_target_pairs={{0,4},{2,6},{4,0},{6,2},{8,12},{10,14},{12,8},{14,10},{1,5},{3,7},... | collective-permute-start | bytes 221192 | tf_op jit(solution)/shard_map/ppermute | solution.py:521
  18.3 14.2 %collective-permute-start.10 = (bf16[144,256]{1,0:T(8,128)(2,1)}, bf16[144,256]{1,0:T(8,128)(2,1)S(1)}, u32[]{:S(2)}, u32[]{:S(2)}) collective-permute-start(bf16[144,256]{1,0:T(8,128)(2,1)} %get-tuple-element.87), channel_id=1, source_target_pairs={{0,6},{2,4},{4,2},{6,0},{8,14},{10,12},{12,10},{14,8},{1,7},{3,5},... | collective-permute-start | bytes 221192 | tf_op jit(solution)/shard_map/ppermute | solution.py:521
  19.3 1.1 %copy-start = (bf16[1,1024,384]{2,1,0:T(8,128)(2,1)S(1)}, bf16[1,1024,384]{2,1,0:T(8,128)(2,1)}, u32[]{:S(2)}) copy-start(bf16[1,1024,384]{2,1,0:T(8,128)(2,1)} %param.15) | copy-start | bytes 2359300
  20.4 1.1 %copy-start.1 = (bf16[1,1024,384]{2,1,0:T(8,128)(2,1)S(1)}, bf16[1,1024,384]{2,1,0:T(8,128)(2,1)}, u32[]{:S(2)}) copy-start(bf16[1,1024,384]{2,1,0:T(8,128)(2,1)} %param.16) | copy-start | bytes 2359300
  21.6 1.1 %copy-start.2 = (bf16[1,1024,384]{2,1,0:T(8,128)(2,1)S(1)}, bf16[1,1024,384]{2,1,0:T(8,128)(2,1)}, u32[]{:S(2)}) copy-start(bf16[1,1024,384]{2,1,0:T(8,128)(2,1)} %param.17) | copy-start | bytes 2359300
  22.9 9.6 %copy-start.3 = (bf16[144,256]{1,0:T(8,128)(2,1)S(1)}, bf16[144,256]{1,0:T(8,128)(2,1)}, u32[]{:S(2)}) copy-start(bf16[144,256]{1,0:T(8,128)(2,1)} %get-tuple-element.84.refs_0_) | copy-start | bytes 221188
  24.2 9.6 %collective-permute-start.4 = (bf16[80,256]{1,0:T(8,128)(2,1)S(1)}, bf16[80,256]{1,0:T(8,128)(2,1)S(1)}, u32[]{:S(2)}, u32[]{:S(2)}) collective-permute-start(bf16[80,256]{1,0:T(8,128)(2,1)S(1)} %get-tuple-element.75), channel_id=1, source_target_pairs={{0,8},{2,10},{4,12},{6,14},{8,0},{10,2},{12,4},{14,6},{1,9},{3,11}... | collective-permute-start | bytes 122888 | tf_op jit(solution)/shard_map/ppermute | solution.py:521
  27.7 6.1 %collective-permute-start.5 = (bf16[80,256]{1,0:T(8,128)(2,1)S(1)}, bf16[80,256]{1,0:T(8,128)(2,1)S(1)}, u32[]{:S(2)}, u32[]{:S(2)}) collective-permute-start(bf16[80,256]{1,0:T(8,128)(2,1)S(1)} %get-tuple-element.76), channel_id=1, source_target_pairs={{0,10},{2,8},{4,14},{6,12},{8,2},{10,0},{12,6},{14,4},{1,11},{3,9}... | collective-permute-start | bytes 122888 | tf_op jit(solution)/shard_map/ppermute | solution.py:521
  28.6 6.0 %collective-permute-start.6 = (bf16[80,256]{1,0:T(8,128)(2,1)S(1)}, bf16[80,256]{1,0:T(8,128)(2,1)S(1)}, u32[]{:S(2)}, u32[]{:S(2)}) collective-permute-start(bf16[80,256]{1,0:T(8,128)(2,1)S(1)} %get-tuple-element.77), channel_id=1, source_target_pairs={{0,12},{2,14},{4,8},{6,10},{8,4},{10,6},{12,0},{14,2},{1,13},{3,15... | collective-permute-start | bytes 122888 | tf_op jit(solution)/shard_map/ppermute | solution.py:521
  30.0 6.7 %collective-permute-start.7 = (bf16[80,256]{1,0:T(8,128)(2,1)S(1)}, bf16[80,256]{1,0:T(8,128)(2,1)S(1)}, u32[]{:S(2)}, u32[]{:S(2)}) collective-permute-start(bf16[80,256]{1,0:T(8,128)(2,1)S(1)} %get-tuple-element.78), channel_id=1, source_target_pairs={{0,14},{2,12},{4,10},{6,8},{8,6},{10,4},{12,2},{14,0},{1,15},{3,13... | collective-permute-start | bytes 122888 | tf_op jit(solution)/shard_map/ppermute | solution.py:521
  37.6 6.9 %copy-start.4 = (s32[128,8]{0,1:T(8,128)S(1)}, s32[128,8]{0,1:T(8,128)}, u32[]{:S(2)}) copy-start(s32[128,8]{0,1:T(8,128)} %param.11) | copy-start | bytes 12292
  37.6 6.9 %copy-start.5 = (s32[8,128]{1,0:T(8,128)S(1)}, s32[8,128]{1,0:T(8,128)}, u32[]{:S(2)}) copy-start(s32[8,128]{1,0:T(8,128)} %get-tuple-element.66.slot_ref) | copy-start | bytes 12292
  37.6 6.9 %copy-start.6 = (f32[8,128]{1,0:T(8,128)S(1)}, f32[8,128]{1,0:T(8,128)}, u32[]{:S(2)}) copy-start(f32[8,128]{1,0:T(8,128)} %get-tuple-element.67.gates_ref) | copy-start | bytes 12292
  37.6 3.6 %collective-permute-start.14 = (bf16[1536,384]{1,0:T(8,128)(2,1)S(1)}, bf16[1536,384]{1,0:T(8,128)(2,1)S(1)}, u32[]{:S(2)}, u32[]{:S(2)}) collective-permute-start(bf16[1536,384]{1,0:T(8,128)(2,1)S(1)} %other_half.1), channel_id=1, source_target_pairs={{0,1},{1,0},{2,3},{3,2},{4,5},{5,4},{6,7},{7,6},{8,9},{9,8},{10,11... | collective-permute-start | bytes 3538952 | tf_op jit(solution)/shard_map/ppermute | solution.py:606
  37.7 5.2 %collective-permute-start.11 = (bf16[80,256]{1,0:T(8,128)(2,1)S(1)}, bf16[80,256]{1,0:T(8,128)(2,1)S(1)}, u32[]{:S(2)}, u32[]{:S(2)}) collective-permute-start(bf16[80,256]{1,0:T(8,128)(2,1)S(1)} %get-tuple-element.98), channel_id=1, source_target_pairs={{0,2},{2,0},{4,6},{6,4},{8,10},{10,8},{12,14},{14,12},{1,3},{3,1},... | collective-permute-start | bytes 122888 | tf_op jit(solution)/shard_map/ppermute | solution.py:521
  39.6 4.1 %collective-permute-start.12 = (bf16[80,256]{1,0:T(8,128)(2,1)S(1)}, bf16[80,256]{1,0:T(8,128)(2,1)S(1)}, u32[]{:S(2)}, u32[]{:S(2)}) collective-permute-start(bf16[80,256]{1,0:T(8,128)(2,1)S(1)} %get-tuple-element.99), channel_id=1, source_target_pairs={{0,4},{2,6},{4,0},{6,2},{8,12},{10,14},{12,8},{14,10},{1,5},{3,7},... | collective-permute-start | bytes 122888 | tf_op jit(solution)/shard_map/ppermute | solution.py:521
  39.6 4.9 %collective-permute-start.13 = (bf16[80,256]{1,0:T(8,128)(2,1)S(1)}, bf16[80,256]{1,0:T(8,128)(2,1)S(1)}, u32[]{:S(2)}, u32[]{:S(2)}) collective-permute-start(bf16[80,256]{1,0:T(8,128)(2,1)S(1)} %get-tuple-element.100), channel_id=1, source_target_pairs={{0,6},{2,4},{4,2},{6,0},{8,14},{10,12},{12,10},{14,8},{1,7},{3,5},... | collective-permute-start | bytes 122888 | tf_op jit(solution)/shard_map/ppermute | solution.py:521

commit v4 on v2

--- a/solution.py
+++ b/solution.py
@@ -236,11 +236,11 @@
 CONTRACT_COLS = (((1,), (1,)), ((), ()))
 MIB = 1024 * 1024
 
+BASES = (4, 6, 2)
 MAIN = 16
 QUARTERS = 4
 SEND_ROWS = 2 * QUARTERS * MAIN + 16
 BACK_ROWS = QUARTERS * MAIN + 16
-STEPS = (0, 1, 4, 5, 6, 7, 2, 3)
 
 
 def copies_of(experts):
@@ -253,10 +253,15 @@
 
 def partners(experts, tokens):
     row = iota((experts, tokens), 0)
-    step = jnp.zeros((experts, tokens), jnp.int32)
-    for c in range(1, experts):
-        step = jnp.where(row == c, STEPS[c], step)
+    step = jnp.bitwise_xor(jnp.bitwise_and(row, 1), lax.axis_index("replica"))
+    for d, base in enumerate(BASES):
+        step = jnp.where(jnp.right_shift(row, 1) == d + 1, step + base, step)
+    step = jnp.where(row < 2, row, step)
     return jnp.bitwise_xor(step, lax.axis_index("expert"))
+
+
+def chunk_views(refs, rows):
+    return [(refs[0], 0), (refs[1], 0)] + [(ref, part * rows) for ref in refs[2:] for part in (0, 1)]
 
 
 def mask(condition):
@@ -274,9 +279,12 @@
     sems = refs[-1]
     plan_ref, ids_ref, pick_ref, gate_ref, tok_ref, cot_ref = refs[-7:-1]
     slot_ref, gates_ref = refs[-9:-7]
-    send_refs = refs[:-9]
+    self_ref, near_ref, keep_ref, give_ref = refs[:-9]
     topk, tokens = ids_ref.shape
-    experts = len(send_refs)
+    experts = slot_ref.shape[0]
+    send_views = [(self_ref, 0), (near_ref, 0)] + [
+        (ref, d * SEND_ROWS) for d in range(len(BASES)) for ref in (keep_ref, give_ref)
+    ]
     width = tok_ref.shape[1] // QUARTERS
     copies = copies_of(experts)
     loads = [
@@ -348,25 +356,37 @@
             preferred_element_type=F32,
         )
     tail = tail.astype(BF)
-    for k in range(experts):
-        here = slice(k * MAIN, (k + 1) * MAIN)
+    for c, (ref, first) in enumerate(send_views):
+        here = slice(c * MAIN, (c + 1) * MAIN)
         for q in range(QUARTERS):
             cols = slice(q * width, (q + 1) * width)
-            send_refs[k][q * MAIN : (q + 1) * MAIN, :] = rows[here, cols]
-            send_refs[k][(QUARTERS + q) * MAIN : (QUARTERS + q + 1) * MAIN, :] = scaled[here, cols]
-        send_refs[k][2 * QUARTERS * MAIN :, :] = tail[here]
+            ref[first + q * MAIN : first + (q + 1) * MAIN, :] = rows[here, cols]
+            low = first + (QUARTERS + q) * MAIN
+            ref[low : low + MAIN, :] = scaled[here, cols]
+        low = first + 2 * QUARTERS * MAIN
+        ref[low : low + 16, :] = tail[here]
+
+
+def join_kernel(self_hbm, keep_ref, came_ref, self_ref, *double_refs):
+    self_ref[...] = self_hbm[...]
+    for d, ref in enumerate(double_refs):
+        rows = slice(d * SEND_ROWS, (d + 1) * SEND_ROWS)
+        ref[:SEND_ROWS, :] = keep_ref[rows, :]
+        ref[SEND_ROWS:, :] = came_ref[rows, :]
 
 
 def expert_kernel(*refs):
-    back_count = len(refs) - 8
-    experts = back_count // 2
-    recv_refs = refs[:experts]
-    gate_ref, up_ref, down_ref = refs[experts : experts + 3]
-    back_refs = refs[experts + 3 : 2 * experts + 3]
-    x_ref, s_ref, dg_ref, du_ref, hid_ref = refs[2 * experts + 3 :]
-    width = recv_refs[0].shape[1]
+    count = 2 + len(BASES)
+    recv_views = chunk_views(refs[:count], SEND_ROWS)
+    gate_ref, up_ref, down_ref = refs[count : count + 3]
+    back_views = chunk_views(refs[count + 3 : 2 * count + 3], BACK_ROWS)
+    x_ref, s_ref, dg_ref, du_ref, hid_ref = refs[2 * count + 3 :]
+    experts = len(recv_views)
+    width = refs[0].shape[1]
     main_rows = experts * MAIN
-    tail = jnp.concatenate([ref[2 * QUARTERS * MAIN :, :] for ref in recv_refs], axis=0)
+    tail = jnp.concatenate(
+        [ref[first + SEND_ROWS - 16 : first + SEND_ROWS, :] for ref, first in recv_views], axis=0
+    )
     row = iota((4 * experts, main_rows), 0)
     col = iota((4 * experts, main_rows), 1)
     kind = (row >= 2 * experts).astype(jnp.int32)
@@ -377,10 +397,11 @@
         picked = jnp.dot(mask(col == base + q), tail, preferred_element_type=F32).astype(BF)
         x_ref[main_rows:, cols] = picked[: 2 * experts]
         s_ref[main_rows:, cols] = picked[2 * experts :]
-        for i, ref in enumerate(recv_refs):
+        for i, (ref, first) in enumerate(recv_views):
             here = slice(i * MAIN, (i + 1) * MAIN)
-            x_ref[here, cols] = ref[q * MAIN : (q + 1) * MAIN, :]
-            s_ref[here, cols] = ref[(QUARTERS + q) * MAIN : (QUARTERS + q + 1) * MAIN, :]
+            x_ref[here, cols] = ref[first + q * MAIN : first + (q + 1) * MAIN, :]
+            low = first + (QUARTERS + q) * MAIN
+            s_ref[here, cols] = ref[low : low + MAIN, :]
     rows = x_ref[...]
     gate_pre = jnp.dot(rows, gate_ref[...], preferred_element_type=F32)
     up_pre = jnp.dot(rows, up_ref[...], preferred_element_type=F32)
@@ -419,10 +440,12 @@
         mine = jnp.logical_and(jnp.bitwise_and(inner, 3) == q, inner < 8)
         place = mask(jnp.logical_and(mine, tcol == source))
         spread += jnp.dot(place, grad[main_rows:, cols], preferred_element_type=F32)
-        for i, ref in enumerate(back_refs):
-            ref[q * MAIN : (q + 1) * MAIN, :] = grad[i * MAIN : (i + 1) * MAIN, cols]
-    for i, ref in enumerate(back_refs):
-        ref[QUARTERS * MAIN :, :] = jnp.concatenate(
+        for i, (ref, first) in enumerate(back_views):
+            low = first + q * MAIN
+            ref[low : low + MAIN, :] = grad[i * MAIN : (i + 1) * MAIN, cols]
+    for i, (ref, first) in enumerate(back_views):
+        low = first + QUARTERS * MAIN
+        ref[low : low + 16, :] = jnp.concatenate(
             [spread[i * MAIN : i * MAIN + 8], gate_lanes], axis=0
         ).astype(BF)
 
@@ -459,10 +482,13 @@
 
 def combine_kernel(ids_ref, slot_ref, gates_ref, *refs):
     token_ref, grad_ref = refs[-2:]
-    ret_refs = refs[:-2]
+    doubles = 2 + len(BASES)
+    ret_views = [(refs[0], 0), (refs[1], 0)]
+    for kept_ref, given_ref in zip(refs[2:doubles], refs[doubles:-2]):
+        ret_views += [(kept_ref, 0), (given_ref, BACK_ROWS)]
     topk, tokens = ids_ref.shape
-    experts = len(ret_refs)
-    width = ret_refs[0].shape[1]
+    experts = len(ret_views)
+    width = refs[0].shape[1]
     ids = ids_ref[...]
     slot = slot_ref[...]
     slot16 = repeat_rows(slot, MAIN)
@@ -471,22 +497,23 @@
     wanted = MAIN + jnp.right_shift(inner, 2)
     last = jnp.where(jnp.logical_and(slot16 == wanted, inner < 8), 1.0, 0.0)
     quarter = jnp.bitwise_and(inner, 3)
-    tail = jnp.concatenate([ref[QUARTERS * MAIN :, :] for ref in ret_refs], axis=0)
+    tails = [ref[first + BACK_ROWS - 16 : first + BACK_ROWS, :] for ref, first in ret_views]
+    tail = jnp.concatenate(tails, axis=0)
     for q in range(QUARTERS):
-        main = jnp.concatenate([ref[q * MAIN : (q + 1) * MAIN, :] for ref in ret_refs], axis=0)
+        main = jnp.concatenate(
+            [ref[first + q * MAIN : first + (q + 1) * MAIN, :] for ref, first in ret_views], axis=0
+        )
         place = jnp.where(quarter == q, last, 0.0).astype(BF)
         total = lax.dot_general(onehot, main, CONTRACT_ROWS, preferred_element_type=F32)
         total += lax.dot_general(place, tail, CONTRACT_ROWS, preferred_element_type=F32)
         token_ref[:, q * width : (q + 1) * width] = total.astype(BF)
     lane_index = iota((width, tokens), 0)
     found = []
-    for k, ref in enumerate(ret_refs):
-        mine = slot[k : k + 1]
-        lane = jnp.where(mine < MAIN, k * MAIN + mine, experts * MAIN + 2 * k + mine - MAIN)
+    for c in range(experts):
+        mine = slot[c : c + 1]
+        lane = jnp.where(mine < MAIN, c * MAIN + mine, experts * MAIN + 2 * c + mine - MAIN)
         lane = jnp.where(mine < 0, -1, lane)
-        sums = jnp.dot(
-            ref[QUARTERS * MAIN :, :], mask(lane_index == lane), preferred_element_type=F32
-        )
+        sums = jnp.dot(tails[c], mask(lane_index == lane), preferred_element_type=F32)
         found.append(sums[8:9])
     found = jnp.concatenate(found, axis=0)
     kept = slot >= 0
@@ -513,13 +540,16 @@
     )(*arrays)
 
 
-def exchange(chunks):
-    count = len(chunks)
-    moved = [
-        lax.ppermute(chunk, "expert", [(i, i ^ step) for i in range(count)])
-        for chunk, step in zip(chunks[1:], STEPS[1:])
-    ]
-    return [chunks[0], *moved]
+def to_step(chunk, base):
+    experts = lax.axis_size("expert")
+    if base == 1:
+        return lax.ppermute(chunk, "expert", [(i, i ^ 1) for i in range(experts)])
+    pairs = [(2 * i + r, 2 * (i ^ (base + r)) + r) for i in range(experts) for r in range(2)]
+    return lax.ppermute(chunk, ("expert", "replica"), pairs)
+
+
+def to_twin(chunk):
+    return lax.ppermute(chunk, "replica", [(0, 1), (1, 0)])
 
 
 def hold_kernel(*refs):
@@ -546,9 +576,11 @@
     width = model_width // QUARTERS
     served = experts * (MAIN + 2)
     small = (topk, token_count)
-    routed = local_call(
+    count = len(BASES)
+    self_rows, near_rows, keep, give, slot, gates = local_call(
         route_kernel,
-        [((SEND_ROWS, width), BF)] * experts
+        [((SEND_ROWS, width), BF)] * 2
+        + [((count * SEND_ROWS, width), BF)] * 2
         + [((experts, token_count), jnp.int32), ((experts, token_count), F32)],
         [replica_plan, expert_ids.T, replica_pick.T, gate_values.T, tokens, cotangent],
         "route",
@@ -566,13 +598,22 @@
             pltpu.SemaphoreType.DMA((6,)),
         ],
     )
-    slot, gates = routed[experts:]
-    recv = exchange(routed[:experts])
-    held = [recv[0], gate_proj[0], up_proj[0], down_proj[0]]
-    held = local_call(
+    came = to_twin(give)
+    near_rows = to_step(near_rows, 1)
+    self_rows, *doubles = local_call(
+        join_kernel,
+        [((SEND_ROWS, width), BF)] + [((2 * SEND_ROWS, width), BF)] * count,
+        [self_rows, keep, came],
+        "join",
+        0,
+        2 * 2 * 7 * SEND_ROWS * width,
+    )
+    recv = [self_rows, near_rows, *map(to_step, doubles, BASES)]
+    matrices = [gate_proj[0], up_proj[0], down_proj[0]]
+    matrices = local_call(
         hold_kernel,
-        [(array.shape, BF) for array in held],
-        held,
+        [(array.shape, BF) for array in matrices],
+        matrices,
         "hold",
         0,
         4 * 3 * model_width * hidden_width,
@@ -580,34 +621,34 @@
     matmul = 2 * served * model_width * hidden_width
     outs = local_call(
         expert_kernel,
-        [((BACK_ROWS, width), BF)] * experts
+        [((BACK_ROWS, width), BF)] * 2
+        + [((2 * BACK_ROWS, width), BF)] * count
         + [((served, model_width), BF)] * 2
         + [((served, hidden_width), BF)] * 3,
-        [held[0], *recv[1:], *held[1:]],
+        [*recv, *matrices],
         "expert_rows",
         5 * matmul,
         2 * 3 * model_width * hidden_width,
     )
-    factors = outs[experts:]
-    returned = exchange(outs[:experts])
-    returned[1], factors = lax.optimization_barrier((returned[1], factors))
+    backs, factors = outs[: 2 + count], outs[2 + count :]
+    kept = list(map(to_step, backs[2:], BASES))
+    returned = [backs[0], to_step(backs[1], 1), *kept, *map(to_twin, kept)]
     half = model_width // 2
     (leaving,) = local_call(
         other_half_kernel,
         [((3 * half, hidden_width), BF)],
         factors,
         "other_half",
-        3 * matmul // 2,
-        2 * 3 * half * hidden_width,
-    )
-    came = lax.ppermute(leaving, "replica", [(0, 1), (1, 0)])
+        1,
+        1,
+    )
     shares = local_call(
         own_half_kernel,
         [((half, hidden_width), BF)] * 3,
-        [*factors, came],
+        [*factors, to_twin(leaving)],
         "own_half",
-        3 * matmul // 2,
-        2 * 2 * 3 * half * hidden_width,
+        1,
+        1,
     )
     returned, shares = lax.optimization_barrier((returned, shares))
     token_grad, gate_grad = local_call(

time: 44 us -> 44.2 us (level)
  waiting for transfers between devices: 7.06 us -> 17.5 us
  starting transfers between devices: 24.4 us -> 14.2 us
    ppermute x15 -> x13, waiting for transfers between devices: 7.06 us -> 17.5 us  [the longest x6 12.2 us: to_step(): return lax.ppermute(chunk, ('expert', 'replica'), pairs)]
    ppermute x15 -> x13, starting transfers between devices: 24.4 us -> 14.2 us  [the longest x6 10.3 us: to_step(): return lax.ppermute(chunk, ('expert', 'replica'), pairs)]
    unnamed x14 -> x16, local copies, waits for them, and re-layouts: 4.3 us -> 4.1 us
    pallas_call x6 -> x7, Pallas kernels: 7.2 us -> 7.31 us  [local_call(): pl.pallas_call(kernel, out_shape=[jax.ShapeDtypeStruct(shape, kind) for s...]
  transfers between devices with their start and end apart: 15 -> 13, of which waited for: 5 -> 8; matrix products, arithmetic and copies ran while one was open for 0% -> 0% of each run, Pallas kernels for 4% -> 4%
where the time goes in v4:
time: 44.2 us; the launch traced here: 43.9 us
  waiting for transfers between devices  17.5 us (40%)
  starting transfers between devices  14.2 us (32%)
  Pallas kernels  7.31 us (17%)
  local copies, waits for them, and re-layouts  4.1 us (9%)
  between operations  0.73 us (2%)
    ppermute x6, waiting for transfers between devices, to_step(): return lax.ppermute(chunk, ('expert', 'replica'), pairs)  12.2 us
    ppermute x6, starting transfers between devices, to_step(): return lax.ppermute(chunk, ('expert', 'replica'), pairs)  10.3 us
    pallas_call x7, Pallas kernels, local_call(): pl.pallas_call(kernel, out_shape=[jax.ShapeDtypeStruct(shape, kind) for s...  7.31 us
    unnamed x16, local copies, waits for them, and re-layouts  4.1 us
    ppermute x2, waiting for transfers between devices, to_step(): return lax.ppermute(chunk, 'expert', [(i, i ^ 1) for i in range(experts)])  3.99 us
    ppermute x2, starting transfers between devices, to_step(): return lax.ppermute(chunk, 'expert', [(i, i ^ 1) for i in range(experts)])  2.64 us
    ppermute x5, waiting for transfers between devices, to_twin(): return lax.ppermute(chunk, 'replica', [(0, 1), (1, 0)])  1.32 us
    ppermute x5, starting transfers between devices, to_twin(): return lax.ppermute(chunk, 'replica', [(0, 1), (1, 0)])  1.23 us
  transfers between devices with their start and end apart: 13, of which 8 were waited for; matrix products, arithmetic and copies ran while one was open for 0% of the time, Pallas kernels for 4%

profile of v4, /device:TPU:0, one launch (start us, length us, event | category | flops | bytes accessed | tf_op | source)
XLA Modules:
  0.0 43.9 jit_solution(10472323406953813319)
XLA Ops:
  0.6 0.0 copy-start
  0.6 2.4 %route.1 = (bf16[144,256]{1,0:T(8,128)(2,1)}, bf16[144,256]{1,0:T(8,128)(2,1)}, bf16[432,256]{1,0:T(8,128)(2,1)}, bf16[432,256]{1,0:T(8,128)(2,1)}, s32[8,128]{1,0:T(8,128)}, /*index=5*/f32[8,128]{1,0:T(8,128)}) custom-call(s32[8]{0:T(128)} %plan_hbm.1, s32[8,128]{1,0:T(8,128)} %bitcast.13, s32[8,128]{1,0:T(8,128)} %bitcast.15, bf16[8,128]{1,0:T(8,128)(2,1)} %bitcast.16, ...), custom_call_target="tpu_custom_call" | custom-call | flops 75497472 | bytes 1114112 | tf_op jit(solution)/shard_map/route/pallas_call | solution.py:531
  3.1 0.5 %collective-permute-start = (bf16[432,256]{1,0:T(8,128)(2,1)}, bf16[432,256]{1,0:T(8,128)(2,1)S(1)}, u32[]{:S(2)}, u32[]{:S(2)}) collective-permute-start(bf16[432,256]{1,0:T(8,128)(2,1)} %get-tuple-element.48), channel_id=1, source_target_pairs={{0,1},{1,0},{2,3},{3,2},{4,5},{5,4},{6,7},{7,6},{8,9},{9,8},{10,11... | collective-permute-start | bytes 663560 | tf_op jit(solution)/shard_map/ppermute | solution.py:552
  3.6 1.3 %collective-permute-done.came_ref = bf16[432,256]{1,0:T(8,128)(2,1)S(1)} collective-permute-done((bf16[432,256]{1,0:T(8,128)(2,1)}, bf16[432,256]{1,0:T(8,128)(2,1)S(1)}, u32[]{:S(2)}, u32[]{:S(2)}) %collective-permute-start) | collective-permute-done | bytes 221216 | tf_op jit(solution)/shard_map/ppermute | solution.py:552
  4.9 0.0 copy-start.3
  4.9 0.9 %copy-done.3 = bf16[432,256]{1,0:T(8,128)(2,1)S(1)} copy-done((bf16[432,256]{1,0:T(8,128)(2,1)S(1)}, bf16[432,256]{1,0:T(8,128)(2,1)}, u32[]{:S(2)}) %copy-start.3) | copy-done | bytes 221208
  5.8 0.0 copy-start.4
  5.8 0.9 %copy-done.4 = bf16[144,256]{1,0:T(8,128)(2,1)S(1)} copy-done((bf16[144,256]{1,0:T(8,128)(2,1)S(1)}, bf16[144,256]{1,0:T(8,128)(2,1)}, u32[]{:S(2)}) %copy-start.4) | copy-done | bytes 73752
  6.8 4.0 %collective-permute-start.2 = (bf16[288,256]{1,0:T(8,128)(2,1)S(1)}, bf16[288,256]{1,0:T(8,128)(2,1)S(1)}, u32[]{:S(2)}, u32[]{:S(2)}) collective-permute-start(bf16[288,256]{1,0:T(8,128)(2,1)S(1)} %get-tuple-element.51), channel_id=1, source_target_pairs={{0,8},{1,11},{2,10},{3,9},{4,12},{5,15},{6,14},{7,13},{8,0},{9,3},... | collective-permute-start | bytes 442376 | tf_op jit(solution)/shard_map/ppermute | solution.py:548
  10.8 1.3 %collective-permute-start.3 = (bf16[288,256]{1,0:T(8,128)(2,1)S(1)}, bf16[288,256]{1,0:T(8,128)(2,1)S(1)}, u32[]{:S(2)}, u32[]{:S(2)}) collective-permute-start(bf16[288,256]{1,0:T(8,128)(2,1)S(1)} %get-tuple-element.52), channel_id=1, source_target_pairs={{0,12},{1,15},{2,14},{3,13},{4,8},{5,11},{6,10},{7,9},{8,4},{9,7},... | collective-permute-start | bytes 442376 | tf_op jit(solution)/shard_map/ppermute | solution.py:548
  12.1 0.2 collective-permute-start.4
  12.4 1.5 %collective-permute-start.1 = (bf16[144,256]{1,0:T(8,128)(2,1)}, bf16[144,256]{1,0:T(8,128)(2,1)S(1)}, u32[]{:S(2)}, u32[]{:S(2)}) collective-permute-start(bf16[144,256]{1,0:T(8,128)(2,1)} %get-tuple-element.50), channel_id=1, source_target_pairs={{0,2},{2,0},{4,6},{6,4},{8,10},{10,8},{12,14},{14,12},{1,3},{3,1},... | collective-permute-start | bytes 221192 | tf_op jit(solution)/shard_map/ppermute | solution.py:546
  13.8 0.0 copy-done
  13.8 0.0 copy-start.1
  13.8 1.1 %copy-done.1 = bf16[1,1024,384]{2,1,0:T(8,128)(2,1)S(1)} copy-done((bf16[1,1024,384]{2,1,0:T(8,128)(2,1)S(1)}, bf16[1,1024,384]{2,1,0:T(8,128)(2,1)}, u32[]{:S(2)}) %copy-start.1) | copy-done | bytes 786456
  15.0 0.0 copy-start.2
  15.0 1.1 %copy-done.2 = bf16[1,1024,384]{2,1,0:T(8,128)(2,1)S(1)} copy-done((bf16[1,1024,384]{2,1,0:T(8,128)(2,1)S(1)}, bf16[1,1024,384]{2,1,0:T(8,128)(2,1)}, u32[]{:S(2)}) %copy-start.2) | copy-done | bytes 786456
  16.1 0.2 hold.1
  16.3 2.5 %collective-permute-done.1.refs_1_ = bf16[144,256]{1,0:T(8,128)(2,1)S(1)} collective-permute-done((bf16[144,256]{1,0:T(8,128)(2,1)}, bf16[144,256]{1,0:T(8,128)(2,1)S(1)}, u32[]{:S(2)}, u32[]{:S(2)}) %collective-permute-start.1) | collective-permute-done | bytes 73760 | tf_op jit(solution)/shard_map/ppermute | solution.py:546
  18.8 2.7 %collective-permute-done.2.refs_2_ = bf16[288,256]{1,0:T(8,128)(2,1)S(1)} collective-permute-done((bf16[288,256]{1,0:T(8,128)(2,1)S(1)}, bf16[288,256]{1,0:T(8,128)(2,1)S(1)}, u32[]{:S(2)}, u32[]{:S(2)}) %collective-permute-start.2) | collective-permute-done | bytes 147488 | tf_op jit(solution)/shard_map/ppermute | solution.py:548
  21.6 0.0 collective-permute-done.3.refs_3_
  21.6 1.8 %collective-permute-done.4.refs_4_ = bf16[288,256]{1,0:T(8,128)(2,1)S(1)} collective-permute-done((bf16[288,256]{1,0:T(8,128)(2,1)S(1)}, bf16[288,256]{1,0:T(8,128)(2,1)S(1)}, u32[]{:S(2)}, u32[]{:S(2)}) %collective-permute-start.4) | collective-permute-done | bytes 147488 | tf_op jit(solution)/shard_map/ppermute | solution.py:548
  23.4 1.6 %expert_rows.1 = (bf16[80,256]{1,0:T(8,128)(2,1)S(1)}, bf16[80,256]{1,0:T(8,128)(2,1)S(1)}, bf16[160,256]{1,0:T(8,128)(2,1)S(1)}, bf16[160,256]{1,0:T(8,128)(2,1...) custom-call(bf16[144,256]{1,0:T(8,128)(2,1)S(1)} %get-tuple-element., ...), custom_call_target="tpu_custom_call" | custom-call | flops 566231040 | bytes 2359296 | tf_op jit(solution)/shard_map/expert_rows/pallas_call | solution.py:531
  25.0 0.6 %other_half.1 = bf16[1536,384]{1,0:T(8,128)(2,1)S(1)} custom-call(bf16[144,1024]{1,0:T(8,128)(2,1)S(1)} %get-tuple-element.62.x_ref, bf16[144,1024]{1,0:T(8,128)(2,1)S(1)} %get-tuple-element.63.s_ref, bf16[144,384]{1,0:T(8,128)(2,1)S(1)} %get-tuple-element.64.dg_ref, bf16[144,384]{1,0:T(8,128)(2,1)S(1)} %get-tuple-element.65.du_ref, ...), custom_call_target="tpu_custom_call" | custom-call | flops 1 | bytes 1 | tf_op jit(solution)/shard_map/other_half/pallas_call | solution.py:531
  25.6 0.0 copy-start.5
  25.6 0.0 copy-start.6
  25.6 0.0 copy-start.7
  25.7 0.6 %collective-permute-start.12 = (bf16[1536,384]{1,0:T(8,128)(2,1)S(1)}, bf16[1536,384]{1,0:T(8,128)(2,1)S(1)}, u32[]{:S(2)}, u32[]{:S(2)}) collective-permute-start(bf16[1536,384]{1,0:T(8,128)(2,1)S(1)} %other_half.1), channel_id=1, source_target_pairs={{0,1},{1,0},{2,3},{3,2},{4,5},{5,4},{6,7},{7,6},{8,9},{9,8},{10,11... | collective-permute-start | bytes 3538952 | tf_op jit(solution)/shard_map/ppermute | solution.py:552
  26.2 4.1 %collective-permute-start.6 = (bf16[160,256]{1,0:T(8,128)(2,1)S(1)}, bf16[160,256]{1,0:T(8,128)(2,1)S(1)}, u32[]{:S(2)}, u32[]{:S(2)}) collective-permute-start(bf16[160,256]{1,0:T(8,128)(2,1)S(1)} %get-tuple-element.59), channel_id=1, source_target_pairs={{0,8},{1,11},{2,10},{3,9},{4,12},{5,15},{6,14},{7,13},{8,0},{9,3},... | collective-permute-start | bytes 245768 | tf_op jit(solution)/shard_map/ppermute | solution.py:548
  30.3 0.5 %collective-permute-start.7 = (bf16[160,256]{1,0:T(8,128)(2,1)S(1)}, bf16[160,256]{1,0:T(8,128)(2,1)S(1)}, u32[]{:S(2)}, u32[]{:S(2)}) collective-permute-start(bf16[160,256]{1,0:T(8,128)(2,1)S(1)} %get-tuple-element.60), channel_id=1, source_target_pairs={{0,12},{1,15},{2,14},{3,13},{4,8},{5,11},{6,10},{7,9},{8,4},{9,7},... | collective-permute-start | bytes 245768 | tf_op jit(solution)/shard_map/ppermute | solution.py:548
  30.8 0.1 collective-permute-start.8
  31.0 4.4 %collective-permute-done.6.refs_2_ = bf16[160,256]{1,0:T(8,128)(2,1)S(1)} collective-permute-done((bf16[160,256]{1,0:T(8,128)(2,1)S(1)}, bf16[160,256]{1,0:T(8,128)(2,1)S(1)}, u32[]{:S(2)}, u32[]{:S(2)}) %collective-permute-start.6) | collective-permute-done | bytes 81952 | tf_op jit(solution)/shard_map/ppermute | solution.py:548
  35.4 0.0 collective-permute-start.9
  35.4 2.1 %collective-permute-done.7.refs_3_ = bf16[160,256]{1,0:T(8,128)(2,1)S(1)} collective-permute-done((bf16[160,256]{1,0:T(8,128)(2,1)S(1)}, bf16[160,256]{1,0:T(8,128)(2,1)S(1)}, u32[]{:S(2)}, u32[]{:S(2)}) %collective-permute-start.7) | collective-permute-done | bytes 81952 | tf_op jit(solution)/shard_map/ppermute | solution.py:548
  37.5 0.0 collective-permute-start.10
  37.5 1.2 %collective-permute-done.8.refs_4_ = bf16[160,256]{1,0:T(8,128)(2,1)S(1)} collective-permute-done((bf16[160,256]{1,0:T(8,128)(2,1)S(1)}, bf16[160,256]{1,0:T(8,128)(2,1)S(1)}, u32[]{:S(2)}, u32[]{:S(2)}) %collective-permute-start.8) | collective-permute-done | bytes 81952 | tf_op jit(solution)/shard_map/ppermute | solution.py:548
  38.6 0.1 collective-permute-start.11
  38.8 1.1 %collective-permute-start.5 = (bf16[80,256]{1,0:T(8,128)(2,1)S(1)}, bf16[80,256]{1,0:T(8,128)(2,1)S(1)}, u32[]{:S(2)}, u32[]{:S(2)}) collective-permute-start(bf16[80,256]{1,0:T(8,128)(2,1)S(1)} %get-tuple-element.58), channel_id=1, source_target_pairs={{0,2},{2,0},{4,6},{6,4},{8,10},{10,8},{12,14},{14,12},{1,3},{3,1},... | collective-permute-start | bytes 122888 | tf_op jit(solution)/shard_map/ppermute | solution.py:546
  39.9 0.0 collective-permute-done.12.came_ref
  39.9 1.4 %own_half.1 = (bf16[512,384]{1,0:T(8,128)(2,1)}, bf16[512,384]{1,0:T(8,128)(2,1)}, bf16[512,384]{1,0:T(8,128)(2,1)}) custom-call(bf16[144,1024]{1,0:T(8,128)(2,1)S(1)} %get-tuple-element.62.x_ref, bf16[144,1024]{1,0:T(8,128)(2,1)S(1)} %get-tuple-element.63.s_ref, bf16[144,384]{1,0:T(8,128)(2,1)S(1)} %get-tuple-element.64.dg_ref, ...), custom_call_target="tpu_custom_call" | custom-call | flops 1 | bytes 1 | tf_op jit(solution)/shard_map/own_half/pallas_call | solution.py:531
  41.3 1.5 %collective-permute-done.5.refs_1_ = bf16[80,256]{1,0:T(8,128)(2,1)S(1)} collective-permute-done((bf16[80,256]{1,0:T(8,128)(2,1)S(1)}, bf16[80,256]{1,0:T(8,128)(2,1)S(1)}, u32[]{:S(2)}, u32[]{:S(2)}) %collective-permute-start.5) | collective-permute-done | bytes 40992 | tf_op jit(solution)/shard_map/ppermute | solution.py:546
  42.8 0.0 collective-permute-done.9.refs_5_
  42.8 0.0 collective-permute-done.10.refs_6_
  42.8 0.0 collective-permute-done.11.refs_7_
  42.8 0.0 copy-done.5
  42.8 0.0 copy-done.6
  42.8 0.0 copy-done.7
  42.8 1.0 %combine.1 = (bf16[128,1024]{1,0:T(8,128)(2,1)}, bf16[8,128]{1,0:T(8,128)(2,1)}) custom-call(s32[8,128]{1,0:T(8,128)S(1)} %bitcast.14, s32[8,128]{1,0:T(8,128)S(1)} %copy-done.6, f32[8,128]{1,0:T(8,128)S(1)} %copy-done.7, bf16[80,256]{1,0:T(8,128)(2,1)S(1)} %get-tuple-element.70.refs_0_, bf16[80,256]{1,0:T(8,128)(2,1)S(1)} %collective-permute-done.5.refs_1_, ...), custom_call_target="tpu_custom_call" | custom-call | flops 37748736 | bytes 524288 | tf_op jit(solution)/shard_map/combine/pallas_call | solution.py:531
  (1 shorter events, 0.0 us)
Async XLA Ops:
  0.6 13.2 %copy-start = (bf16[1,1024,384]{2,1,0:T(8,128)(2,1)S(1)}, bf16[1,1024,384]{2,1,0:T(8,128)(2,1)}, u32[]{:S(2)}) copy-start(bf16[1,1024,384]{2,1,0:T(8,128)(2,1)} %param.15) | copy-start | bytes 2359300
  3.1 1.8 %collective-permute-start = (bf16[432,256]{1,0:T(8,128)(2,1)}, bf16[432,256]{1,0:T(8,128)(2,1)S(1)}, u32[]{:S(2)}, u32[]{:S(2)}) collective-permute-start(bf16[432,256]{1,0:T(8,128)(2,1)} %get-tuple-element.48), channel_id=1, source_target_pairs={{0,1},{1,0},{2,3},{3,2},{4,5},{5,4},{6,7},{7,6},{8,9},{9,8},{10,11... | collective-permute-start | bytes 663560 | tf_op jit(solution)/shard_map/ppermute | solution.py:552
  4.9 0.9 %copy-start.3 = (bf16[432,256]{1,0:T(8,128)(2,1)S(1)}, bf16[432,256]{1,0:T(8,128)(2,1)}, u32[]{:S(2)}) copy-start(bf16[432,256]{1,0:T(8,128)(2,1)} %get-tuple-element.47.keep_ref) | copy-start | bytes 663556
  5.8 0.9 %copy-start.4 = (bf16[144,256]{1,0:T(8,128)(2,1)S(1)}, bf16[144,256]{1,0:T(8,128)(2,1)}, u32[]{:S(2)}) copy-start(bf16[144,256]{1,0:T(8,128)(2,1)} %get-tuple-element.46.self_hbm) | copy-start | bytes 221188
  6.8 14.8 %collective-permute-start.2 = (bf16[288,256]{1,0:T(8,128)(2,1)S(1)}, bf16[288,256]{1,0:T(8,128)(2,1)S(1)}, u32[]{:S(2)}, u32[]{:S(2)}) collective-permute-start(bf16[288,256]{1,0:T(8,128)(2,1)S(1)} %get-tuple-element.51), channel_id=1, source_target_pairs={{0,8},{1,11},{2,10},{3,9},{4,12},{5,15},{6,14},{7,13},{8,0},{9,3},... | collective-permute-start | bytes 442376 | tf_op jit(solution)/shard_map/ppermute | solution.py:548
  10.8 10.8 %collective-permute-start.3 = (bf16[288,256]{1,0:T(8,128)(2,1)S(1)}, bf16[288,256]{1,0:T(8,128)(2,1)S(1)}, u32[]{:S(2)}, u32[]{:S(2)}) collective-permute-start(bf16[288,256]{1,0:T(8,128)(2,1)S(1)} %get-tuple-element.52), channel_id=1, source_target_pairs={{0,12},{1,15},{2,14},{3,13},{4,8},{5,11},{6,10},{7,9},{8,4},{9,7},... | collective-permute-start | bytes 442376 | tf_op jit(solution)/shard_map/ppermute | solution.py:548
  12.1 11.2 %collective-permute-start.4 = (bf16[288,256]{1,0:T(8,128)(2,1)S(1)}, bf16[288,256]{1,0:T(8,128)(2,1)S(1)}, u32[]{:S(2)}, u32[]{:S(2)}) collective-permute-start(bf16[288,256]{1,0:T(8,128)(2,1)S(1)} %get-tuple-element.53), channel_id=1, source_target_pairs={{0,4},{1,7},{2,6},{3,5},{4,0},{5,3},{6,2},{7,1},{8,12},{9,15},{10,... | collective-permute-start | bytes 442376 | tf_op jit(solution)/shard_map/ppermute | solution.py:548
  12.4 6.5 %collective-permute-start.1 = (bf16[144,256]{1,0:T(8,128)(2,1)}, bf16[144,256]{1,0:T(8,128)(2,1)S(1)}, u32[]{:S(2)}, u32[]{:S(2)}) collective-permute-start(bf16[144,256]{1,0:T(8,128)(2,1)} %get-tuple-element.50), channel_id=1, source_target_pairs={{0,2},{2,0},{4,6},{6,4},{8,10},{10,8},{12,14},{14,12},{1,3},{3,1},... | collective-permute-start | bytes 221192 | tf_op jit(solution)/shard_map/ppermute | solution.py:546
  13.8 1.1 %copy-start.1 = (bf16[1,1024,384]{2,1,0:T(8,128)(2,1)S(1)}, bf16[1,1024,384]{2,1,0:T(8,128)(2,1)}, u32[]{:S(2)}) copy-start(bf16[1,1024,384]{2,1,0:T(8,128)(2,1)} %param.16) | copy-start | bytes 2359300
  15.0 1.1 %copy-start.2 = (bf16[1,1024,384]{2,1,0:T(8,128)(2,1)S(1)}, bf16[1,1024,384]{2,1,0:T(8,128)(2,1)}, u32[]{:S(2)}) copy-start(bf16[1,1024,384]{2,1,0:T(8,128)(2,1)} %param.17) | copy-start | bytes 2359300
  25.6 17.2 %copy-start.5 = (s32[128,8]{0,1:T(8,128)S(1)}, s32[128,8]{0,1:T(8,128)}, u32[]{:S(2)}) copy-start(s32[128,8]{0,1:T(8,128)} %param.11) | copy-start | bytes 12292
  25.6 17.2 %copy-start.6 = (s32[8,128]{1,0:T(8,128)S(1)}, s32[8,128]{1,0:T(8,128)}, u32[]{:S(2)}) copy-start(s32[8,128]{1,0:T(8,128)} %get-tuple-element.44.slot_ref) | copy-start | bytes 12292
  25.6 17.2 %copy-start.7 = (f32[8,128]{1,0:T(8,128)S(1)}, f32[8,128]{1,0:T(8,128)}, u32[]{:S(2)}) copy-start(f32[8,128]{1,0:T(8,128)} %get-tuple-element.45.gates_ref) | copy-start | bytes 12292
  25.7 14.3 %collective-permute-start.12 = (bf16[1536,384]{1,0:T(8,128)(2,1)S(1)}, bf16[1536,384]{1,0:T(8,128)(2,1)S(1)}, u32[]{:S(2)}, u32[]{:S(2)}) collective-permute-start(bf16[1536,384]{1,0:T(8,128)(2,1)S(1)} %other_half.1), channel_id=1, source_target_pairs={{0,1},{1,0},{2,3},{3,2},{4,5},{5,4},{6,7},{7,6},{8,9},{9,8},{10,11... | collective-permute-start | bytes 3538952 | tf_op jit(solution)/shard_map/ppermute | solution.py:552
  26.2 9.1 %collective-permute-start.6 = (bf16[160,256]{1,0:T(8,128)(2,1)S(1)}, bf16[160,256]{1,0:T(8,128)(2,1)S(1)}, u32[]{:S(2)}, u32[]{:S(2)}) collective-permute-start(bf16[160,256]{1,0:T(8,128)(2,1)S(1)} %get-tuple-element.59), channel_id=1, source_target_pairs={{0,8},{1,11},{2,10},{3,9},{4,12},{5,15},{6,14},{7,13},{8,0},{9,3},... | collective-permute-start | bytes 245768 | tf_op jit(solution)/shard_map/ppermute | solution.py:548
  30.3 7.1 %collective-permute-start.7 = (bf16[160,256]{1,0:T(8,128)(2,1)S(1)}, bf16[160,256]{1,0:T(8,128)(2,1)S(1)}, u32[]{:S(2)}, u32[]{:S(2)}) collective-permute-start(bf16[160,256]{1,0:T(8,128)(2,1)S(1)} %get-tuple-element.60), channel_id=1, source_target_pairs={{0,12},{1,15},{2,14},{3,13},{4,8},{5,11},{6,10},{7,9},{8,4},{9,7},... | collective-permute-start | bytes 245768 | tf_op jit(solution)/shard_map/ppermute | solution.py:548
  30.8 7.8 %collective-permute-start.8 = (bf16[160,256]{1,0:T(8,128)(2,1)S(1)}, bf16[160,256]{1,0:T(8,128)(2,1)S(1)}, u32[]{:S(2)}, u32[]{:S(2)}) collective-permute-start(bf16[160,256]{1,0:T(8,128)(2,1)S(1)} %get-tuple-element.61), channel_id=1, source_target_pairs={{0,4},{1,7},{2,6},{3,5},{4,0},{5,3},{6,2},{7,1},{8,12},{9,15},{10,... | collective-permute-start | bytes 245768 | tf_op jit(solution)/shard_map/ppermute | solution.py:548
  35.4 7.4 %collective-permute-start.9 = (bf16[160,256]{1,0:T(8,128)(2,1)S(1)}, bf16[160,256]{1,0:T(8,128)(2,1)S(1)}, u32[]{:S(2)}, u32[]{:S(2)}) collective-permute-start(bf16[160,256]{1,0:T(8,128)(2,1)S(1)} %collective-permute-done.6.refs_2_), channel_id=1, source_target_pairs={{0,1},{1,0},{2,3},{3,2},{4,5},{5,4},{6,7},{7,6},{8,9},{9,8},{10,11... | collective-permute-start | bytes 245768 | tf_op jit(solution)/shard_map/ppermute | solution.py:552
  37.5 5.3 %collective-permute-start.10 = (bf16[160,256]{1,0:T(8,128)(2,1)S(1)}, bf16[160,256]{1,0:T(8,128)(2,1)S(1)}, u32[]{:S(2)}, u32[]{:S(2)}) collective-permute-start(bf16[160,256]{1,0:T(8,128)(2,1)S(1)} %collective-permute-done.7.refs_3_), channel_id=1, source_target_pairs={{0,1},{1,0},{2,3},{3,2},{4,5},{5,4},{6,7},{7,6},{8,9},{9,8},{10,11... | collective-permute-start | bytes 245768 | tf_op jit(solution)/shard_map/ppermute | solution.py:552
  38.6 4.2 %collective-permute-start.11 = (bf16[160,256]{1,0:T(8,128)(2,1)S(1)}, bf16[160,256]{1,0:T(8,128)(2,1)S(1)}, u32[]{:S(2)}, u32[]{:S(2)}) collective-permute-start(bf16[160,256]{1,0:T(8,128)(2,1)S(1)} %collective-permute-done.8.refs_4_), channel_id=1, source_target_pairs={{0,1},{1,0},{2,3},{3,2},{4,5},{5,4},{6,7},{7,6},{8,9},{9,8},{10,11... | collective-permute-start | bytes 245768 | tf_op jit(solution)/shard_map/ppermute | solution.py:552
  38.8 4.0 %collective-permute-start.5 = (bf16[80,256]{1,0:T(8,128)(2,1)S(1)}, bf16[80,256]{1,0:T(8,128)(2,1)S(1)}, u32[]{:S(2)}, u32[]{:S(2)}) collective-permute-start(bf16[80,256]{1,0:T(8,128)(2,1)S(1)} %get-tuple-element.58), channel_id=1, source_target_pairs={{0,2},{2,0},{4,6},{6,4},{8,10},{10,8},{12,14},{14,12},{1,3},{3,1},... | collective-permute-start | bytes 122888 | tf_op jit(solution)/shard_map/ppermute | solution.py:546

commit v5 on v2

--- a/solution.py
+++ b/solution.py
@@ -358,12 +358,11 @@
 
 
 def expert_kernel(*refs):
-    back_count = len(refs) - 8
-    experts = back_count // 2
+    experts = len(refs) - 9
     recv_refs = refs[:experts]
-    gate_ref, up_ref, down_ref = refs[experts : experts + 3]
-    back_refs = refs[experts + 3 : 2 * experts + 3]
-    x_ref, s_ref, dg_ref, du_ref, hid_ref = refs[2 * experts + 3 :]
+    gate_ref, up_ref, down_ref, back_ref = refs[experts : experts + 4]
+    x_ref, s_ref, dg_ref, du_ref, hid_ref = refs[experts + 4 :]
+    me = lax.axis_index("expert")
     width = recv_refs[0].shape[1]
     main_rows = experts * MAIN
     tail = jnp.concatenate([ref[2 * QUARTERS * MAIN :, :] for ref in recv_refs], axis=0)
@@ -419,10 +418,10 @@
         mine = jnp.logical_and(jnp.bitwise_and(inner, 3) == q, inner < 8)
         place = mask(jnp.logical_and(mine, tcol == source))
         spread += jnp.dot(place, grad[main_rows:, cols], preferred_element_type=F32)
-        for i, ref in enumerate(back_refs):
-            ref[q * MAIN : (q + 1) * MAIN, :] = grad[i * MAIN : (i + 1) * MAIN, cols]
-    for i, ref in enumerate(back_refs):
-        ref[QUARTERS * MAIN :, :] = jnp.concatenate(
+        for i, step in enumerate(STEPS):
+            back_ref[me ^ step, q * MAIN : (q + 1) * MAIN, :] = grad[i * MAIN : (i + 1) * MAIN, cols]
+    for i, step in enumerate(STEPS):
+        back_ref[me ^ step, QUARTERS * MAIN :, :] = jnp.concatenate(
             [spread[i * MAIN : i * MAIN + 8], gate_lanes], axis=0
         ).astype(BF)
 
@@ -457,12 +456,11 @@
         out_ref[...] = (parts[n].astype(BF).astype(F32) + came).astype(BF)
 
 
-def combine_kernel(ids_ref, slot_ref, gates_ref, *refs):
-    token_ref, grad_ref = refs[-2:]
-    ret_refs = refs[:-2]
+def combine_kernel(ids_ref, slot_ref, gates_ref, ret_ref, token_ref, grad_ref):
     topk, tokens = ids_ref.shape
-    experts = len(ret_refs)
-    width = ret_refs[0].shape[1]
+    experts, unused, width = ret_ref.shape
+    me = lax.axis_index("expert")
+    places = [me ^ step for step in STEPS]
     ids = ids_ref[...]
     slot = slot_ref[...]
     slot16 = repeat_rows(slot, MAIN)
@@ -471,22 +469,23 @@
     wanted = MAIN + jnp.right_shift(inner, 2)
     last = jnp.where(jnp.logical_and(slot16 == wanted, inner < 8), 1.0, 0.0)
     quarter = jnp.bitwise_and(inner, 3)
-    tail = jnp.concatenate([ref[QUARTERS * MAIN :, :] for ref in ret_refs], axis=0)
+    tails = [ret_ref[place, QUARTERS * MAIN :, :] for place in places]
+    tail = jnp.concatenate(tails, axis=0)
     for q in range(QUARTERS):
-        main = jnp.concatenate([ref[q * MAIN : (q + 1) * MAIN, :] for ref in ret_refs], axis=0)
+        main = jnp.concatenate(
+            [ret_ref[place, q * MAIN : (q + 1) * MAIN, :] for place in places], axis=0
+        )
         place = jnp.where(quarter == q, last, 0.0).astype(BF)
         total = lax.dot_general(onehot, main, CONTRACT_ROWS, preferred_element_type=F32)
         total += lax.dot_general(place, tail, CONTRACT_ROWS, preferred_element_type=F32)
         token_ref[:, q * width : (q + 1) * width] = total.astype(BF)
     lane_index = iota((width, tokens), 0)
     found = []
-    for k, ref in enumerate(ret_refs):
-        mine = slot[k : k + 1]
-        lane = jnp.where(mine < MAIN, k * MAIN + mine, experts * MAIN + 2 * k + mine - MAIN)
+    for c in range(experts):
+        mine = slot[c : c + 1]
+        lane = jnp.where(mine < MAIN, c * MAIN + mine, experts * MAIN + 2 * c + mine - MAIN)
         lane = jnp.where(mine < 0, -1, lane)
-        sums = jnp.dot(
-            ref[QUARTERS * MAIN :, :], mask(lane_index == lane), preferred_element_type=F32
-        )
+        sums = jnp.dot(tails[c], mask(lane_index == lane), preferred_element_type=F32)
         found.append(sums[8:9])
     found = jnp.concatenate(found, axis=0)
     kept = slot >= 0
@@ -578,9 +577,9 @@
         4 * 3 * model_width * hidden_width,
     )
     matmul = 2 * served * model_width * hidden_width
-    outs = local_call(
+    back, *factors = local_call(
         expert_kernel,
-        [((BACK_ROWS, width), BF)] * experts
+        [((experts, BACK_ROWS, width), BF)]
         + [((served, model_width), BF)] * 2
         + [((served, hidden_width), BF)] * 3,
         [held[0], *recv[1:], *held[1:]],
@@ -588,17 +587,15 @@
         5 * matmul,
         2 * 3 * model_width * hidden_width,
     )
-    factors = outs[experts:]
-    returned = exchange(outs[:experts])
-    returned[1], factors = lax.optimization_barrier((returned[1], factors))
+    returned = lax.all_to_all(back, "expert", split_axis=0, concat_axis=0, tiled=True)
     half = model_width // 2
     (leaving,) = local_call(
         other_half_kernel,
         [((3 * half, hidden_width), BF)],
         factors,
         "other_half",
-        3 * matmul // 2,
-        2 * 3 * half * hidden_width,
+        1,
+        1,
     )
     came = lax.ppermute(leaving, "replica", [(0, 1), (1, 0)])
     shares = local_call(
@@ -606,14 +603,14 @@
         [((half, hidden_width), BF)] * 3,
         [*factors, came],
         "own_half",
-        3 * matmul // 2,
-        2 * 2 * 3 * half * hidden_width,
+        1,
+        1,
     )
     returned, shares = lax.optimization_barrier((returned, shares))
     token_grad, gate_grad = local_call(
         combine_kernel,
         [((token_count, model_width), BF), ((topk, token_count), BF)],
-        [expert_ids.T, slot, gates, *returned],
+        [expert_ids.T, slot, gates, returned],
         "combine",
         2 * served * token_count * model_width,
         2 * 2 * token_count * model_width,

time: 44 us -> 42.5 us (0.966)
  starting transfers between devices: 24.4 us -> 17 us
  waiting for transfers between devices: 7.06 us -> 12 us
  local copies, waits for them, and re-layouts: 4.3 us -> 5.24 us
    ppermute x14 -> x7, starting transfers between devices: 24.3 us -> 10.8 us  [exchange(): lax.ppermute(chunk, 'expert', [(i, i ^ step) for i in range(count)])]
    all_to_all x0 -> x1, waiting for transfers between devices: none -> 8.59 us  [per_device_moving_rows(): lax.all_to_all(back, 'expert', split_axis=0, concat_axis=0, tiled=True)]
    all_to_all x0 -> x1, starting transfers between devices: none -> 6.09 us  [per_device_moving_rows(): lax.all_to_all(back, 'expert', split_axis=0, concat_axis=0, tiled=True)]
    ppermute x14 -> x7, waiting for transfers between devices: 7.06 us -> 3.37 us  [exchange(): lax.ppermute(chunk, 'expert', [(i, i ^ step) for i in range(count)])]
    unnamed x14 -> x20, local copies, waits for them, and re-layouts: 4.3 us -> 5.24 us
  transfers between devices with their start and end apart: 15 -> 9, of which waited for: 5 -> 3; matrix products, arithmetic and copies ran while one was open for 0% -> 0% of each run, Pallas kernels for 4% -> 4%
where the time goes in v5:
time: 42.5 us; the launch traced here: 42.1 us
  starting transfers between devices  17 us (40%)
  waiting for transfers between devices  12 us (28%)
  Pallas kernels  7.2 us (17%)
  local copies, waits for them, and re-layouts  5.24 us (12%)
  between operations  0.74 us (2%)
    ppermute x7, starting transfers between devices, exchange(): lax.ppermute(chunk, 'expert', [(i, i ^ step) for i in range(count)])  10.8 us
    all_to_all x1, waiting for transfers between devices, per_device_moving_rows(): lax.all_to_all(back, 'expert', split_axis=0, concat_axis=0, tiled=True)  8.59 us
    pallas_call x6, Pallas kernels, local_call(): pl.pallas_call(kernel, out_shape=[jax.ShapeDtypeStruct(shape, kind) for s...  7.2 us
    all_to_all x1, starting transfers between devices, per_device_moving_rows(): lax.all_to_all(back, 'expert', split_axis=0, concat_axis=0, tiled=True)  6.09 us
    unnamed x20, local copies, waits for them, and re-layouts  5.24 us
    ppermute x7, waiting for transfers between devices, exchange(): lax.ppermute(chunk, 'expert', [(i, i ^ step) for i in range(count)])  3.37 us
  transfers between devices with their start and end apart: 9, of which 3 were waited for; matrix products, arithmetic and copies ran while one was open for 0% of the time, Pallas kernels for 4%

profile of v5, /device:TPU:0, one launch (start us, length us, event | category | flops | bytes accessed | tf_op | source)
XLA Modules:
  0.0 42.1 jit_solution(11371308519027629961)
XLA Ops:
  0.6 2.3 %route.1 = (bf16[144,256]{1,0:T(8,128)(2,1)}, bf16[144,256]{1,0:T(8,128)(2,1)}, bf16[144,256]{1,0:T(8,128)(2,1)}, bf16[144,256]{1,0:T(8,128)(2,1)}, bf16[144,256...) custom-call(s32[8]{0:T(128)} %plan_hbm.1, ...), custom_call_target="tpu_custom_call" | custom-call | flops 75497472 | bytes 1114112 | tf_op jit(solution)/shard_map/route/pallas_call | solution.py:503
  3.0 3.0 %collective-permute-start = (bf16[144,256]{1,0:T(8,128)(2,1)}, bf16[144,256]{1,0:T(8,128)(2,1)S(1)}, u32[]{:S(2)}, u32[]{:S(2)}) collective-permute-start(bf16[144,256]{1,0:T(8,128)(2,1)} %get-tuple-element.38), channel_id=1, source_target_pairs={{0,2},{2,0},{4,6},{6,4},{8,10},{10,8},{12,14},{14,12},{1,3},{3,1},... | collective-permute-start | bytes 221192 | tf_op jit(solution)/shard_map/ppermute | solution.py:518
  6.0 2.6 %collective-permute-start.1 = (bf16[144,256]{1,0:T(8,128)(2,1)}, bf16[144,256]{1,0:T(8,128)(2,1)S(1)}, u32[]{:S(2)}, u32[]{:S(2)}) collective-permute-start(bf16[144,256]{1,0:T(8,128)(2,1)} %get-tuple-element.39), channel_id=1, source_target_pairs={{0,8},{2,10},{4,12},{6,14},{8,0},{10,2},{12,4},{14,6},{1,9},{3,11}... | collective-permute-start | bytes 221192 | tf_op jit(solution)/shard_map/ppermute | solution.py:518
  8.6 0.0 collective-permute-start.2
  8.6 3.9 %collective-permute-start.3 = (bf16[144,256]{1,0:T(8,128)(2,1)}, bf16[144,256]{1,0:T(8,128)(2,1)S(1)}, u32[]{:S(2)}, u32[]{:S(2)}) collective-permute-start(bf16[144,256]{1,0:T(8,128)(2,1)} %get-tuple-element.41), channel_id=1, source_target_pairs={{0,12},{2,14},{4,8},{6,10},{8,4},{10,6},{12,0},{14,2},{1,13},{3,15... | collective-permute-start | bytes 221192 | tf_op jit(solution)/shard_map/ppermute | solution.py:518
  12.5 1.1 %collective-permute-start.4 = (bf16[144,256]{1,0:T(8,128)(2,1)}, bf16[144,256]{1,0:T(8,128)(2,1)S(1)}, u32[]{:S(2)}, u32[]{:S(2)}) collective-permute-start(bf16[144,256]{1,0:T(8,128)(2,1)} %get-tuple-element.42), channel_id=1, source_target_pairs={{0,14},{2,12},{4,10},{6,8},{8,6},{10,4},{12,2},{14,0},{1,15},{3,13... | collective-permute-start | bytes 221192 | tf_op jit(solution)/shard_map/ppermute | solution.py:518
  13.6 0.0 collective-permute-done.refs_1_
  13.6 0.0 collective-permute-start.5
  13.6 2.6 %collective-permute-done.1.refs_2_ = bf16[144,256]{1,0:T(8,128)(2,1)S(1)} collective-permute-done((bf16[144,256]{1,0:T(8,128)(2,1)}, bf16[144,256]{1,0:T(8,128)(2,1)S(1)}, u32[]{:S(2)}, u32[]{:S(2)}) %collective-permute-start.1) | collective-permute-done | bytes 73760 | tf_op jit(solution)/shard_map/ppermute | solution.py:518
  16.2 0.1 collective-permute-start.6
  16.3 0.0 copy-start
  16.3 1.1 %copy-done = bf16[1,1024,384]{2,1,0:T(8,128)(2,1)S(1)} copy-done((bf16[1,1024,384]{2,1,0:T(8,128)(2,1)S(1)}, bf16[1,1024,384]{2,1,0:T(8,128)(2,1)}, u32[]{:S(2)}) %copy-start) | copy-done | bytes 786456
  17.5 0.0 copy-start.1
  17.5 1.1 %copy-done.1 = bf16[1,1024,384]{2,1,0:T(8,128)(2,1)S(1)} copy-done((bf16[1,1024,384]{2,1,0:T(8,128)(2,1)S(1)}, bf16[1,1024,384]{2,1,0:T(8,128)(2,1)}, u32[]{:S(2)}) %copy-start.1) | copy-done | bytes 786456
  18.6 0.0 copy-start.2
  18.6 1.1 %copy-done.2 = bf16[1,1024,384]{2,1,0:T(8,128)(2,1)S(1)} copy-done((bf16[1,1024,384]{2,1,0:T(8,128)(2,1)S(1)}, bf16[1,1024,384]{2,1,0:T(8,128)(2,1)}, u32[]{:S(2)}) %copy-start.2) | copy-done | bytes 786456
  19.7 0.0 copy-start.6
  19.7 0.9 %copy-done.6 = bf16[144,256]{1,0:T(8,128)(2,1)S(1)} copy-done((bf16[144,256]{1,0:T(8,128)(2,1)S(1)}, bf16[144,256]{1,0:T(8,128)(2,1)}, u32[]{:S(2)}) %copy-start.6) | copy-done | bytes 73752
  20.6 0.2 hold.1
  20.8 0.0 collective-permute-done.2.refs_3_
  20.9 0.0 collective-permute-done.3.refs_4_
  20.9 0.0 collective-permute-done.4.refs_5_
  20.9 0.0 collective-permute-done.5.refs_6_
  20.9 0.8 %collective-permute-done.6.refs_7_ = bf16[144,256]{1,0:T(8,128)(2,1)S(1)} collective-permute-done((bf16[144,256]{1,0:T(8,128)(2,1)}, bf16[144,256]{1,0:T(8,128)(2,1)S(1)}, u32[]{:S(2)}, u32[]{:S(2)}) %collective-permute-start.6) | collective-permute-done | bytes 73760 | tf_op jit(solution)/shard_map/ppermute | solution.py:518
  21.7 1.6 %expert_rows.1 = (bf16[8,80,256]{2,1,0:T(8,128)(2,1)S(1)}, bf16[144,1024]{1,0:T(8,128)(2,1)S(1)}, bf16[144,1024]{1,0:T(8,128)(2,1)S(1)}, bf16[144,384]{1,0:T(8,1...) custom-call(bf16[144,256]{1,0:T(8,128)(2,1)S(1)} %get-tuple-element.37.refs_0_, ...), custom_call_target="tpu_custom_call" | custom-call | flops 566231040 | bytes 2359296 | tf_op jit(solution)/shard_map/expert_rows/pallas_call | solution.py:503
  23.3 0.0 copy-start.3
  23.3 0.0 copy-start.5
  23.3 0.6 %other_half.1 = bf16[1536,384]{1,0:T(8,128)(2,1)S(1)} custom-call(bf16[144,1024]{1,0:T(8,128)(2,1)S(1)} %get-tuple-element.49.x_ref, bf16[144,1024]{1,0:T(8,128)(2,1)S(1)} %get-tuple-element.50.s_ref, bf16[144,384]{1,0:T(8,128)(2,1)S(1)} %get-tuple-element.51.dg_ref, bf16[144,384]{1,0:T(8,128)(2,1)S(1)} %get-tuple-element.52.du_ref, ...), custom_call_target="tpu_custom_call" | custom-call | flops 1 | bytes 1 | tf_op jit(solution)/shard_map/other_half/pallas_call | solution.py:503
  23.9 0.1 collective-permute-start.7
  24.0 0.0 copy-done.3
  24.0 0.0 copy-done.5
  24.1 6.1 %all-to-all-start = ((bf16[8,80,256]{2,1,0:T(8,128)(2,1)}), bf16[8,80,256]{2,1,0:T(8,128)(2,1)S(1)}, u32[]{:S(2)}, u32[]{:S(2)}) async-start(bf16[8,80,256]{2,1,0:T(8,128)(2,1)} %copy-done.5), calls=%async_computation | async-start | bytes 655360 | tf_op jit(solution)/shard_map/all_to_all | solution.py:590
  30.2 0.0 collective-permute-done.7.came_ref
  30.2 0.0 copy-start.4
  30.2 0.9 %copy-done.4 = bf16[144,384]{1,0:T(8,128)(2,1)S(1)} copy-done((bf16[144,384]{1,0:T(8,128)(2,1)S(1)}, bf16[144,384]{1,0:T(8,128)(2,1)}, u32[]{:S(2)}) %copy-start.4) | copy-done | bytes 110616
  31.1 0.0 copy-start.7
  31.1 0.0 copy-start.8
  31.1 0.0 copy-start.9
  31.1 1.4 %own_half.1 = (bf16[512,384]{1,0:T(8,128)(2,1)}, bf16[512,384]{1,0:T(8,128)(2,1)}, bf16[512,384]{1,0:T(8,128)(2,1)}) custom-call(bf16[144,1024]{1,0:T(8,128)(2,1)S(1)} %get-tuple-element.49.x_ref, bf16[144,1024]{1,0:T(8,128)(2,1)S(1)} %get-tuple-element.50.s_ref, bf16[144,384]{1,0:T(8,128)(2,1)S(1)} %get-tuple-element.51.dg_ref, ...), custom_call_target="tpu_custom_call" | custom-call | flops 1 | bytes 1 | tf_op jit(solution)/shard_map/own_half/pallas_call | solution.py:503
  32.5 8.6 %all-to-all-done.ret_ref = bf16[8,80,256]{2,1,0:T(8,128)(2,1)S(1)} async-done(((bf16[8,80,256]{2,1,0:T(8,128)(2,1)}), bf16[8,80,256]{2,1,0:T(8,128)(2,1)S(1)}, u32[]{:S(2)}, u32[]{:S(2)}) %all-to-all-start) | async-done | bytes 327712 | tf_op jit(solution)/shard_map/all_to_all | solution.py:590
  41.1 0.0 copy-done.7
  41.1 0.0 copy-done.8
  41.1 0.0 copy-done.9
  41.1 1.0 %combine.1 = (bf16[128,1024]{1,0:T(8,128)(2,1)}, bf16[8,128]{1,0:T(8,128)(2,1)}) custom-call(s32[8,128]{1,0:T(8,128)S(1)} %bitcast.14, s32[8,128]{1,0:T(8,128)S(1)} %copy-done.8, f32[8,128]{1,0:T(8,128)S(1)} %copy-done.9, bf16[8,80,256]{2,1,0:T(8,128)(2,1)S(1)} %all-to-all-done.ret_ref), custom_call_target="tpu_custom_call" | custom-call | flops 37748736 | bytes 524288 | tf_op jit(solution)/shard_map/combine/pallas_call | solution.py:503
Async XLA Ops:
  3.0 10.7 %collective-permute-start = (bf16[144,256]{1,0:T(8,128)(2,1)}, bf16[144,256]{1,0:T(8,128)(2,1)S(1)}, u32[]{:S(2)}, u32[]{:S(2)}) collective-permute-start(bf16[144,256]{1,0:T(8,128)(2,1)} %get-tuple-element.38), channel_id=1, source_target_pairs={{0,2},{2,0},{4,6},{6,4},{8,10},{10,8},{12,14},{14,12},{1,3},{3,1},... | collective-permute-start | bytes 221192 | tf_op jit(solution)/shard_map/ppermute | solution.py:518
  6.0 10.2 %collective-permute-start.1 = (bf16[144,256]{1,0:T(8,128)(2,1)}, bf16[144,256]{1,0:T(8,128)(2,1)S(1)}, u32[]{:S(2)}, u32[]{:S(2)}) collective-permute-start(bf16[144,256]{1,0:T(8,128)(2,1)} %get-tuple-element.39), channel_id=1, source_target_pairs={{0,8},{2,10},{4,12},{6,14},{8,0},{10,2},{12,4},{14,6},{1,9},{3,11}... | collective-permute-start | bytes 221192 | tf_op jit(solution)/shard_map/ppermute | solution.py:518
  8.6 12.3 %collective-permute-start.2 = (bf16[144,256]{1,0:T(8,128)(2,1)}, bf16[144,256]{1,0:T(8,128)(2,1)S(1)}, u32[]{:S(2)}, u32[]{:S(2)}) collective-permute-start(bf16[144,256]{1,0:T(8,128)(2,1)} %get-tuple-element.40), channel_id=1, source_target_pairs={{0,10},{2,8},{4,14},{6,12},{8,2},{10,0},{12,6},{14,4},{1,11},{3,9}... | collective-permute-start | bytes 221192 | tf_op jit(solution)/shard_map/ppermute | solution.py:518
  8.6 12.3 %collective-permute-start.3 = (bf16[144,256]{1,0:T(8,128)(2,1)}, bf16[144,256]{1,0:T(8,128)(2,1)S(1)}, u32[]{:S(2)}, u32[]{:S(2)}) collective-permute-start(bf16[144,256]{1,0:T(8,128)(2,1)} %get-tuple-element.41), channel_id=1, source_target_pairs={{0,12},{2,14},{4,8},{6,10},{8,4},{10,6},{12,0},{14,2},{1,13},{3,15... | collective-permute-start | bytes 221192 | tf_op jit(solution)/shard_map/ppermute | solution.py:518
  12.5 8.4 %collective-permute-start.4 = (bf16[144,256]{1,0:T(8,128)(2,1)}, bf16[144,256]{1,0:T(8,128)(2,1)S(1)}, u32[]{:S(2)}, u32[]{:S(2)}) collective-permute-start(bf16[144,256]{1,0:T(8,128)(2,1)} %get-tuple-element.42), channel_id=1, source_target_pairs={{0,14},{2,12},{4,10},{6,8},{8,6},{10,4},{12,2},{14,0},{1,15},{3,13... | collective-permute-start | bytes 221192 | tf_op jit(solution)/shard_map/ppermute | solution.py:518
  13.6 7.3 %collective-permute-start.5 = (bf16[144,256]{1,0:T(8,128)(2,1)}, bf16[144,256]{1,0:T(8,128)(2,1)S(1)}, u32[]{:S(2)}, u32[]{:S(2)}) collective-permute-start(bf16[144,256]{1,0:T(8,128)(2,1)} %get-tuple-element.43), channel_id=1, source_target_pairs={{0,4},{2,6},{4,0},{6,2},{8,12},{10,14},{12,8},{14,10},{1,5},{3,7},... | collective-permute-start | bytes 221192 | tf_op jit(solution)/shard_map/ppermute | solution.py:518
  16.2 5.5 %collective-permute-start.6 = (bf16[144,256]{1,0:T(8,128)(2,1)}, bf16[144,256]{1,0:T(8,128)(2,1)S(1)}, u32[]{:S(2)}, u32[]{:S(2)}) collective-permute-start(bf16[144,256]{1,0:T(8,128)(2,1)} %get-tuple-element.44), channel_id=1, source_target_pairs={{0,6},{2,4},{4,2},{6,0},{8,14},{10,12},{12,10},{14,8},{1,7},{3,5},... | collective-permute-start | bytes 221192 | tf_op jit(solution)/shard_map/ppermute | solution.py:518
  16.3 1.1 %copy-start = (bf16[1,1024,384]{2,1,0:T(8,128)(2,1)S(1)}, bf16[1,1024,384]{2,1,0:T(8,128)(2,1)}, u32[]{:S(2)}) copy-start(bf16[1,1024,384]{2,1,0:T(8,128)(2,1)} %param.15) | copy-start | bytes 2359300
  17.5 1.1 %copy-start.1 = (bf16[1,1024,384]{2,1,0:T(8,128)(2,1)S(1)}, bf16[1,1024,384]{2,1,0:T(8,128)(2,1)}, u32[]{:S(2)}) copy-start(bf16[1,1024,384]{2,1,0:T(8,128)(2,1)} %param.16) | copy-start | bytes 2359300
  18.6 1.1 %copy-start.2 = (bf16[1,1024,384]{2,1,0:T(8,128)(2,1)S(1)}, bf16[1,1024,384]{2,1,0:T(8,128)(2,1)}, u32[]{:S(2)}) copy-start(bf16[1,1024,384]{2,1,0:T(8,128)(2,1)} %param.17) | copy-start | bytes 2359300
  19.7 0.9 %copy-start.6 = (bf16[144,256]{1,0:T(8,128)(2,1)S(1)}, bf16[144,256]{1,0:T(8,128)(2,1)}, u32[]{:S(2)}) copy-start(bf16[144,256]{1,0:T(8,128)(2,1)} %get-tuple-element.36.refs_0_) | copy-start | bytes 221188
  23.3 0.7 %copy-start.3 = (bf16[144,384]{1,0:T(8,128)(2,1)}, bf16[144,384]{1,0:T(8,128)(2,1)S(1)}, u32[]{:S(2)}) copy-start(bf16[144,384]{1,0:T(8,128)(2,1)S(1)} %get-tuple-element.53.hid_ref) | copy-start | bytes 331780
  23.3 0.8 %copy-start.5 = (bf16[8,80,256]{2,1,0:T(8,128)(2,1)}, bf16[8,80,256]{2,1,0:T(8,128)(2,1)S(1)}, u32[]{:S(2)}) copy-start(bf16[8,80,256]{2,1,0:T(8,128)(2,1)S(1)} %get-tuple-element.48) | copy-start | bytes 983044
  23.9 6.2 %collective-permute-start.7 = (bf16[1536,384]{1,0:T(8,128)(2,1)S(1)}, bf16[1536,384]{1,0:T(8,128)(2,1)S(1)}, u32[]{:S(2)}, u32[]{:S(2)}) collective-permute-start(bf16[1536,384]{1,0:T(8,128)(2,1)S(1)} %other_half.1), channel_id=1, source_target_pairs={{0,1},{1,0},{2,3},{3,2},{4,5},{5,4},{6,7},{7,6},{8,9},{9,8},{10,11... | collective-permute-start | bytes 3538952 | tf_op jit(solution)/shard_map/ppermute | solution.py:600
  24.1 17.0 %all-to-all-start = ((bf16[8,80,256]{2,1,0:T(8,128)(2,1)}), bf16[8,80,256]{2,1,0:T(8,128)(2,1)S(1)}, u32[]{:S(2)}, u32[]{:S(2)}) async-start(bf16[8,80,256]{2,1,0:T(8,128)(2,1)} %copy-done.5), calls=%async_computation | async-start | bytes 655360 | tf_op jit(solution)/shard_map/all_to_all | solution.py:590
  30.2 0.9 %copy-start.4 = (bf16[144,384]{1,0:T(8,128)(2,1)S(1)}, bf16[144,384]{1,0:T(8,128)(2,1)}, u32[]{:S(2)}) copy-start(bf16[144,384]{1,0:T(8,128)(2,1)} %copy-done.3) | copy-start | bytes 331780
  31.1 10.0 %copy-start.7 = (s32[128,8]{0,1:T(8,128)S(1)}, s32[128,8]{0,1:T(8,128)}, u32[]{:S(2)}) copy-start(s32[128,8]{0,1:T(8,128)} %param.11) | copy-start | bytes 12292
  31.1 10.0 %copy-start.8 = (s32[8,128]{1,0:T(8,128)S(1)}, s32[8,128]{1,0:T(8,128)}, u32[]{:S(2)}) copy-start(s32[8,128]{1,0:T(8,128)} %get-tuple-element.34.slot_ref) | copy-start | bytes 12292
  31.1 10.0 %copy-start.9 = (f32[8,128]{1,0:T(8,128)S(1)}, f32[8,128]{1,0:T(8,128)}, u32[]{:S(2)}) copy-start(f32[8,128]{1,0:T(8,128)} %get-tuple-element.35.gates_ref) | copy-start | bytes 12292

commit v6 on v3

--- a/solution.py
+++ b/solution.py
@@ -240,7 +240,7 @@
 QUARTERS = 4
 SEND_ROWS = 2 * QUARTERS * MAIN + 16
 BACK_ROWS = QUARTERS * MAIN + 16
-STEPS = (4, 5, 6, 7, 0, 1, 2, 3)
+STEPS = (0, 1, 4, 5, 6, 7, 2, 3)
 GROUP = 4
 GROUP_ROWS = GROUP * MAIN + 16
 
@@ -509,7 +509,7 @@
         in_specs=[pl.BlockSpec(memory_space=space)] * len(arrays),
         out_specs=[vmem] * len(outs),
         scratch_shapes=list(scratch),
-        compiler_params=pltpu.CompilerParams(vmem_limit_bytes=limit * MIB),
+        compiler_params=pltpu.CompilerParams(vmem_limit_bytes=int(limit * MIB)),
         cost_estimate=pl.CostEstimate(flops=flops, bytes_accessed=moved, transcendentals=0),
         name=name,
     )(*arrays)
@@ -524,9 +524,16 @@
 
 
 def hold_kernel(*refs):
+    *refs, sems = refs
     count = len(refs) // 2
-    for source, place in zip(refs[:count], refs[count:]):
-        place[...] = source[...]
+    loads = [
+        pltpu.make_async_copy(source, place, sems.at[n])
+        for n, (source, place) in enumerate(zip(refs[:count], refs[count:]))
+    ]
+    for load in loads:
+        load.start()
+    for load in loads:
+        load.wait()
 
 
 def per_device_moving_rows(
@@ -577,6 +584,9 @@
         "hold",
         0,
         4 * 3 * model_width * hidden_width,
+        space=pltpu.HBM,
+        limit=51.25,
+        scratch=[pltpu.SemaphoreType.DMA((len(matrices),))],
     )
     matmul = 2 * GROUP_ROWS * model_width * hidden_width
     returned, factors = [], []

time: 45.8 us -> 42.8 us (0.934)
  local copies, waits for them, and re-layouts: 3.42 us -> 0.02 us
  starting transfers between devices: 25.7 us -> 22.5 us
  waiting for transfers between devices: 7.08 us -> 9.36 us
  Pallas kernels: 8.57 us -> 10 us
    unnamed x14 -> x8, local copies, waits for them, and re-layouts: 3.42 us -> 0.02 us
    ppermute x14, starting transfers between devices: 25.6 us -> 22.4 us  [exchange(): lax.ppermute(chunk, 'expert', [(i, i ^ step) for i in range(experts)])]
    ppermute x14, waiting for transfers between devices: 7.07 us -> 9.35 us  [exchange(): lax.ppermute(chunk, 'expert', [(i, i ^ step) for i in range(experts)])]
    pallas_call x7, Pallas kernels: 8.57 us -> 10 us  [local_call(): pl.pallas_call(kernel, out_shape=[jax.ShapeDtypeStruct(shape, kind) for s...]
  transfers between devices with their start and end apart: 15 -> 15, of which waited for: 5 -> 5; matrix products, arithmetic and copies ran while one was open for 0% -> 0% of each run, Pallas kernels for 10% -> 14%
where the time goes in v6:
time: 42.8 us; the launch traced here: 42.6 us
  starting transfers between devices  22.5 us (53%)
  Pallas kernels  10 us (23%)
  waiting for transfers between devices  9.36 us (22%)
  between operations  0.73 us (2%)
    ppermute x14, starting transfers between devices, exchange(): lax.ppermute(chunk, 'expert', [(i, i ^ step) for i in range(experts)])  22.4 us
    pallas_call x7, Pallas kernels, local_call(): pl.pallas_call(kernel, out_shape=[jax.ShapeDtypeStruct(shape, kind) for s...  10 us
    ppermute x14, waiting for transfers between devices, exchange(): lax.ppermute(chunk, 'expert', [(i, i ^ step) for i in range(experts)])  9.35 us
  transfers between devices with their start and end apart: 15, of which 5 were waited for; matrix products, arithmetic and copies ran while one was open for 0% of the time, Pallas kernels for 14%

profile of v6, /device:TPU:0, one launch (start us, length us, event | category | flops | bytes accessed | tf_op | source)
XLA Modules:
  0.0 42.6 jit_solution(557595751574644866)
XLA Ops:
  0.6 2.3 %route.1 = (bf16[144,256]{1,0:T(8,128)(2,1)}, bf16[144,256]{1,0:T(8,128)(2,1)}, bf16[144,256]{1,0:T(8,128)(2,1)}, bf16[144,256]{1,0:T(8,128)(2,1)}, bf16[144,256...) custom-call(s32[8]{0:T(128)} %plan_hbm.1, ...), custom_call_target="tpu_custom_call" | custom-call | flops 75497472 | bytes 1114112 | tf_op jit(solution)/shard_map/route/pallas_call | solution.py:506
  3.0 3.0 %collective-permute-start = (bf16[144,256]{1,0:T(8,128)(2,1)}, bf16[144,256]{1,0:T(8,128)(2,1)S(1)}, u32[]{:S(2)}, u32[]{:S(2)}) collective-permute-start(bf16[144,256]{1,0:T(8,128)(2,1)} %get-tuple-element.69), channel_id=1, source_target_pairs={{0,2},{2,0},{4,6},{6,4},{8,10},{10,8},{12,14},{14,12},{1,3},{3,1},... | collective-permute-start | bytes 221192 | tf_op jit(solution)/shard_map/ppermute | solution.py:521
  6.0 2.6 %collective-permute-start.1 = (bf16[144,256]{1,0:T(8,128)(2,1)}, bf16[144,256]{1,0:T(8,128)(2,1)S(1)}, u32[]{:S(2)}, u32[]{:S(2)}) collective-permute-start(bf16[144,256]{1,0:T(8,128)(2,1)} %get-tuple-element.70), channel_id=1, source_target_pairs={{0,8},{2,10},{4,12},{6,14},{8,0},{10,2},{12,4},{14,6},{1,9},{3,11}... | collective-permute-start | bytes 221192 | tf_op jit(solution)/shard_map/ppermute | solution.py:521
  8.6 0.0 collective-permute-start.2
  8.6 3.9 %collective-permute-start.6 = (bf16[144,256]{1,0:T(8,128)(2,1)}, bf16[144,256]{1,0:T(8,128)(2,1)S(1)}, u32[]{:S(2)}, u32[]{:S(2)}) collective-permute-start(bf16[144,256]{1,0:T(8,128)(2,1)} %get-tuple-element.84), channel_id=1, source_target_pairs={{0,12},{2,14},{4,8},{6,10},{8,4},{10,6},{12,0},{14,2},{1,13},{3,15... | collective-permute-start | bytes 221192 | tf_op jit(solution)/shard_map/ppermute | solution.py:521
  12.5 1.1 %collective-permute-start.7 = (bf16[144,256]{1,0:T(8,128)(2,1)}, bf16[144,256]{1,0:T(8,128)(2,1)S(1)}, u32[]{:S(2)}, u32[]{:S(2)}) collective-permute-start(bf16[144,256]{1,0:T(8,128)(2,1)} %get-tuple-element.85), channel_id=1, source_target_pairs={{0,14},{2,12},{4,10},{6,8},{8,6},{10,4},{12,2},{14,0},{1,15},{3,13... | collective-permute-start | bytes 221192 | tf_op jit(solution)/shard_map/ppermute | solution.py:521
  13.6 0.0 collective-permute-done.refs_1_
  13.6 0.0 collective-permute-start.8
  13.6 2.6 %collective-permute-done.1.refs_2_ = bf16[144,256]{1,0:T(8,128)(2,1)S(1)} collective-permute-done((bf16[144,256]{1,0:T(8,128)(2,1)}, bf16[144,256]{1,0:T(8,128)(2,1)S(1)}, u32[]{:S(2)}, u32[]{:S(2)}) %collective-permute-start.1) | collective-permute-done | bytes 73760 | tf_op jit(solution)/shard_map/ppermute | solution.py:521
  16.2 0.1 collective-permute-start.9
  16.3 0.0 copy-start
  16.3 1.7 %hold.1 = (bf16[1024,384]{1,0:T(8,128)(2,1)S(1)}, bf16[1024,384]{1,0:T(8,128)(2,1)S(1)}, bf16[1024,384]{1,0:T(8,128)(2,1)S(1)}) custom-call(bf16[1024,384]{1,0:T(8,128)(2,1)} %bitcast.12, bf16[1024,384]{1,0:T(8,128)(2,1)} %bitcast.13, bf16[1024,384]{1,0:T(8,128)(2,1)} %bitcast.14), custom_call_target="tpu_custom_call" | custom-call | bytes 4718592 | tf_op jit(solution)/shard_map/hold/pallas_call | solution.py:506
  18.0 1.9 %collective-permute-done.2.refs_3_ = bf16[144,256]{1,0:T(8,128)(2,1)S(1)} collective-permute-done((bf16[144,256]{1,0:T(8,128)(2,1)}, bf16[144,256]{1,0:T(8,128)(2,1)S(1)}, u32[]{:S(2)}, u32[]{:S(2)}) %collective-permute-start.2) | collective-permute-done | bytes 73760 | tf_op jit(solution)/shard_map/ppermute | solution.py:521
  19.9 0.0 copy-done
  19.9 1.3 %expert_rows.2 = (bf16[80,256]{1,0:T(8,128)(2,1)S(1)}, bf16[80,256]{1,0:T(8,128)(2,1)S(1)}, bf16[80,256]{1,0:T(8,128)(2,1)S(1)}, bf16[80,256]{1,0:T(8,128)(2,1)S...) custom-call(bf16[144,256]{1,0:T(8,128)(2,1)S(1)} %copy-done, ...), custom_call_target="tpu_custom_call" | custom-call | flops 314572800 | bytes 2359296 | tf_op jit(solution)/shard_map/expert_rows/pallas_call | solution.py:506
  21.2 0.6 %collective-permute-start.3 = (bf16[80,256]{1,0:T(8,128)(2,1)S(1)}, bf16[80,256]{1,0:T(8,128)(2,1)S(1)}, u32[]{:S(2)}, u32[]{:S(2)}) collective-permute-start(bf16[80,256]{1,0:T(8,128)(2,1)S(1)} %get-tuple-element.76), channel_id=1, source_target_pairs={{0,2},{2,0},{4,6},{6,4},{8,10},{10,8},{12,14},{14,12},{1,3},{3,1},... | collective-permute-start | bytes 122888 | tf_op jit(solution)/shard_map/ppermute | solution.py:521
  21.8 0.0 collective-permute-done.6.refs_0_
  21.8 3.7 %collective-permute-start.4 = (bf16[80,256]{1,0:T(8,128)(2,1)S(1)}, bf16[80,256]{1,0:T(8,128)(2,1)S(1)}, u32[]{:S(2)}, u32[]{:S(2)}) collective-permute-start(bf16[80,256]{1,0:T(8,128)(2,1)S(1)} %get-tuple-element.77), channel_id=1, source_target_pairs={{0,8},{2,10},{4,12},{6,14},{8,0},{10,2},{12,4},{14,6},{1,9},{3,11}... | collective-permute-start | bytes 122888 | tf_op jit(solution)/shard_map/ppermute | solution.py:521
  25.6 0.0 collective-permute-done.7.refs_1_
  25.6 0.5 %collective-permute-start.5 = (bf16[80,256]{1,0:T(8,128)(2,1)S(1)}, bf16[80,256]{1,0:T(8,128)(2,1)S(1)}, u32[]{:S(2)}, u32[]{:S(2)}) collective-permute-start(bf16[80,256]{1,0:T(8,128)(2,1)S(1)} %get-tuple-element.78), channel_id=1, source_target_pairs={{0,10},{2,8},{4,14},{6,12},{8,2},{10,0},{12,6},{14,4},{1,11},{3,9}... | collective-permute-start | bytes 122888 | tf_op jit(solution)/shard_map/ppermute | solution.py:521
  26.1 0.0 collective-permute-done.8.refs_2_
  26.1 0.0 collective-permute-done.9.refs_3_
  26.1 1.3 %expert_rows.3 = (bf16[80,256]{1,0:T(8,128)(2,1)S(1)}, bf16[80,256]{1,0:T(8,128)(2,1)S(1)}, bf16[80,256]{1,0:T(8,128)(2,1)S(1)}, bf16[80,256]{1,0:T(8,128)(2,1)S...) custom-call(bf16[144,256]{1,0:T(8,128)(2,1)S(1)} %collective-permute, ...), custom_call_target="tpu_custom_call" | custom-call | flops 314572800 | bytes 2359296 | tf_op jit(solution)/shard_map/expert_rows/pallas_call | solution.py:506
  27.4 0.0 collective-permute-done.3.refs_1_
  27.4 0.2 collective-permute-done.4.refs_2_
  27.6 3.8 %collective-permute-done.5.refs_3_ = bf16[80,256]{1,0:T(8,128)(2,1)S(1)} collective-permute-done((bf16[80,256]{1,0:T(8,128)(2,1)S(1)}, bf16[80,256]{1,0:T(8,128)(2,1)S(1)}, u32[]{:S(2)}, u32[]{:S(2)}) %collective-permute-start.5) | collective-permute-done | bytes 40992 | tf_op jit(solution)/shard_map/ppermute | solution.py:521
  31.4 0.8 %other_half.1 = bf16[1536,384]{1,0:T(8,128)(2,1)S(1)} custom-call(bf16[80,1024]{1,0:T(8,128)(2,1)S(1)} %get-tuple-element.101.refs_0_, bf16[80,1024]{1,0:T(8,128)(2,1)S(1)} %get-tuple-element.102.refs_1_, bf16[80,384]{1,0:T(8,128)(2,1)S(1)} %get-tuple-element.103.refs_2_, bf16[80,384]{1,0:T(8,128)(2,1)S(1)} %get-tuple-element.104.refs_3_, ...), custom_call_target="tpu_custom_call" | custom-call | flops 1 | bytes 1 | tf_op jit(solution)/shard_map/other_half/pallas_call | solution.py:506
  32.2 0.0 copy-start.1
  32.2 0.0 copy-start.2
  32.3 0.0 copy-start.3
  32.3 0.1 collective-permute-start.14
  32.3 0.1 collective-permute-start.10
  32.5 3.7 %collective-permute-start.11 = (bf16[80,256]{1,0:T(8,128)(2,1)S(1)}, bf16[80,256]{1,0:T(8,128)(2,1)S(1)}, u32[]{:S(2)}, u32[]{:S(2)}) collective-permute-start(bf16[80,256]{1,0:T(8,128)(2,1)S(1)} %get-tuple-element.98), channel_id=1, source_target_pairs={{0,14},{2,12},{4,10},{6,8},{8,6},{10,4},{12,2},{14,0},{1,15},{3,13... | collective-permute-start | bytes 122888 | tf_op jit(solution)/shard_map/ppermute | solution.py:521
  36.1 0.0 collective-permute-start.12
  36.1 3.0 %collective-permute-start.13 = (bf16[80,256]{1,0:T(8,128)(2,1)S(1)}, bf16[80,256]{1,0:T(8,128)(2,1)S(1)}, u32[]{:S(2)}, u32[]{:S(2)}) collective-permute-start(bf16[80,256]{1,0:T(8,128)(2,1)S(1)} %get-tuple-element.100), channel_id=1, source_target_pairs={{0,6},{2,4},{4,2},{6,0},{8,14},{10,12},{12,10},{14,8},{1,7},{3,5},... | collective-permute-start | bytes 122888 | tf_op jit(solution)/shard_map/ppermute | solution.py:521
  39.2 0.0 collective-permute-done.14.refs_10_
  39.2 1.6 %own_half.1 = (bf16[512,384]{1,0:T(8,128)(2,1)}, bf16[512,384]{1,0:T(8,128)(2,1)}, bf16[512,384]{1,0:T(8,128)(2,1)}) custom-call(bf16[80,1024]{1,0:T(8,128)(2,1)S(1)} %get-tuple-element.101.refs_0_, bf16[80,1024]{1,0:T(8,128)(2,1)S(1)} %get-tuple-element.102.refs_1_, bf16[80,384]{1,0:T(8,128)(2,1)S(1)} %get-tuple-element.103.refs_2_, ...), custom_call_target="tpu_custom_call" | custom-call | flops 1 | bytes 1 | tf_op jit(solution)/shard_map/own_half/pallas_call | solution.py:506
  40.8 0.0 collective-permute-done.10.refs_4_
  40.8 0.0 collective-permute-done.11.refs_5_
  40.8 0.0 collective-permute-done.12.refs_6_
  40.8 0.8 %collective-permute-done.13.refs_7_ = bf16[80,256]{1,0:T(8,128)(2,1)S(1)} collective-permute-done((bf16[80,256]{1,0:T(8,128)(2,1)S(1)}, bf16[80,256]{1,0:T(8,128)(2,1)S(1)}, u32[]{:S(2)}, u32[]{:S(2)}) %collective-permute-start.13) | collective-permute-done | bytes 40992 | tf_op jit(solution)/shard_map/ppermute | solution.py:521
  41.6 0.0 copy-done.1
  41.6 0.0 copy-done.2
  41.6 0.0 copy-done.3
  41.6 1.0 %combine.1 = (bf16[128,1024]{1,0:T(8,128)(2,1)}, bf16[8,128]{1,0:T(8,128)(2,1)}) custom-call(s32[8,128]{1,0:T(8,128)S(1)} %bitcast.11, s32[8,128]{1,0:T(8,128)S(1)} %copy-done.2, f32[8,128]{1,0:T(8,128)S(1)} %copy-done.3, bf16[80,256]{1,0:T(8,128)(2,1)S(1)} %get-tuple-element.114.refs_0_, bf16[80,256]{1,0:T(8,128)(2,1)S(1)} %collective-permute-done.3.refs_1_, ...), custom_call_target="tpu_custom_call" | custom-call | flops 37748736 | bytes 524288 | tf_op jit(solution)/shard_map/combine/pallas_call | solution.py:506
Async XLA Ops:
  3.0 10.7 %collective-permute-start = (bf16[144,256]{1,0:T(8,128)(2,1)}, bf16[144,256]{1,0:T(8,128)(2,1)S(1)}, u32[]{:S(2)}, u32[]{:S(2)}) collective-permute-start(bf16[144,256]{1,0:T(8,128)(2,1)} %get-tuple-element.69), channel_id=1, source_target_pairs={{0,2},{2,0},{4,6},{6,4},{8,10},{10,8},{12,14},{14,12},{1,3},{3,1},... | collective-permute-start | bytes 221192 | tf_op jit(solution)/shard_map/ppermute | solution.py:521
  6.0 10.2 %collective-permute-start.1 = (bf16[144,256]{1,0:T(8,128)(2,1)}, bf16[144,256]{1,0:T(8,128)(2,1)S(1)}, u32[]{:S(2)}, u32[]{:S(2)}) collective-permute-start(bf16[144,256]{1,0:T(8,128)(2,1)} %get-tuple-element.70), channel_id=1, source_target_pairs={{0,8},{2,10},{4,12},{6,14},{8,0},{10,2},{12,4},{14,6},{1,9},{3,11}... | collective-permute-start | bytes 221192 | tf_op jit(solution)/shard_map/ppermute | solution.py:521
  8.6 11.4 %collective-permute-start.2 = (bf16[144,256]{1,0:T(8,128)(2,1)}, bf16[144,256]{1,0:T(8,128)(2,1)S(1)}, u32[]{:S(2)}, u32[]{:S(2)}) collective-permute-start(bf16[144,256]{1,0:T(8,128)(2,1)} %get-tuple-element.71), channel_id=1, source_target_pairs={{0,10},{2,8},{4,14},{6,12},{8,2},{10,0},{12,6},{14,4},{1,11},{3,9}... | collective-permute-start | bytes 221192 | tf_op jit(solution)/shard_map/ppermute | solution.py:521
  8.6 13.3 %collective-permute-start.6 = (bf16[144,256]{1,0:T(8,128)(2,1)}, bf16[144,256]{1,0:T(8,128)(2,1)S(1)}, u32[]{:S(2)}, u32[]{:S(2)}) collective-permute-start(bf16[144,256]{1,0:T(8,128)(2,1)} %get-tuple-element.84), channel_id=1, source_target_pairs={{0,12},{2,14},{4,8},{6,10},{8,4},{10,6},{12,0},{14,2},{1,13},{3,15... | collective-permute-start | bytes 221192 | tf_op jit(solution)/shard_map/ppermute | solution.py:521
  12.5 13.1 %collective-permute-start.7 = (bf16[144,256]{1,0:T(8,128)(2,1)}, bf16[144,256]{1,0:T(8,128)(2,1)S(1)}, u32[]{:S(2)}, u32[]{:S(2)}) collective-permute-start(bf16[144,256]{1,0:T(8,128)(2,1)} %get-tuple-element.85), channel_id=1, source_target_pairs={{0,14},{2,12},{4,10},{6,8},{8,6},{10,4},{12,2},{14,0},{1,15},{3,13... | collective-permute-start | bytes 221192 | tf_op jit(solution)/shard_map/ppermute | solution.py:521
  13.6 12.4 %collective-permute-start.8 = (bf16[144,256]{1,0:T(8,128)(2,1)}, bf16[144,256]{1,0:T(8,128)(2,1)S(1)}, u32[]{:S(2)}, u32[]{:S(2)}) collective-permute-start(bf16[144,256]{1,0:T(8,128)(2,1)} %get-tuple-element.86), channel_id=1, source_target_pairs={{0,4},{2,6},{4,0},{6,2},{8,12},{10,14},{12,8},{14,10},{1,5},{3,7},... | collective-permute-start | bytes 221192 | tf_op jit(solution)/shard_map/ppermute | solution.py:521
  16.2 9.9 %collective-permute-start.9 = (bf16[144,256]{1,0:T(8,128)(2,1)}, bf16[144,256]{1,0:T(8,128)(2,1)S(1)}, u32[]{:S(2)}, u32[]{:S(2)}) collective-permute-start(bf16[144,256]{1,0:T(8,128)(2,1)} %get-tuple-element.87), channel_id=1, source_target_pairs={{0,6},{2,4},{4,2},{6,0},{8,14},{10,12},{12,10},{14,8},{1,7},{3,5},... | collective-permute-start | bytes 221192 | tf_op jit(solution)/shard_map/ppermute | solution.py:521
  16.3 3.6 %copy-start = (bf16[144,256]{1,0:T(8,128)(2,1)S(1)}, bf16[144,256]{1,0:T(8,128)(2,1)}, u32[]{:S(2)}) copy-start(bf16[144,256]{1,0:T(8,128)(2,1)} %get-tuple-element.68.refs_0_) | copy-start | bytes 221188
  21.2 6.1 %collective-permute-start.3 = (bf16[80,256]{1,0:T(8,128)(2,1)S(1)}, bf16[80,256]{1,0:T(8,128)(2,1)S(1)}, u32[]{:S(2)}, u32[]{:S(2)}) collective-permute-start(bf16[80,256]{1,0:T(8,128)(2,1)S(1)} %get-tuple-element.76), channel_id=1, source_target_pairs={{0,2},{2,0},{4,6},{6,4},{8,10},{10,8},{12,14},{14,12},{1,3},{3,1},... | collective-permute-start | bytes 122888 | tf_op jit(solution)/shard_map/ppermute | solution.py:521
  21.8 5.8 %collective-permute-start.4 = (bf16[80,256]{1,0:T(8,128)(2,1)S(1)}, bf16[80,256]{1,0:T(8,128)(2,1)S(1)}, u32[]{:S(2)}, u32[]{:S(2)}) collective-permute-start(bf16[80,256]{1,0:T(8,128)(2,1)S(1)} %get-tuple-element.77), channel_id=1, source_target_pairs={{0,8},{2,10},{4,12},{6,14},{8,0},{10,2},{12,4},{14,6},{1,9},{3,11}... | collective-permute-start | bytes 122888 | tf_op jit(solution)/shard_map/ppermute | solution.py:521
  25.6 5.8 %collective-permute-start.5 = (bf16[80,256]{1,0:T(8,128)(2,1)S(1)}, bf16[80,256]{1,0:T(8,128)(2,1)S(1)}, u32[]{:S(2)}, u32[]{:S(2)}) collective-permute-start(bf16[80,256]{1,0:T(8,128)(2,1)S(1)} %get-tuple-element.78), channel_id=1, source_target_pairs={{0,10},{2,8},{4,14},{6,12},{8,2},{10,0},{12,6},{14,4},{1,11},{3,9}... | collective-permute-start | bytes 122888 | tf_op jit(solution)/shard_map/ppermute | solution.py:521
  32.2 9.3 %copy-start.1 = (s32[128,8]{0,1:T(8,128)S(1)}, s32[128,8]{0,1:T(8,128)}, u32[]{:S(2)}) copy-start(s32[128,8]{0,1:T(8,128)} %param.11) | copy-start | bytes 12292
  32.2 9.3 %copy-start.2 = (s32[8,128]{1,0:T(8,128)S(1)}, s32[8,128]{1,0:T(8,128)}, u32[]{:S(2)}) copy-start(s32[8,128]{1,0:T(8,128)} %get-tuple-element.66.slot_ref) | copy-start | bytes 12292
  32.3 9.3 %copy-start.3 = (f32[8,128]{1,0:T(8,128)S(1)}, f32[8,128]{1,0:T(8,128)}, u32[]{:S(2)}) copy-start(f32[8,128]{1,0:T(8,128)} %get-tuple-element.67.gates_ref) | copy-start | bytes 12292
  32.3 6.9 %collective-permute-start.14 = (bf16[1536,384]{1,0:T(8,128)(2,1)S(1)}, bf16[1536,384]{1,0:T(8,128)(2,1)S(1)}, u32[]{:S(2)}, u32[]{:S(2)}) collective-permute-start(bf16[1536,384]{1,0:T(8,128)(2,1)S(1)} %other_half.1), channel_id=1, source_target_pairs={{0,1},{1,0},{2,3},{3,2},{4,5},{5,4},{6,7},{7,6},{8,9},{9,8},{10,11... | collective-permute-start | bytes 3538952 | tf_op jit(solution)/shard_map/ppermute | solution.py:616
  32.3 8.4 %collective-permute-start.10 = (bf16[80,256]{1,0:T(8,128)(2,1)S(1)}, bf16[80,256]{1,0:T(8,128)(2,1)S(1)}, u32[]{:S(2)}, u32[]{:S(2)}) collective-permute-start(bf16[80,256]{1,0:T(8,128)(2,1)S(1)} %get-tuple-element.97), channel_id=1, source_target_pairs={{0,12},{2,14},{4,8},{6,10},{8,4},{10,6},{12,0},{14,2},{1,13},{3,15... | collective-permute-start | bytes 122888 | tf_op jit(solution)/shard_map/ppermute | solution.py:521
  32.5 8.3 %collective-permute-start.11 = (bf16[80,256]{1,0:T(8,128)(2,1)S(1)}, bf16[80,256]{1,0:T(8,128)(2,1)S(1)}, u32[]{:S(2)}, u32[]{:S(2)}) collective-permute-start(bf16[80,256]{1,0:T(8,128)(2,1)S(1)} %get-tuple-element.98), channel_id=1, source_target_pairs={{0,14},{2,12},{4,10},{6,8},{8,6},{10,4},{12,2},{14,0},{1,15},{3,13... | collective-permute-start | bytes 122888 | tf_op jit(solution)/shard_map/ppermute | solution.py:521
  36.1 4.6 %collective-permute-start.12 = (bf16[80,256]{1,0:T(8,128)(2,1)S(1)}, bf16[80,256]{1,0:T(8,128)(2,1)S(1)}, u32[]{:S(2)}, u32[]{:S(2)}) collective-permute-start(bf16[80,256]{1,0:T(8,128)(2,1)S(1)} %get-tuple-element.99), channel_id=1, source_target_pairs={{0,4},{2,6},{4,0},{6,2},{8,12},{10,14},{12,8},{14,10},{1,5},{3,7},... | collective-permute-start | bytes 122888 | tf_op jit(solution)/shard_map/ppermute | solution.py:521
  36.1 5.4 %collective-permute-start.13 = (bf16[80,256]{1,0:T(8,128)(2,1)S(1)}, bf16[80,256]{1,0:T(8,128)(2,1)S(1)}, u32[]{:S(2)}, u32[]{:S(2)}) collective-permute-start(bf16[80,256]{1,0:T(8,128)(2,1)S(1)} %get-tuple-element.100), channel_id=1, source_target_pairs={{0,6},{2,4},{4,2},{6,0},{8,14},{10,12},{12,10},{14,8},{1,7},{3,5},... | collective-permute-start | bytes 122888 | tf_op jit(solution)/shard_map/ppermute | solution.py:521

commit v7 on v2

--- a/solution.py
+++ b/solution.py
@@ -240,7 +240,7 @@
 QUARTERS = 4
 SEND_ROWS = 2 * QUARTERS * MAIN + 16
 BACK_ROWS = QUARTERS * MAIN + 16
-STEPS = (0, 1, 4, 5, 6, 7, 2, 3)
+STEPS = (0, 4, 1, 5, 6, 7, 2, 3)
 
 
 def copies_of(experts):
@@ -254,7 +254,7 @@
 def partners(experts, tokens):
     row = iota((experts, tokens), 0)
     step = jnp.zeros((experts, tokens), jnp.int32)
-    for c in range(1, experts):
+    for c in range(experts):
         step = jnp.where(row == c, STEPS[c], step)
     return jnp.bitwise_xor(step, lax.axis_index("expert"))
 
@@ -507,7 +507,7 @@
         in_specs=[pl.BlockSpec(memory_space=space)] * len(arrays),
         out_specs=[vmem] * len(outs),
         scratch_shapes=list(scratch),
-        compiler_params=pltpu.CompilerParams(vmem_limit_bytes=limit * MIB),
+        compiler_params=pltpu.CompilerParams(vmem_limit_bytes=int(limit * MIB)),
         cost_estimate=pl.CostEstimate(flops=flops, bytes_accessed=moved, transcendentals=0),
         name=name,
     )(*arrays)
@@ -523,9 +523,16 @@
 
 
 def hold_kernel(*refs):
+    *refs, sems = refs
     count = len(refs) // 2
-    for source, place in zip(refs[:count], refs[count:]):
-        place[...] = source[...]
+    loads = [
+        pltpu.make_async_copy(source, place, sems.at[n])
+        for n, (source, place) in enumerate(zip(refs[:count], refs[count:]))
+    ]
+    for load in loads:
+        load.start()
+    for load in loads:
+        load.wait()
 
 
 def per_device_moving_rows(
@@ -555,7 +562,7 @@
         2 * 2 * served * token_count * model_width,
         2 * 2 * (token_count + served) * model_width,
         space=pltpu.HBM,
-        limit=58,
+        limit=54,
         scratch=[
             pltpu.SMEM((experts,), jnp.int32),
             pltpu.VMEM(small, jnp.int32),
@@ -576,6 +583,9 @@
         "hold",
         0,
         4 * 3 * model_width * hidden_width,
+        space=pltpu.HBM,
+        limit=51.25,
+        scratch=[pltpu.SemaphoreType.DMA((len(held),))],
     )
     matmul = 2 * served * model_width * hidden_width
     outs = local_call(
@@ -590,15 +600,14 @@
     )
     factors = outs[experts:]
     returned = exchange(outs[:experts])
-    returned[1], factors = lax.optimization_barrier((returned[1], factors))
     half = model_width // 2
     (leaving,) = local_call(
         other_half_kernel,
         [((3 * half, hidden_width), BF)],
         factors,
         "other_half",
-        3 * matmul // 2,
-        2 * 3 * half * hidden_width,
+        1,
+        1,
     )
     came = lax.ppermute(leaving, "replica", [(0, 1), (1, 0)])
     shares = local_call(
@@ -606,8 +615,8 @@
         [((half, hidden_width), BF)] * 3,
         [*factors, came],
         "own_half",
-        3 * matmul // 2,
-        2 * 2 * 3 * half * hidden_width,
+        1,
+        1,
     )
     returned, shares = lax.optimization_barrier((returned, shares))
     token_grad, gate_grad = local_call(

time: 44 us -> 40.8 us (0.927)
  local copies, waits for them, and re-layouts: 4.3 us -> 0.9 us
  waiting for transfers between devices: 7.06 us -> 4.03 us
  starting transfers between devices: 24.4 us -> 26.3 us
  Pallas kernels: 7.2 us -> 8.72 us
    unnamed x14 -> x8, local copies, waits for them, and re-layouts: 4.3 us -> 0.9 us
    ppermute x14, waiting for transfers between devices: 7.06 us -> 4.02 us  [exchange(): lax.ppermute(chunk, 'expert', [(i, i ^ step) for i in range(count)])]
    ppermute x14, starting transfers between devices: 24.3 us -> 26.2 us  [exchange(): lax.ppermute(chunk, 'expert', [(i, i ^ step) for i in range(count)])]
    pallas_call x6, Pallas kernels: 7.2 us -> 8.72 us  [local_call(): pl.pallas_call(kernel, out_shape=[jax.ShapeDtypeStruct(shape, kind) for s...]
  transfers between devices with their start and end apart: 15 -> 15, of which waited for: 5 -> 6; matrix products, arithmetic and copies ran while one was open for 0% -> 0% of each run, Pallas kernels for 4% -> 8%
where the time goes in v7:
time: 40.8 us; the launch traced here: 40.6 us
  starting transfers between devices  26.3 us (64%)
  Pallas kernels  8.72 us (21%)
  waiting for transfers between devices  4.03 us (10%)
  local copies, waits for them, and re-layouts  0.9 us (2%)
  between operations  0.71 us (2%)
    ppermute x14, starting transfers between devices, exchange(): lax.ppermute(chunk, 'expert', [(i, i ^ step) for i in range(count)])  26.2 us
    pallas_call x6, Pallas kernels, local_call(): pl.pallas_call(kernel, out_shape=[jax.ShapeDtypeStruct(shape, kind) for s...  8.72 us
    ppermute x14, waiting for transfers between devices, exchange(): lax.ppermute(chunk, 'expert', [(i, i ^ step) for i in range(count)])  4.02 us
    unnamed x8, local copies, waits for them, and re-layouts  0.9 us
  transfers between devices with their start and end apart: 15, of which 6 were waited for; matrix products, arithmetic and copies ran while one was open for 0% of the time, Pallas kernels for 8%

profile of v7, /device:TPU:0, one launch (start us, length us, event | category | flops | bytes accessed | tf_op | source)
XLA Modules:
  0.0 40.6 jit_solution(8694529894279013678)
XLA Ops:
  0.6 2.3 %route.1 = (bf16[144,256]{1,0:T(8,128)(2,1)}, bf16[144,256]{1,0:T(8,128)(2,1)}, bf16[144,256]{1,0:T(8,128)(2,1)}, bf16[144,256]{1,0:T(8,128)(2,1)}, bf16[144,256...) custom-call(s32[8]{0:T(128)} %plan_hbm.1, ...), custom_call_target="tpu_custom_call" | custom-call | flops 75497472 | bytes 1114112 | tf_op jit(solution)/shard_map/route/pallas_call | solution.py:504
  3.0 4.1 %collective-permute-start = (bf16[144,256]{1,0:T(8,128)(2,1)}, bf16[144,256]{1,0:T(8,128)(2,1)S(1)}, u32[]{:S(2)}, u32[]{:S(2)}) collective-permute-start(bf16[144,256]{1,0:T(8,128)(2,1)} %get-tuple-element.52), channel_id=1, source_target_pairs={{0,8},{2,10},{4,12},{6,14},{8,0},{10,2},{12,4},{14,6},{1,9},{3,11}... | collective-permute-start | bytes 221192 | tf_op jit(solution)/shard_map/ppermute | solution.py:519
  7.1 1.5 %collective-permute-start.1 = (bf16[144,256]{1,0:T(8,128)(2,1)}, bf16[144,256]{1,0:T(8,128)(2,1)S(1)}, u32[]{:S(2)}, u32[]{:S(2)}) collective-permute-start(bf16[144,256]{1,0:T(8,128)(2,1)} %get-tuple-element.53), channel_id=1, source_target_pairs={{0,2},{2,0},{4,6},{6,4},{8,10},{10,8},{12,14},{14,12},{1,3},{3,1},... | collective-permute-start | bytes 221192 | tf_op jit(solution)/shard_map/ppermute | solution.py:519
  8.6 0.0 collective-permute-start.2
  8.6 3.9 %collective-permute-start.3 = (bf16[144,256]{1,0:T(8,128)(2,1)}, bf16[144,256]{1,0:T(8,128)(2,1)S(1)}, u32[]{:S(2)}, u32[]{:S(2)}) collective-permute-start(bf16[144,256]{1,0:T(8,128)(2,1)} %get-tuple-element.55), channel_id=1, source_target_pairs={{0,12},{2,14},{4,8},{6,10},{8,4},{10,6},{12,0},{14,2},{1,13},{3,15... | collective-permute-start | bytes 221192 | tf_op jit(solution)/shard_map/ppermute | solution.py:519
  12.5 1.1 %collective-permute-start.4 = (bf16[144,256]{1,0:T(8,128)(2,1)}, bf16[144,256]{1,0:T(8,128)(2,1)S(1)}, u32[]{:S(2)}, u32[]{:S(2)}) collective-permute-start(bf16[144,256]{1,0:T(8,128)(2,1)} %get-tuple-element.56), channel_id=1, source_target_pairs={{0,14},{2,12},{4,10},{6,8},{8,6},{10,4},{12,2},{14,0},{1,15},{3,13... | collective-permute-start | bytes 221192 | tf_op jit(solution)/shard_map/ppermute | solution.py:519
  13.6 0.0 collective-permute-done.refs_1_
  13.6 1.7 %collective-permute-start.5 = (bf16[144,256]{1,0:T(8,128)(2,1)}, bf16[144,256]{1,0:T(8,128)(2,1)S(1)}, u32[]{:S(2)}, u32[]{:S(2)}) collective-permute-start(bf16[144,256]{1,0:T(8,128)(2,1)} %get-tuple-element.57), channel_id=1, source_target_pairs={{0,4},{2,6},{4,0},{6,2},{8,12},{10,14},{12,8},{14,10},{1,5},{3,7},... | collective-permute-start | bytes 221192 | tf_op jit(solution)/shard_map/ppermute | solution.py:519
  15.3 0.0 collective-permute-done.1.refs_2_
  15.3 0.9 %collective-permute-start.6 = (bf16[144,256]{1,0:T(8,128)(2,1)}, bf16[144,256]{1,0:T(8,128)(2,1)S(1)}, u32[]{:S(2)}, u32[]{:S(2)}) collective-permute-start(bf16[144,256]{1,0:T(8,128)(2,1)} %get-tuple-element.58), channel_id=1, source_target_pairs={{0,6},{2,4},{4,2},{6,0},{8,14},{10,12},{12,10},{14,8},{1,7},{3,5},... | collective-permute-start | bytes 221192 | tf_op jit(solution)/shard_map/ppermute | solution.py:519
  16.2 0.0 copy-start
  16.3 0.9 %copy-done = bf16[144,256]{1,0:T(8,128)(2,1)S(1)} copy-done((bf16[144,256]{1,0:T(8,128)(2,1)S(1)}, bf16[144,256]{1,0:T(8,128)(2,1)}, u32[]{:S(2)}) %copy-start) | copy-done | bytes 73752
  17.1 1.7 %hold.1 = (bf16[144,256]{1,0:T(8,128)(2,1)S(1)}, bf16[1024,384]{1,0:T(8,128)(2,1)S(1)}, bf16[1024,384]{1,0:T(8,128)(2,1)S(1)}, bf16[1024,384]{1,0:T(8,128)(2,1)S(1)}) custom-call(bf16[144,256]{1,0:T(8,128)(2,1)S(1)} %copy-done, bf16[1024,384]{1,0:T(8,128)(2,1)} %bitcast.12, bf16[1024,384]{1,0:T(8,128)(2,1)} %bitcast.13, bf16[1024,384]{1,0:T(8,128)(2,1)} %bitcast.14), custom_call_target="tpu_custom_call" | custom-call | bytes 4718592 | tf_op jit(solution)/shard_map/hold/pallas_call | solution.py:504
  18.8 0.9 %collective-permute-done.2.refs_3_ = bf16[144,256]{1,0:T(8,128)(2,1)S(1)} collective-permute-done((bf16[144,256]{1,0:T(8,128)(2,1)}, bf16[144,256]{1,0:T(8,128)(2,1)S(1)}, u32[]{:S(2)}, u32[]{:S(2)}) %collective-permute-start.2) | collective-permute-done | bytes 73760 | tf_op jit(solution)/shard_map/ppermute | solution.py:519
  19.8 0.0 collective-permute-done.3.refs_4_
  19.8 0.3 collective-permute-done.4.refs_5_
  20.1 0.3 collective-permute-done.5.refs_6_
  20.4 1.1 %collective-permute-done.6.refs_7_ = bf16[144,256]{1,0:T(8,128)(2,1)S(1)} collective-permute-done((bf16[144,256]{1,0:T(8,128)(2,1)}, bf16[144,256]{1,0:T(8,128)(2,1)S(1)}, u32[]{:S(2)}, u32[]{:S(2)}) %collective-permute-start.6) | collective-permute-done | bytes 73760 | tf_op jit(solution)/shard_map/ppermute | solution.py:519
  21.5 1.6 %expert_rows.1 = (bf16[80,256]{1,0:T(8,128)(2,1)S(1)}, bf16[80,256]{1,0:T(8,128)(2,1)S(1)}, bf16[80,256]{1,0:T(8,128)(2,1)S(1)}, bf16[80,256]{1,0:T(8,128)(2,1)S...) custom-call(bf16[144,256]{1,0:T(8,128)(2,1)S(1)} %get-tuple-element., ...), custom_call_target="tpu_custom_call" | custom-call | flops 566231040 | bytes 2359296 | tf_op jit(solution)/shard_map/expert_rows/pallas_call | solution.py:504
  23.1 0.6 %other_half.1 = bf16[1536,384]{1,0:T(8,128)(2,1)S(1)} custom-call(bf16[144,1024]{1,0:T(8,128)(2,1)S(1)} %get-tuple-element.70.x_ref, bf16[144,1024]{1,0:T(8,128)(2,1)S(1)} %get-tuple-element.71.s_ref, bf16[144,384]{1,0:T(8,128)(2,1)S(1)} %get-tuple-element.72.dg_ref, bf16[144,384]{1,0:T(8,128)(2,1)S(1)} %get-tuple-element.73.du_ref, ...), custom_call_target="tpu_custom_call" | custom-call | flops 1 | bytes 1 | tf_op jit(solution)/shard_map/other_half/pallas_call | solution.py:504
  23.7 0.0 copy-start.1
  23.7 0.0 copy-start.2
  23.8 0.0 copy-start.3
  23.8 0.1 collective-permute-start.14
  23.8 3.5 %collective-permute-start.7 = (bf16[80,256]{1,0:T(8,128)(2,1)S(1)}, bf16[80,256]{1,0:T(8,128)(2,1)S(1)}, u32[]{:S(2)}, u32[]{:S(2)}) collective-permute-start(bf16[80,256]{1,0:T(8,128)(2,1)S(1)} %get-tuple-element.63), channel_id=1, source_target_pairs={{0,8},{2,10},{4,12},{6,14},{8,0},{10,2},{12,4},{14,6},{1,9},{3,11}... | collective-permute-start | bytes 122888 | tf_op jit(solution)/shard_map/ppermute | solution.py:519
  27.4 0.9 %collective-permute-start.8 = (bf16[80,256]{1,0:T(8,128)(2,1)S(1)}, bf16[80,256]{1,0:T(8,128)(2,1)S(1)}, u32[]{:S(2)}, u32[]{:S(2)}) collective-permute-start(bf16[80,256]{1,0:T(8,128)(2,1)S(1)} %get-tuple-element.64), channel_id=1, source_target_pairs={{0,2},{2,0},{4,6},{6,4},{8,10},{10,8},{12,14},{14,12},{1,3},{3,1},... | collective-permute-start | bytes 122888 | tf_op jit(solution)/shard_map/ppermute | solution.py:519
  28.2 0.7 %collective-permute-start.9 = (bf16[80,256]{1,0:T(8,128)(2,1)S(1)}, bf16[80,256]{1,0:T(8,128)(2,1)S(1)}, u32[]{:S(2)}, u32[]{:S(2)}) collective-permute-start(bf16[80,256]{1,0:T(8,128)(2,1)S(1)} %get-tuple-element.65), channel_id=1, source_target_pairs={{0,10},{2,8},{4,14},{6,12},{8,2},{10,0},{12,6},{14,4},{1,11},{3,9}... | collective-permute-start | bytes 122888 | tf_op jit(solution)/shard_map/ppermute | solution.py:519
  28.9 3.0 %collective-permute-start.10 = (bf16[80,256]{1,0:T(8,128)(2,1)S(1)}, bf16[80,256]{1,0:T(8,128)(2,1)S(1)}, u32[]{:S(2)}, u32[]{:S(2)}) collective-permute-start(bf16[80,256]{1,0:T(8,128)(2,1)S(1)} %get-tuple-element.66), channel_id=1, source_target_pairs={{0,12},{2,14},{4,8},{6,10},{8,4},{10,6},{12,0},{14,2},{1,13},{3,15... | collective-permute-start | bytes 122888 | tf_op jit(solution)/shard_map/ppermute | solution.py:519
  31.9 0.0 collective-permute-done.7.refs_1_
  31.9 1.2 %collective-permute-start.11 = (bf16[80,256]{1,0:T(8,128)(2,1)S(1)}, bf16[80,256]{1,0:T(8,128)(2,1)S(1)}, u32[]{:S(2)}, u32[]{:S(2)}) collective-permute-start(bf16[80,256]{1,0:T(8,128)(2,1)S(1)} %get-tuple-element.67), channel_id=1, source_target_pairs={{0,14},{2,12},{4,10},{6,8},{8,6},{10,4},{12,2},{14,0},{1,15},{3,13... | collective-permute-start | bytes 122888 | tf_op jit(solution)/shard_map/ppermute | solution.py:519
  33.1 0.0 collective-permute-done.8.refs_2_
  33.1 0.1 collective-permute-start.12
  33.2 0.0 collective-permute-done.14.came_ref
  33.2 3.6 %collective-permute-start.13 = (bf16[80,256]{1,0:T(8,128)(2,1)S(1)}, bf16[80,256]{1,0:T(8,128)(2,1)S(1)}, u32[]{:S(2)}, u32[]{:S(2)}) collective-permute-start(bf16[80,256]{1,0:T(8,128)(2,1)S(1)} %get-tuple-element.69), channel_id=1, source_target_pairs={{0,6},{2,4},{4,2},{6,0},{8,14},{10,12},{12,10},{14,8},{1,7},{3,5},... | collective-permute-start | bytes 122888 | tf_op jit(solution)/shard_map/ppermute | solution.py:519
  36.8 1.4 %own_half.1 = (bf16[512,384]{1,0:T(8,128)(2,1)}, bf16[512,384]{1,0:T(8,128)(2,1)}, bf16[512,384]{1,0:T(8,128)(2,1)}) custom-call(bf16[144,1024]{1,0:T(8,128)(2,1)S(1)} %get-tuple-element.70.x_ref, bf16[144,1024]{1,0:T(8,128)(2,1)S(1)} %get-tuple-element.71.s_ref, bf16[144,384]{1,0:T(8,128)(2,1)S(1)} %get-tuple-element.72.dg_ref, ...), custom_call_target="tpu_custom_call" | custom-call | flops 1 | bytes 1 | tf_op jit(solution)/shard_map/own_half/pallas_call | solution.py:504
  38.2 0.0 collective-permute-done.9.refs_3_
  38.2 0.0 collective-permute-done.10.refs_4_
  38.2 0.7 %collective-permute-done.11.refs_5_ = bf16[80,256]{1,0:T(8,128)(2,1)S(1)} collective-permute-done((bf16[80,256]{1,0:T(8,128)(2,1)S(1)}, bf16[80,256]{1,0:T(8,128)(2,1)S(1)}, u32[]{:S(2)}, u32[]{:S(2)}) %collective-permute-start.11) | collective-permute-done | bytes 40992 | tf_op jit(solution)/shard_map/ppermute | solution.py:519
  38.9 0.0 collective-permute-done.12.refs_6_
  38.9 0.6 %collective-permute-done.13.refs_7_ = bf16[80,256]{1,0:T(8,128)(2,1)S(1)} collective-permute-done((bf16[80,256]{1,0:T(8,128)(2,1)S(1)}, bf16[80,256]{1,0:T(8,128)(2,1)S(1)}, u32[]{:S(2)}, u32[]{:S(2)}) %collective-permute-start.13) | collective-permute-done | bytes 40992 | tf_op jit(solution)/shard_map/ppermute | solution.py:519
  39.6 0.0 copy-done.1
  39.6 0.0 copy-done.2
  39.6 0.0 copy-done.3
  39.6 1.1 %combine.1 = (bf16[128,1024]{1,0:T(8,128)(2,1)}, bf16[8,128]{1,0:T(8,128)(2,1)}) custom-call(s32[8,128]{1,0:T(8,128)S(1)} %bitcast.11, s32[8,128]{1,0:T(8,128)S(1)} %copy-done.2, f32[8,128]{1,0:T(8,128)S(1)} %copy-done.3, bf16[80,256]{1,0:T(8,128)(2,1)S(1)} %get-tuple-element.78.refs_0_, bf16[80,256]{1,0:T(8,128)(2,1)S(1)} %collective-permute-done.7.refs_1_, ...), custom_call_target="tpu_custom_call" | custom-call | flops 37748736 | bytes 524288 | tf_op jit(solution)/shard_map/combine/pallas_call | solution.py:504
Async XLA Ops:
  3.0 10.7 %collective-permute-start = (bf16[144,256]{1,0:T(8,128)(2,1)}, bf16[144,256]{1,0:T(8,128)(2,1)S(1)}, u32[]{:S(2)}, u32[]{:S(2)}) collective-permute-start(bf16[144,256]{1,0:T(8,128)(2,1)} %get-tuple-element.52), channel_id=1, source_target_pairs={{0,8},{2,10},{4,12},{6,14},{8,0},{10,2},{12,4},{14,6},{1,9},{3,11}... | collective-permute-start | bytes 221192 | tf_op jit(solution)/shard_map/ppermute | solution.py:519
  7.1 8.2 %collective-permute-start.1 = (bf16[144,256]{1,0:T(8,128)(2,1)}, bf16[144,256]{1,0:T(8,128)(2,1)S(1)}, u32[]{:S(2)}, u32[]{:S(2)}) collective-permute-start(bf16[144,256]{1,0:T(8,128)(2,1)} %get-tuple-element.53), channel_id=1, source_target_pairs={{0,2},{2,0},{4,6},{6,4},{8,10},{10,8},{12,14},{14,12},{1,3},{3,1},... | collective-permute-start | bytes 221192 | tf_op jit(solution)/shard_map/ppermute | solution.py:519
  8.6 11.2 %collective-permute-start.2 = (bf16[144,256]{1,0:T(8,128)(2,1)}, bf16[144,256]{1,0:T(8,128)(2,1)S(1)}, u32[]{:S(2)}, u32[]{:S(2)}) collective-permute-start(bf16[144,256]{1,0:T(8,128)(2,1)} %get-tuple-element.54), channel_id=1, source_target_pairs={{0,10},{2,8},{4,14},{6,12},{8,2},{10,0},{12,6},{14,4},{1,11},{3,9}... | collective-permute-start | bytes 221192 | tf_op jit(solution)/shard_map/ppermute | solution.py:519
  8.6 11.2 %collective-permute-start.3 = (bf16[144,256]{1,0:T(8,128)(2,1)}, bf16[144,256]{1,0:T(8,128)(2,1)S(1)}, u32[]{:S(2)}, u32[]{:S(2)}) collective-permute-start(bf16[144,256]{1,0:T(8,128)(2,1)} %get-tuple-element.55), channel_id=1, source_target_pairs={{0,12},{2,14},{4,8},{6,10},{8,4},{10,6},{12,0},{14,2},{1,13},{3,15... | collective-permute-start | bytes 221192 | tf_op jit(solution)/shard_map/ppermute | solution.py:519
  12.5 7.6 %collective-permute-start.4 = (bf16[144,256]{1,0:T(8,128)(2,1)}, bf16[144,256]{1,0:T(8,128)(2,1)S(1)}, u32[]{:S(2)}, u32[]{:S(2)}) collective-permute-start(bf16[144,256]{1,0:T(8,128)(2,1)} %get-tuple-element.56), channel_id=1, source_target_pairs={{0,14},{2,12},{4,10},{6,8},{8,6},{10,4},{12,2},{14,0},{1,15},{3,13... | collective-permute-start | bytes 221192 | tf_op jit(solution)/shard_map/ppermute | solution.py:519
  13.6 6.8 %collective-permute-start.5 = (bf16[144,256]{1,0:T(8,128)(2,1)}, bf16[144,256]{1,0:T(8,128)(2,1)S(1)}, u32[]{:S(2)}, u32[]{:S(2)}) collective-permute-start(bf16[144,256]{1,0:T(8,128)(2,1)} %get-tuple-element.57), channel_id=1, source_target_pairs={{0,4},{2,6},{4,0},{6,2},{8,12},{10,14},{12,8},{14,10},{1,5},{3,7},... | collective-permute-start | bytes 221192 | tf_op jit(solution)/shard_map/ppermute | solution.py:519
  15.3 6.2 %collective-permute-start.6 = (bf16[144,256]{1,0:T(8,128)(2,1)}, bf16[144,256]{1,0:T(8,128)(2,1)S(1)}, u32[]{:S(2)}, u32[]{:S(2)}) collective-permute-start(bf16[144,256]{1,0:T(8,128)(2,1)} %get-tuple-element.58), channel_id=1, source_target_pairs={{0,6},{2,4},{4,2},{6,0},{8,14},{10,12},{12,10},{14,8},{1,7},{3,5},... | collective-permute-start | bytes 221192 | tf_op jit(solution)/shard_map/ppermute | solution.py:519
  16.2 0.9 %copy-start = (bf16[144,256]{1,0:T(8,128)(2,1)S(1)}, bf16[144,256]{1,0:T(8,128)(2,1)}, u32[]{:S(2)}) copy-start(bf16[144,256]{1,0:T(8,128)(2,1)} %get-tuple-element.50.refs_0_) | copy-start | bytes 221188
  23.7 15.8 %copy-start.1 = (s32[128,8]{0,1:T(8,128)S(1)}, s32[128,8]{0,1:T(8,128)}, u32[]{:S(2)}) copy-start(s32[128,8]{0,1:T(8,128)} %param.11) | copy-start | bytes 12292
  23.7 15.8 %copy-start.2 = (s32[8,128]{1,0:T(8,128)S(1)}, s32[8,128]{1,0:T(8,128)}, u32[]{:S(2)}) copy-start(s32[8,128]{1,0:T(8,128)} %get-tuple-element.48.slot_ref) | copy-start | bytes 12292
  23.8 15.8 %copy-start.3 = (f32[8,128]{1,0:T(8,128)S(1)}, f32[8,128]{1,0:T(8,128)}, u32[]{:S(2)}) copy-start(f32[8,128]{1,0:T(8,128)} %get-tuple-element.49.gates_ref) | copy-start | bytes 12292
  23.8 9.4 %collective-permute-start.14 = (bf16[1536,384]{1,0:T(8,128)(2,1)S(1)}, bf16[1536,384]{1,0:T(8,128)(2,1)S(1)}, u32[]{:S(2)}, u32[]{:S(2)}) collective-permute-start(bf16[1536,384]{1,0:T(8,128)(2,1)S(1)} %other_half.1), channel_id=1, source_target_pairs={{0,1},{1,0},{2,3},{3,2},{4,5},{5,4},{6,7},{7,6},{8,9},{9,8},{10,11... | collective-permute-start | bytes 3538952 | tf_op jit(solution)/shard_map/ppermute | solution.py:612
  23.8 8.1 %collective-permute-start.7 = (bf16[80,256]{1,0:T(8,128)(2,1)S(1)}, bf16[80,256]{1,0:T(8,128)(2,1)S(1)}, u32[]{:S(2)}, u32[]{:S(2)}) collective-permute-start(bf16[80,256]{1,0:T(8,128)(2,1)S(1)} %get-tuple-element.63), channel_id=1, source_target_pairs={{0,8},{2,10},{4,12},{6,14},{8,0},{10,2},{12,4},{14,6},{1,9},{3,11}... | collective-permute-start | bytes 122888 | tf_op jit(solution)/shard_map/ppermute | solution.py:519
  27.4 5.7 %collective-permute-start.8 = (bf16[80,256]{1,0:T(8,128)(2,1)S(1)}, bf16[80,256]{1,0:T(8,128)(2,1)S(1)}, u32[]{:S(2)}, u32[]{:S(2)}) collective-permute-start(bf16[80,256]{1,0:T(8,128)(2,1)S(1)} %get-tuple-element.64), channel_id=1, source_target_pairs={{0,2},{2,0},{4,6},{6,4},{8,10},{10,8},{12,14},{14,12},{1,3},{3,1},... | collective-permute-start | bytes 122888 | tf_op jit(solution)/shard_map/ppermute | solution.py:519
  28.2 9.9 %collective-permute-start.9 = (bf16[80,256]{1,0:T(8,128)(2,1)S(1)}, bf16[80,256]{1,0:T(8,128)(2,1)S(1)}, u32[]{:S(2)}, u32[]{:S(2)}) collective-permute-start(bf16[80,256]{1,0:T(8,128)(2,1)S(1)} %get-tuple-element.65), channel_id=1, source_target_pairs={{0,10},{2,8},{4,14},{6,12},{8,2},{10,0},{12,6},{14,4},{1,11},{3,9}... | collective-permute-start | bytes 122888 | tf_op jit(solution)/shard_map/ppermute | solution.py:519
  28.9 9.3 %collective-permute-start.10 = (bf16[80,256]{1,0:T(8,128)(2,1)S(1)}, bf16[80,256]{1,0:T(8,128)(2,1)S(1)}, u32[]{:S(2)}, u32[]{:S(2)}) collective-permute-start(bf16[80,256]{1,0:T(8,128)(2,1)S(1)} %get-tuple-element.66), channel_id=1, source_target_pairs={{0,12},{2,14},{4,8},{6,10},{8,4},{10,6},{12,0},{14,2},{1,13},{3,15... | collective-permute-start | bytes 122888 | tf_op jit(solution)/shard_map/ppermute | solution.py:519
  31.9 7.0 %collective-permute-start.11 = (bf16[80,256]{1,0:T(8,128)(2,1)S(1)}, bf16[80,256]{1,0:T(8,128)(2,1)S(1)}, u32[]{:S(2)}, u32[]{:S(2)}) collective-permute-start(bf16[80,256]{1,0:T(8,128)(2,1)S(1)} %get-tuple-element.67), channel_id=1, source_target_pairs={{0,14},{2,12},{4,10},{6,8},{8,6},{10,4},{12,2},{14,0},{1,15},{3,13... | collective-permute-start | bytes 122888 | tf_op jit(solution)/shard_map/ppermute | solution.py:519
  33.1 5.9 %collective-permute-start.12 = (bf16[80,256]{1,0:T(8,128)(2,1)S(1)}, bf16[80,256]{1,0:T(8,128)(2,1)S(1)}, u32[]{:S(2)}, u32[]{:S(2)}) collective-permute-start(bf16[80,256]{1,0:T(8,128)(2,1)S(1)} %get-tuple-element.68), channel_id=1, source_target_pairs={{0,4},{2,6},{4,0},{6,2},{8,12},{10,14},{12,8},{14,10},{1,5},{3,7},... | collective-permute-start | bytes 122888 | tf_op jit(solution)/shard_map/ppermute | solution.py:519
  33.2 6.4 %collective-permute-start.13 = (bf16[80,256]{1,0:T(8,128)(2,1)S(1)}, bf16[80,256]{1,0:T(8,128)(2,1)S(1)}, u32[]{:S(2)}, u32[]{:S(2)}) collective-permute-start(bf16[80,256]{1,0:T(8,128)(2,1)S(1)} %get-tuple-element.69), channel_id=1, source_target_pairs={{0,6},{2,4},{4,2},{6,0},{8,14},{10,12},{12,10},{14,8},{1,7},{3,5},... | collective-permute-start | bytes 122888 | tf_op jit(solution)/shard_map/ppermute | solution.py:519

commit v8 on v4

--- a/solution.py
+++ b/solution.py
@@ -237,6 +237,8 @@
 MIB = 1024 * 1024
 
 BASES = (4, 6, 2)
+ORDER = (0, 2, 4, 3, 5, 1, 6, 7)
+LONG = 8 * 10**9
 MAIN = 16
 QUARTERS = 4
 SEND_ROWS = 2 * QUARTERS * MAIN + 16
@@ -279,12 +281,9 @@
     sems = refs[-1]
     plan_ref, ids_ref, pick_ref, gate_ref, tok_ref, cot_ref = refs[-7:-1]
     slot_ref, gates_ref = refs[-9:-7]
-    self_ref, near_ref, keep_ref, give_ref = refs[:-9]
+    send_refs = refs[:-9]
     topk, tokens = ids_ref.shape
-    experts = slot_ref.shape[0]
-    send_views = [(self_ref, 0), (near_ref, 0)] + [
-        (ref, d * SEND_ROWS) for d in range(len(BASES)) for ref in (keep_ref, give_ref)
-    ]
+    experts = len(send_refs)
     width = tok_ref.shape[1] // QUARTERS
     copies = copies_of(experts)
     loads = [
@@ -356,37 +355,24 @@
             preferred_element_type=F32,
         )
     tail = tail.astype(BF)
-    for c, (ref, first) in enumerate(send_views):
+    for c, ref in enumerate(send_refs):
         here = slice(c * MAIN, (c + 1) * MAIN)
         for q in range(QUARTERS):
             cols = slice(q * width, (q + 1) * width)
-            ref[first + q * MAIN : first + (q + 1) * MAIN, :] = rows[here, cols]
-            low = first + (QUARTERS + q) * MAIN
-            ref[low : low + MAIN, :] = scaled[here, cols]
-        low = first + 2 * QUARTERS * MAIN
-        ref[low : low + 16, :] = tail[here]
-
-
-def join_kernel(self_hbm, keep_ref, came_ref, self_ref, *double_refs):
-    self_ref[...] = self_hbm[...]
-    for d, ref in enumerate(double_refs):
-        rows = slice(d * SEND_ROWS, (d + 1) * SEND_ROWS)
-        ref[:SEND_ROWS, :] = keep_ref[rows, :]
-        ref[SEND_ROWS:, :] = came_ref[rows, :]
+            ref[q * MAIN : (q + 1) * MAIN, :] = rows[here, cols]
+            ref[(QUARTERS + q) * MAIN : (QUARTERS + q + 1) * MAIN, :] = scaled[here, cols]
+        ref[2 * QUARTERS * MAIN :, :] = tail[here]
 
 
 def expert_kernel(*refs):
-    count = 2 + len(BASES)
-    recv_views = chunk_views(refs[:count], SEND_ROWS)
-    gate_ref, up_ref, down_ref = refs[count : count + 3]
-    back_views = chunk_views(refs[count + 3 : 2 * count + 3], BACK_ROWS)
-    x_ref, s_ref, dg_ref, du_ref, hid_ref = refs[2 * count + 3 :]
-    experts = len(recv_views)
+    experts = len(ORDER)
+    recv_refs = [refs[ORDER.index(c)] for c in range(experts)]
+    gate_ref, up_ref, down_ref = refs[experts : experts + 3]
+    back_views = chunk_views(refs[experts + 3 : -5], BACK_ROWS)
+    x_ref, s_ref, dg_ref, du_ref, hid_ref = refs[-5:]
     width = refs[0].shape[1]
     main_rows = experts * MAIN
-    tail = jnp.concatenate(
-        [ref[first + SEND_ROWS - 16 : first + SEND_ROWS, :] for ref, first in recv_views], axis=0
-    )
+    tail = jnp.concatenate([ref[2 * QUARTERS * MAIN :, :] for ref in recv_refs], axis=0)
     row = iota((4 * experts, main_rows), 0)
     col = iota((4 * experts, main_rows), 1)
     kind = (row >= 2 * experts).astype(jnp.int32)
@@ -397,11 +383,10 @@
         picked = jnp.dot(mask(col == base + q), tail, preferred_element_type=F32).astype(BF)
         x_ref[main_rows:, cols] = picked[: 2 * experts]
         s_ref[main_rows:, cols] = picked[2 * experts :]
-        for i, (ref, first) in enumerate(recv_views):
+        for i, ref in enumerate(recv_refs):
             here = slice(i * MAIN, (i + 1) * MAIN)
-            x_ref[here, cols] = ref[first + q * MAIN : first + (q + 1) * MAIN, :]
-            low = first + (QUARTERS + q) * MAIN
-            s_ref[here, cols] = ref[low : low + MAIN, :]
+            x_ref[here, cols] = ref[q * MAIN : (q + 1) * MAIN, :]
+            s_ref[here, cols] = ref[(QUARTERS + q) * MAIN : (QUARTERS + q + 1) * MAIN, :]
     rows = x_ref[...]
     gate_pre = jnp.dot(rows, gate_ref[...], preferred_element_type=F32)
     up_pre = jnp.dot(rows, up_ref[...], preferred_element_type=F32)
@@ -552,12 +537,6 @@
     return lax.ppermute(chunk, "replica", [(0, 1), (1, 0)])
 
 
-def hold_kernel(*refs):
-    count = len(refs) // 2
-    for source, place in zip(refs[:count], refs[count:]):
-        place[...] = source[...]
-
-
 def per_device_moving_rows(
     tokens,
     cotangent,
@@ -577,17 +556,16 @@
     served = experts * (MAIN + 2)
     small = (topk, token_count)
     count = len(BASES)
-    self_rows, near_rows, keep, give, slot, gates = local_call(
+    *chunks, slot, gates = local_call(
         route_kernel,
-        [((SEND_ROWS, width), BF)] * 2
-        + [((count * SEND_ROWS, width), BF)] * 2
+        [((SEND_ROWS, width), BF)] * experts
         + [((experts, token_count), jnp.int32), ((experts, token_count), F32)],
         [replica_plan, expert_ids.T, replica_pick.T, gate_values.T, tokens, cotangent],
         "route",
-        2 * 2 * served * token_count * model_width,
+        LONG,
         2 * 2 * (token_count + served) * model_width,
         space=pltpu.HBM,
-        limit=58,
+        limit=54,
         scratch=[
             pltpu.SMEM((experts,), jnp.int32),
             pltpu.VMEM(small, jnp.int32),
@@ -598,26 +576,15 @@
             pltpu.SemaphoreType.DMA((6,)),
         ],
     )
-    came = to_twin(give)
-    near_rows = to_step(near_rows, 1)
-    self_rows, *doubles = local_call(
-        join_kernel,
-        [((SEND_ROWS, width), BF)] + [((2 * SEND_ROWS, width), BF)] * count,
-        [self_rows, keep, came],
-        "join",
-        0,
-        2 * 2 * 7 * SEND_ROWS * width,
-    )
-    recv = [self_rows, near_rows, *map(to_step, doubles, BASES)]
-    matrices = [gate_proj[0], up_proj[0], down_proj[0]]
-    matrices = local_call(
-        hold_kernel,
-        [(array.shape, BF) for array in matrices],
-        matrices,
-        "hold",
-        0,
-        4 * 3 * model_width * hidden_width,
-    )
+    recv = list(chunks)
+    far = [to_twin(chunks[3]), to_twin(chunks[5])]
+    far, near = lax.optimization_barrier((far, [chunks[1], chunks[6]]))
+    for d, twin in enumerate([*far, to_twin(chunks[7])]):
+        recv[3 + 2 * d] = to_step(twin, BASES[d])
+    recv[2] = to_step(chunks[2], 4)
+    recv[4] = to_step(chunks[4], 6)
+    recv[6] = to_step(near[1], 2)
+    recv[1] = to_step(near[0], 1)
     matmul = 2 * served * model_width * hidden_width
     outs = local_call(
         expert_kernel,
@@ -625,14 +592,14 @@
         + [((2 * BACK_ROWS, width), BF)] * count
         + [((served, model_width), BF)] * 2
         + [((served, hidden_width), BF)] * 3,
-        [*recv, *matrices],
+        [*(recv[c] for c in ORDER), gate_proj[0], up_proj[0], down_proj[0]],
         "expert_rows",
         5 * matmul,
         2 * 3 * model_width * hidden_width,
     )
     backs, factors = outs[: 2 + count], outs[2 + count :]
     kept = list(map(to_step, backs[2:], BASES))
-    returned = [backs[0], to_step(backs[1], 1), *kept, *map(to_twin, kept)]
+    near = to_step(backs[1], 1)
     half = model_width // 2
     (leaving,) = local_call(
         other_half_kernel,
@@ -650,7 +617,9 @@
         1,
         1,
     )
-    returned, shares = lax.optimization_barrier((returned, shares))
+    kept[0], near = lax.optimization_barrier((kept[0], near))
+    kept[1], shares = lax.optimization_barrier((kept[1], shares))
+    returned = [backs[0], near, *kept, *map(to_twin, kept)]
     token_grad, gate_grad = local_call(
         combine_kernel,
         [((token_count, model_width), BF), ((topk, token_count), BF)],

time: 44.2 us -> 44 us (level)
  starting transfers between devices: 14.2 us -> 22.3 us
  waiting for transfers between devices: 17.5 us -> 12.7 us
  local copies, waits for them, and re-layouts: 4.1 us -> 0.91 us
    ppermute x6 -> x9, starting transfers between devices: 10.3 us -> 18.6 us  [to_step(): return lax.ppermute(chunk, ('expert', 'replica'), pairs)]
    ppermute x6 -> x9, waiting for transfers between devices: 12.2 us -> 7.88 us  [to_step(): return lax.ppermute(chunk, ('expert', 'replica'), pairs)]
    unnamed x16 -> x14, local copies, waits for them, and re-layouts: 4.1 us -> 0.91 us
    ppermute x2, starting transfers between devices: 2.64 us -> 2.18 us  [to_step(): return lax.ppermute(chunk, 'expert', [(i, i ^ 1) for i in range(experts)])]
    ppermute x5 -> x7, waiting for transfers between devices: 1.32 us -> 0.93 us  [to_twin(): return lax.ppermute(chunk, 'replica', [(0, 1), (1, 0)])]
    ppermute x5 -> x7, starting transfers between devices: 1.23 us -> 1.6 us  [to_twin(): return lax.ppermute(chunk, 'replica', [(0, 1), (1, 0)])]
    pallas_call x7 -> x5, Pallas kernels: 7.31 us -> 7.15 us  [local_call(): pl.pallas_call(kernel, out_shape=[jax.ShapeDtypeStruct(shape, kind) for s...]
  transfers between devices with their start and end apart: 13 -> 18, of which waited for: 8 -> 7; matrix products, arithmetic and copies ran while one was open for 0% -> 0% of each run, Pallas kernels for 4% -> 3%
where the time goes in v8:
time: 44 us; the launch traced here: 43.9 us
  starting transfers between devices  22.3 us (51%)
  waiting for transfers between devices  12.7 us (29%)
  Pallas kernels  7.15 us (16%)
  local copies, waits for them, and re-layouts  0.91 us (2%)
  between operations  0.74 us (2%)
    ppermute x9, starting transfers between devices, to_step(): return lax.ppermute(chunk, ('expert', 'replica'), pairs)  18.6 us
    ppermute x9, waiting for transfers between devices, to_step(): return lax.ppermute(chunk, ('expert', 'replica'), pairs)  7.88 us
    pallas_call x5, Pallas kernels, local_call(): pl.pallas_call(kernel, out_shape=[jax.ShapeDtypeStruct(shape, kind) for s...  7.15 us
    ppermute x2, waiting for transfers between devices, to_step(): return lax.ppermute(chunk, 'expert', [(i, i ^ 1) for i in range(experts)])  3.92 us
    ppermute x2, starting transfers between devices, to_step(): return lax.ppermute(chunk, 'expert', [(i, i ^ 1) for i in range(experts)])  2.18 us
    ppermute x7, starting transfers between devices, to_twin(): return lax.ppermute(chunk, 'replica', [(0, 1), (1, 0)])  1.6 us
    ppermute x7, waiting for transfers between devices, to_twin(): return lax.ppermute(chunk, 'replica', [(0, 1), (1, 0)])  0.93 us
    unnamed x14, local copies, waits for them, and re-layouts  0.91 us
  transfers between devices with their start and end apart: 18, of which 7 were waited for; matrix products, arithmetic and copies ran while one was open for 0% of the time, Pallas kernels for 3%

profile of v8, /device:TPU:0, one launch (start us, length us, event | category | flops | bytes accessed | tf_op | source)
XLA Modules:
  0.0 43.9 jit_solution(5173703418995079529)
XLA Ops:
  0.7 2.5 %route.1 = (bf16[144,256]{1,0:T(8,128)(2,1)}, bf16[144,256]{1,0:T(8,128)(2,1)}, bf16[144,256]{1,0:T(8,128)(2,1)}, bf16[144,256]{1,0:T(8,128)(2,1)}, bf16[144,256...) custom-call(s32[8]{0:T(128)} %plan_hbm.1, ...), custom_call_target="tpu_custom_call" | custom-call | flops 8000000000 | bytes 1114112 | tf_op jit(solution)/shard_map/route/pallas_call | solution.py:516
  3.2 0.5 %collective-permute-start.2 = (bf16[144,256]{1,0:T(8,128)(2,1)}, bf16[144,256]{1,0:T(8,128)(2,1)S(1)}, u32[]{:S(2)}, u32[]{:S(2)}) collective-permute-start(bf16[144,256]{1,0:T(8,128)(2,1)} %get-tuple-element.45), channel_id=1, source_target_pairs={{0,1},{1,0},{2,3},{3,2},{4,5},{5,4},{6,7},{7,6},{8,9},{9,8},{10,11... | collective-permute-start | bytes 221192 | tf_op jit(solution)/shard_map/ppermute | solution.py:537
  3.7 0.1 collective-permute-start.3
  3.7 4.0 %collective-permute-start = (bf16[144,256]{1,0:T(8,128)(2,1)}, bf16[144,256]{1,0:T(8,128)(2,1)S(1)}, u32[]{:S(2)}, u32[]{:S(2)}) collective-permute-start(bf16[144,256]{1,0:T(8,128)(2,1)} %get-tuple-element.43), channel_id=1, source_target_pairs={{0,8},{1,11},{2,10},{3,9},{4,12},{5,15},{6,14},{7,13},{8,0},{9,3},... | collective-permute-start | bytes 221192 | tf_op jit(solution)/shard_map/ppermute | solution.py:533
  7.8 1.3 %collective-permute-start.1 = (bf16[144,256]{1,0:T(8,128)(2,1)}, bf16[144,256]{1,0:T(8,128)(2,1)S(1)}, u32[]{:S(2)}, u32[]{:S(2)}) collective-permute-start(bf16[144,256]{1,0:T(8,128)(2,1)} %get-tuple-element.44), channel_id=1, source_target_pairs={{0,12},{1,15},{2,14},{3,13},{4,8},{5,11},{6,10},{7,9},{8,4},{9,7},... | collective-permute-start | bytes 221192 | tf_op jit(solution)/shard_map/ppermute | solution.py:533
  9.1 0.4 collective-permute-start.8
  9.5 0.0 collective-permute-done.2
  9.5 0.0 collective-permute-done.3
  9.5 1.7 %collective-permute-start.4 = (bf16[144,256]{1,0:T(8,128)(2,1)S(1)}, bf16[144,256]{1,0:T(8,128)(2,1)S(1)}, u32[]{:S(2)}, u32[]{:S(2)}) collective-permute-start(bf16[144,256]{1,0:T(8,128)(2,1)S(1)} %collective-permute-done.2), channel_id=1, source_target_pairs={{0,8},{1,11},{2,10},{3,9},{4,12},{5,15},{6,14},{7,13},{8,0},{9,3},... | collective-permute-start | bytes 221192 | tf_op jit(solution)/shard_map/ppermute | solution.py:533
  11.2 1.2 %collective-permute-start.5 = (bf16[144,256]{1,0:T(8,128)(2,1)S(1)}, bf16[144,256]{1,0:T(8,128)(2,1)S(1)}, u32[]{:S(2)}, u32[]{:S(2)}) collective-permute-start(bf16[144,256]{1,0:T(8,128)(2,1)S(1)} %collective-permute-done.3), channel_id=1, source_target_pairs={{0,12},{1,15},{2,14},{3,13},{4,8},{5,11},{6,10},{7,9},{8,4},{9,7},... | collective-permute-start | bytes 221192 | tf_op jit(solution)/shard_map/ppermute | solution.py:533
  12.4 0.0 collective-permute-done.refs_1_
  12.4 1.3 %collective-permute-start.6 = (bf16[144,256]{1,0:T(8,128)(2,1)}, bf16[144,256]{1,0:T(8,128)(2,1)S(1)}, u32[]{:S(2)}, u32[]{:S(2)}) collective-permute-start(bf16[144,256]{1,0:T(8,128)(2,1)} %get-tuple-element.51), channel_id=1, source_target_pairs={{0,2},{2,0},{4,6},{6,4},{8,10},{10,8},{12,14},{14,12},{1,3},{3,1},... | collective-permute-start | bytes 221192 | tf_op jit(solution)/shard_map/ppermute | solution.py:531
  13.7 1.3 %collective-permute-done.1.refs_2_ = bf16[144,256]{1,0:T(8,128)(2,1)S(1)} collective-permute-done((bf16[144,256]{1,0:T(8,128)(2,1)}, bf16[144,256]{1,0:T(8,128)(2,1)S(1)}, u32[]{:S(2)}, u32[]{:S(2)}) %collective-permute-start.1) | collective-permute-done | bytes 73760 | tf_op jit(solution)/shard_map/ppermute | solution.py:533
  15.0 5.1 %collective-permute-start.7 = (bf16[144,256]{1,0:T(8,128)(2,1)}, bf16[144,256]{1,0:T(8,128)(2,1)S(1)}, u32[]{:S(2)}, u32[]{:S(2)}) collective-permute-start(bf16[144,256]{1,0:T(8,128)(2,1)} %get-tuple-element.52), channel_id=1, source_target_pairs={{0,4},{1,7},{2,6},{3,5},{4,0},{5,3},{6,2},{7,1},{8,12},{9,15},{10,... | collective-permute-start | bytes 221192 | tf_op jit(solution)/shard_map/ppermute | solution.py:533
  20.1 0.0 collective-permute-done.8
  20.1 0.0 collective-permute-start.9
  20.1 0.4 collective-permute-done.4.refs_3_
  20.5 0.0 collective-permute-done.5.refs_4_
  20.5 0.0 collective-permute-done.6.refs_5_
  20.5 2.5 %collective-permute-done.7.refs_6_ = bf16[144,256]{1,0:T(8,128)(2,1)S(1)} collective-permute-done((bf16[144,256]{1,0:T(8,128)(2,1)}, bf16[144,256]{1,0:T(8,128)(2,1)S(1)}, u32[]{:S(2)}, u32[]{:S(2)}) %collective-permute-start.7) | collective-permute-done | bytes 73760 | tf_op jit(solution)/shard_map/ppermute | solution.py:533
  23.0 2.0 %collective-permute-done.9.refs_7_ = bf16[144,256]{1,0:T(8,128)(2,1)S(1)} collective-permute-done((bf16[144,256]{1,0:T(8,128)(2,1)S(1)}, bf16[144,256]{1,0:T(8,128)(2,1)S(1)}, u32[]{:S(2)}, u32[]{:S(2)}) %collective-permute-start.9) | collective-permute-done | bytes 73760 | tf_op jit(solution)/shard_map/ppermute | solution.py:533
  25.0 0.0 copy-done.1
  25.0 0.0 copy-start.3
  25.0 0.9 %copy-done.3 = bf16[144,256]{1,0:T(8,128)(2,1)S(1)} copy-done((bf16[144,256]{1,0:T(8,128)(2,1)S(1)}, bf16[144,256]{1,0:T(8,128)(2,1)}, u32[]{:S(2)}) %copy-start.3) | copy-done | bytes 73752
  25.9 1.6 %expert_rows.1 = (bf16[80,256]{1,0:T(8,128)(2,1)S(1)}, bf16[80,256]{1,0:T(8,128)(2,1)S(1)}, bf16[160,256]{1,0:T(8,128)(2,1)S(1)}, bf16[160,256]{1,0:T(8,128)(2,1...) custom-call(bf16[144,256]{1,0:T(8,128)(2,1)S(1)} %copy-done.3, ...), custom_call_target="tpu_custom_call" | custom-call | flops 566231040 | bytes 2359296 | tf_op jit(solution)/shard_map/expert_rows/pallas_call | solution.py:516
  27.5 0.6 %other_half.1 = bf16[1536,384]{1,0:T(8,128)(2,1)S(1)} custom-call(bf16[144,1024]{1,0:T(8,128)(2,1)S(1)} %get-tuple-element.60.x_ref, bf16[144,1024]{1,0:T(8,128)(2,1)S(1)} %get-tuple-element.61.s_ref, bf16[144,384]{1,0:T(8,128)(2,1)S(1)} %get-tuple-element.62.dg_ref, bf16[144,384]{1,0:T(8,128)(2,1)S(1)} %get-tuple-element.63.du_ref, ...), custom_call_target="tpu_custom_call" | custom-call | flops 1 | bytes 1 | tf_op jit(solution)/shard_map/other_half/pallas_call | solution.py:516
  28.2 0.0 copy-start.4
  28.2 0.0 copy-start.5
  28.2 0.0 copy-start.6
  28.2 0.1 collective-permute-start.13
  28.3 3.6 %collective-permute-start.10 = (bf16[160,256]{1,0:T(8,128)(2,1)S(1)}, bf16[160,256]{1,0:T(8,128)(2,1)S(1)}, u32[]{:S(2)}, u32[]{:S(2)}) collective-permute-start(bf16[160,256]{1,0:T(8,128)(2,1)S(1)} %get-tuple-element.55), channel_id=1, source_target_pairs={{0,8},{1,11},{2,10},{3,9},{4,12},{5,15},{6,14},{7,13},{8,0},{9,3},... | collective-permute-start | bytes 245768 | tf_op jit(solution)/shard_map/ppermute | solution.py:533
  31.9 0.6 %collective-permute-start.14 = (bf16[160,256]{1,0:T(8,128)(2,1)S(1)}, bf16[160,256]{1,0:T(8,128)(2,1)S(1)}, u32[]{:S(2)}, u32[]{:S(2)}) collective-permute-start(bf16[160,256]{1,0:T(8,128)(2,1)S(1)} %get-tuple-element.69), channel_id=1, source_target_pairs={{0,4},{1,7},{2,6},{3,5},{4,0},{5,3},{6,2},{7,1},{8,12},{9,15},{10,... | collective-permute-start | bytes 245768 | tf_op jit(solution)/shard_map/ppermute | solution.py:533
  32.5 1.0 %collective-permute-start.12 = (bf16[160,256]{1,0:T(8,128)(2,1)S(1)}, bf16[160,256]{1,0:T(8,128)(2,1)S(1)}, u32[]{:S(2)}, u32[]{:S(2)}) collective-permute-start(bf16[160,256]{1,0:T(8,128)(2,1)S(1)} %get-tuple-element.59), channel_id=1, source_target_pairs={{0,12},{1,15},{2,14},{3,13},{4,8},{5,11},{6,10},{7,9},{8,4},{9,7},... | collective-permute-start | bytes 245768 | tf_op jit(solution)/shard_map/ppermute | solution.py:533
  33.5 0.9 %collective-permute-start.11 = (bf16[80,256]{1,0:T(8,128)(2,1)S(1)}, bf16[80,256]{1,0:T(8,128)(2,1)S(1)}, u32[]{:S(2)}, u32[]{:S(2)}) collective-permute-start(bf16[80,256]{1,0:T(8,128)(2,1)S(1)} %get-tuple-element.56), channel_id=1, source_target_pairs={{0,2},{2,0},{4,6},{6,4},{8,10},{10,8},{12,14},{14,12},{1,3},{3,1},... | collective-permute-start | bytes 122888 | tf_op jit(solution)/shard_map/ppermute | solution.py:531
  34.4 3.9 %collective-permute-done.11.refs_1_ = bf16[80,256]{1,0:T(8,128)(2,1)S(1)} collective-permute-done((bf16[80,256]{1,0:T(8,128)(2,1)S(1)}, bf16[80,256]{1,0:T(8,128)(2,1)S(1)}, u32[]{:S(2)}, u32[]{:S(2)}) %collective-permute-start.11) | collective-permute-done | bytes 40992 | tf_op jit(solution)/shard_map/ppermute | solution.py:531
  38.3 0.0 collective-permute-done.10.refs_2_
  38.3 0.0 collective-permute-start.15
  38.3 1.7 %collective-permute-done.14.refs_4_ = bf16[160,256]{1,0:T(8,128)(2,1)S(1)} collective-permute-done((bf16[160,256]{1,0:T(8,128)(2,1)S(1)}, bf16[160,256]{1,0:T(8,128)(2,1)S(1)}, u32[]{:S(2)}, u32[]{:S(2)}) %collective-permute-start.14) | collective-permute-done | bytes 81952 | tf_op jit(solution)/shard_map/ppermute | solution.py:533
  40.0 0.0 collective-permute-start.17
  40.0 0.0 collective-permute-done.13.came_ref
  40.0 1.4 %own_half.1 = (bf16[512,384]{1,0:T(8,128)(2,1)}, bf16[512,384]{1,0:T(8,128)(2,1)}, bf16[512,384]{1,0:T(8,128)(2,1)}) custom-call(bf16[144,1024]{1,0:T(8,128)(2,1)S(1)} %get-tuple-element.60.x_ref, bf16[144,1024]{1,0:T(8,128)(2,1)S(1)} %get-tuple-element.61.s_ref, bf16[144,384]{1,0:T(8,128)(2,1)S(1)} %get-tuple-element.62.dg_ref, ...), custom_call_target="tpu_custom_call" | custom-call | flops 1 | bytes 1 | tf_op jit(solution)/shard_map/own_half/pallas_call | solution.py:516
  41.4 0.0 collective-permute-done.12.refs_3_
  41.4 0.5 %collective-permute-start.16 = (bf16[160,256]{1,0:T(8,128)(2,1)S(1)}, bf16[160,256]{1,0:T(8,128)(2,1)S(1)}, u32[]{:S(2)}, u32[]{:S(2)}) collective-permute-start(bf16[160,256]{1,0:T(8,128)(2,1)S(1)} %collective-permute-done.12.refs_3_), channel_id=1, source_target_pairs={{0,1},{1,0},{2,3},{3,2},{4,5},{5,4},{6,7},{7,6},{8,9},{9,8},{10,11... | collective-permute-start | bytes 245768 | tf_op jit(solution)/shard_map/ppermute | solution.py:537
  41.9 0.0 collective-permute-done.15.refs_5_
  41.9 0.0 collective-permute-done.17.refs_7_
  41.9 0.9 %collective-permute-done.16.refs_6_ = bf16[160,256]{1,0:T(8,128)(2,1)S(1)} collective-permute-done((bf16[160,256]{1,0:T(8,128)(2,1)S(1)}, bf16[160,256]{1,0:T(8,128)(2,1)S(1)}, u32[]{:S(2)}, u32[]{:S(2)}) %collective-permute-start.16) | collective-permute-done | bytes 81952 | tf_op jit(solution)/shard_map/ppermute | solution.py:537
  42.8 0.0 copy-done.4
  42.8 1.0 %combine.1 = (bf16[128,1024]{1,0:T(8,128)(2,1)}, bf16[8,128]{1,0:T(8,128)(2,1)}) custom-call(s32[8,128]{1,0:T(8,128)S(1)} %bitcast.14, s32[8,128]{1,0:T(8,128)S(1)} %copy-done.5, f32[8,128]{1,0:T(8,128)S(1)} %copy-done.6, bf16[80,256]{1,0:T(8,128)(2,1)S(1)} %get-tuple-element.54.refs_0_, bf16[80,256]{1,0:T(8,128)(2,1)S(1)} %collective-permute-done.11.refs_1_, ...), custom_call_target="tpu_custom_call" | custom-call | flops 37748736 | bytes 524288 | tf_op jit(solution)/shard_map/combine/pallas_call | solution.py:516
  (7 shorter events, 0.0 us)
Async XLA Ops:
  0.6 24.4 %copy-start = (bf16[1,1024,384]{2,1,0:T(8,128)(2,1)S(1)}, bf16[1,1024,384]{2,1,0:T(8,128)(2,1)}, u32[]{:S(2)}) copy-start(bf16[1,1024,384]{2,1,0:T(8,128)(2,1)} %param.15) | copy-start | bytes 2359300
  0.6 24.4 %copy-start.1 = (bf16[1,1024,384]{2,1,0:T(8,128)(2,1)S(1)}, bf16[1,1024,384]{2,1,0:T(8,128)(2,1)}, u32[]{:S(2)}) copy-start(bf16[1,1024,384]{2,1,0:T(8,128)(2,1)} %param.16) | copy-start | bytes 2359300
  0.7 24.4 %copy-start.2 = (bf16[1,1024,384]{2,1,0:T(8,128)(2,1)S(1)}, bf16[1,1024,384]{2,1,0:T(8,128)(2,1)}, u32[]{:S(2)}) copy-start(bf16[1,1024,384]{2,1,0:T(8,128)(2,1)} %param.17) | copy-start | bytes 2359300
  3.2 6.4 %collective-permute-start.2 = (bf16[144,256]{1,0:T(8,128)(2,1)}, bf16[144,256]{1,0:T(8,128)(2,1)S(1)}, u32[]{:S(2)}, u32[]{:S(2)}) collective-permute-start(bf16[144,256]{1,0:T(8,128)(2,1)} %get-tuple-element.45), channel_id=1, source_target_pairs={{0,1},{1,0},{2,3},{3,2},{4,5},{5,4},{6,7},{7,6},{8,9},{9,8},{10,11... | collective-permute-start | bytes 221192 | tf_op jit(solution)/shard_map/ppermute | solution.py:537
  3.7 5.9 %collective-permute-start.3 = (bf16[144,256]{1,0:T(8,128)(2,1)}, bf16[144,256]{1,0:T(8,128)(2,1)S(1)}, u32[]{:S(2)}, u32[]{:S(2)}) collective-permute-start(bf16[144,256]{1,0:T(8,128)(2,1)} %get-tuple-element.46), channel_id=1, source_target_pairs={{0,1},{1,0},{2,3},{3,2},{4,5},{5,4},{6,7},{7,6},{8,9},{9,8},{10,11... | collective-permute-start | bytes 221192 | tf_op jit(solution)/shard_map/ppermute | solution.py:537
  3.7 8.7 %collective-permute-start = (bf16[144,256]{1,0:T(8,128)(2,1)}, bf16[144,256]{1,0:T(8,128)(2,1)S(1)}, u32[]{:S(2)}, u32[]{:S(2)}) collective-permute-start(bf16[144,256]{1,0:T(8,128)(2,1)} %get-tuple-element.43), channel_id=1, source_target_pairs={{0,8},{1,11},{2,10},{3,9},{4,12},{5,15},{6,14},{7,13},{8,0},{9,3},... | collective-permute-start | bytes 221192 | tf_op jit(solution)/shard_map/ppermute | solution.py:533
  7.8 7.2 %collective-permute-start.1 = (bf16[144,256]{1,0:T(8,128)(2,1)}, bf16[144,256]{1,0:T(8,128)(2,1)S(1)}, u32[]{:S(2)}, u32[]{:S(2)}) collective-permute-start(bf16[144,256]{1,0:T(8,128)(2,1)} %get-tuple-element.44), channel_id=1, source_target_pairs={{0,12},{1,15},{2,14},{3,13},{4,8},{5,11},{6,10},{7,9},{8,4},{9,7},... | collective-permute-start | bytes 221192 | tf_op jit(solution)/shard_map/ppermute | solution.py:533
  9.1 11.0 %collective-permute-start.8 = (bf16[144,256]{1,0:T(8,128)(2,1)}, bf16[144,256]{1,0:T(8,128)(2,1)S(1)}, u32[]{:S(2)}, u32[]{:S(2)}) collective-permute-start(bf16[144,256]{1,0:T(8,128)(2,1)} %get-tuple-element.53), channel_id=1, source_target_pairs={{0,1},{1,0},{2,3},{3,2},{4,5},{5,4},{6,7},{7,6},{8,9},{9,8},{10,11... | collective-permute-start | bytes 221192 | tf_op jit(solution)/shard_map/ppermute | solution.py:537
  9.5 11.0 %collective-permute-start.4 = (bf16[144,256]{1,0:T(8,128)(2,1)S(1)}, bf16[144,256]{1,0:T(8,128)(2,1)S(1)}, u32[]{:S(2)}, u32[]{:S(2)}) collective-permute-start(bf16[144,256]{1,0:T(8,128)(2,1)S(1)} %collective-permute-done.2), channel_id=1, source_target_pairs={{0,8},{1,11},{2,10},{3,9},{4,12},{5,15},{6,14},{7,13},{8,0},{9,3},... | collective-permute-start | bytes 221192 | tf_op jit(solution)/shard_map/ppermute | solution.py:533
  11.2 9.3 %collective-permute-start.5 = (bf16[144,256]{1,0:T(8,128)(2,1)S(1)}, bf16[144,256]{1,0:T(8,128)(2,1)S(1)}, u32[]{:S(2)}, u32[]{:S(2)}) collective-permute-start(bf16[144,256]{1,0:T(8,128)(2,1)S(1)} %collective-permute-done.3), channel_id=1, source_target_pairs={{0,12},{1,15},{2,14},{3,13},{4,8},{5,11},{6,10},{7,9},{8,4},{9,7},... | collective-permute-start | bytes 221192 | tf_op jit(solution)/shard_map/ppermute | solution.py:533
  12.4 8.1 %collective-permute-start.6 = (bf16[144,256]{1,0:T(8,128)(2,1)}, bf16[144,256]{1,0:T(8,128)(2,1)S(1)}, u32[]{:S(2)}, u32[]{:S(2)}) collective-permute-start(bf16[144,256]{1,0:T(8,128)(2,1)} %get-tuple-element.51), channel_id=1, source_target_pairs={{0,2},{2,0},{4,6},{6,4},{8,10},{10,8},{12,14},{14,12},{1,3},{3,1},... | collective-permute-start | bytes 221192 | tf_op jit(solution)/shard_map/ppermute | solution.py:531
  15.0 8.0 %collective-permute-start.7 = (bf16[144,256]{1,0:T(8,128)(2,1)}, bf16[144,256]{1,0:T(8,128)(2,1)S(1)}, u32[]{:S(2)}, u32[]{:S(2)}) collective-permute-start(bf16[144,256]{1,0:T(8,128)(2,1)} %get-tuple-element.52), channel_id=1, source_target_pairs={{0,4},{1,7},{2,6},{3,5},{4,0},{5,3},{6,2},{7,1},{8,12},{9,15},{10,... | collective-permute-start | bytes 221192 | tf_op jit(solution)/shard_map/ppermute | solution.py:533
  20.1 4.9 %collective-permute-start.9 = (bf16[144,256]{1,0:T(8,128)(2,1)S(1)}, bf16[144,256]{1,0:T(8,128)(2,1)S(1)}, u32[]{:S(2)}, u32[]{:S(2)}) collective-permute-start(bf16[144,256]{1,0:T(8,128)(2,1)S(1)} %collective-permute-done.8), channel_id=1, source_target_pairs={{0,4},{1,7},{2,6},{3,5},{4,0},{5,3},{6,2},{7,1},{8,12},{9,15},{10,... | collective-permute-start | bytes 221192 | tf_op jit(solution)/shard_map/ppermute | solution.py:533
  25.0 0.9 %copy-start.3 = (bf16[144,256]{1,0:T(8,128)(2,1)S(1)}, bf16[144,256]{1,0:T(8,128)(2,1)}, u32[]{:S(2)}) copy-start(bf16[144,256]{1,0:T(8,128)(2,1)} %get-tuple-element.42.refs_0_) | copy-start | bytes 221188
  28.2 14.6 %copy-start.4 = (s32[128,8]{0,1:T(8,128)S(1)}, s32[128,8]{0,1:T(8,128)}, u32[]{:S(2)}) copy-start(s32[128,8]{0,1:T(8,128)} %param.11) | copy-start | bytes 12292
  28.2 14.6 %copy-start.5 = (s32[8,128]{1,0:T(8,128)S(1)}, s32[8,128]{1,0:T(8,128)}, u32[]{:S(2)}) copy-start(s32[8,128]{1,0:T(8,128)} %get-tuple-element.40.slot_ref) | copy-start | bytes 12292
  28.2 14.6 %copy-start.6 = (f32[8,128]{1,0:T(8,128)S(1)}, f32[8,128]{1,0:T(8,128)}, u32[]{:S(2)}) copy-start(f32[8,128]{1,0:T(8,128)} %get-tuple-element.41.gates_ref) | copy-start | bytes 12292
  28.2 11.8 %collective-permute-start.13 = (bf16[1536,384]{1,0:T(8,128)(2,1)S(1)}, bf16[1536,384]{1,0:T(8,128)(2,1)S(1)}, u32[]{:S(2)}, u32[]{:S(2)}) collective-permute-start(bf16[1536,384]{1,0:T(8,128)(2,1)S(1)} %other_half.1), channel_id=1, source_target_pairs={{0,1},{1,0},{2,3},{3,2},{4,5},{5,4},{6,7},{7,6},{8,9},{9,8},{10,11... | collective-permute-start | bytes 3538952 | tf_op jit(solution)/shard_map/ppermute | solution.py:537
  28.3 10.0 %collective-permute-start.10 = (bf16[160,256]{1,0:T(8,128)(2,1)S(1)}, bf16[160,256]{1,0:T(8,128)(2,1)S(1)}, u32[]{:S(2)}, u32[]{:S(2)}) collective-permute-start(bf16[160,256]{1,0:T(8,128)(2,1)S(1)} %get-tuple-element.55), channel_id=1, source_target_pairs={{0,8},{1,11},{2,10},{3,9},{4,12},{5,15},{6,14},{7,13},{8,0},{9,3},... | collective-permute-start | bytes 245768 | tf_op jit(solution)/shard_map/ppermute | solution.py:533
  31.9 8.1 %collective-permute-start.14 = (bf16[160,256]{1,0:T(8,128)(2,1)S(1)}, bf16[160,256]{1,0:T(8,128)(2,1)S(1)}, u32[]{:S(2)}, u32[]{:S(2)}) collective-permute-start(bf16[160,256]{1,0:T(8,128)(2,1)S(1)} %get-tuple-element.69), channel_id=1, source_target_pairs={{0,4},{1,7},{2,6},{3,5},{4,0},{5,3},{6,2},{7,1},{8,12},{9,15},{10,... | collective-permute-start | bytes 245768 | tf_op jit(solution)/shard_map/ppermute | solution.py:533
  32.5 8.9 %collective-permute-start.12 = (bf16[160,256]{1,0:T(8,128)(2,1)S(1)}, bf16[160,256]{1,0:T(8,128)(2,1)S(1)}, u32[]{:S(2)}, u32[]{:S(2)}) collective-permute-start(bf16[160,256]{1,0:T(8,128)(2,1)S(1)} %get-tuple-element.59), channel_id=1, source_target_pairs={{0,12},{1,15},{2,14},{3,13},{4,8},{5,11},{6,10},{7,9},{8,4},{9,7},... | collective-permute-start | bytes 245768 | tf_op jit(solution)/shard_map/ppermute | solution.py:533
  33.5 4.8 %collective-permute-start.11 = (bf16[80,256]{1,0:T(8,128)(2,1)S(1)}, bf16[80,256]{1,0:T(8,128)(2,1)S(1)}, u32[]{:S(2)}, u32[]{:S(2)}) collective-permute-start(bf16[80,256]{1,0:T(8,128)(2,1)S(1)} %get-tuple-element.56), channel_id=1, source_target_pairs={{0,2},{2,0},{4,6},{6,4},{8,10},{10,8},{12,14},{14,12},{1,3},{3,1},... | collective-permute-start | bytes 122888 | tf_op jit(solution)/shard_map/ppermute | solution.py:531
  38.3 3.6 %collective-permute-start.15 = (bf16[160,256]{1,0:T(8,128)(2,1)S(1)}, bf16[160,256]{1,0:T(8,128)(2,1)S(1)}, u32[]{:S(2)}, u32[]{:S(2)}) collective-permute-start(bf16[160,256]{1,0:T(8,128)(2,1)S(1)} %collective-permute-done.10.refs_2_), channel_id=1, source_target_pairs={{0,1},{1,0},{2,3},{3,2},{4,5},{5,4},{6,7},{7,6},{8,9},{9,8},{10,11... | collective-permute-start | bytes 245768 | tf_op jit(solution)/shard_map/ppermute | solution.py:537
  40.0 1.9 %collective-permute-start.17 = (bf16[160,256]{1,0:T(8,128)(2,1)S(1)}, bf16[160,256]{1,0:T(8,128)(2,1)S(1)}, u32[]{:S(2)}, u32[]{:S(2)}) collective-permute-start(bf16[160,256]{1,0:T(8,128)(2,1)S(1)} %collective-permute-done.14.refs_4_), channel_id=1, source_target_pairs={{0,1},{1,0},{2,3},{3,2},{4,5},{5,4},{6,7},{7,6},{8,9},{9,8},{10,11... | collective-permute-start | bytes 245768 | tf_op jit(solution)/shard_map/ppermute | solution.py:537
  41.4 1.4 %collective-permute-start.16 = (bf16[160,256]{1,0:T(8,128)(2,1)S(1)}, bf16[160,256]{1,0:T(8,128)(2,1)S(1)}, u32[]{:S(2)}, u32[]{:S(2)}) collective-permute-start(bf16[160,256]{1,0:T(8,128)(2,1)S(1)} %collective-permute-done.12.refs_3_), channel_id=1, source_target_pairs={{0,1},{1,0},{2,3},{3,2},{4,5},{5,4},{6,7},{7,6},{8,9},{9,8},{10,11... | collective-permute-start | bytes 245768 | tf_op jit(solution)/shard_map/ppermute | solution.py:537

commit v9 on v8

--- a/solution.py
+++ b/solution.py
@@ -237,7 +237,7 @@
 MIB = 1024 * 1024
 
 BASES = (4, 6, 2)
-ORDER = (0, 2, 4, 3, 5, 1, 6, 7)
+ORDER = (0, 1, 2, 4, 6, 3, 5, 7)
 LONG = 8 * 10**9
 MAIN = 16
 QUARTERS = 4
@@ -578,13 +578,13 @@
     )
     recv = list(chunks)
     far = [to_twin(chunks[3]), to_twin(chunks[5])]
-    far, near = lax.optimization_barrier((far, [chunks[1], chunks[6]]))
-    for d, twin in enumerate([*far, to_twin(chunks[7])]):
+    far, near = lax.optimization_barrier((far, [chunks[6], chunks[7]]))
+    for d, twin in enumerate([*far, to_twin(near[1])]):
         recv[3 + 2 * d] = to_step(twin, BASES[d])
     recv[2] = to_step(chunks[2], 4)
     recv[4] = to_step(chunks[4], 6)
-    recv[6] = to_step(near[1], 2)
-    recv[1] = to_step(near[0], 1)
+    recv[6] = to_step(near[0], 2)
+    recv[1] = to_step(chunks[1], 1)
     matmul = 2 * served * model_width * hidden_width
     outs = local_call(
         expert_kernel,
@@ -617,8 +617,7 @@
         1,
         1,
     )
-    kept[0], near = lax.optimization_barrier((kept[0], near))
-    kept[1], shares = lax.optimization_barrier((kept[1], shares))
+    kept[0], near, shares = lax.optimization_barrier((kept[0], near, shares))
     returned = [backs[0], near, *kept, *map(to_twin, kept)]
     token_grad, gate_grad = local_call(
         combine_kernel,

time: 44 us -> 42 us (0.955)
  waiting for transfers between devices: 12.7 us -> 10.6 us
    ppermute x2, waiting for transfers between devices: 3.92 us -> 0.01 us  [to_step(): return lax.ppermute(chunk, 'expert', [(i, i ^ 1) for i in range(experts)])]
    ppermute x2, starting transfers between devices: 2.18 us -> 4.18 us  [to_step(): return lax.ppermute(chunk, 'expert', [(i, i ^ 1) for i in range(experts)])]
    ppermute x9, starting transfers between devices: 18.6 us -> 16.6 us  [to_step(): return lax.ppermute(chunk, ('expert', 'replica'), pairs)]
    ppermute x9, waiting for transfers between devices: 7.88 us -> 9.31 us  [to_step(): return lax.ppermute(chunk, ('expert', 'replica'), pairs)]
  transfers between devices with their start and end apart: 18 -> 18, of which waited for: 7 -> 5; matrix products, arithmetic and copies ran while one was open for 0% -> 0% of each run, Pallas kernels for 3% -> 3%
where the time goes in v9:
time: 42 us; the launch traced here: 41.8 us
  starting transfers between devices  22.4 us (53%)
  waiting for transfers between devices  10.6 us (25%)
  Pallas kernels  7.13 us (17%)
  local copies, waits for them, and re-layouts  0.91 us (2%)
  between operations  0.77 us (2%)
    ppermute x9, starting transfers between devices, to_step(): return lax.ppermute(chunk, ('expert', 'replica'), pairs)  16.6 us
    ppermute x9, waiting for transfers between devices, to_step(): return lax.ppermute(chunk, ('expert', 'replica'), pairs)  9.31 us
    pallas_call x5, Pallas kernels, local_call(): pl.pallas_call(kernel, out_shape=[jax.ShapeDtypeStruct(shape, kind) for s...  7.13 us
    ppermute x2, starting transfers between devices, to_step(): return lax.ppermute(chunk, 'expert', [(i, i ^ 1) for i in range(experts)])  4.18 us
    ppermute x7, starting transfers between devices, to_twin(): return lax.ppermute(chunk, 'replica', [(0, 1), (1, 0)])  1.67 us
    ppermute x7, waiting for transfers between devices, to_twin(): return lax.ppermute(chunk, 'replica', [(0, 1), (1, 0)])  1.27 us
    unnamed x14, local copies, waits for them, and re-layouts  0.91 us
  transfers between devices with their start and end apart: 18, of which 5 were waited for; matrix products, arithmetic and copies ran while one was open for 0% of the time, Pallas kernels for 3%

profile of v9, /device:TPU:0, one launch (start us, length us, event | category | flops | bytes accessed | tf_op | source)
XLA Modules:
  0.0 41.8 jit_solution(1499601869562062545)
XLA Ops:
  0.6 0.0 copy-start
  0.6 0.0 copy-start.1
  0.7 0.0 copy-start.2
  0.7 2.5 %route.1 = (bf16[144,256]{1,0:T(8,128)(2,1)}, bf16[144,256]{1,0:T(8,128)(2,1)}, bf16[144,256]{1,0:T(8,128)(2,1)}, bf16[144,256]{1,0:T(8,128)(2,1)}, bf16[144,256...) custom-call(s32[8]{0:T(128)} %plan_hbm.1, ...), custom_call_target="tpu_custom_call" | custom-call | flops 8000000000 | bytes 1114112 | tf_op jit(solution)/shard_map/route/pallas_call | solution.py:516
  3.2 0.5 %collective-permute-start.3 = (bf16[144,256]{1,0:T(8,128)(2,1)}, bf16[144,256]{1,0:T(8,128)(2,1)S(1)}, u32[]{:S(2)}, u32[]{:S(2)}) collective-permute-start(bf16[144,256]{1,0:T(8,128)(2,1)} %get-tuple-element.45), channel_id=1, source_target_pairs={{0,1},{1,0},{2,3},{3,2},{4,5},{5,4},{6,7},{7,6},{8,9},{9,8},{10,11... | collective-permute-start | bytes 221192 | tf_op jit(solution)/shard_map/ppermute | solution.py:537
  3.7 0.1 collective-permute-start.4
  3.7 2.9 %collective-permute-start = (bf16[144,256]{1,0:T(8,128)(2,1)}, bf16[144,256]{1,0:T(8,128)(2,1)S(1)}, u32[]{:S(2)}, u32[]{:S(2)}) collective-permute-start(bf16[144,256]{1,0:T(8,128)(2,1)} %get-tuple-element.42), channel_id=1, source_target_pairs={{0,2},{2,0},{4,6},{6,4},{8,10},{10,8},{12,14},{14,12},{1,3},{3,1},... | collective-permute-start | bytes 221192 | tf_op jit(solution)/shard_map/ppermute | solution.py:531
  6.7 2.6 %collective-permute-start.1 = (bf16[144,256]{1,0:T(8,128)(2,1)}, bf16[144,256]{1,0:T(8,128)(2,1)S(1)}, u32[]{:S(2)}, u32[]{:S(2)}) collective-permute-start(bf16[144,256]{1,0:T(8,128)(2,1)} %get-tuple-element.43), channel_id=1, source_target_pairs={{0,8},{1,11},{2,10},{3,9},{4,12},{5,15},{6,14},{7,13},{8,0},{9,3},... | collective-permute-start | bytes 221192 | tf_op jit(solution)/shard_map/ppermute | solution.py:533
  9.3 0.0 collective-permute-done.3
  9.3 0.0 collective-permute-done.4
  9.3 0.0 collective-permute-start.8
  9.3 1.4 %collective-permute-start.2 = (bf16[144,256]{1,0:T(8,128)(2,1)}, bf16[144,256]{1,0:T(8,128)(2,1)S(1)}, u32[]{:S(2)}, u32[]{:S(2)}) collective-permute-start(bf16[144,256]{1,0:T(8,128)(2,1)} %get-tuple-element.44), channel_id=1, source_target_pairs={{0,12},{1,15},{2,14},{3,13},{4,8},{5,11},{6,10},{7,9},{8,4},{9,7},... | collective-permute-start | bytes 221192 | tf_op jit(solution)/shard_map/ppermute | solution.py:533
  10.7 0.3 collective-permute-start.5
  11.0 0.0 collective-permute-done.refs_1_
  11.0 2.7 %collective-permute-start.6 = (bf16[144,256]{1,0:T(8,128)(2,1)S(1)}, bf16[144,256]{1,0:T(8,128)(2,1)S(1)}, u32[]{:S(2)}, u32[]{:S(2)}) collective-permute-start(bf16[144,256]{1,0:T(8,128)(2,1)S(1)} %collective-permute-done.3), channel_id=1, source_target_pairs={{0,8},{1,11},{2,10},{3,9},{4,12},{5,15},{6,14},{7,13},{8,0},{9,3},... | collective-permute-start | bytes 221192 | tf_op jit(solution)/shard_map/ppermute | solution.py:533
  13.7 0.0 collective-permute-done.1.refs_2_
  13.7 5.1 %collective-permute-start.7 = (bf16[144,256]{1,0:T(8,128)(2,1)S(1)}, bf16[144,256]{1,0:T(8,128)(2,1)S(1)}, u32[]{:S(2)}, u32[]{:S(2)}) collective-permute-start(bf16[144,256]{1,0:T(8,128)(2,1)S(1)} %collective-permute-done.4), channel_id=1, source_target_pairs={{0,12},{1,15},{2,14},{3,13},{4,8},{5,11},{6,10},{7,9},{8,4},{9,7},... | collective-permute-start | bytes 221192 | tf_op jit(solution)/shard_map/ppermute | solution.py:533
  18.8 0.0 collective-permute-done.8
  18.8 0.0 collective-permute-start.9
  18.8 0.0 collective-permute-done.2.refs_3_
  18.8 0.0 collective-permute-done.5.refs_4_
  18.8 3.1 %collective-permute-done.6.refs_5_ = bf16[144,256]{1,0:T(8,128)(2,1)S(1)} collective-permute-done((bf16[144,256]{1,0:T(8,128)(2,1)S(1)}, bf16[144,256]{1,0:T(8,128)(2,1)S(1)}, u32[]{:S(2)}, u32[]{:S(2)}) %collective-permute-start.6) | collective-permute-done | bytes 73760 | tf_op jit(solution)/shard_map/ppermute | solution.py:533
  21.9 0.0 collective-permute-done.7.refs_6_
  22.0 1.9 %collective-permute-done.9.refs_7_ = bf16[144,256]{1,0:T(8,128)(2,1)S(1)} collective-permute-done((bf16[144,256]{1,0:T(8,128)(2,1)S(1)}, bf16[144,256]{1,0:T(8,128)(2,1)S(1)}, u32[]{:S(2)}, u32[]{:S(2)}) %collective-permute-start.9) | collective-permute-done | bytes 73760 | tf_op jit(solution)/shard_map/ppermute | solution.py:533
  23.9 0.0 copy-done
  23.9 0.0 copy-start.3
  23.9 0.9 %copy-done.3 = bf16[144,256]{1,0:T(8,128)(2,1)S(1)} copy-done((bf16[144,256]{1,0:T(8,128)(2,1)S(1)}, bf16[144,256]{1,0:T(8,128)(2,1)}, u32[]{:S(2)}) %copy-start.3) | copy-done | bytes 73752
  24.8 1.6 %expert_rows.1 = (bf16[80,256]{1,0:T(8,128)(2,1)S(1)}, bf16[80,256]{1,0:T(8,128)(2,1)S(1)}, bf16[160,256]{1,0:T(8,128)(2,1)S(1)}, bf16[160,256]{1,0:T(8,128)(2,1...) custom-call(bf16[144,256]{1,0:T(8,128)(2,1)S(1)} %copy-done.3, ...), custom_call_target="tpu_custom_call" | custom-call | flops 566231040 | bytes 2359296 | tf_op jit(solution)/shard_map/expert_rows/pallas_call | solution.py:516
  26.4 0.6 %other_half.1 = bf16[1536,384]{1,0:T(8,128)(2,1)S(1)} custom-call(bf16[144,1024]{1,0:T(8,128)(2,1)S(1)} %get-tuple-element.56.x_ref, bf16[144,1024]{1,0:T(8,128)(2,1)S(1)} %get-tuple-element.57.s_ref, bf16[144,384]{1,0:T(8,128)(2,1)S(1)} %get-tuple-element.58.dg_ref, bf16[144,384]{1,0:T(8,128)(2,1)S(1)} %get-tuple-element.59.du_ref, ...), custom_call_target="tpu_custom_call" | custom-call | flops 1 | bytes 1 | tf_op jit(solution)/shard_map/other_half/pallas_call | solution.py:516
  27.0 0.0 copy-start.4
  27.1 0.1 collective-permute-start.12
  27.2 3.1 %collective-permute-start.13 = (bf16[160,256]{1,0:T(8,128)(2,1)S(1)}, bf16[160,256]{1,0:T(8,128)(2,1)S(1)}, u32[]{:S(2)}, u32[]{:S(2)}) collective-permute-start(bf16[160,256]{1,0:T(8,128)(2,1)S(1)} %get-tuple-element.66), channel_id=1, source_target_pairs={{0,12},{1,15},{2,14},{3,13},{4,8},{5,11},{6,10},{7,9},{8,4},{9,7},... | collective-permute-start | bytes 245768 | tf_op jit(solution)/shard_map/ppermute | solution.py:533
  30.3 0.0 collective-permute-start.14
  30.3 1.3 %collective-permute-start.10 = (bf16[160,256]{1,0:T(8,128)(2,1)S(1)}, bf16[160,256]{1,0:T(8,128)(2,1)S(1)}, u32[]{:S(2)}, u32[]{:S(2)}) collective-permute-start(bf16[160,256]{1,0:T(8,128)(2,1)S(1)} %get-tuple-element.54), channel_id=1, source_target_pairs={{0,8},{1,11},{2,10},{3,9},{4,12},{5,15},{6,14},{7,13},{8,0},{9,3},... | collective-permute-start | bytes 245768 | tf_op jit(solution)/shard_map/ppermute | solution.py:533
  31.6 1.3 %collective-permute-start.11 = (bf16[80,256]{1,0:T(8,128)(2,1)S(1)}, bf16[80,256]{1,0:T(8,128)(2,1)S(1)}, u32[]{:S(2)}, u32[]{:S(2)}) collective-permute-start(bf16[80,256]{1,0:T(8,128)(2,1)S(1)} %get-tuple-element.55), channel_id=1, source_target_pairs={{0,2},{2,0},{4,6},{6,4},{8,10},{10,8},{12,14},{14,12},{1,3},{3,1},... | collective-permute-start | bytes 122888 | tf_op jit(solution)/shard_map/ppermute | solution.py:531
  32.9 1.5 %collective-permute-done.13.refs_3_ = bf16[160,256]{1,0:T(8,128)(2,1)S(1)} collective-permute-done((bf16[160,256]{1,0:T(8,128)(2,1)S(1)}, bf16[160,256]{1,0:T(8,128)(2,1)S(1)}, u32[]{:S(2)}, u32[]{:S(2)}) %collective-permute-start.13) | collective-permute-done | bytes 81952 | tf_op jit(solution)/shard_map/ppermute | solution.py:533
  34.4 0.0 collective-permute-start.16
  34.4 2.7 %collective-permute-done.14.refs_4_ = bf16[160,256]{1,0:T(8,128)(2,1)S(1)} collective-permute-done((bf16[160,256]{1,0:T(8,128)(2,1)S(1)}, bf16[160,256]{1,0:T(8,128)(2,1)S(1)}, u32[]{:S(2)}, u32[]{:S(2)}) %collective-permute-start.14) | collective-permute-done | bytes 81952 | tf_op jit(solution)/shard_map/ppermute | solution.py:533
  37.1 1.0 %collective-permute-start.17 = (bf16[160,256]{1,0:T(8,128)(2,1)S(1)}, bf16[160,256]{1,0:T(8,128)(2,1)S(1)}, u32[]{:S(2)}, u32[]{:S(2)}) collective-permute-start(bf16[160,256]{1,0:T(8,128)(2,1)S(1)} %collective-permute-done.14.refs_4_), channel_id=1, source_target_pairs={{0,1},{1,0},{2,3},{3,2},{4,5},{5,4},{6,7},{7,6},{8,9},{9,8},{10,11... | collective-permute-start | bytes 245768 | tf_op jit(solution)/shard_map/ppermute | solution.py:537
  38.1 0.0 collective-permute-done.12.came_ref
  38.1 1.4 %own_half.1 = (bf16[512,384]{1,0:T(8,128)(2,1)}, bf16[512,384]{1,0:T(8,128)(2,1)}, bf16[512,384]{1,0:T(8,128)(2,1)}) custom-call(bf16[144,1024]{1,0:T(8,128)(2,1)S(1)} %get-tuple-element.56.x_ref, bf16[144,1024]{1,0:T(8,128)(2,1)S(1)} %get-tuple-element.57.s_ref, bf16[144,384]{1,0:T(8,128)(2,1)S(1)} %get-tuple-element.58.dg_ref, ...), custom_call_target="tpu_custom_call" | custom-call | flops 1 | bytes 1 | tf_op jit(solution)/shard_map/own_half/pallas_call | solution.py:516
  39.5 0.0 collective-permute-done.11.refs_1_
  39.5 0.0 collective-permute-done.10.refs_2_
  39.5 0.0 collective-permute-start.15
  39.5 0.0 collective-permute-done.16.refs_6_
  39.5 0.0 collective-permute-done.17.refs_7_
  39.5 1.2 %collective-permute-done.15.refs_5_ = bf16[160,256]{1,0:T(8,128)(2,1)S(1)} collective-permute-done((bf16[160,256]{1,0:T(8,128)(2,1)S(1)}, bf16[160,256]{1,0:T(8,128)(2,1)S(1)}, u32[]{:S(2)}, u32[]{:S(2)}) %collective-permute-start.15) | collective-permute-done | bytes 81952 | tf_op jit(solution)/shard_map/ppermute | solution.py:537
  40.8 1.0 %combine.1 = (bf16[128,1024]{1,0:T(8,128)(2,1)}, bf16[8,128]{1,0:T(8,128)(2,1)}) custom-call(s32[8,128]{1,0:T(8,128)S(1)} %bitcast.14, s32[8,128]{1,0:T(8,128)S(1)} %copy-done.5, f32[8,128]{1,0:T(8,128)S(1)} %copy-done.6, bf16[80,256]{1,0:T(8,128)(2,1)S(1)} %get-tuple-element.53.refs_0_, bf16[80,256]{1,0:T(8,128)(2,1)S(1)} %collective-permute-done.11.refs_1_, ...), custom_call_target="tpu_custom_call" | custom-call | flops 37748736 | bytes 524288 | tf_op jit(solution)/shard_map/combine/pallas_call | solution.py:516
  (7 shorter events, 0.0 us)
Async XLA Ops:
  0.6 23.3 %copy-start = (bf16[1,1024,384]{2,1,0:T(8,128)(2,1)S(1)}, bf16[1,1024,384]{2,1,0:T(8,128)(2,1)}, u32[]{:S(2)}) copy-start(bf16[1,1024,384]{2,1,0:T(8,128)(2,1)} %param.15) | copy-start | bytes 2359300
  0.6 23.3 %copy-start.1 = (bf16[1,1024,384]{2,1,0:T(8,128)(2,1)S(1)}, bf16[1,1024,384]{2,1,0:T(8,128)(2,1)}, u32[]{:S(2)}) copy-start(bf16[1,1024,384]{2,1,0:T(8,128)(2,1)} %param.16) | copy-start | bytes 2359300
  0.7 23.3 %copy-start.2 = (bf16[1,1024,384]{2,1,0:T(8,128)(2,1)S(1)}, bf16[1,1024,384]{2,1,0:T(8,128)(2,1)}, u32[]{:S(2)}) copy-start(bf16[1,1024,384]{2,1,0:T(8,128)(2,1)} %param.17) | copy-start | bytes 2359300
  3.2 6.1 %collective-permute-start.3 = (bf16[144,256]{1,0:T(8,128)(2,1)}, bf16[144,256]{1,0:T(8,128)(2,1)S(1)}, u32[]{:S(2)}, u32[]{:S(2)}) collective-permute-start(bf16[144,256]{1,0:T(8,128)(2,1)} %get-tuple-element.45), channel_id=1, source_target_pairs={{0,1},{1,0},{2,3},{3,2},{4,5},{5,4},{6,7},{7,6},{8,9},{9,8},{10,11... | collective-permute-start | bytes 221192 | tf_op jit(solution)/shard_map/ppermute | solution.py:537
  3.7 5.6 %collective-permute-start.4 = (bf16[144,256]{1,0:T(8,128)(2,1)}, bf16[144,256]{1,0:T(8,128)(2,1)S(1)}, u32[]{:S(2)}, u32[]{:S(2)}) collective-permute-start(bf16[144,256]{1,0:T(8,128)(2,1)} %get-tuple-element.46), channel_id=1, source_target_pairs={{0,1},{1,0},{2,3},{3,2},{4,5},{5,4},{6,7},{7,6},{8,9},{9,8},{10,11... | collective-permute-start | bytes 221192 | tf_op jit(solution)/shard_map/ppermute | solution.py:537
  3.7 7.2 %collective-permute-start = (bf16[144,256]{1,0:T(8,128)(2,1)}, bf16[144,256]{1,0:T(8,128)(2,1)S(1)}, u32[]{:S(2)}, u32[]{:S(2)}) collective-permute-start(bf16[144,256]{1,0:T(8,128)(2,1)} %get-tuple-element.42), channel_id=1, source_target_pairs={{0,2},{2,0},{4,6},{6,4},{8,10},{10,8},{12,14},{14,12},{1,3},{3,1},... | collective-permute-start | bytes 221192 | tf_op jit(solution)/shard_map/ppermute | solution.py:531
  6.7 7.1 %collective-permute-start.1 = (bf16[144,256]{1,0:T(8,128)(2,1)}, bf16[144,256]{1,0:T(8,128)(2,1)S(1)}, u32[]{:S(2)}, u32[]{:S(2)}) collective-permute-start(bf16[144,256]{1,0:T(8,128)(2,1)} %get-tuple-element.43), channel_id=1, source_target_pairs={{0,8},{1,11},{2,10},{3,9},{4,12},{5,15},{6,14},{7,13},{8,0},{9,3},... | collective-permute-start | bytes 221192 | tf_op jit(solution)/shard_map/ppermute | solution.py:533
  9.3 9.5 %collective-permute-start.8 = (bf16[144,256]{1,0:T(8,128)(2,1)}, bf16[144,256]{1,0:T(8,128)(2,1)S(1)}, u32[]{:S(2)}, u32[]{:S(2)}) collective-permute-start(bf16[144,256]{1,0:T(8,128)(2,1)} %get-tuple-element.52), channel_id=1, source_target_pairs={{0,1},{1,0},{2,3},{3,2},{4,5},{5,4},{6,7},{7,6},{8,9},{9,8},{10,11... | collective-permute-start | bytes 221192 | tf_op jit(solution)/shard_map/ppermute | solution.py:537
  9.3 9.5 %collective-permute-start.2 = (bf16[144,256]{1,0:T(8,128)(2,1)}, bf16[144,256]{1,0:T(8,128)(2,1)S(1)}, u32[]{:S(2)}, u32[]{:S(2)}) collective-permute-start(bf16[144,256]{1,0:T(8,128)(2,1)} %get-tuple-element.44), channel_id=1, source_target_pairs={{0,12},{1,15},{2,14},{3,13},{4,8},{5,11},{6,10},{7,9},{8,4},{9,7},... | collective-permute-start | bytes 221192 | tf_op jit(solution)/shard_map/ppermute | solution.py:533
  10.7 8.1 %collective-permute-start.5 = (bf16[144,256]{1,0:T(8,128)(2,1)}, bf16[144,256]{1,0:T(8,128)(2,1)S(1)}, u32[]{:S(2)}, u32[]{:S(2)}) collective-permute-start(bf16[144,256]{1,0:T(8,128)(2,1)} %get-tuple-element.49), channel_id=1, source_target_pairs={{0,4},{1,7},{2,6},{3,5},{4,0},{5,3},{6,2},{7,1},{8,12},{9,15},{10,... | collective-permute-start | bytes 221192 | tf_op jit(solution)/shard_map/ppermute | solution.py:533
  11.0 10.9 %collective-permute-start.6 = (bf16[144,256]{1,0:T(8,128)(2,1)S(1)}, bf16[144,256]{1,0:T(8,128)(2,1)S(1)}, u32[]{:S(2)}, u32[]{:S(2)}) collective-permute-start(bf16[144,256]{1,0:T(8,128)(2,1)S(1)} %collective-permute-done.3), channel_id=1, source_target_pairs={{0,8},{1,11},{2,10},{3,9},{4,12},{5,15},{6,14},{7,13},{8,0},{9,3},... | collective-permute-start | bytes 221192 | tf_op jit(solution)/shard_map/ppermute | solution.py:533
  13.7 8.2 %collective-permute-start.7 = (bf16[144,256]{1,0:T(8,128)(2,1)S(1)}, bf16[144,256]{1,0:T(8,128)(2,1)S(1)}, u32[]{:S(2)}, u32[]{:S(2)}) collective-permute-start(bf16[144,256]{1,0:T(8,128)(2,1)S(1)} %collective-permute-done.4), channel_id=1, source_target_pairs={{0,12},{1,15},{2,14},{3,13},{4,8},{5,11},{6,10},{7,9},{8,4},{9,7},... | collective-permute-start | bytes 221192 | tf_op jit(solution)/shard_map/ppermute | solution.py:533
  18.8 5.1 %collective-permute-start.9 = (bf16[144,256]{1,0:T(8,128)(2,1)S(1)}, bf16[144,256]{1,0:T(8,128)(2,1)S(1)}, u32[]{:S(2)}, u32[]{:S(2)}) collective-permute-start(bf16[144,256]{1,0:T(8,128)(2,1)S(1)} %collective-permute-done.8), channel_id=1, source_target_pairs={{0,4},{1,7},{2,6},{3,5},{4,0},{5,3},{6,2},{7,1},{8,12},{9,15},{10,... | collective-permute-start | bytes 221192 | tf_op jit(solution)/shard_map/ppermute | solution.py:533
  23.9 0.9 %copy-start.3 = (bf16[144,256]{1,0:T(8,128)(2,1)S(1)}, bf16[144,256]{1,0:T(8,128)(2,1)}, u32[]{:S(2)}) copy-start(bf16[144,256]{1,0:T(8,128)(2,1)} %get-tuple-element.41.refs_0_) | copy-start | bytes 221188
  27.0 13.7 %copy-start.4 = (s32[128,8]{0,1:T(8,128)S(1)}, s32[128,8]{0,1:T(8,128)}, u32[]{:S(2)}) copy-start(s32[128,8]{0,1:T(8,128)} %param.11) | copy-start | bytes 12292
  27.1 13.7 %copy-start.5 = (s32[8,128]{1,0:T(8,128)S(1)}, s32[8,128]{1,0:T(8,128)}, u32[]{:S(2)}) copy-start(s32[8,128]{1,0:T(8,128)} %get-tuple-element.39.slot_ref) | copy-start | bytes 12292
  27.1 13.7 %copy-start.6 = (f32[8,128]{1,0:T(8,128)S(1)}, f32[8,128]{1,0:T(8,128)}, u32[]{:S(2)}) copy-start(f32[8,128]{1,0:T(8,128)} %get-tuple-element.40.gates_ref) | copy-start | bytes 12292
  27.1 11.0 %collective-permute-start.12 = (bf16[1536,384]{1,0:T(8,128)(2,1)S(1)}, bf16[1536,384]{1,0:T(8,128)(2,1)S(1)}, u32[]{:S(2)}, u32[]{:S(2)}) collective-permute-start(bf16[1536,384]{1,0:T(8,128)(2,1)S(1)} %other_half.1), channel_id=1, source_target_pairs={{0,1},{1,0},{2,3},{3,2},{4,5},{5,4},{6,7},{7,6},{8,9},{9,8},{10,11... | collective-permute-start | bytes 3538952 | tf_op jit(solution)/shard_map/ppermute | solution.py:537
  27.2 7.2 %collective-permute-start.13 = (bf16[160,256]{1,0:T(8,128)(2,1)S(1)}, bf16[160,256]{1,0:T(8,128)(2,1)S(1)}, u32[]{:S(2)}, u32[]{:S(2)}) collective-permute-start(bf16[160,256]{1,0:T(8,128)(2,1)S(1)} %get-tuple-element.66), channel_id=1, source_target_pairs={{0,12},{1,15},{2,14},{3,13},{4,8},{5,11},{6,10},{7,9},{8,4},{9,7},... | collective-permute-start | bytes 245768 | tf_op jit(solution)/shard_map/ppermute | solution.py:533
  30.3 6.8 %collective-permute-start.14 = (bf16[160,256]{1,0:T(8,128)(2,1)S(1)}, bf16[160,256]{1,0:T(8,128)(2,1)S(1)}, u32[]{:S(2)}, u32[]{:S(2)}) collective-permute-start(bf16[160,256]{1,0:T(8,128)(2,1)S(1)} %get-tuple-element.67), channel_id=1, source_target_pairs={{0,4},{1,7},{2,6},{3,5},{4,0},{5,3},{6,2},{7,1},{8,12},{9,15},{10,... | collective-permute-start | bytes 245768 | tf_op jit(solution)/shard_map/ppermute | solution.py:533
  30.3 9.2 %collective-permute-start.10 = (bf16[160,256]{1,0:T(8,128)(2,1)S(1)}, bf16[160,256]{1,0:T(8,128)(2,1)S(1)}, u32[]{:S(2)}, u32[]{:S(2)}) collective-permute-start(bf16[160,256]{1,0:T(8,128)(2,1)S(1)} %get-tuple-element.54), channel_id=1, source_target_pairs={{0,8},{1,11},{2,10},{3,9},{4,12},{5,15},{6,14},{7,13},{8,0},{9,3},... | collective-permute-start | bytes 245768 | tf_op jit(solution)/shard_map/ppermute | solution.py:533
  31.6 7.9 %collective-permute-start.11 = (bf16[80,256]{1,0:T(8,128)(2,1)S(1)}, bf16[80,256]{1,0:T(8,128)(2,1)S(1)}, u32[]{:S(2)}, u32[]{:S(2)}) collective-permute-start(bf16[80,256]{1,0:T(8,128)(2,1)S(1)} %get-tuple-element.55), channel_id=1, source_target_pairs={{0,2},{2,0},{4,6},{6,4},{8,10},{10,8},{12,14},{14,12},{1,3},{3,1},... | collective-permute-start | bytes 122888 | tf_op jit(solution)/shard_map/ppermute | solution.py:531
  34.4 5.1 %collective-permute-start.16 = (bf16[160,256]{1,0:T(8,128)(2,1)S(1)}, bf16[160,256]{1,0:T(8,128)(2,1)S(1)}, u32[]{:S(2)}, u32[]{:S(2)}) collective-permute-start(bf16[160,256]{1,0:T(8,128)(2,1)S(1)} %collective-permute-done.13.refs_3_), channel_id=1, source_target_pairs={{0,1},{1,0},{2,3},{3,2},{4,5},{5,4},{6,7},{7,6},{8,9},{9,8},{10,11... | collective-permute-start | bytes 245768 | tf_op jit(solution)/shard_map/ppermute | solution.py:537
  37.1 2.4 %collective-permute-start.17 = (bf16[160,256]{1,0:T(8,128)(2,1)S(1)}, bf16[160,256]{1,0:T(8,128)(2,1)S(1)}, u32[]{:S(2)}, u32[]{:S(2)}) collective-permute-start(bf16[160,256]{1,0:T(8,128)(2,1)S(1)} %collective-permute-done.14.refs_4_), channel_id=1, source_target_pairs={{0,1},{1,0},{2,3},{3,2},{4,5},{5,4},{6,7},{7,6},{8,9},{9,8},{10,11... | collective-permute-start | bytes 245768 | tf_op jit(solution)/shard_map/ppermute | solution.py:537
  39.5 1.3 %collective-permute-start.15 = (bf16[160,256]{1,0:T(8,128)(2,1)S(1)}, bf16[160,256]{1,0:T(8,128)(2,1)S(1)}, u32[]{:S(2)}, u32[]{:S(2)}) collective-permute-start(bf16[160,256]{1,0:T(8,128)(2,1)S(1)} %collective-permute-done.10.refs_2_), channel_id=1, source_target_pairs={{0,1},{1,0},{2,3},{3,2},{4,5},{5,4},{6,7},{7,6},{8,9},{9,8},{10,11... | collective-permute-start | bytes 245768 | tf_op jit(solution)/shard_map/ppermute | solution.py:537

commit v10 on v9

--- a/solution.py
+++ b/solution.py
@@ -237,7 +237,7 @@
 MIB = 1024 * 1024
 
 BASES = (4, 6, 2)
-ORDER = (0, 1, 2, 4, 6, 3, 5, 7)
+ORDER = (0, 1, 2, 4, 6, 3, 7, 5)
 LONG = 8 * 10**9
 MAIN = 16
 QUARTERS = 4
@@ -537,6 +537,10 @@
     return lax.ppermute(chunk, "replica", [(0, 1), (1, 0)])
 
 
+def hold_kernel(source_ref, place_ref):
+    place_ref[...] = source_ref[...]
+
+
 def per_device_moving_rows(
     tokens,
     cotangent,
@@ -577,14 +581,13 @@
         ],
     )
     recv = list(chunks)
-    far = [to_twin(chunks[3]), to_twin(chunks[5])]
-    far, near = lax.optimization_barrier((far, [chunks[6], chunks[7]]))
-    for d, twin in enumerate([*far, to_twin(near[1])]):
-        recv[3 + 2 * d] = to_step(twin, BASES[d])
-    recv[2] = to_step(chunks[2], 4)
-    recv[4] = to_step(chunks[4], 6)
-    recv[6] = to_step(near[0], 2)
     recv[1] = to_step(chunks[1], 1)
+    twin = [to_twin(chunks[c]) for c in (3, 5, 7)]
+    twin, mine = lax.optimization_barrier((twin, chunks[4]))
+    for d, base in enumerate(BASES):
+        recv[2 + 2 * d] = to_step(mine if base == 6 else chunks[2 + 2 * d], base)
+        recv[3 + 2 * d] = to_step(twin[d], base)
+    (held,) = local_call(hold_kernel, [(recv[0].shape, BF)], [recv[0]], "hold", 1, 1)
     matmul = 2 * served * model_width * hidden_width
     outs = local_call(
         expert_kernel,
@@ -592,7 +595,7 @@
         + [((2 * BACK_ROWS, width), BF)] * count
         + [((served, model_width), BF)] * 2
         + [((served, hidden_width), BF)] * 3,
-        [*(recv[c] for c in ORDER), gate_proj[0], up_proj[0], down_proj[0]],
+        [held, *(recv[c] for c in ORDER[1:]), gate_proj[0], up_proj[0], down_proj[0]],
         "expert_rows",
         5 * matmul,
         2 * 3 * model_width * hidden_width,

time: 42 us -> 39.8 us (0.948)
  starting transfers between devices: 22.4 us -> 21.1 us
  waiting for transfers between devices: 10.6 us -> 9.69 us
    ppermute x9, starting transfers between devices: 16.6 us -> 15 us  [to_step(): return lax.ppermute(chunk, ('expert', 'replica'), pairs)]
    ppermute x7, starting transfers between devices: 1.67 us -> 2.58 us  [to_twin(): return lax.ppermute(chunk, 'replica', [(0, 1), (1, 0)])]
    ppermute x9, waiting for transfers between devices: 9.31 us -> 8.54 us  [to_step(): return lax.ppermute(chunk, ('expert', 'replica'), pairs)]
    ppermute x2, starting transfers between devices: 4.18 us -> 3.56 us  [to_step(): return lax.ppermute(chunk, 'expert', [(i, i ^ 1) for i in range(experts)])]
    pallas_call x5 -> x6, Pallas kernels: 7.13 us -> 7.16 us  [local_call(): pl.pallas_call(kernel, out_shape=[jax.ShapeDtypeStruct(shape, kind) for s...]
  transfers between devices with their start and end apart: 18 -> 18, of which waited for: 5 -> 6; matrix products, arithmetic and copies ran while one was open for 0% -> 0% of each run, Pallas kernels for 3% -> 3%
where the time goes in v10:
time: 39.8 us; the launch traced here: 39.6 us
  starting transfers between devices  21.1 us (53%)
  waiting for transfers between devices  9.69 us (24%)
  Pallas kernels  7.16 us (18%)
  local copies, waits for them, and re-layouts  0.91 us (2%)
  between operations  0.74 us (2%)
    ppermute x9, starting transfers between devices, to_step(): return lax.ppermute(chunk, ('expert', 'replica'), pairs)  15 us
    ppermute x9, waiting for transfers between devices, to_step(): return lax.ppermute(chunk, ('expert', 'replica'), pairs)  8.54 us
    pallas_call x6, Pallas kernels, local_call(): pl.pallas_call(kernel, out_shape=[jax.ShapeDtypeStruct(shape, kind) for s...  7.16 us
    ppermute x2, starting transfers between devices, to_step(): return lax.ppermute(chunk, 'expert', [(i, i ^ 1) for i in range(experts)])  3.56 us
    ppermute x7, starting transfers between devices, to_twin(): return lax.ppermute(chunk, 'replica', [(0, 1), (1, 0)])  2.58 us
    ppermute x7, waiting for transfers between devices, to_twin(): return lax.ppermute(chunk, 'replica', [(0, 1), (1, 0)])  1.15 us
    unnamed x14, local copies, waits for them, and re-layouts  0.91 us
  transfers between devices with their start and end apart: 18, of which 6 were waited for; matrix products, arithmetic and copies ran while one was open for 0% of the time, Pallas kernels for 3%

profile of v10, /device:TPU:0, one launch (start us, length us, event | category | flops | bytes accessed | tf_op | source)
XLA Modules:
  0.0 39.6 jit_solution(11106595640148470081)
XLA Ops:
  0.6 0.0 copy-start
  0.7 2.5 %route.1 = (bf16[144,256]{1,0:T(8,128)(2,1)}, bf16[144,256]{1,0:T(8,128)(2,1)}, bf16[144,256]{1,0:T(8,128)(2,1)}, bf16[144,256]{1,0:T(8,128)(2,1)}, bf16[144,256...) custom-call(s32[8]{0:T(128)} %plan_hbm.1, ...), custom_call_target="tpu_custom_call" | custom-call | flops 8000000000 | bytes 1114112 | tf_op jit(solution)/shard_map/route/pallas_call | solution.py:516
  3.2 0.5 %collective-permute-start.2 = (bf16[144,256]{1,0:T(8,128)(2,1)}, bf16[144,256]{1,0:T(8,128)(2,1)S(1)}, u32[]{:S(2)}, u32[]{:S(2)}) collective-permute-start(bf16[144,256]{1,0:T(8,128)(2,1)} %get-tuple-element.44), channel_id=1, source_target_pairs={{0,1},{1,0},{2,3},{3,2},{4,5},{5,4},{6,7},{7,6},{8,9},{9,8},{10,11... | collective-permute-start | bytes 221192 | tf_op jit(solution)/shard_map/ppermute | solution.py:537
  3.7 0.1 collective-permute-start.3
  3.7 0.4 %collective-permute-start.4 = (bf16[144,256]{1,0:T(8,128)(2,1)}, bf16[144,256]{1,0:T(8,128)(2,1)S(1)}, u32[]{:S(2)}, u32[]{:S(2)}) collective-permute-start(bf16[144,256]{1,0:T(8,128)(2,1)} %get-tuple-element.46), channel_id=1, source_target_pairs={{0,1},{1,0},{2,3},{3,2},{4,5},{5,4},{6,7},{7,6},{8,9},{9,8},{10,11... | collective-permute-start | bytes 221192 | tf_op jit(solution)/shard_map/ppermute | solution.py:537
  4.2 2.6 %collective-permute-start = (bf16[144,256]{1,0:T(8,128)(2,1)}, bf16[144,256]{1,0:T(8,128)(2,1)S(1)}, u32[]{:S(2)}, u32[]{:S(2)}) collective-permute-start(bf16[144,256]{1,0:T(8,128)(2,1)} %get-tuple-element.42), channel_id=1, source_target_pairs={{0,2},{2,0},{4,6},{6,4},{8,10},{10,8},{12,14},{14,12},{1,3},{3,1},... | collective-permute-start | bytes 221192 | tf_op jit(solution)/shard_map/ppermute | solution.py:531
  6.7 2.6 %collective-permute-start.1 = (bf16[144,256]{1,0:T(8,128)(2,1)}, bf16[144,256]{1,0:T(8,128)(2,1)S(1)}, u32[]{:S(2)}, u32[]{:S(2)}) collective-permute-start(bf16[144,256]{1,0:T(8,128)(2,1)} %get-tuple-element.43), channel_id=1, source_target_pairs={{0,8},{1,11},{2,10},{3,9},{4,12},{5,15},{6,14},{7,13},{8,0},{9,3},... | collective-permute-start | bytes 221192 | tf_op jit(solution)/shard_map/ppermute | solution.py:533
  9.3 0.0 collective-permute-done.2
  9.3 1.6 %collective-permute-start.6 = (bf16[144,256]{1,0:T(8,128)(2,1)}, bf16[144,256]{1,0:T(8,128)(2,1)S(1)}, u32[]{:S(2)}, u32[]{:S(2)}) collective-permute-start(bf16[144,256]{1,0:T(8,128)(2,1)} %get-tuple-element.49), channel_id=1, source_target_pairs={{0,4},{1,7},{2,6},{3,5},{4,0},{5,3},{6,2},{7,1},{8,12},{9,15},{10,... | collective-permute-start | bytes 221192 | tf_op jit(solution)/shard_map/ppermute | solution.py:533
  10.9 0.0 collective-permute-done.3
  10.9 0.0 collective-permute-done.4
  10.9 0.2 collective-permute-start.5
  11.1 1.7 %collective-permute-start.7 = (bf16[144,256]{1,0:T(8,128)(2,1)S(1)}, bf16[144,256]{1,0:T(8,128)(2,1)S(1)}, u32[]{:S(2)}, u32[]{:S(2)}) collective-permute-start(bf16[144,256]{1,0:T(8,128)(2,1)S(1)} %collective-permute-done.2), channel_id=1, source_target_pairs={{0,8},{1,11},{2,10},{3,9},{4,12},{5,15},{6,14},{7,13},{8,0},{9,3},... | collective-permute-start | bytes 221192 | tf_op jit(solution)/shard_map/ppermute | solution.py:533
  12.8 0.0 collective-permute-done.refs_1_
  12.8 2.5 %collective-permute-start.8 = (bf16[144,256]{1,0:T(8,128)(2,1)S(1)}, bf16[144,256]{1,0:T(8,128)(2,1)S(1)}, u32[]{:S(2)}, u32[]{:S(2)}) collective-permute-start(bf16[144,256]{1,0:T(8,128)(2,1)S(1)} %collective-permute-done.4), channel_id=1, source_target_pairs={{0,4},{1,7},{2,6},{3,5},{4,0},{5,3},{6,2},{7,1},{8,12},{9,15},{10,... | collective-permute-start | bytes 221192 | tf_op jit(solution)/shard_map/ppermute | solution.py:533
  15.3 0.0 collective-permute-done.1.refs_2_
  15.3 2.0 %collective-permute-start.9 = (bf16[144,256]{1,0:T(8,128)(2,1)S(1)}, bf16[144,256]{1,0:T(8,128)(2,1)S(1)}, u32[]{:S(2)}, u32[]{:S(2)}) collective-permute-start(bf16[144,256]{1,0:T(8,128)(2,1)S(1)} %collective-permute-done.3), channel_id=1, source_target_pairs={{0,12},{1,15},{2,14},{3,13},{4,8},{5,11},{6,10},{7,9},{8,4},{9,7},... | collective-permute-start | bytes 221192 | tf_op jit(solution)/shard_map/ppermute | solution.py:533
  17.4 0.9 %copy-done.3 = bf16[144,256]{1,0:T(8,128)(2,1)S(1)} copy-done((bf16[144,256]{1,0:T(8,128)(2,1)S(1)}, bf16[144,256]{1,0:T(8,128)(2,1)}, u32[]{:S(2)}) %copy-start.3) | copy-done | bytes 73752
  18.2 0.0 collective-permute-done.6.refs_4_
  18.3 0.0 collective-permute-done.5.refs_3_
  18.3 2.0 %collective-permute-done.7.refs_5_ = bf16[144,256]{1,0:T(8,128)(2,1)S(1)} collective-permute-done((bf16[144,256]{1,0:T(8,128)(2,1)S(1)}, bf16[144,256]{1,0:T(8,128)(2,1)S(1)}, u32[]{:S(2)}, u32[]{:S(2)}) %collective-permute-start.7) | collective-permute-done | bytes 73760 | tf_op jit(solution)/shard_map/ppermute | solution.py:533
  20.3 0.0 collective-permute-done.8.refs_6_
  20.3 1.7 %collective-permute-done.9.refs_7_ = bf16[144,256]{1,0:T(8,128)(2,1)S(1)} collective-permute-done((bf16[144,256]{1,0:T(8,128)(2,1)S(1)}, bf16[144,256]{1,0:T(8,128)(2,1)S(1)}, u32[]{:S(2)}, u32[]{:S(2)}) %collective-permute-start.9) | collective-permute-done | bytes 73760 | tf_op jit(solution)/shard_map/ppermute | solution.py:533
  22.0 0.0 copy-done
  22.0 0.0 copy-done.2
  22.0 1.6 %expert_rows.1 = (bf16[80,256]{1,0:T(8,128)(2,1)S(1)}, bf16[80,256]{1,0:T(8,128)(2,1)S(1)}, bf16[160,256]{1,0:T(8,128)(2,1)S(1)}, bf16[160,256]{1,0:T(8,128)(2,1...) custom-call(bf16[144,256]{1,0:T(8,128)(2,1)S(1)} %hold.1.refs_0_, ...), custom_call_target="tpu_custom_call" | custom-call | flops 566231040 | bytes 2359296 | tf_op jit(solution)/shard_map/expert_rows/pallas_call | solution.py:516
  23.6 0.6 %other_half.1 = bf16[1536,384]{1,0:T(8,128)(2,1)S(1)} custom-call(bf16[144,1024]{1,0:T(8,128)(2,1)S(1)} %get-tuple-element.56.x_ref, bf16[144,1024]{1,0:T(8,128)(2,1)S(1)} %get-tuple-element.57.s_ref, bf16[144,384]{1,0:T(8,128)(2,1)S(1)} %get-tuple-element.58.dg_ref, bf16[144,384]{1,0:T(8,128)(2,1)S(1)} %get-tuple-element.59.du_ref, ...), custom_call_target="tpu_custom_call" | custom-call | flops 1 | bytes 1 | tf_op jit(solution)/shard_map/other_half/pallas_call | solution.py:516
  24.3 0.0 copy-start.4
  24.3 0.0 copy-start.5
  24.3 0.0 copy-start.6
  24.3 0.8 %collective-permute-start.12 = (bf16[1536,384]{1,0:T(8,128)(2,1)S(1)}, bf16[1536,384]{1,0:T(8,128)(2,1)S(1)}, u32[]{:S(2)}, u32[]{:S(2)}) collective-permute-start(bf16[1536,384]{1,0:T(8,128)(2,1)S(1)} %other_half.1), channel_id=1, source_target_pairs={{0,1},{1,0},{2,3},{3,2},{4,5},{5,4},{6,7},{7,6},{8,9},{9,8},{10,11... | collective-permute-start | bytes 3538952 | tf_op jit(solution)/shard_map/ppermute | solution.py:537
  25.1 3.0 %collective-permute-start.13 = (bf16[160,256]{1,0:T(8,128)(2,1)S(1)}, bf16[160,256]{1,0:T(8,128)(2,1)S(1)}, u32[]{:S(2)}, u32[]{:S(2)}) collective-permute-start(bf16[160,256]{1,0:T(8,128)(2,1)S(1)} %get-tuple-element.66), channel_id=1, source_target_pairs={{0,12},{1,15},{2,14},{3,13},{4,8},{5,11},{6,10},{7,9},{8,4},{9,7},... | collective-permute-start | bytes 245768 | tf_op jit(solution)/shard_map/ppermute | solution.py:533
  28.2 1.2 %collective-permute-start.14 = (bf16[160,256]{1,0:T(8,128)(2,1)S(1)}, bf16[160,256]{1,0:T(8,128)(2,1)S(1)}, u32[]{:S(2)}, u32[]{:S(2)}) collective-permute-start(bf16[160,256]{1,0:T(8,128)(2,1)S(1)} %get-tuple-element.67), channel_id=1, source_target_pairs={{0,4},{1,7},{2,6},{3,5},{4,0},{5,3},{6,2},{7,1},{8,12},{9,15},{10,... | collective-permute-start | bytes 245768 | tf_op jit(solution)/shard_map/ppermute | solution.py:533
  29.4 0.1 collective-permute-start.10
  29.5 1.0 %collective-permute-start.11 = (bf16[80,256]{1,0:T(8,128)(2,1)S(1)}, bf16[80,256]{1,0:T(8,128)(2,1)S(1)}, u32[]{:S(2)}, u32[]{:S(2)}) collective-permute-start(bf16[80,256]{1,0:T(8,128)(2,1)S(1)} %get-tuple-element.55), channel_id=1, source_target_pairs={{0,2},{2,0},{4,6},{6,4},{8,10},{10,8},{12,14},{14,12},{1,3},{3,1},... | collective-permute-start | bytes 122888 | tf_op jit(solution)/shard_map/ppermute | solution.py:531
  30.5 1.6 %collective-permute-done.13.refs_3_ = bf16[160,256]{1,0:T(8,128)(2,1)S(1)} collective-permute-done((bf16[160,256]{1,0:T(8,128)(2,1)S(1)}, bf16[160,256]{1,0:T(8,128)(2,1)S(1)}, u32[]{:S(2)}, u32[]{:S(2)}) %collective-permute-start.13) | collective-permute-done | bytes 81952 | tf_op jit(solution)/shard_map/ppermute | solution.py:533
  32.1 0.0 collective-permute-start.16
  32.1 1.5 %collective-permute-done.14.refs_4_ = bf16[160,256]{1,0:T(8,128)(2,1)S(1)} collective-permute-done((bf16[160,256]{1,0:T(8,128)(2,1)S(1)}, bf16[160,256]{1,0:T(8,128)(2,1)S(1)}, u32[]{:S(2)}, u32[]{:S(2)}) %collective-permute-start.14) | collective-permute-done | bytes 81952 | tf_op jit(solution)/shard_map/ppermute | solution.py:533
  33.6 0.6 %collective-permute-start.17 = (bf16[160,256]{1,0:T(8,128)(2,1)S(1)}, bf16[160,256]{1,0:T(8,128)(2,1)S(1)}, u32[]{:S(2)}, u32[]{:S(2)}) collective-permute-start(bf16[160,256]{1,0:T(8,128)(2,1)S(1)} %collective-permute-done.14.refs_4_), channel_id=1, source_target_pairs={{0,1},{1,0},{2,3},{3,2},{4,5},{5,4},{6,7},{7,6},{8,9},{9,8},{10,11... | collective-permute-start | bytes 245768 | tf_op jit(solution)/shard_map/ppermute | solution.py:537
  34.2 0.0 collective-permute-done.12.came_ref
  34.2 1.4 %own_half.1 = (bf16[512,384]{1,0:T(8,128)(2,1)}, bf16[512,384]{1,0:T(8,128)(2,1)}, bf16[512,384]{1,0:T(8,128)(2,1)}) custom-call(bf16[144,1024]{1,0:T(8,128)(2,1)S(1)} %get-tuple-element.56.x_ref, bf16[144,1024]{1,0:T(8,128)(2,1)S(1)} %get-tuple-element.57.s_ref, bf16[144,384]{1,0:T(8,128)(2,1)S(1)} %get-tuple-element.58.dg_ref, ...), custom_call_target="tpu_custom_call" | custom-call | flops 1 | bytes 1 | tf_op jit(solution)/shard_map/own_half/pallas_call | solution.py:516
  35.6 0.0 collective-permute-done.11.refs_1_
  35.6 1.7 %collective-permute-done.10.refs_2_ = bf16[160,256]{1,0:T(8,128)(2,1)S(1)} collective-permute-done((bf16[160,256]{1,0:T(8,128)(2,1)S(1)}, bf16[160,256]{1,0:T(8,128)(2,1)S(1)}, u32[]{:S(2)}, u32[]{:S(2)}) %collective-permute-start.10) | collective-permute-done | bytes 81952 | tf_op jit(solution)/shard_map/ppermute | solution.py:533
  37.3 0.1 collective-permute-start.15
  37.4 0.0 collective-permute-done.16.refs_6_
  37.4 0.0 collective-permute-done.17.refs_7_
  37.4 1.1 %collective-permute-done.15.refs_5_ = bf16[160,256]{1,0:T(8,128)(2,1)S(1)} collective-permute-done((bf16[160,256]{1,0:T(8,128)(2,1)S(1)}, bf16[160,256]{1,0:T(8,128)(2,1)S(1)}, u32[]{:S(2)}, u32[]{:S(2)}) %collective-permute-start.15) | collective-permute-done | bytes 81952 | tf_op jit(solution)/shard_map/ppermute | solution.py:537
  38.6 1.0 %combine.1 = (bf16[128,1024]{1,0:T(8,128)(2,1)}, bf16[8,128]{1,0:T(8,128)(2,1)}) custom-call(s32[8,128]{1,0:T(8,128)S(1)} %bitcast.14, s32[8,128]{1,0:T(8,128)S(1)} %copy-done.5, f32[8,128]{1,0:T(8,128)S(1)} %copy-done.6, bf16[80,256]{1,0:T(8,128)(2,1)S(1)} %get-tuple-element.53.refs_0_, bf16[80,256]{1,0:T(8,128)(2,1)S(1)} %collective-permute-done.11.refs_1_, ...), custom_call_target="tpu_custom_call" | custom-call | flops 37748736 | bytes 524288 | tf_op jit(solution)/shard_map/combine/pallas_call | solution.py:516
  (8 shorter events, 0.0 us)
Async XLA Ops:
  0.6 21.4 %copy-start = (bf16[1,1024,384]{2,1,0:T(8,128)(2,1)S(1)}, bf16[1,1024,384]{2,1,0:T(8,128)(2,1)}, u32[]{:S(2)}) copy-start(bf16[1,1024,384]{2,1,0:T(8,128)(2,1)} %param.15) | copy-start | bytes 2359300
  0.6 21.4 %copy-start.1 = (bf16[1,1024,384]{2,1,0:T(8,128)(2,1)S(1)}, bf16[1,1024,384]{2,1,0:T(8,128)(2,1)}, u32[]{:S(2)}) copy-start(bf16[1,1024,384]{2,1,0:T(8,128)(2,1)} %param.16) | copy-start | bytes 2359300
  0.7 21.4 %copy-start.2 = (bf16[1,1024,384]{2,1,0:T(8,128)(2,1)S(1)}, bf16[1,1024,384]{2,1,0:T(8,128)(2,1)}, u32[]{:S(2)}) copy-start(bf16[1,1024,384]{2,1,0:T(8,128)(2,1)} %param.17) | copy-start | bytes 2359300
  3.2 6.2 %collective-permute-start.2 = (bf16[144,256]{1,0:T(8,128)(2,1)}, bf16[144,256]{1,0:T(8,128)(2,1)S(1)}, u32[]{:S(2)}, u32[]{:S(2)}) collective-permute-start(bf16[144,256]{1,0:T(8,128)(2,1)} %get-tuple-element.44), channel_id=1, source_target_pairs={{0,1},{1,0},{2,3},{3,2},{4,5},{5,4},{6,7},{7,6},{8,9},{9,8},{10,11... | collective-permute-start | bytes 221192 | tf_op jit(solution)/shard_map/ppermute | solution.py:537
  3.7 7.2 %collective-permute-start.3 = (bf16[144,256]{1,0:T(8,128)(2,1)}, bf16[144,256]{1,0:T(8,128)(2,1)S(1)}, u32[]{:S(2)}, u32[]{:S(2)}) collective-permute-start(bf16[144,256]{1,0:T(8,128)(2,1)} %get-tuple-element.45), channel_id=1, source_target_pairs={{0,1},{1,0},{2,3},{3,2},{4,5},{5,4},{6,7},{7,6},{8,9},{9,8},{10,11... | collective-permute-start | bytes 221192 | tf_op jit(solution)/shard_map/ppermute | solution.py:537
  3.7 7.2 %collective-permute-start.4 = (bf16[144,256]{1,0:T(8,128)(2,1)}, bf16[144,256]{1,0:T(8,128)(2,1)S(1)}, u32[]{:S(2)}, u32[]{:S(2)}) collective-permute-start(bf16[144,256]{1,0:T(8,128)(2,1)} %get-tuple-element.46), channel_id=1, source_target_pairs={{0,1},{1,0},{2,3},{3,2},{4,5},{5,4},{6,7},{7,6},{8,9},{9,8},{10,11... | collective-permute-start | bytes 221192 | tf_op jit(solution)/shard_map/ppermute | solution.py:537
  4.2 8.7 %collective-permute-start = (bf16[144,256]{1,0:T(8,128)(2,1)}, bf16[144,256]{1,0:T(8,128)(2,1)S(1)}, u32[]{:S(2)}, u32[]{:S(2)}) collective-permute-start(bf16[144,256]{1,0:T(8,128)(2,1)} %get-tuple-element.42), channel_id=1, source_target_pairs={{0,2},{2,0},{4,6},{6,4},{8,10},{10,8},{12,14},{14,12},{1,3},{3,1},... | collective-permute-start | bytes 221192 | tf_op jit(solution)/shard_map/ppermute | solution.py:531
  6.7 8.6 %collective-permute-start.1 = (bf16[144,256]{1,0:T(8,128)(2,1)}, bf16[144,256]{1,0:T(8,128)(2,1)S(1)}, u32[]{:S(2)}, u32[]{:S(2)}) collective-permute-start(bf16[144,256]{1,0:T(8,128)(2,1)} %get-tuple-element.43), channel_id=1, source_target_pairs={{0,8},{1,11},{2,10},{3,9},{4,12},{5,15},{6,14},{7,13},{8,0},{9,3},... | collective-permute-start | bytes 221192 | tf_op jit(solution)/shard_map/ppermute | solution.py:533
  9.3 8.9 %collective-permute-start.6 = (bf16[144,256]{1,0:T(8,128)(2,1)}, bf16[144,256]{1,0:T(8,128)(2,1)S(1)}, u32[]{:S(2)}, u32[]{:S(2)}) collective-permute-start(bf16[144,256]{1,0:T(8,128)(2,1)} %get-tuple-element.49), channel_id=1, source_target_pairs={{0,4},{1,7},{2,6},{3,5},{4,0},{5,3},{6,2},{7,1},{8,12},{9,15},{10,... | collective-permute-start | bytes 221192 | tf_op jit(solution)/shard_map/ppermute | solution.py:533
  10.9 7.3 %collective-permute-start.5 = (bf16[144,256]{1,0:T(8,128)(2,1)}, bf16[144,256]{1,0:T(8,128)(2,1)S(1)}, u32[]{:S(2)}, u32[]{:S(2)}) collective-permute-start(bf16[144,256]{1,0:T(8,128)(2,1)} %get-tuple-element.48), channel_id=1, source_target_pairs={{0,12},{1,15},{2,14},{3,13},{4,8},{5,11},{6,10},{7,9},{8,4},{9,7},... | collective-permute-start | bytes 221192 | tf_op jit(solution)/shard_map/ppermute | solution.py:533
  11.1 9.1 %collective-permute-start.7 = (bf16[144,256]{1,0:T(8,128)(2,1)S(1)}, bf16[144,256]{1,0:T(8,128)(2,1)S(1)}, u32[]{:S(2)}, u32[]{:S(2)}) collective-permute-start(bf16[144,256]{1,0:T(8,128)(2,1)S(1)} %collective-permute-done.2), channel_id=1, source_target_pairs={{0,8},{1,11},{2,10},{3,9},{4,12},{5,15},{6,14},{7,13},{8,0},{9,3},... | collective-permute-start | bytes 221192 | tf_op jit(solution)/shard_map/ppermute | solution.py:533
  12.8 7.5 %collective-permute-start.8 = (bf16[144,256]{1,0:T(8,128)(2,1)S(1)}, bf16[144,256]{1,0:T(8,128)(2,1)S(1)}, u32[]{:S(2)}, u32[]{:S(2)}) collective-permute-start(bf16[144,256]{1,0:T(8,128)(2,1)S(1)} %collective-permute-done.4), channel_id=1, source_target_pairs={{0,4},{1,7},{2,6},{3,5},{4,0},{5,3},{6,2},{7,1},{8,12},{9,15},{10,... | collective-permute-start | bytes 221192 | tf_op jit(solution)/shard_map/ppermute | solution.py:533
  15.3 6.7 %collective-permute-start.9 = (bf16[144,256]{1,0:T(8,128)(2,1)S(1)}, bf16[144,256]{1,0:T(8,128)(2,1)S(1)}, u32[]{:S(2)}, u32[]{:S(2)}) collective-permute-start(bf16[144,256]{1,0:T(8,128)(2,1)S(1)} %collective-permute-done.3), channel_id=1, source_target_pairs={{0,12},{1,15},{2,14},{3,13},{4,8},{5,11},{6,10},{7,9},{8,4},{9,7},... | collective-permute-start | bytes 221192 | tf_op jit(solution)/shard_map/ppermute | solution.py:533
  17.4 0.9 %copy-start.3 = (bf16[144,256]{1,0:T(8,128)(2,1)S(1)}, bf16[144,256]{1,0:T(8,128)(2,1)}, u32[]{:S(2)}) copy-start(bf16[144,256]{1,0:T(8,128)(2,1)} %get-tuple-element.41.source_ref) | copy-start | bytes 221188
  24.3 14.3 %copy-start.4 = (s32[128,8]{0,1:T(8,128)S(1)}, s32[128,8]{0,1:T(8,128)}, u32[]{:S(2)}) copy-start(s32[128,8]{0,1:T(8,128)} %param.11) | copy-start | bytes 12292
  24.3 14.3 %copy-start.5 = (s32[8,128]{1,0:T(8,128)S(1)}, s32[8,128]{1,0:T(8,128)}, u32[]{:S(2)}) copy-start(s32[8,128]{1,0:T(8,128)} %get-tuple-element.39.slot_ref) | copy-start | bytes 12292
  24.3 14.3 %copy-start.6 = (f32[8,128]{1,0:T(8,128)S(1)}, f32[8,128]{1,0:T(8,128)}, u32[]{:S(2)}) copy-start(f32[8,128]{1,0:T(8,128)} %get-tuple-element.40.gates_ref) | copy-start | bytes 12292
  24.3 9.9 %collective-permute-start.12 = (bf16[1536,384]{1,0:T(8,128)(2,1)S(1)}, bf16[1536,384]{1,0:T(8,128)(2,1)S(1)}, u32[]{:S(2)}, u32[]{:S(2)}) collective-permute-start(bf16[1536,384]{1,0:T(8,128)(2,1)S(1)} %other_half.1), channel_id=1, source_target_pairs={{0,1},{1,0},{2,3},{3,2},{4,5},{5,4},{6,7},{7,6},{8,9},{9,8},{10,11... | collective-permute-start | bytes 3538952 | tf_op jit(solution)/shard_map/ppermute | solution.py:537
  25.1 7.0 %collective-permute-start.13 = (bf16[160,256]{1,0:T(8,128)(2,1)S(1)}, bf16[160,256]{1,0:T(8,128)(2,1)S(1)}, u32[]{:S(2)}, u32[]{:S(2)}) collective-permute-start(bf16[160,256]{1,0:T(8,128)(2,1)S(1)} %get-tuple-element.66), channel_id=1, source_target_pairs={{0,12},{1,15},{2,14},{3,13},{4,8},{5,11},{6,10},{7,9},{8,4},{9,7},... | collective-permute-start | bytes 245768 | tf_op jit(solution)/shard_map/ppermute | solution.py:533
  28.2 5.5 %collective-permute-start.14 = (bf16[160,256]{1,0:T(8,128)(2,1)S(1)}, bf16[160,256]{1,0:T(8,128)(2,1)S(1)}, u32[]{:S(2)}, u32[]{:S(2)}) collective-permute-start(bf16[160,256]{1,0:T(8,128)(2,1)S(1)} %get-tuple-element.67), channel_id=1, source_target_pairs={{0,4},{1,7},{2,6},{3,5},{4,0},{5,3},{6,2},{7,1},{8,12},{9,15},{10,... | collective-permute-start | bytes 245768 | tf_op jit(solution)/shard_map/ppermute | solution.py:533
  29.4 7.9 %collective-permute-start.10 = (bf16[160,256]{1,0:T(8,128)(2,1)S(1)}, bf16[160,256]{1,0:T(8,128)(2,1)S(1)}, u32[]{:S(2)}, u32[]{:S(2)}) collective-permute-start(bf16[160,256]{1,0:T(8,128)(2,1)S(1)} %get-tuple-element.54), channel_id=1, source_target_pairs={{0,8},{1,11},{2,10},{3,9},{4,12},{5,15},{6,14},{7,13},{8,0},{9,3},... | collective-permute-start | bytes 245768 | tf_op jit(solution)/shard_map/ppermute | solution.py:533
  29.5 6.1 %collective-permute-start.11 = (bf16[80,256]{1,0:T(8,128)(2,1)S(1)}, bf16[80,256]{1,0:T(8,128)(2,1)S(1)}, u32[]{:S(2)}, u32[]{:S(2)}) collective-permute-start(bf16[80,256]{1,0:T(8,128)(2,1)S(1)} %get-tuple-element.55), channel_id=1, source_target_pairs={{0,2},{2,0},{4,6},{6,4},{8,10},{10,8},{12,14},{14,12},{1,3},{3,1},... | collective-permute-start | bytes 122888 | tf_op jit(solution)/shard_map/ppermute | solution.py:531
  32.1 5.3 %collective-permute-start.16 = (bf16[160,256]{1,0:T(8,128)(2,1)S(1)}, bf16[160,256]{1,0:T(8,128)(2,1)S(1)}, u32[]{:S(2)}, u32[]{:S(2)}) collective-permute-start(bf16[160,256]{1,0:T(8,128)(2,1)S(1)} %collective-permute-done.13.refs_3_), channel_id=1, source_target_pairs={{0,1},{1,0},{2,3},{3,2},{4,5},{5,4},{6,7},{7,6},{8,9},{9,8},{10,11... | collective-permute-start | bytes 245768 | tf_op jit(solution)/shard_map/ppermute | solution.py:537
  33.6 3.8 %collective-permute-start.17 = (bf16[160,256]{1,0:T(8,128)(2,1)S(1)}, bf16[160,256]{1,0:T(8,128)(2,1)S(1)}, u32[]{:S(2)}, u32[]{:S(2)}) collective-permute-start(bf16[160,256]{1,0:T(8,128)(2,1)S(1)} %collective-permute-done.14.refs_4_), channel_id=1, source_target_pairs={{0,1},{1,0},{2,3},{3,2},{4,5},{5,4},{6,7},{7,6},{8,9},{9,8},{10,11... | collective-permute-start | bytes 245768 | tf_op jit(solution)/shard_map/ppermute | solution.py:537
  37.3 1.3 %collective-permute-start.15 = (bf16[160,256]{1,0:T(8,128)(2,1)S(1)}, bf16[160,256]{1,0:T(8,128)(2,1)S(1)}, u32[]{:S(2)}, u32[]{:S(2)}) collective-permute-start(bf16[160,256]{1,0:T(8,128)(2,1)S(1)} %collective-permute-done.10.refs_2_), channel_id=1, source_target_pairs={{0,1},{1,0},{2,3},{3,2},{4,5},{5,4},{6,7},{7,6},{8,9},{9,8},{10,11... | collective-permute-start | bytes 245768 | tf_op jit(solution)/shard_map/ppermute | solution.py:537

commit v11 on v10

--- a/solution.py
+++ b/solution.py
@@ -583,9 +583,9 @@
     recv = list(chunks)
     recv[1] = to_step(chunks[1], 1)
     twin = [to_twin(chunks[c]) for c in (3, 5, 7)]
-    twin, mine = lax.optimization_barrier((twin, chunks[4]))
+    twin, mine = lax.optimization_barrier((twin, [chunks[4], chunks[6]]))
     for d, base in enumerate(BASES):
-        recv[2 + 2 * d] = to_step(mine if base == 6 else chunks[2 + 2 * d], base)
+        recv[2 + 2 * d] = to_step(mine[d - 1] if d else chunks[2], base)
         recv[3 + 2 * d] = to_step(twin[d], base)
     (held,) = local_call(hold_kernel, [(recv[0].shape, BF)], [recv[0]], "hold", 1, 1)
     matmul = 2 * served * model_width * hidden_width
@@ -620,7 +620,8 @@
         1,
         1,
     )
-    kept[0], near, shares = lax.optimization_barrier((kept[0], near, shares))
+    kept[1], near, shares = lax.optimization_barrier((kept[1], near, shares))
+    kept[2], near = lax.optimization_barrier((kept[2], near))
     returned = [backs[0], near, *kept, *map(to_twin, kept)]
     token_grad, gate_grad = local_call(
         combine_kernel,

time: 39.8 us -> 39.7 us (level)
  waiting for transfers between devices: 9.69 us -> 9.27 us
  starting transfers between devices: 21.1 us -> 21.5 us
    ppermute x9, starting transfers between devices: 15 us -> 16.3 us  [to_step(): return lax.ppermute(chunk, ('expert', 'replica'), pairs)]
    ppermute x7, starting transfers between devices: 2.58 us -> 1.61 us  [to_twin(): return lax.ppermute(chunk, 'replica', [(0, 1), (1, 0)])]
    ppermute x9, waiting for transfers between devices: 8.54 us -> 8.06 us  [to_step(): return lax.ppermute(chunk, ('expert', 'replica'), pairs)]
  transfers between devices with their start and end apart: 18 -> 18, of which waited for: 6 -> 7; matrix products, arithmetic and copies ran while one was open for 0% -> 0% of each run, Pallas kernels for 3% -> 4%
where the time goes in v11:
time: 39.7 us; the launch traced here: 39.5 us
  starting transfers between devices  21.5 us (54%)
  waiting for transfers between devices  9.27 us (23%)
  Pallas kernels  7.15 us (18%)
  local copies, waits for them, and re-layouts  0.91 us (2%)
  between operations  0.75 us (2%)
    ppermute x9, starting transfers between devices, to_step(): return lax.ppermute(chunk, ('expert', 'replica'), pairs)  16.3 us
    ppermute x9, waiting for transfers between devices, to_step(): return lax.ppermute(chunk, ('expert', 'replica'), pairs)  8.06 us
    pallas_call x6, Pallas kernels, local_call(): pl.pallas_call(kernel, out_shape=[jax.ShapeDtypeStruct(shape, kind) for s...  7.15 us
    ppermute x2, starting transfers between devices, to_step(): return lax.ppermute(chunk, 'expert', [(i, i ^ 1) for i in range(experts)])  3.52 us
    ppermute x7, starting transfers between devices, to_twin(): return lax.ppermute(chunk, 'replica', [(0, 1), (1, 0)])  1.61 us
    ppermute x7, waiting for transfers between devices, to_twin(): return lax.ppermute(chunk, 'replica', [(0, 1), (1, 0)])  1.21 us
    unnamed x14, local copies, waits for them, and re-layouts  0.91 us
  transfers between devices with their start and end apart: 18, of which 7 were waited for; matrix products, arithmetic and copies ran while one was open for 0% of the time, Pallas kernels for 4%

profile of v11, /device:TPU:0, one launch (start us, length us, event | category | flops | bytes accessed | tf_op | source)
XLA Modules:
  0.0 39.5 jit_solution(11698766348059321799)
XLA Ops:
  0.6 0.0 copy-start
  0.6 0.0 copy-start.1
  0.7 0.0 copy-start.2
  0.7 2.5 %route.1 = (bf16[144,256]{1,0:T(8,128)(2,1)}, bf16[144,256]{1,0:T(8,128)(2,1)}, bf16[144,256]{1,0:T(8,128)(2,1)}, bf16[144,256]{1,0:T(8,128)(2,1)}, bf16[144,256...) custom-call(s32[8]{0:T(128)} %plan_hbm.1, ...), custom_call_target="tpu_custom_call" | custom-call | flops 8000000000 | bytes 1114112 | tf_op jit(solution)/shard_map/route/pallas_call | solution.py:516
  3.2 0.5 %collective-permute-start.2 = (bf16[144,256]{1,0:T(8,128)(2,1)}, bf16[144,256]{1,0:T(8,128)(2,1)S(1)}, u32[]{:S(2)}, u32[]{:S(2)}) collective-permute-start(bf16[144,256]{1,0:T(8,128)(2,1)} %get-tuple-element.47), channel_id=1, source_target_pairs={{0,1},{1,0},{2,3},{3,2},{4,5},{5,4},{6,7},{7,6},{8,9},{9,8},{10,11... | collective-permute-start | bytes 221192 | tf_op jit(solution)/shard_map/ppermute | solution.py:537
  3.7 0.1 collective-permute-start.3
  3.7 0.4 %collective-permute-start.4 = (bf16[144,256]{1,0:T(8,128)(2,1)}, bf16[144,256]{1,0:T(8,128)(2,1)S(1)}, u32[]{:S(2)}, u32[]{:S(2)}) collective-permute-start(bf16[144,256]{1,0:T(8,128)(2,1)} %get-tuple-element.49), channel_id=1, source_target_pairs={{0,1},{1,0},{2,3},{3,2},{4,5},{5,4},{6,7},{7,6},{8,9},{9,8},{10,11... | collective-permute-start | bytes 221192 | tf_op jit(solution)/shard_map/ppermute | solution.py:537
  4.2 2.6 %collective-permute-start = (bf16[144,256]{1,0:T(8,128)(2,1)}, bf16[144,256]{1,0:T(8,128)(2,1)S(1)}, u32[]{:S(2)}, u32[]{:S(2)}) collective-permute-start(bf16[144,256]{1,0:T(8,128)(2,1)} %get-tuple-element.45), channel_id=1, source_target_pairs={{0,2},{2,0},{4,6},{6,4},{8,10},{10,8},{12,14},{14,12},{1,3},{3,1},... | collective-permute-start | bytes 221192 | tf_op jit(solution)/shard_map/ppermute | solution.py:531
  6.7 2.6 %collective-permute-start.1 = (bf16[144,256]{1,0:T(8,128)(2,1)}, bf16[144,256]{1,0:T(8,128)(2,1)S(1)}, u32[]{:S(2)}, u32[]{:S(2)}) collective-permute-start(bf16[144,256]{1,0:T(8,128)(2,1)} %get-tuple-element.46), channel_id=1, source_target_pairs={{0,8},{1,11},{2,10},{3,9},{4,12},{5,15},{6,14},{7,13},{8,0},{9,3},... | collective-permute-start | bytes 221192 | tf_op jit(solution)/shard_map/ppermute | solution.py:533
  9.3 0.0 collective-permute-done.2
  9.3 0.0 collective-permute-done.3
  9.3 0.0 collective-permute-done.4
  9.3 1.4 %collective-permute-start.5 = (bf16[144,256]{1,0:T(8,128)(2,1)}, bf16[144,256]{1,0:T(8,128)(2,1)S(1)}, u32[]{:S(2)}, u32[]{:S(2)}) collective-permute-start(bf16[144,256]{1,0:T(8,128)(2,1)} %get-tuple-element.52), channel_id=1, source_target_pairs={{0,12},{1,15},{2,14},{3,13},{4,8},{5,11},{6,10},{7,9},{8,4},{9,7},... | collective-permute-start | bytes 221192 | tf_op jit(solution)/shard_map/ppermute | solution.py:533
  10.8 0.3 collective-permute-start.6
  11.1 2.7 %collective-permute-start.7 = (bf16[144,256]{1,0:T(8,128)(2,1)S(1)}, bf16[144,256]{1,0:T(8,128)(2,1)S(1)}, u32[]{:S(2)}, u32[]{:S(2)}) collective-permute-start(bf16[144,256]{1,0:T(8,128)(2,1)S(1)} %collective-permute-done.2), channel_id=1, source_target_pairs={{0,8},{1,11},{2,10},{3,9},{4,12},{5,15},{6,14},{7,13},{8,0},{9,3},... | collective-permute-start | bytes 221192 | tf_op jit(solution)/shard_map/ppermute | solution.py:533
  13.8 0.0 collective-permute-done.refs_1_
  13.8 0.7 %collective-permute-start.8 = (bf16[144,256]{1,0:T(8,128)(2,1)S(1)}, bf16[144,256]{1,0:T(8,128)(2,1)S(1)}, u32[]{:S(2)}, u32[]{:S(2)}) collective-permute-start(bf16[144,256]{1,0:T(8,128)(2,1)S(1)} %collective-permute-done.4), channel_id=1, source_target_pairs={{0,4},{1,7},{2,6},{3,5},{4,0},{5,3},{6,2},{7,1},{8,12},{9,15},{10,... | collective-permute-start | bytes 221192 | tf_op jit(solution)/shard_map/ppermute | solution.py:533
  14.5 0.0 collective-permute-done.1.refs_2_
  14.5 4.5 %collective-permute-start.9 = (bf16[144,256]{1,0:T(8,128)(2,1)S(1)}, bf16[144,256]{1,0:T(8,128)(2,1)S(1)}, u32[]{:S(2)}, u32[]{:S(2)}) collective-permute-start(bf16[144,256]{1,0:T(8,128)(2,1)S(1)} %collective-permute-done.3), channel_id=1, source_target_pairs={{0,12},{1,15},{2,14},{3,13},{4,8},{5,11},{6,10},{7,9},{8,4},{9,7},... | collective-permute-start | bytes 221192 | tf_op jit(solution)/shard_map/ppermute | solution.py:533
  18.9 0.9 %copy-done.3 = bf16[144,256]{1,0:T(8,128)(2,1)S(1)} copy-done((bf16[144,256]{1,0:T(8,128)(2,1)S(1)}, bf16[144,256]{1,0:T(8,128)(2,1)}, u32[]{:S(2)}) %copy-start.3) | copy-done | bytes 73752
  19.8 0.0 collective-permute-done.5.refs_3_
  19.8 0.0 collective-permute-done.6.refs_4_
  19.8 0.7 %collective-permute-done.7.refs_5_ = bf16[144,256]{1,0:T(8,128)(2,1)S(1)} collective-permute-done((bf16[144,256]{1,0:T(8,128)(2,1)S(1)}, bf16[144,256]{1,0:T(8,128)(2,1)S(1)}, u32[]{:S(2)}, u32[]{:S(2)}) %collective-permute-start.7) | collective-permute-done | bytes 73760 | tf_op jit(solution)/shard_map/ppermute | solution.py:533
  20.5 0.0 collective-permute-done.8.refs_6_
  20.5 2.4 %collective-permute-done.9.refs_7_ = bf16[144,256]{1,0:T(8,128)(2,1)S(1)} collective-permute-done((bf16[144,256]{1,0:T(8,128)(2,1)S(1)}, bf16[144,256]{1,0:T(8,128)(2,1)S(1)}, u32[]{:S(2)}, u32[]{:S(2)}) %collective-permute-start.9) | collective-permute-done | bytes 73760 | tf_op jit(solution)/shard_map/ppermute | solution.py:533
  22.9 0.0 copy-done
  22.9 0.0 copy-done.1
  22.9 1.6 %expert_rows.1 = (bf16[80,256]{1,0:T(8,128)(2,1)S(1)}, bf16[80,256]{1,0:T(8,128)(2,1)S(1)}, bf16[160,256]{1,0:T(8,128)(2,1)S(1)}, bf16[160,256]{1,0:T(8,128)(2,1...) custom-call(bf16[144,256]{1,0:T(8,128)(2,1)S(1)} %hold.1.refs_0_, ...), custom_call_target="tpu_custom_call" | custom-call | flops 566231040 | bytes 2359296 | tf_op jit(solution)/shard_map/expert_rows/pallas_call | solution.py:516
  24.5 0.6 %other_half.1 = bf16[1536,384]{1,0:T(8,128)(2,1)S(1)} custom-call(bf16[144,1024]{1,0:T(8,128)(2,1)S(1)} %get-tuple-element.61.x_ref, bf16[144,1024]{1,0:T(8,128)(2,1)S(1)} %get-tuple-element.62.s_ref, bf16[144,384]{1,0:T(8,128)(2,1)S(1)} %get-tuple-element.63.dg_ref, bf16[144,384]{1,0:T(8,128)(2,1)S(1)} %get-tuple-element.64.du_ref, ...), custom_call_target="tpu_custom_call" | custom-call | flops 1 | bytes 1 | tf_op jit(solution)/shard_map/other_half/pallas_call | solution.py:516
  25.2 0.0 copy-start.4
  25.2 0.1 collective-permute-start.13
  25.3 3.6 %collective-permute-start.14 = (bf16[160,256]{1,0:T(8,128)(2,1)S(1)}, bf16[160,256]{1,0:T(8,128)(2,1)S(1)}, u32[]{:S(2)}, u32[]{:S(2)}) collective-permute-start(bf16[160,256]{1,0:T(8,128)(2,1)S(1)} %get-tuple-element.71), channel_id=1, source_target_pairs={{0,8},{1,11},{2,10},{3,9},{4,12},{5,15},{6,14},{7,13},{8,0},{9,3},... | collective-permute-start | bytes 245768 | tf_op jit(solution)/shard_map/ppermute | solution.py:533
  28.9 0.0 collective-permute-start.11
  28.9 0.6 %collective-permute-start.10 = (bf16[160,256]{1,0:T(8,128)(2,1)S(1)}, bf16[160,256]{1,0:T(8,128)(2,1)S(1)}, u32[]{:S(2)}, u32[]{:S(2)}) collective-permute-start(bf16[160,256]{1,0:T(8,128)(2,1)S(1)} %get-tuple-element.58), channel_id=1, source_target_pairs={{0,4},{1,7},{2,6},{3,5},{4,0},{5,3},{6,2},{7,1},{8,12},{9,15},{10,... | collective-permute-start | bytes 245768 | tf_op jit(solution)/shard_map/ppermute | solution.py:533
  29.4 1.0 %collective-permute-start.12 = (bf16[80,256]{1,0:T(8,128)(2,1)S(1)}, bf16[80,256]{1,0:T(8,128)(2,1)S(1)}, u32[]{:S(2)}, u32[]{:S(2)}) collective-permute-start(bf16[80,256]{1,0:T(8,128)(2,1)S(1)} %get-tuple-element.60), channel_id=1, source_target_pairs={{0,2},{2,0},{4,6},{6,4},{8,10},{10,8},{12,14},{14,12},{1,3},{3,1},... | collective-permute-start | bytes 122888 | tf_op jit(solution)/shard_map/ppermute | solution.py:531
  30.4 3.5 %collective-permute-done.14.refs_2_ = bf16[160,256]{1,0:T(8,128)(2,1)S(1)} collective-permute-done((bf16[160,256]{1,0:T(8,128)(2,1)S(1)}, bf16[160,256]{1,0:T(8,128)(2,1)S(1)}, u32[]{:S(2)}, u32[]{:S(2)}) %collective-permute-start.14) | collective-permute-done | bytes 81952 | tf_op jit(solution)/shard_map/ppermute | solution.py:533
  33.8 0.0 collective-permute-start.15
  33.8 0.0 collective-permute-done.13.came_ref
  33.8 1.4 %own_half.1 = (bf16[512,384]{1,0:T(8,128)(2,1)}, bf16[512,384]{1,0:T(8,128)(2,1)}, bf16[512,384]{1,0:T(8,128)(2,1)}) custom-call(bf16[144,1024]{1,0:T(8,128)(2,1)S(1)} %get-tuple-element.61.x_ref, bf16[144,1024]{1,0:T(8,128)(2,1)S(1)} %get-tuple-element.62.s_ref, bf16[144,384]{1,0:T(8,128)(2,1)S(1)} %get-tuple-element.63.dg_ref, ...), custom_call_target="tpu_custom_call" | custom-call | flops 1 | bytes 1 | tf_op jit(solution)/shard_map/own_half/pallas_call | solution.py:516
  35.2 0.0 collective-permute-done.12.refs_1_
  35.2 0.8 %collective-permute-done.11.refs_3_ = bf16[160,256]{1,0:T(8,128)(2,1)S(1)} collective-permute-done((bf16[160,256]{1,0:T(8,128)(2,1)S(1)}, bf16[160,256]{1,0:T(8,128)(2,1)S(1)}, u32[]{:S(2)}, u32[]{:S(2)}) %collective-permute-start.11) | collective-permute-done | bytes 81952 | tf_op jit(solution)/shard_map/ppermute | solution.py:533
  36.0 0.8 %collective-permute-done.10.refs_4_ = bf16[160,256]{1,0:T(8,128)(2,1)S(1)} collective-permute-done((bf16[160,256]{1,0:T(8,128)(2,1)S(1)}, bf16[160,256]{1,0:T(8,128)(2,1)S(1)}, u32[]{:S(2)}, u32[]{:S(2)}) %collective-permute-start.10) | collective-permute-done | bytes 81952 | tf_op jit(solution)/shard_map/ppermute | solution.py:533
  36.8 0.4 %collective-permute-start.16 = (bf16[160,256]{1,0:T(8,128)(2,1)S(1)}, bf16[160,256]{1,0:T(8,128)(2,1)S(1)}, u32[]{:S(2)}, u32[]{:S(2)}) collective-permute-start(bf16[160,256]{1,0:T(8,128)(2,1)S(1)} %collective-permute-done.11.refs_3_), channel_id=1, source_target_pairs={{0,1},{1,0},{2,3},{3,2},{4,5},{5,4},{6,7},{7,6},{8,9},{9,8},{10,11... | collective-permute-start | bytes 245768 | tf_op jit(solution)/shard_map/ppermute | solution.py:537
  37.2 0.1 collective-permute-start.17
  37.3 0.0 collective-permute-done.15.refs_5_
  37.3 0.8 %collective-permute-done.16.refs_6_ = bf16[160,256]{1,0:T(8,128)(2,1)S(1)} collective-permute-done((bf16[160,256]{1,0:T(8,128)(2,1)S(1)}, bf16[160,256]{1,0:T(8,128)(2,1)S(1)}, u32[]{:S(2)}, u32[]{:S(2)}) %collective-permute-start.16) | collective-permute-done | bytes 81952 | tf_op jit(solution)/shard_map/ppermute | solution.py:537
  38.1 0.4 collective-permute-done.17.refs_7_
  38.5 1.0 %combine.1 = (bf16[128,1024]{1,0:T(8,128)(2,1)}, bf16[8,128]{1,0:T(8,128)(2,1)}) custom-call(s32[8,128]{1,0:T(8,128)S(1)} %bitcast.14, s32[8,128]{1,0:T(8,128)S(1)} %copy-done.5, f32[8,128]{1,0:T(8,128)S(1)} %copy-done.6, bf16[80,256]{1,0:T(8,128)(2,1)S(1)} %get-tuple-element.57.refs_0_, bf16[80,256]{1,0:T(8,128)(2,1)S(1)} %collective-permute-done.12.refs_1_, ...), custom_call_target="tpu_custom_call" | custom-call | flops 37748736 | bytes 524288 | tf_op jit(solution)/shard_map/combine/pallas_call | solution.py:516
  (8 shorter events, 0.0 us)
Async XLA Ops:
  0.6 22.3 %copy-start = (bf16[1,1024,384]{2,1,0:T(8,128)(2,1)S(1)}, bf16[1,1024,384]{2,1,0:T(8,128)(2,1)}, u32[]{:S(2)}) copy-start(bf16[1,1024,384]{2,1,0:T(8,128)(2,1)} %param.15) | copy-start | bytes 2359300
  0.6 22.2 %copy-start.1 = (bf16[1,1024,384]{2,1,0:T(8,128)(2,1)S(1)}, bf16[1,1024,384]{2,1,0:T(8,128)(2,1)}, u32[]{:S(2)}) copy-start(bf16[1,1024,384]{2,1,0:T(8,128)(2,1)} %param.16) | copy-start | bytes 2359300
  0.7 22.2 %copy-start.2 = (bf16[1,1024,384]{2,1,0:T(8,128)(2,1)S(1)}, bf16[1,1024,384]{2,1,0:T(8,128)(2,1)}, u32[]{:S(2)}) copy-start(bf16[1,1024,384]{2,1,0:T(8,128)(2,1)} %param.17) | copy-start | bytes 2359300
  3.2 6.2 %collective-permute-start.2 = (bf16[144,256]{1,0:T(8,128)(2,1)}, bf16[144,256]{1,0:T(8,128)(2,1)S(1)}, u32[]{:S(2)}, u32[]{:S(2)}) collective-permute-start(bf16[144,256]{1,0:T(8,128)(2,1)} %get-tuple-element.47), channel_id=1, source_target_pairs={{0,1},{1,0},{2,3},{3,2},{4,5},{5,4},{6,7},{7,6},{8,9},{9,8},{10,11... | collective-permute-start | bytes 221192 | tf_op jit(solution)/shard_map/ppermute | solution.py:537
  3.7 5.7 %collective-permute-start.3 = (bf16[144,256]{1,0:T(8,128)(2,1)}, bf16[144,256]{1,0:T(8,128)(2,1)S(1)}, u32[]{:S(2)}, u32[]{:S(2)}) collective-permute-start(bf16[144,256]{1,0:T(8,128)(2,1)} %get-tuple-element.48), channel_id=1, source_target_pairs={{0,1},{1,0},{2,3},{3,2},{4,5},{5,4},{6,7},{7,6},{8,9},{9,8},{10,11... | collective-permute-start | bytes 221192 | tf_op jit(solution)/shard_map/ppermute | solution.py:537
  3.7 5.6 %collective-permute-start.4 = (bf16[144,256]{1,0:T(8,128)(2,1)}, bf16[144,256]{1,0:T(8,128)(2,1)S(1)}, u32[]{:S(2)}, u32[]{:S(2)}) collective-permute-start(bf16[144,256]{1,0:T(8,128)(2,1)} %get-tuple-element.49), channel_id=1, source_target_pairs={{0,1},{1,0},{2,3},{3,2},{4,5},{5,4},{6,7},{7,6},{8,9},{9,8},{10,11... | collective-permute-start | bytes 221192 | tf_op jit(solution)/shard_map/ppermute | solution.py:537
  4.2 9.6 %collective-permute-start = (bf16[144,256]{1,0:T(8,128)(2,1)}, bf16[144,256]{1,0:T(8,128)(2,1)S(1)}, u32[]{:S(2)}, u32[]{:S(2)}) collective-permute-start(bf16[144,256]{1,0:T(8,128)(2,1)} %get-tuple-element.45), channel_id=1, source_target_pairs={{0,2},{2,0},{4,6},{6,4},{8,10},{10,8},{12,14},{14,12},{1,3},{3,1},... | collective-permute-start | bytes 221192 | tf_op jit(solution)/shard_map/ppermute | solution.py:531
  6.7 7.7 %collective-permute-start.1 = (bf16[144,256]{1,0:T(8,128)(2,1)}, bf16[144,256]{1,0:T(8,128)(2,1)S(1)}, u32[]{:S(2)}, u32[]{:S(2)}) collective-permute-start(bf16[144,256]{1,0:T(8,128)(2,1)} %get-tuple-element.46), channel_id=1, source_target_pairs={{0,8},{1,11},{2,10},{3,9},{4,12},{5,15},{6,14},{7,13},{8,0},{9,3},... | collective-permute-start | bytes 221192 | tf_op jit(solution)/shard_map/ppermute | solution.py:533
  9.3 10.5 %collective-permute-start.5 = (bf16[144,256]{1,0:T(8,128)(2,1)}, bf16[144,256]{1,0:T(8,128)(2,1)S(1)}, u32[]{:S(2)}, u32[]{:S(2)}) collective-permute-start(bf16[144,256]{1,0:T(8,128)(2,1)} %get-tuple-element.52), channel_id=1, source_target_pairs={{0,12},{1,15},{2,14},{3,13},{4,8},{5,11},{6,10},{7,9},{8,4},{9,7},... | collective-permute-start | bytes 221192 | tf_op jit(solution)/shard_map/ppermute | solution.py:533
  10.8 9.1 %collective-permute-start.6 = (bf16[144,256]{1,0:T(8,128)(2,1)}, bf16[144,256]{1,0:T(8,128)(2,1)S(1)}, u32[]{:S(2)}, u32[]{:S(2)}) collective-permute-start(bf16[144,256]{1,0:T(8,128)(2,1)} %get-tuple-element.53), channel_id=1, source_target_pairs={{0,4},{1,7},{2,6},{3,5},{4,0},{5,3},{6,2},{7,1},{8,12},{9,15},{10,... | collective-permute-start | bytes 221192 | tf_op jit(solution)/shard_map/ppermute | solution.py:533
  11.1 9.4 %collective-permute-start.7 = (bf16[144,256]{1,0:T(8,128)(2,1)S(1)}, bf16[144,256]{1,0:T(8,128)(2,1)S(1)}, u32[]{:S(2)}, u32[]{:S(2)}) collective-permute-start(bf16[144,256]{1,0:T(8,128)(2,1)S(1)} %collective-permute-done.2), channel_id=1, source_target_pairs={{0,8},{1,11},{2,10},{3,9},{4,12},{5,15},{6,14},{7,13},{8,0},{9,3},... | collective-permute-start | bytes 221192 | tf_op jit(solution)/shard_map/ppermute | solution.py:533
  13.8 6.7 %collective-permute-start.8 = (bf16[144,256]{1,0:T(8,128)(2,1)S(1)}, bf16[144,256]{1,0:T(8,128)(2,1)S(1)}, u32[]{:S(2)}, u32[]{:S(2)}) collective-permute-start(bf16[144,256]{1,0:T(8,128)(2,1)S(1)} %collective-permute-done.4), channel_id=1, source_target_pairs={{0,4},{1,7},{2,6},{3,5},{4,0},{5,3},{6,2},{7,1},{8,12},{9,15},{10,... | collective-permute-start | bytes 221192 | tf_op jit(solution)/shard_map/ppermute | solution.py:533
  14.5 8.4 %collective-permute-start.9 = (bf16[144,256]{1,0:T(8,128)(2,1)S(1)}, bf16[144,256]{1,0:T(8,128)(2,1)S(1)}, u32[]{:S(2)}, u32[]{:S(2)}) collective-permute-start(bf16[144,256]{1,0:T(8,128)(2,1)S(1)} %collective-permute-done.3), channel_id=1, source_target_pairs={{0,12},{1,15},{2,14},{3,13},{4,8},{5,11},{6,10},{7,9},{8,4},{9,7},... | collective-permute-start | bytes 221192 | tf_op jit(solution)/shard_map/ppermute | solution.py:533
  18.9 0.9 %copy-start.3 = (bf16[144,256]{1,0:T(8,128)(2,1)S(1)}, bf16[144,256]{1,0:T(8,128)(2,1)}, u32[]{:S(2)}) copy-start(bf16[144,256]{1,0:T(8,128)(2,1)} %get-tuple-element.44.source_ref) | copy-start | bytes 221188
  25.2 13.3 %copy-start.4 = (s32[128,8]{0,1:T(8,128)S(1)}, s32[128,8]{0,1:T(8,128)}, u32[]{:S(2)}) copy-start(s32[128,8]{0,1:T(8,128)} %param.11) | copy-start | bytes 12292
  25.2 13.3 %copy-start.5 = (s32[8,128]{1,0:T(8,128)S(1)}, s32[8,128]{1,0:T(8,128)}, u32[]{:S(2)}) copy-start(s32[8,128]{1,0:T(8,128)} %get-tuple-element.42.slot_ref) | copy-start | bytes 12292
  25.2 13.3 %copy-start.6 = (f32[8,128]{1,0:T(8,128)S(1)}, f32[8,128]{1,0:T(8,128)}, u32[]{:S(2)}) copy-start(f32[8,128]{1,0:T(8,128)} %get-tuple-element.43.gates_ref) | copy-start | bytes 12292
  25.2 8.7 %collective-permute-start.13 = (bf16[1536,384]{1,0:T(8,128)(2,1)S(1)}, bf16[1536,384]{1,0:T(8,128)(2,1)S(1)}, u32[]{:S(2)}, u32[]{:S(2)}) collective-permute-start(bf16[1536,384]{1,0:T(8,128)(2,1)S(1)} %other_half.1), channel_id=1, source_target_pairs={{0,1},{1,0},{2,3},{3,2},{4,5},{5,4},{6,7},{7,6},{8,9},{9,8},{10,11... | collective-permute-start | bytes 3538952 | tf_op jit(solution)/shard_map/ppermute | solution.py:537
  25.3 8.6 %collective-permute-start.14 = (bf16[160,256]{1,0:T(8,128)(2,1)S(1)}, bf16[160,256]{1,0:T(8,128)(2,1)S(1)}, u32[]{:S(2)}, u32[]{:S(2)}) collective-permute-start(bf16[160,256]{1,0:T(8,128)(2,1)S(1)} %get-tuple-element.71), channel_id=1, source_target_pairs={{0,8},{1,11},{2,10},{3,9},{4,12},{5,15},{6,14},{7,13},{8,0},{9,3},... | collective-permute-start | bytes 245768 | tf_op jit(solution)/shard_map/ppermute | solution.py:533
  28.9 7.2 %collective-permute-start.11 = (bf16[160,256]{1,0:T(8,128)(2,1)S(1)}, bf16[160,256]{1,0:T(8,128)(2,1)S(1)}, u32[]{:S(2)}, u32[]{:S(2)}) collective-permute-start(bf16[160,256]{1,0:T(8,128)(2,1)S(1)} %get-tuple-element.59), channel_id=1, source_target_pairs={{0,12},{1,15},{2,14},{3,13},{4,8},{5,11},{6,10},{7,9},{8,4},{9,7},... | collective-permute-start | bytes 245768 | tf_op jit(solution)/shard_map/ppermute | solution.py:533
  28.9 7.9 %collective-permute-start.10 = (bf16[160,256]{1,0:T(8,128)(2,1)S(1)}, bf16[160,256]{1,0:T(8,128)(2,1)S(1)}, u32[]{:S(2)}, u32[]{:S(2)}) collective-permute-start(bf16[160,256]{1,0:T(8,128)(2,1)S(1)} %get-tuple-element.58), channel_id=1, source_target_pairs={{0,4},{1,7},{2,6},{3,5},{4,0},{5,3},{6,2},{7,1},{8,12},{9,15},{10,... | collective-permute-start | bytes 245768 | tf_op jit(solution)/shard_map/ppermute | solution.py:533
  29.4 5.8 %collective-permute-start.12 = (bf16[80,256]{1,0:T(8,128)(2,1)S(1)}, bf16[80,256]{1,0:T(8,128)(2,1)S(1)}, u32[]{:S(2)}, u32[]{:S(2)}) collective-permute-start(bf16[80,256]{1,0:T(8,128)(2,1)S(1)} %get-tuple-element.60), channel_id=1, source_target_pairs={{0,2},{2,0},{4,6},{6,4},{8,10},{10,8},{12,14},{14,12},{1,3},{3,1},... | collective-permute-start | bytes 122888 | tf_op jit(solution)/shard_map/ppermute | solution.py:531
  33.8 3.5 %collective-permute-start.15 = (bf16[160,256]{1,0:T(8,128)(2,1)S(1)}, bf16[160,256]{1,0:T(8,128)(2,1)S(1)}, u32[]{:S(2)}, u32[]{:S(2)}) collective-permute-start(bf16[160,256]{1,0:T(8,128)(2,1)S(1)} %collective-permute-done.14.refs_2_), channel_id=1, source_target_pairs={{0,1},{1,0},{2,3},{3,2},{4,5},{5,4},{6,7},{7,6},{8,9},{9,8},{10,11... | collective-permute-start | bytes 245768 | tf_op jit(solution)/shard_map/ppermute | solution.py:537
  36.8 1.4 %collective-permute-start.16 = (bf16[160,256]{1,0:T(8,128)(2,1)S(1)}, bf16[160,256]{1,0:T(8,128)(2,1)S(1)}, u32[]{:S(2)}, u32[]{:S(2)}) collective-permute-start(bf16[160,256]{1,0:T(8,128)(2,1)S(1)} %collective-permute-done.11.refs_3_), channel_id=1, source_target_pairs={{0,1},{1,0},{2,3},{3,2},{4,5},{5,4},{6,7},{7,6},{8,9},{9,8},{10,11... | collective-permute-start | bytes 245768 | tf_op jit(solution)/shard_map/ppermute | solution.py:537
  37.2 1.3 %collective-permute-start.17 = (bf16[160,256]{1,0:T(8,128)(2,1)S(1)}, bf16[160,256]{1,0:T(8,128)(2,1)S(1)}, u32[]{:S(2)}, u32[]{:S(2)}) collective-permute-start(bf16[160,256]{1,0:T(8,128)(2,1)S(1)} %collective-permute-done.10.refs_4_), channel_id=1, source_target_pairs={{0,1},{1,0},{2,3},{3,2},{4,5},{5,4},{6,7},{7,6},{8,9},{9,8},{10,11... | collective-permute-start | bytes 245768 | tf_op jit(solution)/shard_map/ppermute | solution.py:537

commit v12 on v10

--- a/solution.py
+++ b/solution.py
@@ -236,8 +236,9 @@
 CONTRACT_COLS = (((1,), (1,)), ((), ()))
 MIB = 1024 * 1024
 
-BASES = (4, 6, 2)
-ORDER = (0, 1, 2, 4, 6, 3, 7, 5)
+SINGLES = 4
+BASES = (4, 6)
+ORDER = (0, 1, 4, 6, 2, 5, 7, 3)
 LONG = 8 * 10**9
 MAIN = 16
 QUARTERS = 4
@@ -257,13 +258,14 @@
     row = iota((experts, tokens), 0)
     step = jnp.bitwise_xor(jnp.bitwise_and(row, 1), lax.axis_index("replica"))
     for d, base in enumerate(BASES):
-        step = jnp.where(jnp.right_shift(row, 1) == d + 1, step + base, step)
-    step = jnp.where(row < 2, row, step)
+        step = jnp.where(jnp.right_shift(row - SINGLES, 1) == d, step + base, step)
+    step = jnp.where(row < SINGLES, row, step)
     return jnp.bitwise_xor(step, lax.axis_index("expert"))
 
 
 def chunk_views(refs, rows):
-    return [(refs[0], 0), (refs[1], 0)] + [(ref, part * rows) for ref in refs[2:] for part in (0, 1)]
+    singles, doubles = refs[:SINGLES], refs[SINGLES:]
+    return [(ref, 0) for ref in singles] + [(ref, part * rows) for ref in doubles for part in (0, 1)]
 
 
 def mask(condition):
@@ -467,9 +469,9 @@
 
 def combine_kernel(ids_ref, slot_ref, gates_ref, *refs):
     token_ref, grad_ref = refs[-2:]
-    doubles = 2 + len(BASES)
-    ret_views = [(refs[0], 0), (refs[1], 0)]
-    for kept_ref, given_ref in zip(refs[2:doubles], refs[doubles:-2]):
+    doubles = SINGLES + len(BASES)
+    ret_views = [(ref, 0) for ref in refs[:SINGLES]]
+    for kept_ref, given_ref in zip(refs[SINGLES:doubles], refs[doubles:-2]):
         ret_views += [(kept_ref, 0), (given_ref, BACK_ROWS)]
     topk, tokens = ids_ref.shape
     experts = len(ret_views)
@@ -525,11 +527,11 @@
     )(*arrays)
 
 
-def to_step(chunk, base):
+def to_step(chunk, step):
     experts = lax.axis_size("expert")
-    if base == 1:
-        return lax.ppermute(chunk, "expert", [(i, i ^ 1) for i in range(experts)])
-    pairs = [(2 * i + r, 2 * (i ^ (base + r)) + r) for i in range(experts) for r in range(2)]
+    if step < SINGLES:
+        return lax.ppermute(chunk, "expert", [(i, i ^ step) for i in range(experts)])
+    pairs = [(2 * i + r, 2 * (i ^ (step + r)) + r) for i in range(experts) for r in range(2)]
     return lax.ppermute(chunk, ("expert", "replica"), pairs)
 
 
@@ -559,7 +561,6 @@
     width = model_width // QUARTERS
     served = experts * (MAIN + 2)
     small = (topk, token_count)
-    count = len(BASES)
     *chunks, slot, gates = local_call(
         route_kernel,
         [((SEND_ROWS, width), BF)] * experts
@@ -581,18 +582,21 @@
         ],
     )
     recv = list(chunks)
+    twin = [to_twin(chunks[c]) for c in (5, 7)]
+    twin, far, near = lax.optimization_barrier((twin, chunks[6], chunks[2:4]))
     recv[1] = to_step(chunks[1], 1)
-    twin = [to_twin(chunks[c]) for c in (3, 5, 7)]
-    twin, mine = lax.optimization_barrier((twin, chunks[4]))
-    for d, base in enumerate(BASES):
-        recv[2 + 2 * d] = to_step(mine if base == 6 else chunks[2 + 2 * d], base)
-        recv[3 + 2 * d] = to_step(twin[d], base)
+    recv[2] = to_step(near[0], 2)
+    recv[3] = to_step(near[1], 3)
+    recv[4] = to_step(chunks[4], 4)
+    recv[5] = to_step(twin[0], 4)
+    recv[6] = to_step(far, 6)
+    recv[7] = to_step(twin[1], 6)
     (held,) = local_call(hold_kernel, [(recv[0].shape, BF)], [recv[0]], "hold", 1, 1)
     matmul = 2 * served * model_width * hidden_width
     outs = local_call(
         expert_kernel,
-        [((BACK_ROWS, width), BF)] * 2
-        + [((2 * BACK_ROWS, width), BF)] * count
+        [((BACK_ROWS, width), BF)] * SINGLES
+        + [((2 * BACK_ROWS, width), BF)] * len(BASES)
         + [((served, model_width), BF)] * 2
         + [((served, hidden_width), BF)] * 3,
         [held, *(recv[c] for c in ORDER[1:]), gate_proj[0], up_proj[0], down_proj[0]],
@@ -600,9 +604,9 @@
         5 * matmul,
         2 * 3 * model_width * hidden_width,
     )
-    backs, factors = outs[: 2 + count], outs[2 + count :]
-    kept = list(map(to_step, backs[2:], BASES))
-    near = to_step(backs[1], 1)
+    backs, factors = outs[:-5], outs[-5:]
+    kept = list(map(to_step, backs[SINGLES:], BASES))
+    near = [to_step(backs[c], c) for c in range(1, SINGLES)]
     half = model_width // 2
     (leaving,) = local_call(
         other_half_kernel,
@@ -620,8 +624,10 @@
         1,
         1,
     )
-    kept[0], near, shares = lax.optimization_barrier((kept[0], near, shares))
-    returned = [backs[0], near, *kept, *map(to_twin, kept)]
+    kept, near, shares = lax.optimization_barrier((kept, near, shares))
+    first = to_twin(kept[0])
+    kept[1], first = lax.optimization_barrier((kept[1], first))
+    returned = [backs[0], *near, *kept, first, to_twin(kept[1])]
     token_grad, gate_grad = local_call(
         combine_kernel,
         [((token_count, model_width), BF), ((topk, token_count), BF)],

time: 39.8 us -> 41.2 us (1.035)
  waiting for transfers between devices: 9.69 us -> 11.8 us
  starting transfers between devices: 21.1 us -> 20.4 us
    ppermute x2 -> x6, waiting for transfers between devices: 0.01 us -> 5.1 us  [to_step(): lax.ppermute(chunk, 'expert', [(i, i ^ step) for i in range(experts)])]
    ppermute x2 -> x6, starting transfers between devices: 3.56 us -> 8.43 us  [to_step(): lax.ppermute(chunk, 'expert', [(i, i ^ step) for i in range(experts)])]
    ppermute x9 -> x6, waiting for transfers between devices: 8.54 us -> 4.31 us  [to_step(): return lax.ppermute(chunk, ('expert', 'replica'), pairs)]
    ppermute x9 -> x6, starting transfers between devices: 15 us -> 11.1 us  [to_step(): return lax.ppermute(chunk, ('expert', 'replica'), pairs)]
    ppermute x7 -> x5, starting transfers between devices: 2.58 us -> 0.86 us  [to_twin(): return lax.ppermute(chunk, 'replica', [(0, 1), (1, 0)])]
    ppermute x7 -> x5, waiting for transfers between devices: 1.15 us -> 2.37 us  [to_twin(): return lax.ppermute(chunk, 'replica', [(0, 1), (1, 0)])]
  transfers between devices with their start and end apart: 18 -> 17, of which waited for: 6 -> 6; matrix products, arithmetic and copies ran while one was open for 0% -> 0% of each run, Pallas kernels for 3% -> 3%
where the time goes in v12:
time: 41.2 us; the launch traced here: 41 us
  starting transfers between devices  20.4 us (50%)
  waiting for transfers between devices  11.8 us (29%)
  Pallas kernels  7.17 us (17%)
  local copies, waits for them, and re-layouts  0.91 us (2%)
  between operations  0.74 us (2%)
    ppermute x6, starting transfers between devices, to_step(): return lax.ppermute(chunk, ('expert', 'replica'), pairs)  11.1 us
    ppermute x6, starting transfers between devices, to_step(): lax.ppermute(chunk, 'expert', [(i, i ^ step) for i in range(experts)])  8.43 us
    pallas_call x6, Pallas kernels, local_call(): pl.pallas_call(kernel, out_shape=[jax.ShapeDtypeStruct(shape, kind) for s...  7.17 us
    ppermute x6, waiting for transfers between devices, to_step(): lax.ppermute(chunk, 'expert', [(i, i ^ step) for i in range(experts)])  5.1 us
    ppermute x6, waiting for transfers between devices, to_step(): return lax.ppermute(chunk, ('expert', 'replica'), pairs)  4.31 us
    ppermute x5, waiting for transfers between devices, to_twin(): return lax.ppermute(chunk, 'replica', [(0, 1), (1, 0)])  2.37 us
    unnamed x14, local copies, waits for them, and re-layouts  0.91 us
    ppermute x5, starting transfers between devices, to_twin(): return lax.ppermute(chunk, 'replica', [(0, 1), (1, 0)])  0.86 us
  transfers between devices with their start and end apart: 17, of which 6 were waited for; matrix products, arithmetic and copies ran while one was open for 0% of the time, Pallas kernels for 3%

profile of v12, /device:TPU:0, one launch (start us, length us, event | category | flops | bytes accessed | tf_op | source)
XLA Modules:
  0.0 41.0 jit_solution(15293877814207733290)
XLA Ops:
  0.6 0.0 copy-start
  0.6 0.0 copy-start.1
  0.7 0.0 copy-start.2
  0.7 2.5 %route.1 = (bf16[144,256]{1,0:T(8,128)(2,1)}, bf16[144,256]{1,0:T(8,128)(2,1)}, bf16[144,256]{1,0:T(8,128)(2,1)}, bf16[144,256]{1,0:T(8,128)(2,1)}, bf16[144,256...) custom-call(s32[8]{0:T(128)} %plan_hbm.1, ...), custom_call_target="tpu_custom_call" | custom-call | flops 8000000000 | bytes 1114112 | tf_op jit(solution)/shard_map/route/pallas_call | solution.py:518
  3.1 0.5 %collective-permute-start.2 = (bf16[144,256]{1,0:T(8,128)(2,1)}, bf16[144,256]{1,0:T(8,128)(2,1)S(1)}, u32[]{:S(2)}, u32[]{:S(2)}) collective-permute-start(bf16[144,256]{1,0:T(8,128)(2,1)} %get-tuple-element.51), channel_id=1, source_target_pairs={{0,1},{1,0},{2,3},{3,2},{4,5},{5,4},{6,7},{7,6},{8,9},{9,8},{10,11... | collective-permute-start | bytes 221192 | tf_op jit(solution)/shard_map/ppermute | solution.py:539
  3.7 0.1 collective-permute-start.3
  3.7 2.9 %collective-permute-start = (bf16[144,256]{1,0:T(8,128)(2,1)}, bf16[144,256]{1,0:T(8,128)(2,1)S(1)}, u32[]{:S(2)}, u32[]{:S(2)}) collective-permute-start(bf16[144,256]{1,0:T(8,128)(2,1)} %get-tuple-element.49), channel_id=1, source_target_pairs={{0,2},{2,0},{4,6},{6,4},{8,10},{10,8},{12,14},{14,12},{1,3},{3,1},... | collective-permute-start | bytes 221192 | tf_op jit(solution)/shard_map/ppermute | solution.py:533
  6.7 2.6 %collective-permute-start.1 = (bf16[144,256]{1,0:T(8,128)(2,1)}, bf16[144,256]{1,0:T(8,128)(2,1)S(1)}, u32[]{:S(2)}, u32[]{:S(2)}) collective-permute-start(bf16[144,256]{1,0:T(8,128)(2,1)} %get-tuple-element.50), channel_id=1, source_target_pairs={{0,8},{1,11},{2,10},{3,9},{4,12},{5,15},{6,14},{7,13},{8,0},{9,3},... | collective-permute-start | bytes 221192 | tf_op jit(solution)/shard_map/ppermute | solution.py:535
  9.3 0.0 collective-permute-done.2
  9.3 0.0 collective-permute-done.3
  9.3 1.4 %collective-permute-start.4 = (bf16[144,256]{1,0:T(8,128)(2,1)}, bf16[144,256]{1,0:T(8,128)(2,1)S(1)}, u32[]{:S(2)}, u32[]{:S(2)}) collective-permute-start(bf16[144,256]{1,0:T(8,128)(2,1)} %get-tuple-element.56), channel_id=1, source_target_pairs={{0,12},{1,15},{2,14},{3,13},{4,8},{5,11},{6,10},{7,9},{8,4},{9,7},... | collective-permute-start | bytes 221192 | tf_op jit(solution)/shard_map/ppermute | solution.py:535
  10.6 0.3 collective-permute-start.5
  10.9 2.7 %collective-permute-start.6 = (bf16[144,256]{1,0:T(8,128)(2,1)S(1)}, bf16[144,256]{1,0:T(8,128)(2,1)S(1)}, u32[]{:S(2)}, u32[]{:S(2)}) collective-permute-start(bf16[144,256]{1,0:T(8,128)(2,1)S(1)} %collective-permute-done.2), channel_id=1, source_target_pairs={{0,8},{1,11},{2,10},{3,9},{4,12},{5,15},{6,14},{7,13},{8,0},{9,3},... | collective-permute-start | bytes 221192 | tf_op jit(solution)/shard_map/ppermute | solution.py:535
  13.6 0.0 collective-permute-done.refs_1_
  13.7 1.3 %collective-permute-start.7 = (bf16[144,256]{1,0:T(8,128)(2,1)S(1)}, bf16[144,256]{1,0:T(8,128)(2,1)S(1)}, u32[]{:S(2)}, u32[]{:S(2)}) collective-permute-start(bf16[144,256]{1,0:T(8,128)(2,1)S(1)} %collective-permute-done.3), channel_id=1, source_target_pairs={{0,12},{1,15},{2,14},{3,13},{4,8},{5,11},{6,10},{7,9},{8,4},{9,7},... | collective-permute-start | bytes 221192 | tf_op jit(solution)/shard_map/ppermute | solution.py:535
  15.0 0.0 collective-permute-done.1.refs_2_
  15.0 1.7 %collective-permute-start.8 = (bf16[144,256]{1,0:T(8,128)(2,1)}, bf16[144,256]{1,0:T(8,128)(2,1)S(1)}, u32[]{:S(2)}, u32[]{:S(2)}) collective-permute-start(bf16[144,256]{1,0:T(8,128)(2,1)} %get-tuple-element.60), channel_id=1, source_target_pairs={{0,6},{2,4},{4,2},{6,0},{8,14},{10,12},{12,10},{14,8},{1,7},{3,5},... | collective-permute-start | bytes 221192 | tf_op jit(solution)/shard_map/ppermute | solution.py:533
  16.7 0.9 %copy-done.3 = bf16[144,256]{1,0:T(8,128)(2,1)S(1)} copy-done((bf16[144,256]{1,0:T(8,128)(2,1)S(1)}, bf16[144,256]{1,0:T(8,128)(2,1)}, u32[]{:S(2)}) %copy-start.3) | copy-done | bytes 73752
  17.6 0.0 collective-permute-done.4.refs_3_
  17.6 0.0 collective-permute-done.5.refs_4_
  17.6 4.3 %collective-permute-done.6.refs_5_ = bf16[144,256]{1,0:T(8,128)(2,1)S(1)} collective-permute-done((bf16[144,256]{1,0:T(8,128)(2,1)S(1)}, bf16[144,256]{1,0:T(8,128)(2,1)S(1)}, u32[]{:S(2)}, u32[]{:S(2)}) %collective-permute-start.6) | collective-permute-done | bytes 73760 | tf_op jit(solution)/shard_map/ppermute | solution.py:535
  21.9 0.0 collective-permute-done.7.refs_6_
  21.9 1.4 %collective-permute-done.8.refs_7_ = bf16[144,256]{1,0:T(8,128)(2,1)S(1)} collective-permute-done((bf16[144,256]{1,0:T(8,128)(2,1)}, bf16[144,256]{1,0:T(8,128)(2,1)S(1)}, u32[]{:S(2)}, u32[]{:S(2)}) %collective-permute-start.8) | collective-permute-done | bytes 73760 | tf_op jit(solution)/shard_map/ppermute | solution.py:533
  23.3 0.0 copy-done.1
  23.3 1.6 %expert_rows.1 = (bf16[80,256]{1,0:T(8,128)(2,1)S(1)}, bf16[80,256]{1,0:T(8,128)(2,1)S(1)}, bf16[80,256]{1,0:T(8,128)(2,1)S(1)}, bf16[80,256]{1,0:T(8,128)(2,1)S...) custom-call(bf16[144,256]{1,0:T(8,128)(2,1)S(1)} %hold.1.refs_0_, ...), custom_call_target="tpu_custom_call" | custom-call | flops 566231040 | bytes 2359296 | tf_op jit(solution)/shard_map/expert_rows/pallas_call | solution.py:518
  25.0 0.6 %other_half.1 = bf16[1536,384]{1,0:T(8,128)(2,1)S(1)} custom-call(bf16[144,1024]{1,0:T(8,128)(2,1)S(1)} %get-tuple-element.67.x_ref, bf16[144,1024]{1,0:T(8,128)(2,1)S(1)} %get-tuple-element.68.s_ref, bf16[144,384]{1,0:T(8,128)(2,1)S(1)} %get-tuple-element.69.dg_ref, bf16[144,384]{1,0:T(8,128)(2,1)S(1)} %get-tuple-element.70.du_ref, ...), custom_call_target="tpu_custom_call" | custom-call | flops 1 | bytes 1 | tf_op jit(solution)/shard_map/other_half/pallas_call | solution.py:518
  25.6 0.0 copy-start.4
  25.6 0.0 copy-start.5
  25.6 0.0 copy-start.6
  25.6 0.1 collective-permute-start.14
  25.7 2.8 %collective-permute-start.9 = (bf16[160,256]{1,0:T(8,128)(2,1)S(1)}, bf16[160,256]{1,0:T(8,128)(2,1)S(1)}, u32[]{:S(2)}, u32[]{:S(2)}) collective-permute-start(bf16[160,256]{1,0:T(8,128)(2,1)S(1)} %get-tuple-element.62), channel_id=1, source_target_pairs={{0,8},{1,11},{2,10},{3,9},{4,12},{5,15},{6,14},{7,13},{8,0},{9,3},... | collective-permute-start | bytes 245768 | tf_op jit(solution)/shard_map/ppermute | solution.py:535
  28.6 0.2 collective-permute-start.10
  28.8 1.1 %collective-permute-start.11 = (bf16[80,256]{1,0:T(8,128)(2,1)S(1)}, bf16[80,256]{1,0:T(8,128)(2,1)S(1)}, u32[]{:S(2)}, u32[]{:S(2)}) collective-permute-start(bf16[80,256]{1,0:T(8,128)(2,1)S(1)} %get-tuple-element.64), channel_id=1, source_target_pairs={{0,2},{2,0},{4,6},{6,4},{8,10},{10,8},{12,14},{14,12},{1,3},{3,1},... | collective-permute-start | bytes 122888 | tf_op jit(solution)/shard_map/ppermute | solution.py:533
  29.9 0.2 collective-permute-start.12
  30.1 0.0 collective-permute-done.14.came_ref
  30.1 2.2 %collective-permute-start.13 = (bf16[80,256]{1,0:T(8,128)(2,1)S(1)}, bf16[80,256]{1,0:T(8,128)(2,1)S(1)}, u32[]{:S(2)}, u32[]{:S(2)}) collective-permute-start(bf16[80,256]{1,0:T(8,128)(2,1)S(1)} %get-tuple-element.66), channel_id=1, source_target_pairs={{0,6},{2,4},{4,2},{6,0},{8,14},{10,12},{12,10},{14,8},{1,7},{3,5},... | collective-permute-start | bytes 122888 | tf_op jit(solution)/shard_map/ppermute | solution.py:533
  32.3 1.4 %own_half.1 = (bf16[512,384]{1,0:T(8,128)(2,1)}, bf16[512,384]{1,0:T(8,128)(2,1)}, bf16[512,384]{1,0:T(8,128)(2,1)}) custom-call(bf16[144,1024]{1,0:T(8,128)(2,1)S(1)} %get-tuple-element.67.x_ref, bf16[144,1024]{1,0:T(8,128)(2,1)S(1)} %get-tuple-element.68.s_ref, bf16[144,384]{1,0:T(8,128)(2,1)S(1)} %get-tuple-element.69.dg_ref, ...), custom_call_target="tpu_custom_call" | custom-call | flops 1 | bytes 1 | tf_op jit(solution)/shard_map/own_half/pallas_call | solution.py:518
  33.7 0.0 collective-permute-done.11.refs_1_
  33.7 2.5 %collective-permute-done.12.refs_2_ = bf16[80,256]{1,0:T(8,128)(2,1)S(1)} collective-permute-done((bf16[80,256]{1,0:T(8,128)(2,1)S(1)}, bf16[80,256]{1,0:T(8,128)(2,1)S(1)}, u32[]{:S(2)}, u32[]{:S(2)}) %collective-permute-start.12) | collective-permute-done | bytes 40992 | tf_op jit(solution)/shard_map/ppermute | solution.py:533
  36.2 1.2 %collective-permute-done.13.refs_3_ = bf16[80,256]{1,0:T(8,128)(2,1)S(1)} collective-permute-done((bf16[80,256]{1,0:T(8,128)(2,1)S(1)}, bf16[80,256]{1,0:T(8,128)(2,1)S(1)}, u32[]{:S(2)}, u32[]{:S(2)}) %collective-permute-start.13) | collective-permute-done | bytes 40992 | tf_op jit(solution)/shard_map/ppermute | solution.py:533
  37.4 0.0 collective-permute-done.9.refs_4_
  37.4 0.0 collective-permute-done.10.refs_5_
  37.4 0.0 collective-permute-start.15
  37.4 1.2 %collective-permute-done.15.refs_6_ = bf16[160,256]{1,0:T(8,128)(2,1)S(1)} collective-permute-done((bf16[160,256]{1,0:T(8,128)(2,1)S(1)}, bf16[160,256]{1,0:T(8,128)(2,1)S(1)}, u32[]{:S(2)}, u32[]{:S(2)}) %collective-permute-start.15) | collective-permute-done | bytes 81952 | tf_op jit(solution)/shard_map/ppermute | solution.py:539
  38.6 0.2 collective-permute-start.16
  38.8 1.1 %collective-permute-done.16.refs_7_ = bf16[160,256]{1,0:T(8,128)(2,1)S(1)} collective-permute-done((bf16[160,256]{1,0:T(8,128)(2,1)S(1)}, bf16[160,256]{1,0:T(8,128)(2,1)S(1)}, u32[]{:S(2)}, u32[]{:S(2)}) %collective-permute-start.16) | collective-permute-done | bytes 81952 | tf_op jit(solution)/shard_map/ppermute | solution.py:539
  39.9 0.0 copy-done.5
  39.9 1.0 %combine.1 = (bf16[128,1024]{1,0:T(8,128)(2,1)}, bf16[8,128]{1,0:T(8,128)(2,1)}) custom-call(s32[8,128]{1,0:T(8,128)S(1)} %bitcast.14, s32[8,128]{1,0:T(8,128)S(1)} %copy-done.5, f32[8,128]{1,0:T(8,128)S(1)} %copy-done.6, bf16[80,256]{1,0:T(8,128)(2,1)S(1)} %get-tuple-element.61.refs_0_, bf16[80,256]{1,0:T(8,128)(2,1)S(1)} %collective-permute-done.11.refs_1_, ...), custom_call_target="tpu_custom_call" | custom-call | flops 37748736 | bytes 524288 | tf_op jit(solution)/shard_map/combine/pallas_call | solution.py:518
  (6 shorter events, 0.0 us)
Async XLA Ops:
  0.6 22.7 %copy-start = (bf16[1,1024,384]{2,1,0:T(8,128)(2,1)S(1)}, bf16[1,1024,384]{2,1,0:T(8,128)(2,1)}, u32[]{:S(2)}) copy-start(bf16[1,1024,384]{2,1,0:T(8,128)(2,1)} %param.15) | copy-start | bytes 2359300
  0.6 22.7 %copy-start.1 = (bf16[1,1024,384]{2,1,0:T(8,128)(2,1)S(1)}, bf16[1,1024,384]{2,1,0:T(8,128)(2,1)}, u32[]{:S(2)}) copy-start(bf16[1,1024,384]{2,1,0:T(8,128)(2,1)} %param.16) | copy-start | bytes 2359300
  0.7 22.7 %copy-start.2 = (bf16[1,1024,384]{2,1,0:T(8,128)(2,1)S(1)}, bf16[1,1024,384]{2,1,0:T(8,128)(2,1)}, u32[]{:S(2)}) copy-start(bf16[1,1024,384]{2,1,0:T(8,128)(2,1)} %param.17) | copy-start | bytes 2359300
  3.1 6.1 %collective-permute-start.2 = (bf16[144,256]{1,0:T(8,128)(2,1)}, bf16[144,256]{1,0:T(8,128)(2,1)S(1)}, u32[]{:S(2)}, u32[]{:S(2)}) collective-permute-start(bf16[144,256]{1,0:T(8,128)(2,1)} %get-tuple-element.51), channel_id=1, source_target_pairs={{0,1},{1,0},{2,3},{3,2},{4,5},{5,4},{6,7},{7,6},{8,9},{9,8},{10,11... | collective-permute-start | bytes 221192 | tf_op jit(solution)/shard_map/ppermute | solution.py:539
  3.7 5.6 %collective-permute-start.3 = (bf16[144,256]{1,0:T(8,128)(2,1)}, bf16[144,256]{1,0:T(8,128)(2,1)S(1)}, u32[]{:S(2)}, u32[]{:S(2)}) collective-permute-start(bf16[144,256]{1,0:T(8,128)(2,1)} %get-tuple-element.52), channel_id=1, source_target_pairs={{0,1},{1,0},{2,3},{3,2},{4,5},{5,4},{6,7},{7,6},{8,9},{9,8},{10,11... | collective-permute-start | bytes 221192 | tf_op jit(solution)/shard_map/ppermute | solution.py:539
  3.7 9.9 %collective-permute-start = (bf16[144,256]{1,0:T(8,128)(2,1)}, bf16[144,256]{1,0:T(8,128)(2,1)S(1)}, u32[]{:S(2)}, u32[]{:S(2)}) collective-permute-start(bf16[144,256]{1,0:T(8,128)(2,1)} %get-tuple-element.49), channel_id=1, source_target_pairs={{0,2},{2,0},{4,6},{6,4},{8,10},{10,8},{12,14},{14,12},{1,3},{3,1},... | collective-permute-start | bytes 221192 | tf_op jit(solution)/shard_map/ppermute | solution.py:533
  6.7 8.3 %collective-permute-start.1 = (bf16[144,256]{1,0:T(8,128)(2,1)}, bf16[144,256]{1,0:T(8,128)(2,1)S(1)}, u32[]{:S(2)}, u32[]{:S(2)}) collective-permute-start(bf16[144,256]{1,0:T(8,128)(2,1)} %get-tuple-element.50), channel_id=1, source_target_pairs={{0,8},{1,11},{2,10},{3,9},{4,12},{5,15},{6,14},{7,13},{8,0},{9,3},... | collective-permute-start | bytes 221192 | tf_op jit(solution)/shard_map/ppermute | solution.py:535
  9.3 8.4 %collective-permute-start.4 = (bf16[144,256]{1,0:T(8,128)(2,1)}, bf16[144,256]{1,0:T(8,128)(2,1)S(1)}, u32[]{:S(2)}, u32[]{:S(2)}) collective-permute-start(bf16[144,256]{1,0:T(8,128)(2,1)} %get-tuple-element.56), channel_id=1, source_target_pairs={{0,12},{1,15},{2,14},{3,13},{4,8},{5,11},{6,10},{7,9},{8,4},{9,7},... | collective-permute-start | bytes 221192 | tf_op jit(solution)/shard_map/ppermute | solution.py:535
  10.6 7.0 %collective-permute-start.5 = (bf16[144,256]{1,0:T(8,128)(2,1)}, bf16[144,256]{1,0:T(8,128)(2,1)S(1)}, u32[]{:S(2)}, u32[]{:S(2)}) collective-permute-start(bf16[144,256]{1,0:T(8,128)(2,1)} %get-tuple-element.57), channel_id=1, source_target_pairs={{0,4},{2,6},{4,0},{6,2},{8,12},{10,14},{12,8},{14,10},{1,5},{3,7},... | collective-permute-start | bytes 221192 | tf_op jit(solution)/shard_map/ppermute | solution.py:533
  10.9 11.0 %collective-permute-start.6 = (bf16[144,256]{1,0:T(8,128)(2,1)S(1)}, bf16[144,256]{1,0:T(8,128)(2,1)S(1)}, u32[]{:S(2)}, u32[]{:S(2)}) collective-permute-start(bf16[144,256]{1,0:T(8,128)(2,1)S(1)} %collective-permute-done.2), channel_id=1, source_target_pairs={{0,8},{1,11},{2,10},{3,9},{4,12},{5,15},{6,14},{7,13},{8,0},{9,3},... | collective-permute-start | bytes 221192 | tf_op jit(solution)/shard_map/ppermute | solution.py:535
  13.7 8.3 %collective-permute-start.7 = (bf16[144,256]{1,0:T(8,128)(2,1)S(1)}, bf16[144,256]{1,0:T(8,128)(2,1)S(1)}, u32[]{:S(2)}, u32[]{:S(2)}) collective-permute-start(bf16[144,256]{1,0:T(8,128)(2,1)S(1)} %collective-permute-done.3), channel_id=1, source_target_pairs={{0,12},{1,15},{2,14},{3,13},{4,8},{5,11},{6,10},{7,9},{8,4},{9,7},... | collective-permute-start | bytes 221192 | tf_op jit(solution)/shard_map/ppermute | solution.py:535
  15.0 8.3 %collective-permute-start.8 = (bf16[144,256]{1,0:T(8,128)(2,1)}, bf16[144,256]{1,0:T(8,128)(2,1)S(1)}, u32[]{:S(2)}, u32[]{:S(2)}) collective-permute-start(bf16[144,256]{1,0:T(8,128)(2,1)} %get-tuple-element.60), channel_id=1, source_target_pairs={{0,6},{2,4},{4,2},{6,0},{8,14},{10,12},{12,10},{14,8},{1,7},{3,5},... | collective-permute-start | bytes 221192 | tf_op jit(solution)/shard_map/ppermute | solution.py:533
  16.7 0.9 %copy-start.3 = (bf16[144,256]{1,0:T(8,128)(2,1)S(1)}, bf16[144,256]{1,0:T(8,128)(2,1)}, u32[]{:S(2)}) copy-start(bf16[144,256]{1,0:T(8,128)(2,1)} %get-tuple-element.48.source_ref) | copy-start | bytes 221188
  25.6 14.3 %copy-start.4 = (s32[128,8]{0,1:T(8,128)S(1)}, s32[128,8]{0,1:T(8,128)}, u32[]{:S(2)}) copy-start(s32[128,8]{0,1:T(8,128)} %param.11) | copy-start | bytes 12292
  25.6 14.3 %copy-start.5 = (s32[8,128]{1,0:T(8,128)S(1)}, s32[8,128]{1,0:T(8,128)}, u32[]{:S(2)}) copy-start(s32[8,128]{1,0:T(8,128)} %get-tuple-element.46.slot_ref) | copy-start | bytes 12292
  25.6 14.3 %copy-start.6 = (f32[8,128]{1,0:T(8,128)S(1)}, f32[8,128]{1,0:T(8,128)}, u32[]{:S(2)}) copy-start(f32[8,128]{1,0:T(8,128)} %get-tuple-element.47.gates_ref) | copy-start | bytes 12292
  25.6 4.4 %collective-permute-start.14 = (bf16[1536,384]{1,0:T(8,128)(2,1)S(1)}, bf16[1536,384]{1,0:T(8,128)(2,1)S(1)}, u32[]{:S(2)}, u32[]{:S(2)}) collective-permute-start(bf16[1536,384]{1,0:T(8,128)(2,1)S(1)} %other_half.1), channel_id=1, source_target_pairs={{0,1},{1,0},{2,3},{3,2},{4,5},{5,4},{6,7},{7,6},{8,9},{9,8},{10,11... | collective-permute-start | bytes 3538952 | tf_op jit(solution)/shard_map/ppermute | solution.py:539
  25.7 11.6 %collective-permute-start.9 = (bf16[160,256]{1,0:T(8,128)(2,1)S(1)}, bf16[160,256]{1,0:T(8,128)(2,1)S(1)}, u32[]{:S(2)}, u32[]{:S(2)}) collective-permute-start(bf16[160,256]{1,0:T(8,128)(2,1)S(1)} %get-tuple-element.62), channel_id=1, source_target_pairs={{0,8},{1,11},{2,10},{3,9},{4,12},{5,15},{6,14},{7,13},{8,0},{9,3},... | collective-permute-start | bytes 245768 | tf_op jit(solution)/shard_map/ppermute | solution.py:535
  28.6 8.8 %collective-permute-start.10 = (bf16[160,256]{1,0:T(8,128)(2,1)S(1)}, bf16[160,256]{1,0:T(8,128)(2,1)S(1)}, u32[]{:S(2)}, u32[]{:S(2)}) collective-permute-start(bf16[160,256]{1,0:T(8,128)(2,1)S(1)} %get-tuple-element.63), channel_id=1, source_target_pairs={{0,12},{1,15},{2,14},{3,13},{4,8},{5,11},{6,10},{7,9},{8,4},{9,7},... | collective-permute-start | bytes 245768 | tf_op jit(solution)/shard_map/ppermute | solution.py:535
  28.8 4.9 %collective-permute-start.11 = (bf16[80,256]{1,0:T(8,128)(2,1)S(1)}, bf16[80,256]{1,0:T(8,128)(2,1)S(1)}, u32[]{:S(2)}, u32[]{:S(2)}) collective-permute-start(bf16[80,256]{1,0:T(8,128)(2,1)S(1)} %get-tuple-element.64), channel_id=1, source_target_pairs={{0,2},{2,0},{4,6},{6,4},{8,10},{10,8},{12,14},{14,12},{1,3},{3,1},... | collective-permute-start | bytes 122888 | tf_op jit(solution)/shard_map/ppermute | solution.py:533
  29.9 6.3 %collective-permute-start.12 = (bf16[80,256]{1,0:T(8,128)(2,1)S(1)}, bf16[80,256]{1,0:T(8,128)(2,1)S(1)}, u32[]{:S(2)}, u32[]{:S(2)}) collective-permute-start(bf16[80,256]{1,0:T(8,128)(2,1)S(1)} %get-tuple-element.65), channel_id=1, source_target_pairs={{0,4},{2,6},{4,0},{6,2},{8,12},{10,14},{12,8},{14,10},{1,5},{3,7},... | collective-permute-start | bytes 122888 | tf_op jit(solution)/shard_map/ppermute | solution.py:533
  30.1 7.3 %collective-permute-start.13 = (bf16[80,256]{1,0:T(8,128)(2,1)S(1)}, bf16[80,256]{1,0:T(8,128)(2,1)S(1)}, u32[]{:S(2)}, u32[]{:S(2)}) collective-permute-start(bf16[80,256]{1,0:T(8,128)(2,1)S(1)} %get-tuple-element.66), channel_id=1, source_target_pairs={{0,6},{2,4},{4,2},{6,0},{8,14},{10,12},{12,10},{14,8},{1,7},{3,5},... | collective-permute-start | bytes 122888 | tf_op jit(solution)/shard_map/ppermute | solution.py:533
  37.4 1.3 %collective-permute-start.15 = (bf16[160,256]{1,0:T(8,128)(2,1)S(1)}, bf16[160,256]{1,0:T(8,128)(2,1)S(1)}, u32[]{:S(2)}, u32[]{:S(2)}) collective-permute-start(bf16[160,256]{1,0:T(8,128)(2,1)S(1)} %collective-permute-done.9.refs_4_), channel_id=1, source_target_pairs={{0,1},{1,0},{2,3},{3,2},{4,5},{5,4},{6,7},{7,6},{8,9},{9,8},{10,11... | collective-permute-start | bytes 245768 | tf_op jit(solution)/shard_map/ppermute | solution.py:539
  38.6 1.3 %collective-permute-start.16 = (bf16[160,256]{1,0:T(8,128)(2,1)S(1)}, bf16[160,256]{1,0:T(8,128)(2,1)S(1)}, u32[]{:S(2)}, u32[]{:S(2)}) collective-permute-start(bf16[160,256]{1,0:T(8,128)(2,1)S(1)} %collective-permute-done.10.refs_5_), channel_id=1, source_target_pairs={{0,1},{1,0},{2,3},{3,2},{4,5},{5,4},{6,7},{7,6},{8,9},{9,8},{10,11... | collective-permute-start | bytes 245768 | tf_op jit(solution)/shard_map/ppermute | solution.py:539

commit v13 on v10

--- a/solution.py
+++ b/solution.py
@@ -408,13 +408,12 @@
     product = jnp.concatenate(
         [product, jnp.zeros((width - product.shape[0], product.shape[1]), F32)], axis=0
     )
+    high = product.astype(BF)
+    low = (product - high.astype(F32)).astype(BF)
+    ones = jnp.ones((8, product.shape[1]), BF)
     gate_lanes = lax.dot_general(
-        jnp.ones((8, product.shape[1]), F32),
-        product,
-        CONTRACT_COLS,
-        preferred_element_type=F32,
-        precision=lax.Precision.HIGHEST,
-    )
+        ones, high, CONTRACT_COLS, preferred_element_type=F32
+    ) + lax.dot_general(ones, low, CONTRACT_COLS, preferred_element_type=F32)
     trow = iota((main_rows, 2 * experts), 0)
     tcol = iota((main_rows, 2 * experts), 1)
     inner = jnp.bitwise_and(trow, MAIN - 1)
@@ -465,50 +464,76 @@
         out_ref[...] = (parts[n].astype(BF).astype(F32) + came).astype(BF)
 
 
-def combine_kernel(ids_ref, slot_ref, gates_ref, *refs):
-    token_ref, grad_ref = refs[-2:]
-    doubles = 2 + len(BASES)
-    ret_views = [(refs[0], 0), (refs[1], 0)]
-    for kept_ref, given_ref in zip(refs[2:doubles], refs[doubles:-2]):
-        ret_views += [(kept_ref, 0), (given_ref, BACK_ROWS)]
+def combine_chunks(chunks, views, ids_ref, slot_ref, gates_ref):
     topk, tokens = ids_ref.shape
-    experts = len(ret_views)
-    width = refs[0].shape[1]
-    ids = ids_ref[...]
-    slot = slot_ref[...]
+    experts = slot_ref.shape[0]
+    width = views[0][0].shape[1]
+    slot = jnp.concatenate([slot_ref[c : c + 1] for c in chunks], axis=0)
     slot16 = repeat_rows(slot, MAIN)
     inner = jnp.bitwise_and(iota(slot16.shape, 0), MAIN - 1)
     onehot = mask(slot16 == inner)
     wanted = MAIN + jnp.right_shift(inner, 2)
     last = jnp.where(jnp.logical_and(slot16 == wanted, inner < 8), 1.0, 0.0)
     quarter = jnp.bitwise_and(inner, 3)
-    tails = [ref[first + BACK_ROWS - 16 : first + BACK_ROWS, :] for ref, first in ret_views]
+    tails = [ref[first + BACK_ROWS - 16 : first + BACK_ROWS, :] for ref, first in views]
     tail = jnp.concatenate(tails, axis=0)
+    totals = []
     for q in range(QUARTERS):
         main = jnp.concatenate(
-            [ref[first + q * MAIN : first + (q + 1) * MAIN, :] for ref, first in ret_views], axis=0
+            [ref[first + q * MAIN : first + (q + 1) * MAIN, :] for ref, first in views], axis=0
         )
         place = jnp.where(quarter == q, last, 0.0).astype(BF)
         total = lax.dot_general(onehot, main, CONTRACT_ROWS, preferred_element_type=F32)
         total += lax.dot_general(place, tail, CONTRACT_ROWS, preferred_element_type=F32)
-        token_ref[:, q * width : (q + 1) * width] = total.astype(BF)
+        totals.append(total)
     lane_index = iota((width, tokens), 0)
-    found = []
-    for c in range(experts):
-        mine = slot[c : c + 1]
+    expert_row = partners(experts, tokens)
+    by_choice = jnp.zeros((topk, tokens), F32)
+    for place, c in enumerate(chunks):
+        mine = slot[place : place + 1]
         lane = jnp.where(mine < MAIN, c * MAIN + mine, experts * MAIN + 2 * c + mine - MAIN)
         lane = jnp.where(mine < 0, -1, lane)
-        sums = jnp.dot(tails[c], mask(lane_index == lane), preferred_element_type=F32)
-        found.append(sums[8:9])
-    found = jnp.concatenate(found, axis=0)
-    kept = slot >= 0
-    grads = jnp.where(kept, found / jnp.where(kept, gates_ref[...], 1.0), 0.0)
-    expert_row = partners(experts, tokens)
-    by_choice = [
-        jnp.sum(jnp.where(expert_row == ids[k : k + 1], grads, 0.0), axis=0, keepdims=True)
-        for k in range(topk)
-    ]
-    grad_ref[...] = jnp.concatenate(by_choice, axis=0).astype(BF)
+        sums = jnp.dot(tails[place], mask(lane_index == lane), preferred_element_type=F32)
+        kept = mine >= 0
+        grad = jnp.where(kept, sums[8:9] / jnp.where(kept, gates_ref[c : c + 1], 1.0), 0.0)
+        by_choice += jnp.where(ids_ref[...] == expert_row[c : c + 1], grad, 0.0)
+    return totals, by_choice
+
+
+LAST = 3
+
+
+def combine_kernel(ids_ref, slot_ref, gates_ref, *refs):
+    token_ref, grad_ref = refs[-2:]
+    singles = [(refs[0], 0), (refs[1], 0)]
+    kept_refs = refs[2 : 2 + len(BASES)]
+    given_refs = refs[2 + len(BASES) : -2]
+    views = dict(enumerate(singles))
+    for d, ref in enumerate(kept_refs):
+        views[2 + 2 * d] = (ref, 0)
+    for d, ref in enumerate(given_refs):
+        views[LAST + 2 + 2 * d] = (ref, BACK_ROWS)
+    chunks = sorted(views)
+    totals, by_choice = combine_chunks(
+        chunks, [views[c] for c in chunks], ids_ref, slot_ref, gates_ref
+    )
+    width = totals[0].shape[1]
+    for q, total in enumerate(totals):
+        token_ref[:, q * width : (q + 1) * width] = total
+    grad_ref[...] = by_choice
+
+
+def combine_last_kernel(
+    ids_ref, slot_ref, gates_ref, given_ref, token_sum_ref, grad_sum_ref, token_ref, grad_ref
+):
+    totals, by_choice = combine_chunks(
+        [LAST], [(given_ref, BACK_ROWS)], ids_ref, slot_ref, gates_ref
+    )
+    width = totals[0].shape[1]
+    for q, total in enumerate(totals):
+        cols = slice(q * width, (q + 1) * width)
+        token_ref[:, cols] = (token_sum_ref[:, cols] + total).astype(BF)
+    grad_ref[...] = (grad_sum_ref[...] + by_choice).astype(BF)
 
 
 def local_call(kernel, outs, arrays, name, flops, moved, space=pltpu.VMEM, scratch=(), limit=16):
@@ -621,14 +646,22 @@
         1,
     )
     kept[0], near, shares = lax.optimization_barrier((kept[0], near, shares))
-    returned = [backs[0], near, *kept, *map(to_twin, kept)]
+    routes = [expert_ids.T, slot, gates]
+    sums = local_call(
+        combine_kernel,
+        [((token_count, model_width), F32), ((topk, token_count), F32)],
+        [*routes, backs[0], near, *kept, *map(to_twin, kept[1:])],
+        "combine",
+        1,
+        1,
+    )
     token_grad, gate_grad = local_call(
-        combine_kernel,
+        combine_last_kernel,
         [((token_count, model_width), BF), ((topk, token_count), BF)],
-        [expert_ids.T, slot, gates, *returned],
-        "combine",
-        2 * served * token_count * model_width,
-        2 * 2 * token_count * model_width,
+        [*routes, to_twin(kept[0]), *sums],
+        "combine_last",
+        1,
+        1,
     )
     return (token_grad, gate_grad.T, shares[0][None], shares[1][None], shares[2][None])
 

time: 39.8 us -> 39.7 us (level)
    ppermute x7, waiting for transfers between devices: 1.15 us -> 0.74 us  [to_twin(): return lax.ppermute(chunk, 'replica', [(0, 1), (1, 0)])]
    pallas_call x6 -> x7, Pallas kernels: 7.16 us -> 7.43 us  [local_call(): pl.pallas_call(kernel, out_shape=[jax.ShapeDtypeStruct(shape, kind) for s...]
  transfers between devices with their start and end apart: 18 -> 18, of which waited for: 6 -> 6; matrix products, arithmetic and copies ran while one was open for 0% -> 0% of each run, Pallas kernels for 3% -> 4%
where the time goes in v13:
time: 39.7 us; the launch traced here: 39.5 us
  starting transfers between devices  21.1 us (53%)
  waiting for transfers between devices  9.3 us (23%)
  Pallas kernels  7.43 us (19%)
  local copies, waits for them, and re-layouts  0.91 us (2%)
  between operations  0.77 us (2%)
    ppermute x9, starting transfers between devices, to_step(): return lax.ppermute(chunk, ('expert', 'replica'), pairs)  15 us
    ppermute x9, waiting for transfers between devices, to_step(): return lax.ppermute(chunk, ('expert', 'replica'), pairs)  8.55 us
    pallas_call x7, Pallas kernels, local_call(): pl.pallas_call(kernel, out_shape=[jax.ShapeDtypeStruct(shape, kind) for s...  7.43 us
    ppermute x2, starting transfers between devices, to_step(): return lax.ppermute(chunk, 'expert', [(i, i ^ 1) for i in range(experts)])  3.56 us
    ppermute x7, starting transfers between devices, to_twin(): return lax.ppermute(chunk, 'replica', [(0, 1), (1, 0)])  2.55 us
    unnamed x14, local copies, waits for them, and re-layouts  0.91 us
  transfers between devices with their start and end apart: 18, of which 6 were waited for; matrix products, arithmetic and copies ran while one was open for 0% of the time, Pallas kernels for 4%

profile of v13, /device:TPU:0, one launch (start us, length us, event | category | flops | bytes accessed | tf_op | source)
XLA Modules:
  0.0 39.5 jit_solution(3265174156307364296)
XLA Ops:
  0.6 0.0 copy-start
  0.6 0.0 copy-start.1
  0.7 2.5 %route.1 = (bf16[144,256]{1,0:T(8,128)(2,1)}, bf16[144,256]{1,0:T(8,128)(2,1)}, bf16[144,256]{1,0:T(8,128)(2,1)}, bf16[144,256]{1,0:T(8,128)(2,1)}, bf16[144,256...) custom-call(s32[8]{0:T(128)} %plan_hbm.1, ...), custom_call_target="tpu_custom_call" | custom-call | flops 8000000000 | bytes 1114112 | tf_op jit(solution)/shard_map/route/pallas_call | solution.py:541
  3.1 0.5 %collective-permute-start.2 = (bf16[144,256]{1,0:T(8,128)(2,1)}, bf16[144,256]{1,0:T(8,128)(2,1)S(1)}, u32[]{:S(2)}, u32[]{:S(2)}) collective-permute-start(bf16[144,256]{1,0:T(8,128)(2,1)} %get-tuple-element.46), channel_id=1, source_target_pairs={{0,1},{1,0},{2,3},{3,2},{4,5},{5,4},{6,7},{7,6},{8,9},{9,8},{10,11... | collective-permute-start | bytes 221192 | tf_op jit(solution)/shard_map/ppermute | solution.py:562
  3.7 0.1 collective-permute-start.3
  3.7 0.4 %collective-permute-start.4 = (bf16[144,256]{1,0:T(8,128)(2,1)}, bf16[144,256]{1,0:T(8,128)(2,1)S(1)}, u32[]{:S(2)}, u32[]{:S(2)}) collective-permute-start(bf16[144,256]{1,0:T(8,128)(2,1)} %get-tuple-element.48), channel_id=1, source_target_pairs={{0,1},{1,0},{2,3},{3,2},{4,5},{5,4},{6,7},{7,6},{8,9},{9,8},{10,11... | collective-permute-start | bytes 221192 | tf_op jit(solution)/shard_map/ppermute | solution.py:562
  4.2 2.6 %collective-permute-start = (bf16[144,256]{1,0:T(8,128)(2,1)}, bf16[144,256]{1,0:T(8,128)(2,1)S(1)}, u32[]{:S(2)}, u32[]{:S(2)}) collective-permute-start(bf16[144,256]{1,0:T(8,128)(2,1)} %get-tuple-element.44), channel_id=1, source_target_pairs={{0,2},{2,0},{4,6},{6,4},{8,10},{10,8},{12,14},{14,12},{1,3},{3,1},... | collective-permute-start | bytes 221192 | tf_op jit(solution)/shard_map/ppermute | solution.py:556
  6.7 2.6 %collective-permute-start.1 = (bf16[144,256]{1,0:T(8,128)(2,1)}, bf16[144,256]{1,0:T(8,128)(2,1)S(1)}, u32[]{:S(2)}, u32[]{:S(2)}) collective-permute-start(bf16[144,256]{1,0:T(8,128)(2,1)} %get-tuple-element.45), channel_id=1, source_target_pairs={{0,8},{1,11},{2,10},{3,9},{4,12},{5,15},{6,14},{7,13},{8,0},{9,3},... | collective-permute-start | bytes 221192 | tf_op jit(solution)/shard_map/ppermute | solution.py:558
  9.3 0.0 collective-permute-done.2
  9.3 1.6 %collective-permute-start.6 = (bf16[144,256]{1,0:T(8,128)(2,1)}, bf16[144,256]{1,0:T(8,128)(2,1)S(1)}, u32[]{:S(2)}, u32[]{:S(2)}) collective-permute-start(bf16[144,256]{1,0:T(8,128)(2,1)} %get-tuple-element.51), channel_id=1, source_target_pairs={{0,4},{1,7},{2,6},{3,5},{4,0},{5,3},{6,2},{7,1},{8,12},{9,15},{10,... | collective-permute-start | bytes 221192 | tf_op jit(solution)/shard_map/ppermute | solution.py:558
  10.9 0.0 collective-permute-done.3
  10.9 0.0 collective-permute-done.4
  10.9 0.2 collective-permute-start.5
  11.1 1.7 %collective-permute-start.7 = (bf16[144,256]{1,0:T(8,128)(2,1)S(1)}, bf16[144,256]{1,0:T(8,128)(2,1)S(1)}, u32[]{:S(2)}, u32[]{:S(2)}) collective-permute-start(bf16[144,256]{1,0:T(8,128)(2,1)S(1)} %collective-permute-done.2), channel_id=1, source_target_pairs={{0,8},{1,11},{2,10},{3,9},{4,12},{5,15},{6,14},{7,13},{8,0},{9,3},... | collective-permute-start | bytes 221192 | tf_op jit(solution)/shard_map/ppermute | solution.py:558
  12.8 0.0 collective-permute-done.refs_1_
  12.8 2.5 %collective-permute-start.8 = (bf16[144,256]{1,0:T(8,128)(2,1)S(1)}, bf16[144,256]{1,0:T(8,128)(2,1)S(1)}, u32[]{:S(2)}, u32[]{:S(2)}) collective-permute-start(bf16[144,256]{1,0:T(8,128)(2,1)S(1)} %collective-permute-done.4), channel_id=1, source_target_pairs={{0,4},{1,7},{2,6},{3,5},{4,0},{5,3},{6,2},{7,1},{8,12},{9,15},{10,... | collective-permute-start | bytes 221192 | tf_op jit(solution)/shard_map/ppermute | solution.py:558
  15.3 0.0 collective-permute-done.1.refs_2_
  15.3 2.0 %collective-permute-start.9 = (bf16[144,256]{1,0:T(8,128)(2,1)S(1)}, bf16[144,256]{1,0:T(8,128)(2,1)S(1)}, u32[]{:S(2)}, u32[]{:S(2)}) collective-permute-start(bf16[144,256]{1,0:T(8,128)(2,1)S(1)} %collective-permute-done.3), channel_id=1, source_target_pairs={{0,12},{1,15},{2,14},{3,13},{4,8},{5,11},{6,10},{7,9},{8,4},{9,7},... | collective-permute-start | bytes 221192 | tf_op jit(solution)/shard_map/ppermute | solution.py:558
  17.4 0.9 %copy-done.3 = bf16[144,256]{1,0:T(8,128)(2,1)S(1)} copy-done((bf16[144,256]{1,0:T(8,128)(2,1)S(1)}, bf16[144,256]{1,0:T(8,128)(2,1)}, u32[]{:S(2)}) %copy-start.3) | copy-done | bytes 73752
  18.2 0.0 collective-permute-done.6.refs_4_
  18.3 0.0 collective-permute-done.5.refs_3_
  18.3 2.0 %collective-permute-done.7.refs_5_ = bf16[144,256]{1,0:T(8,128)(2,1)S(1)} collective-permute-done((bf16[144,256]{1,0:T(8,128)(2,1)S(1)}, bf16[144,256]{1,0:T(8,128)(2,1)S(1)}, u32[]{:S(2)}, u32[]{:S(2)}) %collective-permute-start.7) | collective-permute-done | bytes 73760 | tf_op jit(solution)/shard_map/ppermute | solution.py:558
  20.3 0.0 collective-permute-done.8.refs_6_
  20.3 1.7 %collective-permute-done.9.refs_7_ = bf16[144,256]{1,0:T(8,128)(2,1)S(1)} collective-permute-done((bf16[144,256]{1,0:T(8,128)(2,1)S(1)}, bf16[144,256]{1,0:T(8,128)(2,1)S(1)}, u32[]{:S(2)}, u32[]{:S(2)}) %collective-permute-start.9) | collective-permute-done | bytes 73760 | tf_op jit(solution)/shard_map/ppermute | solution.py:558
  22.0 1.5 %expert_rows.1 = (bf16[80,256]{1,0:T(8,128)(2,1)S(1)}, bf16[80,256]{1,0:T(8,128)(2,1)S(1)}, bf16[160,256]{1,0:T(8,128)(2,1)S(1)}, bf16[160,256]{1,0:T(8,128)(2,1...) custom-call(bf16[144,256]{1,0:T(8,128)(2,1)S(1)} %hold.1.refs_0_, ...), custom_call_target="tpu_custom_call" | custom-call | flops 566231040 | bytes 2359296 | tf_op jit(solution)/shard_map/expert_rows/pallas_call | solution.py:541
  23.5 0.6 %other_half.1 = bf16[1536,384]{1,0:T(8,128)(2,1)S(1)} custom-call(bf16[144,1024]{1,0:T(8,128)(2,1)S(1)} %get-tuple-element.57.x_ref, bf16[144,1024]{1,0:T(8,128)(2,1)S(1)} %get-tuple-element.58.s_ref, bf16[144,384]{1,0:T(8,128)(2,1)S(1)} %get-tuple-element.59.dg_ref, bf16[144,384]{1,0:T(8,128)(2,1)S(1)} %get-tuple-element.60.du_ref, ...), custom_call_target="tpu_custom_call" | custom-call | flops 1 | bytes 1 | tf_op jit(solution)/shard_map/other_half/pallas_call | solution.py:541
  24.2 0.0 copy-start.4
  24.2 0.8 %collective-permute-start.12 = (bf16[1536,384]{1,0:T(8,128)(2,1)S(1)}, bf16[1536,384]{1,0:T(8,128)(2,1)S(1)}, u32[]{:S(2)}, u32[]{:S(2)}) collective-permute-start(bf16[1536,384]{1,0:T(8,128)(2,1)S(1)} %other_half.1), channel_id=1, source_target_pairs={{0,1},{1,0},{2,3},{3,2},{4,5},{5,4},{6,7},{7,6},{8,9},{9,8},{10,11... | collective-permute-start | bytes 3538952 | tf_op jit(solution)/shard_map/ppermute | solution.py:562
  25.0 3.0 %collective-permute-start.14 = (bf16[160,256]{1,0:T(8,128)(2,1)S(1)}, bf16[160,256]{1,0:T(8,128)(2,1)S(1)}, u32[]{:S(2)}, u32[]{:S(2)}) collective-permute-start(bf16[160,256]{1,0:T(8,128)(2,1)S(1)} %get-tuple-element.68), channel_id=1, source_target_pairs={{0,12},{1,15},{2,14},{3,13},{4,8},{5,11},{6,10},{7,9},{8,4},{9,7},... | collective-permute-start | bytes 245768 | tf_op jit(solution)/shard_map/ppermute | solution.py:558
  28.0 1.2 %collective-permute-start.15 = (bf16[160,256]{1,0:T(8,128)(2,1)S(1)}, bf16[160,256]{1,0:T(8,128)(2,1)S(1)}, u32[]{:S(2)}, u32[]{:S(2)}) collective-permute-start(bf16[160,256]{1,0:T(8,128)(2,1)S(1)} %get-tuple-element.69), channel_id=1, source_target_pairs={{0,4},{1,7},{2,6},{3,5},{4,0},{5,3},{6,2},{7,1},{8,12},{9,15},{10,... | collective-permute-start | bytes 245768 | tf_op jit(solution)/shard_map/ppermute | solution.py:558
  29.3 0.1 collective-permute-start.10
  29.4 1.0 %collective-permute-start.11 = (bf16[80,256]{1,0:T(8,128)(2,1)S(1)}, bf16[80,256]{1,0:T(8,128)(2,1)S(1)}, u32[]{:S(2)}, u32[]{:S(2)}) collective-permute-start(bf16[80,256]{1,0:T(8,128)(2,1)S(1)} %get-tuple-element.56), channel_id=1, source_target_pairs={{0,2},{2,0},{4,6},{6,4},{8,10},{10,8},{12,14},{14,12},{1,3},{3,1},... | collective-permute-start | bytes 122888 | tf_op jit(solution)/shard_map/ppermute | solution.py:556
  30.4 1.6 %collective-permute-done.14.refs_3_ = bf16[160,256]{1,0:T(8,128)(2,1)S(1)} collective-permute-done((bf16[160,256]{1,0:T(8,128)(2,1)S(1)}, bf16[160,256]{1,0:T(8,128)(2,1)S(1)}, u32[]{:S(2)}, u32[]{:S(2)}) %collective-permute-start.14) | collective-permute-done | bytes 81952 | tf_op jit(solution)/shard_map/ppermute | solution.py:558
  32.0 0.0 collective-permute-start.16
  32.0 1.5 %collective-permute-done.15.refs_4_ = bf16[160,256]{1,0:T(8,128)(2,1)S(1)} collective-permute-done((bf16[160,256]{1,0:T(8,128)(2,1)S(1)}, bf16[160,256]{1,0:T(8,128)(2,1)S(1)}, u32[]{:S(2)}, u32[]{:S(2)}) %collective-permute-start.15) | collective-permute-done | bytes 81952 | tf_op jit(solution)/shard_map/ppermute | solution.py:558
  33.5 0.6 %collective-permute-start.17 = (bf16[160,256]{1,0:T(8,128)(2,1)S(1)}, bf16[160,256]{1,0:T(8,128)(2,1)S(1)}, u32[]{:S(2)}, u32[]{:S(2)}) collective-permute-start(bf16[160,256]{1,0:T(8,128)(2,1)S(1)} %collective-permute-done.15.refs_4_), channel_id=1, source_target_pairs={{0,1},{1,0},{2,3},{3,2},{4,5},{5,4},{6,7},{7,6},{8,9},{9,8},{10,11... | collective-permute-start | bytes 245768 | tf_op jit(solution)/shard_map/ppermute | solution.py:562
  34.1 0.0 collective-permute-done.12.came_ref
  34.1 1.4 %own_half.1 = (bf16[512,384]{1,0:T(8,128)(2,1)}, bf16[512,384]{1,0:T(8,128)(2,1)}, bf16[512,384]{1,0:T(8,128)(2,1)}) custom-call(bf16[144,1024]{1,0:T(8,128)(2,1)S(1)} %get-tuple-element.57.x_ref, bf16[144,1024]{1,0:T(8,128)(2,1)S(1)} %get-tuple-element.58.s_ref, bf16[144,384]{1,0:T(8,128)(2,1)S(1)} %get-tuple-element.59.dg_ref, ...), custom_call_target="tpu_custom_call" | custom-call | flops 1 | bytes 1 | tf_op jit(solution)/shard_map/own_half/pallas_call | solution.py:541
  35.5 0.0 collective-permute-done.11.refs_1_
  35.5 1.7 %collective-permute-done.10.refs_2_ = bf16[160,256]{1,0:T(8,128)(2,1)S(1)} collective-permute-done((bf16[160,256]{1,0:T(8,128)(2,1)S(1)}, bf16[160,256]{1,0:T(8,128)(2,1)S(1)}, u32[]{:S(2)}, u32[]{:S(2)}) %collective-permute-start.10) | collective-permute-done | bytes 81952 | tf_op jit(solution)/shard_map/ppermute | solution.py:558
  37.2 0.1 collective-permute-start.13
  37.3 0.0 collective-permute-done.16.refs_5_
  37.3 0.0 collective-permute-done.17.refs_6_
  37.3 0.0 copy-done.5
  37.3 0.0 copy-done.6
  37.3 0.4 combine.1
  37.7 0.7 %collective-permute-done.13.given_ref = bf16[160,256]{1,0:T(8,128)(2,1)S(1)} collective-permute-done((bf16[160,256]{1,0:T(8,128)(2,1)S(1)}, bf16[160,256]{1,0:T(8,128)(2,1)S(1)}, u32[]{:S(2)}, u32[]{:S(2)}) %collective-permute-start.13) | collective-permute-done | bytes 81952 | tf_op jit(solution)/shard_map/ppermute | solution.py:562
  38.5 1.0 %combine_last.1 = (bf16[128,1024]{1,0:T(8,128)(2,1)}, bf16[8,128]{1,0:T(8,128)(2,1)}) custom-call(s32[8,128]{1,0:T(8,128)S(1)} %bitcast.15, s32[8,128]{1,0:T(8,128)S(1)} %copy-done.5, f32[8,128]{1,0:T(8,128)S(1)} %copy-done.6, bf16[160,256]{1,0:T(8,128)(2,1)S(1)} %collective-permute-done.13.given_ref, f32[128,1024]{1,0:T(8,128)S(1)} %get-tuple-element.70.token_sum_ref, ...), custom_call_target="tpu_custom_call" | custom-call | flops 1 | bytes 1 | tf_op jit(solution)/shard_map/combine_last/pallas_call | solution.py:541
  (9 shorter events, 0.0 us)
Async XLA Ops:
  0.6 21.4 %copy-start = (bf16[1,1024,384]{2,1,0:T(8,128)(2,1)S(1)}, bf16[1,1024,384]{2,1,0:T(8,128)(2,1)}, u32[]{:S(2)}) copy-start(bf16[1,1024,384]{2,1,0:T(8,128)(2,1)} %param.15) | copy-start | bytes 2359300
  0.6 21.4 %copy-start.1 = (bf16[1,1024,384]{2,1,0:T(8,128)(2,1)S(1)}, bf16[1,1024,384]{2,1,0:T(8,128)(2,1)}, u32[]{:S(2)}) copy-start(bf16[1,1024,384]{2,1,0:T(8,128)(2,1)} %param.16) | copy-start | bytes 2359300
  0.7 21.4 %copy-start.2 = (bf16[1,1024,384]{2,1,0:T(8,128)(2,1)S(1)}, bf16[1,1024,384]{2,1,0:T(8,128)(2,1)}, u32[]{:S(2)}) copy-start(bf16[1,1024,384]{2,1,0:T(8,128)(2,1)} %param.17) | copy-start | bytes 2359300
  3.1 6.2 %collective-permute-start.2 = (bf16[144,256]{1,0:T(8,128)(2,1)}, bf16[144,256]{1,0:T(8,128)(2,1)S(1)}, u32[]{:S(2)}, u32[]{:S(2)}) collective-permute-start(bf16[144,256]{1,0:T(8,128)(2,1)} %get-tuple-element.46), channel_id=1, source_target_pairs={{0,1},{1,0},{2,3},{3,2},{4,5},{5,4},{6,7},{7,6},{8,9},{9,8},{10,11... | collective-permute-start | bytes 221192 | tf_op jit(solution)/shard_map/ppermute | solution.py:562
  3.7 7.2 %collective-permute-start.3 = (bf16[144,256]{1,0:T(8,128)(2,1)}, bf16[144,256]{1,0:T(8,128)(2,1)S(1)}, u32[]{:S(2)}, u32[]{:S(2)}) collective-permute-start(bf16[144,256]{1,0:T(8,128)(2,1)} %get-tuple-element.47), channel_id=1, source_target_pairs={{0,1},{1,0},{2,3},{3,2},{4,5},{5,4},{6,7},{7,6},{8,9},{9,8},{10,11... | collective-permute-start | bytes 221192 | tf_op jit(solution)/shard_map/ppermute | solution.py:562
  3.7 7.2 %collective-permute-start.4 = (bf16[144,256]{1,0:T(8,128)(2,1)}, bf16[144,256]{1,0:T(8,128)(2,1)S(1)}, u32[]{:S(2)}, u32[]{:S(2)}) collective-permute-start(bf16[144,256]{1,0:T(8,128)(2,1)} %get-tuple-element.48), channel_id=1, source_target_pairs={{0,1},{1,0},{2,3},{3,2},{4,5},{5,4},{6,7},{7,6},{8,9},{9,8},{10,11... | collective-permute-start | bytes 221192 | tf_op jit(solution)/shard_map/ppermute | solution.py:562
  4.2 8.7 %collective-permute-start = (bf16[144,256]{1,0:T(8,128)(2,1)}, bf16[144,256]{1,0:T(8,128)(2,1)S(1)}, u32[]{:S(2)}, u32[]{:S(2)}) collective-permute-start(bf16[144,256]{1,0:T(8,128)(2,1)} %get-tuple-element.44), channel_id=1, source_target_pairs={{0,2},{2,0},{4,6},{6,4},{8,10},{10,8},{12,14},{14,12},{1,3},{3,1},... | collective-permute-start | bytes 221192 | tf_op jit(solution)/shard_map/ppermute | solution.py:556
  6.7 8.6 %collective-permute-start.1 = (bf16[144,256]{1,0:T(8,128)(2,1)}, bf16[144,256]{1,0:T(8,128)(2,1)S(1)}, u32[]{:S(2)}, u32[]{:S(2)}) collective-permute-start(bf16[144,256]{1,0:T(8,128)(2,1)} %get-tuple-element.45), channel_id=1, source_target_pairs={{0,8},{1,11},{2,10},{3,9},{4,12},{5,15},{6,14},{7,13},{8,0},{9,3},... | collective-permute-start | bytes 221192 | tf_op jit(solution)/shard_map/ppermute | solution.py:558
  9.3 8.9 %collective-permute-start.6 = (bf16[144,256]{1,0:T(8,128)(2,1)}, bf16[144,256]{1,0:T(8,128)(2,1)S(1)}, u32[]{:S(2)}, u32[]{:S(2)}) collective-permute-start(bf16[144,256]{1,0:T(8,128)(2,1)} %get-tuple-element.51), channel_id=1, source_target_pairs={{0,4},{1,7},{2,6},{3,5},{4,0},{5,3},{6,2},{7,1},{8,12},{9,15},{10,... | collective-permute-start | bytes 221192 | tf_op jit(solution)/shard_map/ppermute | solution.py:558
  10.9 7.3 %collective-permute-start.5 = (bf16[144,256]{1,0:T(8,128)(2,1)}, bf16[144,256]{1,0:T(8,128)(2,1)S(1)}, u32[]{:S(2)}, u32[]{:S(2)}) collective-permute-start(bf16[144,256]{1,0:T(8,128)(2,1)} %get-tuple-element.50), channel_id=1, source_target_pairs={{0,12},{1,15},{2,14},{3,13},{4,8},{5,11},{6,10},{7,9},{8,4},{9,7},... | collective-permute-start | bytes 221192 | tf_op jit(solution)/shard_map/ppermute | solution.py:558
  11.1 9.1 %collective-permute-start.7 = (bf16[144,256]{1,0:T(8,128)(2,1)S(1)}, bf16[144,256]{1,0:T(8,128)(2,1)S(1)}, u32[]{:S(2)}, u32[]{:S(2)}) collective-permute-start(bf16[144,256]{1,0:T(8,128)(2,1)S(1)} %collective-permute-done.2), channel_id=1, source_target_pairs={{0,8},{1,11},{2,10},{3,9},{4,12},{5,15},{6,14},{7,13},{8,0},{9,3},... | collective-permute-start | bytes 221192 | tf_op jit(solution)/shard_map/ppermute | solution.py:558
  12.8 7.5 %collective-permute-start.8 = (bf16[144,256]{1,0:T(8,128)(2,1)S(1)}, bf16[144,256]{1,0:T(8,128)(2,1)S(1)}, u32[]{:S(2)}, u32[]{:S(2)}) collective-permute-start(bf16[144,256]{1,0:T(8,128)(2,1)S(1)} %collective-permute-done.4), channel_id=1, source_target_pairs={{0,4},{1,7},{2,6},{3,5},{4,0},{5,3},{6,2},{7,1},{8,12},{9,15},{10,... | collective-permute-start | bytes 221192 | tf_op jit(solution)/shard_map/ppermute | solution.py:558
  15.3 6.7 %collective-permute-start.9 = (bf16[144,256]{1,0:T(8,128)(2,1)S(1)}, bf16[144,256]{1,0:T(8,128)(2,1)S(1)}, u32[]{:S(2)}, u32[]{:S(2)}) collective-permute-start(bf16[144,256]{1,0:T(8,128)(2,1)S(1)} %collective-permute-done.3), channel_id=1, source_target_pairs={{0,12},{1,15},{2,14},{3,13},{4,8},{5,11},{6,10},{7,9},{8,4},{9,7},... | collective-permute-start | bytes 221192 | tf_op jit(solution)/shard_map/ppermute | solution.py:558
  17.4 0.9 %copy-start.3 = (bf16[144,256]{1,0:T(8,128)(2,1)S(1)}, bf16[144,256]{1,0:T(8,128)(2,1)}, u32[]{:S(2)}) copy-start(bf16[144,256]{1,0:T(8,128)(2,1)} %get-tuple-element.43.source_ref) | copy-start | bytes 221188
  24.2 13.1 %copy-start.4 = (s32[128,8]{0,1:T(8,128)S(1)}, s32[128,8]{0,1:T(8,128)}, u32[]{:S(2)}) copy-start(s32[128,8]{0,1:T(8,128)} %param.11) | copy-start | bytes 12292
  24.2 13.1 %copy-start.5 = (s32[8,128]{1,0:T(8,128)S(1)}, s32[8,128]{1,0:T(8,128)}, u32[]{:S(2)}) copy-start(s32[8,128]{1,0:T(8,128)} %get-tuple-element.41.slot_ref) | copy-start | bytes 12292
  24.2 13.1 %copy-start.6 = (f32[8,128]{1,0:T(8,128)S(1)}, f32[8,128]{1,0:T(8,128)}, u32[]{:S(2)}) copy-start(f32[8,128]{1,0:T(8,128)} %get-tuple-element.42.gates_ref) | copy-start | bytes 12292
  24.2 9.9 %collective-permute-start.12 = (bf16[1536,384]{1,0:T(8,128)(2,1)S(1)}, bf16[1536,384]{1,0:T(8,128)(2,1)S(1)}, u32[]{:S(2)}, u32[]{:S(2)}) collective-permute-start(bf16[1536,384]{1,0:T(8,128)(2,1)S(1)} %other_half.1), channel_id=1, source_target_pairs={{0,1},{1,0},{2,3},{3,2},{4,5},{5,4},{6,7},{7,6},{8,9},{9,8},{10,11... | collective-permute-start | bytes 3538952 | tf_op jit(solution)/shard_map/ppermute | solution.py:562
  25.0 7.0 %collective-permute-start.14 = (bf16[160,256]{1,0:T(8,128)(2,1)S(1)}, bf16[160,256]{1,0:T(8,128)(2,1)S(1)}, u32[]{:S(2)}, u32[]{:S(2)}) collective-permute-start(bf16[160,256]{1,0:T(8,128)(2,1)S(1)} %get-tuple-element.68), channel_id=1, source_target_pairs={{0,12},{1,15},{2,14},{3,13},{4,8},{5,11},{6,10},{7,9},{8,4},{9,7},... | collective-permute-start | bytes 245768 | tf_op jit(solution)/shard_map/ppermute | solution.py:558
  28.0 5.5 %collective-permute-start.15 = (bf16[160,256]{1,0:T(8,128)(2,1)S(1)}, bf16[160,256]{1,0:T(8,128)(2,1)S(1)}, u32[]{:S(2)}, u32[]{:S(2)}) collective-permute-start(bf16[160,256]{1,0:T(8,128)(2,1)S(1)} %get-tuple-element.69), channel_id=1, source_target_pairs={{0,4},{1,7},{2,6},{3,5},{4,0},{5,3},{6,2},{7,1},{8,12},{9,15},{10,... | collective-permute-start | bytes 245768 | tf_op jit(solution)/shard_map/ppermute | solution.py:558
  29.3 7.9 %collective-permute-start.10 = (bf16[160,256]{1,0:T(8,128)(2,1)S(1)}, bf16[160,256]{1,0:T(8,128)(2,1)S(1)}, u32[]{:S(2)}, u32[]{:S(2)}) collective-permute-start(bf16[160,256]{1,0:T(8,128)(2,1)S(1)} %get-tuple-element.55), channel_id=1, source_target_pairs={{0,8},{1,11},{2,10},{3,9},{4,12},{5,15},{6,14},{7,13},{8,0},{9,3},... | collective-permute-start | bytes 245768 | tf_op jit(solution)/shard_map/ppermute | solution.py:558
  29.4 6.1 %collective-permute-start.11 = (bf16[80,256]{1,0:T(8,128)(2,1)S(1)}, bf16[80,256]{1,0:T(8,128)(2,1)S(1)}, u32[]{:S(2)}, u32[]{:S(2)}) collective-permute-start(bf16[80,256]{1,0:T(8,128)(2,1)S(1)} %get-tuple-element.56), channel_id=1, source_target_pairs={{0,2},{2,0},{4,6},{6,4},{8,10},{10,8},{12,14},{14,12},{1,3},{3,1},... | collective-permute-start | bytes 122888 | tf_op jit(solution)/shard_map/ppermute | solution.py:556
  32.0 5.3 %collective-permute-start.16 = (bf16[160,256]{1,0:T(8,128)(2,1)S(1)}, bf16[160,256]{1,0:T(8,128)(2,1)S(1)}, u32[]{:S(2)}, u32[]{:S(2)}) collective-permute-start(bf16[160,256]{1,0:T(8,128)(2,1)S(1)} %collective-permute-done.14.refs_3_), channel_id=1, source_target_pairs={{0,1},{1,0},{2,3},{3,2},{4,5},{5,4},{6,7},{7,6},{8,9},{9,8},{10,11... | collective-permute-start | bytes 245768 | tf_op jit(solution)/shard_map/ppermute | solution.py:562
  33.5 3.8 %collective-permute-start.17 = (bf16[160,256]{1,0:T(8,128)(2,1)S(1)}, bf16[160,256]{1,0:T(8,128)(2,1)S(1)}, u32[]{:S(2)}, u32[]{:S(2)}) collective-permute-start(bf16[160,256]{1,0:T(8,128)(2,1)S(1)} %collective-permute-done.15.refs_4_), channel_id=1, source_target_pairs={{0,1},{1,0},{2,3},{3,2},{4,5},{5,4},{6,7},{7,6},{8,9},{9,8},{10,11... | collective-permute-start | bytes 245768 | tf_op jit(solution)/shard_map/ppermute | solution.py:562
  37.2 1.3 %collective-permute-start.13 = (bf16[160,256]{1,0:T(8,128)(2,1)S(1)}, bf16[160,256]{1,0:T(8,128)(2,1)S(1)}, u32[]{:S(2)}, u32[]{:S(2)}) collective-permute-start(bf16[160,256]{1,0:T(8,128)(2,1)S(1)} %collective-permute-done.10.refs_2_), channel_id=1, source_target_pairs={{0,1},{1,0},{2,3},{3,2},{4,5},{5,4},{6,7},{7,6},{8,9},{9,8},{10,11... | collective-permute-start | bytes 245768 | tf_op jit(solution)/shard_map/ppermute | solution.py:562

commit v14 on v13

--- a/solution.py
+++ b/solution.py
@@ -237,7 +237,7 @@
 MIB = 1024 * 1024
 
 BASES = (4, 6, 2)
-ORDER = (0, 1, 2, 4, 6, 3, 7, 5)
+ORDER = (0, 2, 1, 4, 3, 6, 5, 7)
 LONG = 8 * 10**9
 MAIN = 16
 QUARTERS = 4
@@ -607,11 +607,14 @@
     )
     recv = list(chunks)
     recv[1] = to_step(chunks[1], 1)
+    recv[2] = to_step(chunks[2], 4)
     twin = [to_twin(chunks[c]) for c in (3, 5, 7)]
-    twin, mine = lax.optimization_barrier((twin, chunks[4]))
-    for d, base in enumerate(BASES):
-        recv[2 + 2 * d] = to_step(mine if base == 6 else chunks[2 + 2 * d], base)
-        recv[3 + 2 * d] = to_step(twin[d], base)
+    recv[1], twin, mine = lax.optimization_barrier((recv[1], twin, chunks[6]))
+    recv[4] = to_step(chunks[4], 6)
+    recv[6] = to_step(mine, 2)
+    recv[3] = to_step(twin[0], 4)
+    recv[5] = to_step(twin[1], 6)
+    recv[7] = to_step(twin[2], 2)
     (held,) = local_call(hold_kernel, [(recv[0].shape, BF)], [recv[0]], "hold", 1, 1)
     matmul = 2 * served * model_width * hidden_width
     outs = local_call(

time: 39.7 us -> 40.8 us (1.028)
  waiting for transfers between devices: 9.3 us -> 10.6 us
    ppermute x7, starting transfers between devices: 2.55 us -> 1.24 us  [to_twin(): return lax.ppermute(chunk, 'replica', [(0, 1), (1, 0)])]
    ppermute x9, waiting for transfers between devices: 8.55 us -> 9.72 us  [to_step(): return lax.ppermute(chunk, ('expert', 'replica'), pairs)]
    ppermute x2, starting transfers between devices: 3.56 us -> 4.15 us  [to_step(): return lax.ppermute(chunk, 'expert', [(i, i ^ 1) for i in range(experts)])]
    ppermute x9, starting transfers between devices: 15 us -> 15.6 us  [to_step(): return lax.ppermute(chunk, ('expert', 'replica'), pairs)]
where the time goes in v14:
time: 40.8 us; the launch traced here: 40.6 us
  starting transfers between devices  20.9 us (51%)
  waiting for transfers between devices  10.6 us (26%)
  Pallas kernels  7.42 us (18%)
  local copies, waits for them, and re-layouts  0.91 us (2%)
  between operations  0.8 us (2%)
    ppermute x9, starting transfers between devices, to_step(): return lax.ppermute(chunk, ('expert', 'replica'), pairs)  15.6 us
    ppermute x9, waiting for transfers between devices, to_step(): return lax.ppermute(chunk, ('expert', 'replica'), pairs)  9.72 us
    pallas_call x7, Pallas kernels, local_call(): pl.pallas_call(kernel, out_shape=[jax.ShapeDtypeStruct(shape, kind) for s...  7.42 us
    ppermute x2, starting transfers between devices, to_step(): return lax.ppermute(chunk, 'expert', [(i, i ^ 1) for i in range(experts)])  4.15 us
    ppermute x7, starting transfers between devices, to_twin(): return lax.ppermute(chunk, 'replica', [(0, 1), (1, 0)])  1.24 us
    unnamed x14, local copies, waits for them, and re-layouts  0.91 us
    ppermute x7, waiting for transfers between devices, to_twin(): return lax.ppermute(chunk, 'replica', [(0, 1), (1, 0)])  0.84 us
  transfers between devices with their start and end apart: 18, of which 6 were waited for; matrix products, arithmetic and copies ran while one was open for 0% of the time, Pallas kernels for 4%

profile of v14, /device:TPU:0, one launch (start us, length us, event | category | flops | bytes accessed | tf_op | source)
XLA Modules:
  0.0 40.6 jit_solution(1043279412793558492)
XLA Ops:
  0.6 0.0 copy-start
  0.6 0.0 copy-start.1
  0.7 0.0 copy-start.2
  0.7 2.5 %route.1 = (bf16[144,256]{1,0:T(8,128)(2,1)}, bf16[144,256]{1,0:T(8,128)(2,1)}, bf16[144,256]{1,0:T(8,128)(2,1)}, bf16[144,256]{1,0:T(8,128)(2,1)}, bf16[144,256...) custom-call(s32[8]{0:T(128)} %plan_hbm.1, ...), custom_call_target="tpu_custom_call" | custom-call | flops 8000000000 | bytes 1114112 | tf_op jit(solution)/shard_map/route/pallas_call | solution.py:541
  3.1 3.0 %collective-permute-start.1 = (bf16[144,256]{1,0:T(8,128)(2,1)}, bf16[144,256]{1,0:T(8,128)(2,1)S(1)}, u32[]{:S(2)}, u32[]{:S(2)}) collective-permute-start(bf16[144,256]{1,0:T(8,128)(2,1)} %get-tuple-element.46), channel_id=1, source_target_pairs={{0,2},{2,0},{4,6},{6,4},{8,10},{10,8},{12,14},{14,12},{1,3},{3,1},... | collective-permute-start | bytes 221192 | tf_op jit(solution)/shard_map/ppermute | solution.py:556
  6.2 0.0 collective-permute-start.2
  6.2 0.5 %collective-permute-start.3 = (bf16[144,256]{1,0:T(8,128)(2,1)}, bf16[144,256]{1,0:T(8,128)(2,1)S(1)}, u32[]{:S(2)}, u32[]{:S(2)}) collective-permute-start(bf16[144,256]{1,0:T(8,128)(2,1)} %get-tuple-element.48), channel_id=1, source_target_pairs={{0,1},{1,0},{2,3},{3,2},{4,5},{5,4},{6,7},{7,6},{8,9},{9,8},{10,11... | collective-permute-start | bytes 221192 | tf_op jit(solution)/shard_map/ppermute | solution.py:562
  6.7 0.0 collective-permute-start.4
  6.7 2.6 %collective-permute-start = (bf16[144,256]{1,0:T(8,128)(2,1)}, bf16[144,256]{1,0:T(8,128)(2,1)S(1)}, u32[]{:S(2)}, u32[]{:S(2)}) collective-permute-start(bf16[144,256]{1,0:T(8,128)(2,1)} %get-tuple-element.45), channel_id=1, source_target_pairs={{0,8},{1,11},{2,10},{3,9},{4,12},{5,15},{6,14},{7,13},{8,0},{9,3},... | collective-permute-start | bytes 221192 | tf_op jit(solution)/shard_map/ppermute | solution.py:558
  9.3 0.0 collective-permute-done.1.refs_2_
  9.3 3.6 %collective-permute-start.5 = (bf16[144,256]{1,0:T(8,128)(2,1)}, bf16[144,256]{1,0:T(8,128)(2,1)S(1)}, u32[]{:S(2)}, u32[]{:S(2)}) collective-permute-start(bf16[144,256]{1,0:T(8,128)(2,1)} %get-tuple-element.52), channel_id=1, source_target_pairs={{0,12},{1,15},{2,14},{3,13},{4,8},{5,11},{6,10},{7,9},{8,4},{9,7},... | collective-permute-start | bytes 221192 | tf_op jit(solution)/shard_map/ppermute | solution.py:558
  12.8 0.0 collective-permute-done.2
  12.8 0.0 collective-permute-done.3
  12.8 0.0 collective-permute-done.4
  12.8 0.1 collective-permute-start.6
  12.9 0.8 %collective-permute-start.7 = (bf16[144,256]{1,0:T(8,128)(2,1)}, bf16[144,256]{1,0:T(8,128)(2,1)S(1)}, u32[]{:S(2)}, u32[]{:S(2)}) collective-permute-start(bf16[144,256]{1,0:T(8,128)(2,1)} %get-tuple-element.54), channel_id=1, source_target_pairs={{0,4},{1,7},{2,6},{3,5},{4,0},{5,3},{6,2},{7,1},{8,12},{9,15},{10,... | collective-permute-start | bytes 221192 | tf_op jit(solution)/shard_map/ppermute | solution.py:558
  13.7 3.6 %collective-permute-start.8 = (bf16[144,256]{1,0:T(8,128)(2,1)S(1)}, bf16[144,256]{1,0:T(8,128)(2,1)S(1)}, u32[]{:S(2)}, u32[]{:S(2)}) collective-permute-start(bf16[144,256]{1,0:T(8,128)(2,1)S(1)} %collective-permute-done.3), channel_id=1, source_target_pairs={{0,12},{1,15},{2,14},{3,13},{4,8},{5,11},{6,10},{7,9},{8,4},{9,7},... | collective-permute-start | bytes 221192 | tf_op jit(solution)/shard_map/ppermute | solution.py:558
  17.3 0.0 collective-permute-done.refs_1_
  17.3 0.5 %collective-permute-start.9 = (bf16[144,256]{1,0:T(8,128)(2,1)S(1)}, bf16[144,256]{1,0:T(8,128)(2,1)S(1)}, u32[]{:S(2)}, u32[]{:S(2)}) collective-permute-start(bf16[144,256]{1,0:T(8,128)(2,1)S(1)} %collective-permute-done.4), channel_id=1, source_target_pairs={{0,4},{1,7},{2,6},{3,5},{4,0},{5,3},{6,2},{7,1},{8,12},{9,15},{10,... | collective-permute-start | bytes 221192 | tf_op jit(solution)/shard_map/ppermute | solution.py:558
  17.8 0.9 %copy-done.3 = bf16[144,256]{1,0:T(8,128)(2,1)S(1)} copy-done((bf16[144,256]{1,0:T(8,128)(2,1)S(1)}, bf16[144,256]{1,0:T(8,128)(2,1)}, u32[]{:S(2)}) %copy-start.3) | copy-done | bytes 73752
  18.7 0.0 collective-permute-done.5.refs_3_
  18.7 3.0 %collective-permute-done.6.refs_4_ = bf16[144,256]{1,0:T(8,128)(2,1)S(1)} collective-permute-done((bf16[144,256]{1,0:T(8,128)(2,1)S(1)}, bf16[144,256]{1,0:T(8,128)(2,1)S(1)}, u32[]{:S(2)}, u32[]{:S(2)}) %collective-permute-start.6) | collective-permute-done | bytes 73760 | tf_op jit(solution)/shard_map/ppermute | solution.py:558
  21.7 0.0 collective-permute-done.7.refs_5_
  21.7 0.3 collective-permute-done.8.refs_6_
  22.0 1.5 %collective-permute-done.9.refs_7_ = bf16[144,256]{1,0:T(8,128)(2,1)S(1)} collective-permute-done((bf16[144,256]{1,0:T(8,128)(2,1)S(1)}, bf16[144,256]{1,0:T(8,128)(2,1)S(1)}, u32[]{:S(2)}, u32[]{:S(2)}) %collective-permute-start.9) | collective-permute-done | bytes 73760 | tf_op jit(solution)/shard_map/ppermute | solution.py:558
  23.5 0.0 copy-done
  23.5 1.5 %expert_rows.1 = (bf16[80,256]{1,0:T(8,128)(2,1)S(1)}, bf16[80,256]{1,0:T(8,128)(2,1)S(1)}, bf16[160,256]{1,0:T(8,128)(2,1)S(1)}, bf16[160,256]{1,0:T(8,128)(2,1...) custom-call(bf16[144,256]{1,0:T(8,128)(2,1)S(1)} %hold.1.refs_0_, ...), custom_call_target="tpu_custom_call" | custom-call | flops 566231040 | bytes 2359296 | tf_op jit(solution)/shard_map/expert_rows/pallas_call | solution.py:541
  25.0 0.6 %other_half.1 = bf16[1536,384]{1,0:T(8,128)(2,1)S(1)} custom-call(bf16[144,1024]{1,0:T(8,128)(2,1)S(1)} %get-tuple-element.59.x_ref, bf16[144,1024]{1,0:T(8,128)(2,1)S(1)} %get-tuple-element.60.s_ref, bf16[144,384]{1,0:T(8,128)(2,1)S(1)} %get-tuple-element.61.dg_ref, bf16[144,384]{1,0:T(8,128)(2,1)S(1)} %get-tuple-element.62.du_ref, ...), custom_call_target="tpu_custom_call" | custom-call | flops 1 | bytes 1 | tf_op jit(solution)/shard_map/other_half/pallas_call | solution.py:541
  25.7 0.0 copy-start.4
  25.7 0.1 collective-permute-start.12
  25.8 3.6 %collective-permute-start.14 = (bf16[160,256]{1,0:T(8,128)(2,1)S(1)}, bf16[160,256]{1,0:T(8,128)(2,1)S(1)}, u32[]{:S(2)}, u32[]{:S(2)}) collective-permute-start(bf16[160,256]{1,0:T(8,128)(2,1)S(1)} %get-tuple-element.70), channel_id=1, source_target_pairs={{0,12},{1,15},{2,14},{3,13},{4,8},{5,11},{6,10},{7,9},{8,4},{9,7},... | collective-permute-start | bytes 245768 | tf_op jit(solution)/shard_map/ppermute | solution.py:558
  29.4 0.0 collective-permute-start.15
  29.4 0.8 %collective-permute-start.10 = (bf16[160,256]{1,0:T(8,128)(2,1)S(1)}, bf16[160,256]{1,0:T(8,128)(2,1)S(1)}, u32[]{:S(2)}, u32[]{:S(2)}) collective-permute-start(bf16[160,256]{1,0:T(8,128)(2,1)S(1)} %get-tuple-element.57), channel_id=1, source_target_pairs={{0,8},{1,11},{2,10},{3,9},{4,12},{5,15},{6,14},{7,13},{8,0},{9,3},... | collective-permute-start | bytes 245768 | tf_op jit(solution)/shard_map/ppermute | solution.py:558
  30.2 1.1 %collective-permute-start.11 = (bf16[80,256]{1,0:T(8,128)(2,1)S(1)}, bf16[80,256]{1,0:T(8,128)(2,1)S(1)}, u32[]{:S(2)}, u32[]{:S(2)}) collective-permute-start(bf16[80,256]{1,0:T(8,128)(2,1)S(1)} %get-tuple-element.58), channel_id=1, source_target_pairs={{0,2},{2,0},{4,6},{6,4},{8,10},{10,8},{12,14},{14,12},{1,3},{3,1},... | collective-permute-start | bytes 122888 | tf_op jit(solution)/shard_map/ppermute | solution.py:556
  31.4 1.6 %collective-permute-done.14.refs_3_ = bf16[160,256]{1,0:T(8,128)(2,1)S(1)} collective-permute-done((bf16[160,256]{1,0:T(8,128)(2,1)S(1)}, bf16[160,256]{1,0:T(8,128)(2,1)S(1)}, u32[]{:S(2)}, u32[]{:S(2)}) %collective-permute-start.14) | collective-permute-done | bytes 81952 | tf_op jit(solution)/shard_map/ppermute | solution.py:558
  33.0 0.0 collective-permute-start.16
  33.0 3.3 %collective-permute-done.15.refs_4_ = bf16[160,256]{1,0:T(8,128)(2,1)S(1)} collective-permute-done((bf16[160,256]{1,0:T(8,128)(2,1)S(1)}, bf16[160,256]{1,0:T(8,128)(2,1)S(1)}, u32[]{:S(2)}, u32[]{:S(2)}) %collective-permute-start.15) | collective-permute-done | bytes 81952 | tf_op jit(solution)/shard_map/ppermute | solution.py:558
  36.3 0.6 %collective-permute-start.17 = (bf16[160,256]{1,0:T(8,128)(2,1)S(1)}, bf16[160,256]{1,0:T(8,128)(2,1)S(1)}, u32[]{:S(2)}, u32[]{:S(2)}) collective-permute-start(bf16[160,256]{1,0:T(8,128)(2,1)S(1)} %collective-permute-done.15.refs_4_), channel_id=1, source_target_pairs={{0,1},{1,0},{2,3},{3,2},{4,5},{5,4},{6,7},{7,6},{8,9},{9,8},{10,11... | collective-permute-start | bytes 245768 | tf_op jit(solution)/shard_map/ppermute | solution.py:562
  36.9 0.0 collective-permute-done.12.came_ref
  36.9 1.4 %own_half.1 = (bf16[512,384]{1,0:T(8,128)(2,1)}, bf16[512,384]{1,0:T(8,128)(2,1)}, bf16[512,384]{1,0:T(8,128)(2,1)}) custom-call(bf16[144,1024]{1,0:T(8,128)(2,1)S(1)} %get-tuple-element.59.x_ref, bf16[144,1024]{1,0:T(8,128)(2,1)S(1)} %get-tuple-element.60.s_ref, bf16[144,384]{1,0:T(8,128)(2,1)S(1)} %get-tuple-element.61.dg_ref, ...), custom_call_target="tpu_custom_call" | custom-call | flops 1 | bytes 1 | tf_op jit(solution)/shard_map/own_half/pallas_call | solution.py:541
  38.3 0.0 collective-permute-done.11.refs_1_
  38.3 0.0 collective-permute-done.10.refs_2_
  38.3 0.0 collective-permute-start.13
  38.3 0.0 collective-permute-done.16.refs_5_
  38.3 0.0 collective-permute-done.17.refs_6_
  38.4 0.4 combine.1
  38.8 0.8 %collective-permute-done.13.given_ref = bf16[160,256]{1,0:T(8,128)(2,1)S(1)} collective-permute-done((bf16[160,256]{1,0:T(8,128)(2,1)S(1)}, bf16[160,256]{1,0:T(8,128)(2,1)S(1)}, u32[]{:S(2)}, u32[]{:S(2)}) %collective-permute-start.13) | collective-permute-done | bytes 81952 | tf_op jit(solution)/shard_map/ppermute | solution.py:562
  39.6 1.0 %combine_last.1 = (bf16[128,1024]{1,0:T(8,128)(2,1)}, bf16[8,128]{1,0:T(8,128)(2,1)}) custom-call(s32[8,128]{1,0:T(8,128)S(1)} %bitcast.15, s32[8,128]{1,0:T(8,128)S(1)} %copy-done.5, f32[8,128]{1,0:T(8,128)S(1)} %copy-done.6, bf16[160,256]{1,0:T(8,128)(2,1)S(1)} %collective-permute-done.13.given_ref, f32[128,1024]{1,0:T(8,128)S(1)} %get-tuple-element.72.token_sum_ref, ...), custom_call_target="tpu_custom_call" | custom-call | flops 1 | bytes 1 | tf_op jit(solution)/shard_map/combine_last/pallas_call | solution.py:541
  (9 shorter events, 0.0 us)
Async XLA Ops:
  0.6 22.9 %copy-start = (bf16[1,1024,384]{2,1,0:T(8,128)(2,1)S(1)}, bf16[1,1024,384]{2,1,0:T(8,128)(2,1)}, u32[]{:S(2)}) copy-start(bf16[1,1024,384]{2,1,0:T(8,128)(2,1)} %param.15) | copy-start | bytes 2359300
  0.6 22.9 %copy-start.1 = (bf16[1,1024,384]{2,1,0:T(8,128)(2,1)S(1)}, bf16[1,1024,384]{2,1,0:T(8,128)(2,1)}, u32[]{:S(2)}) copy-start(bf16[1,1024,384]{2,1,0:T(8,128)(2,1)} %param.16) | copy-start | bytes 2359300
  0.7 22.9 %copy-start.2 = (bf16[1,1024,384]{2,1,0:T(8,128)(2,1)S(1)}, bf16[1,1024,384]{2,1,0:T(8,128)(2,1)}, u32[]{:S(2)}) copy-start(bf16[1,1024,384]{2,1,0:T(8,128)(2,1)} %param.17) | copy-start | bytes 2359300
  3.1 6.1 %collective-permute-start.1 = (bf16[144,256]{1,0:T(8,128)(2,1)}, bf16[144,256]{1,0:T(8,128)(2,1)S(1)}, u32[]{:S(2)}, u32[]{:S(2)}) collective-permute-start(bf16[144,256]{1,0:T(8,128)(2,1)} %get-tuple-element.46), channel_id=1, source_target_pairs={{0,2},{2,0},{4,6},{6,4},{8,10},{10,8},{12,14},{14,12},{1,3},{3,1},... | collective-permute-start | bytes 221192 | tf_op jit(solution)/shard_map/ppermute | solution.py:556
  6.2 6.7 %collective-permute-start.2 = (bf16[144,256]{1,0:T(8,128)(2,1)}, bf16[144,256]{1,0:T(8,128)(2,1)S(1)}, u32[]{:S(2)}, u32[]{:S(2)}) collective-permute-start(bf16[144,256]{1,0:T(8,128)(2,1)} %get-tuple-element.47), channel_id=1, source_target_pairs={{0,1},{1,0},{2,3},{3,2},{4,5},{5,4},{6,7},{7,6},{8,9},{9,8},{10,11... | collective-permute-start | bytes 221192 | tf_op jit(solution)/shard_map/ppermute | solution.py:562
  6.2 6.7 %collective-permute-start.3 = (bf16[144,256]{1,0:T(8,128)(2,1)}, bf16[144,256]{1,0:T(8,128)(2,1)S(1)}, u32[]{:S(2)}, u32[]{:S(2)}) collective-permute-start(bf16[144,256]{1,0:T(8,128)(2,1)} %get-tuple-element.48), channel_id=1, source_target_pairs={{0,1},{1,0},{2,3},{3,2},{4,5},{5,4},{6,7},{7,6},{8,9},{9,8},{10,11... | collective-permute-start | bytes 221192 | tf_op jit(solution)/shard_map/ppermute | solution.py:562
  6.7 6.2 %collective-permute-start.4 = (bf16[144,256]{1,0:T(8,128)(2,1)}, bf16[144,256]{1,0:T(8,128)(2,1)S(1)}, u32[]{:S(2)}, u32[]{:S(2)}) collective-permute-start(bf16[144,256]{1,0:T(8,128)(2,1)} %get-tuple-element.49), channel_id=1, source_target_pairs={{0,1},{1,0},{2,3},{3,2},{4,5},{5,4},{6,7},{7,6},{8,9},{9,8},{10,11... | collective-permute-start | bytes 221192 | tf_op jit(solution)/shard_map/ppermute | solution.py:562
  6.7 10.6 %collective-permute-start = (bf16[144,256]{1,0:T(8,128)(2,1)}, bf16[144,256]{1,0:T(8,128)(2,1)S(1)}, u32[]{:S(2)}, u32[]{:S(2)}) collective-permute-start(bf16[144,256]{1,0:T(8,128)(2,1)} %get-tuple-element.45), channel_id=1, source_target_pairs={{0,8},{1,11},{2,10},{3,9},{4,12},{5,15},{6,14},{7,13},{8,0},{9,3},... | collective-permute-start | bytes 221192 | tf_op jit(solution)/shard_map/ppermute | solution.py:558
  9.3 9.4 %collective-permute-start.5 = (bf16[144,256]{1,0:T(8,128)(2,1)}, bf16[144,256]{1,0:T(8,128)(2,1)S(1)}, u32[]{:S(2)}, u32[]{:S(2)}) collective-permute-start(bf16[144,256]{1,0:T(8,128)(2,1)} %get-tuple-element.52), channel_id=1, source_target_pairs={{0,12},{1,15},{2,14},{3,13},{4,8},{5,11},{6,10},{7,9},{8,4},{9,7},... | collective-permute-start | bytes 221192 | tf_op jit(solution)/shard_map/ppermute | solution.py:558
  12.8 8.9 %collective-permute-start.6 = (bf16[144,256]{1,0:T(8,128)(2,1)S(1)}, bf16[144,256]{1,0:T(8,128)(2,1)S(1)}, u32[]{:S(2)}, u32[]{:S(2)}) collective-permute-start(bf16[144,256]{1,0:T(8,128)(2,1)S(1)} %collective-permute-done.2), channel_id=1, source_target_pairs={{0,8},{1,11},{2,10},{3,9},{4,12},{5,15},{6,14},{7,13},{8,0},{9,3},... | collective-permute-start | bytes 221192 | tf_op jit(solution)/shard_map/ppermute | solution.py:558
  12.9 8.8 %collective-permute-start.7 = (bf16[144,256]{1,0:T(8,128)(2,1)}, bf16[144,256]{1,0:T(8,128)(2,1)S(1)}, u32[]{:S(2)}, u32[]{:S(2)}) collective-permute-start(bf16[144,256]{1,0:T(8,128)(2,1)} %get-tuple-element.54), channel_id=1, source_target_pairs={{0,4},{1,7},{2,6},{3,5},{4,0},{5,3},{6,2},{7,1},{8,12},{9,15},{10,... | collective-permute-start | bytes 221192 | tf_op jit(solution)/shard_map/ppermute | solution.py:558
  13.7 8.3 %collective-permute-start.8 = (bf16[144,256]{1,0:T(8,128)(2,1)S(1)}, bf16[144,256]{1,0:T(8,128)(2,1)S(1)}, u32[]{:S(2)}, u32[]{:S(2)}) collective-permute-start(bf16[144,256]{1,0:T(8,128)(2,1)S(1)} %collective-permute-done.3), channel_id=1, source_target_pairs={{0,12},{1,15},{2,14},{3,13},{4,8},{5,11},{6,10},{7,9},{8,4},{9,7},... | collective-permute-start | bytes 221192 | tf_op jit(solution)/shard_map/ppermute | solution.py:558
  17.3 6.2 %collective-permute-start.9 = (bf16[144,256]{1,0:T(8,128)(2,1)S(1)}, bf16[144,256]{1,0:T(8,128)(2,1)S(1)}, u32[]{:S(2)}, u32[]{:S(2)}) collective-permute-start(bf16[144,256]{1,0:T(8,128)(2,1)S(1)} %collective-permute-done.4), channel_id=1, source_target_pairs={{0,4},{1,7},{2,6},{3,5},{4,0},{5,3},{6,2},{7,1},{8,12},{9,15},{10,... | collective-permute-start | bytes 221192 | tf_op jit(solution)/shard_map/ppermute | solution.py:558
  17.8 0.9 %copy-start.3 = (bf16[144,256]{1,0:T(8,128)(2,1)S(1)}, bf16[144,256]{1,0:T(8,128)(2,1)}, u32[]{:S(2)}) copy-start(bf16[144,256]{1,0:T(8,128)(2,1)} %get-tuple-element.44.source_ref) | copy-start | bytes 221188
  25.7 12.7 %copy-start.4 = (s32[128,8]{0,1:T(8,128)S(1)}, s32[128,8]{0,1:T(8,128)}, u32[]{:S(2)}) copy-start(s32[128,8]{0,1:T(8,128)} %param.11) | copy-start | bytes 12292
  25.7 12.7 %copy-start.5 = (s32[8,128]{1,0:T(8,128)S(1)}, s32[8,128]{1,0:T(8,128)}, u32[]{:S(2)}) copy-start(s32[8,128]{1,0:T(8,128)} %get-tuple-element.42.slot_ref) | copy-start | bytes 12292
  25.7 12.7 %copy-start.6 = (f32[8,128]{1,0:T(8,128)S(1)}, f32[8,128]{1,0:T(8,128)}, u32[]{:S(2)}) copy-start(f32[8,128]{1,0:T(8,128)} %get-tuple-element.43.gates_ref) | copy-start | bytes 12292
  25.7 11.2 %collective-permute-start.12 = (bf16[1536,384]{1,0:T(8,128)(2,1)S(1)}, bf16[1536,384]{1,0:T(8,128)(2,1)S(1)}, u32[]{:S(2)}, u32[]{:S(2)}) collective-permute-start(bf16[1536,384]{1,0:T(8,128)(2,1)S(1)} %other_half.1), channel_id=1, source_target_pairs={{0,1},{1,0},{2,3},{3,2},{4,5},{5,4},{6,7},{7,6},{8,9},{9,8},{10,11... | collective-permute-start | bytes 3538952 | tf_op jit(solution)/shard_map/ppermute | solution.py:562
  25.8 7.2 %collective-permute-start.14 = (bf16[160,256]{1,0:T(8,128)(2,1)S(1)}, bf16[160,256]{1,0:T(8,128)(2,1)S(1)}, u32[]{:S(2)}, u32[]{:S(2)}) collective-permute-start(bf16[160,256]{1,0:T(8,128)(2,1)S(1)} %get-tuple-element.70), channel_id=1, source_target_pairs={{0,12},{1,15},{2,14},{3,13},{4,8},{5,11},{6,10},{7,9},{8,4},{9,7},... | collective-permute-start | bytes 245768 | tf_op jit(solution)/shard_map/ppermute | solution.py:558
  29.4 6.9 %collective-permute-start.15 = (bf16[160,256]{1,0:T(8,128)(2,1)S(1)}, bf16[160,256]{1,0:T(8,128)(2,1)S(1)}, u32[]{:S(2)}, u32[]{:S(2)}) collective-permute-start(bf16[160,256]{1,0:T(8,128)(2,1)S(1)} %get-tuple-element.71), channel_id=1, source_target_pairs={{0,4},{1,7},{2,6},{3,5},{4,0},{5,3},{6,2},{7,1},{8,12},{9,15},{10,... | collective-permute-start | bytes 245768 | tf_op jit(solution)/shard_map/ppermute | solution.py:558
  29.4 8.9 %collective-permute-start.10 = (bf16[160,256]{1,0:T(8,128)(2,1)S(1)}, bf16[160,256]{1,0:T(8,128)(2,1)S(1)}, u32[]{:S(2)}, u32[]{:S(2)}) collective-permute-start(bf16[160,256]{1,0:T(8,128)(2,1)S(1)} %get-tuple-element.57), channel_id=1, source_target_pairs={{0,8},{1,11},{2,10},{3,9},{4,12},{5,15},{6,14},{7,13},{8,0},{9,3},... | collective-permute-start | bytes 245768 | tf_op jit(solution)/shard_map/ppermute | solution.py:558
  30.2 8.1 %collective-permute-start.11 = (bf16[80,256]{1,0:T(8,128)(2,1)S(1)}, bf16[80,256]{1,0:T(8,128)(2,1)S(1)}, u32[]{:S(2)}, u32[]{:S(2)}) collective-permute-start(bf16[80,256]{1,0:T(8,128)(2,1)S(1)} %get-tuple-element.58), channel_id=1, source_target_pairs={{0,2},{2,0},{4,6},{6,4},{8,10},{10,8},{12,14},{14,12},{1,3},{3,1},... | collective-permute-start | bytes 122888 | tf_op jit(solution)/shard_map/ppermute | solution.py:556
  33.0 5.3 %collective-permute-start.16 = (bf16[160,256]{1,0:T(8,128)(2,1)S(1)}, bf16[160,256]{1,0:T(8,128)(2,1)S(1)}, u32[]{:S(2)}, u32[]{:S(2)}) collective-permute-start(bf16[160,256]{1,0:T(8,128)(2,1)S(1)} %collective-permute-done.14.refs_3_), channel_id=1, source_target_pairs={{0,1},{1,0},{2,3},{3,2},{4,5},{5,4},{6,7},{7,6},{8,9},{9,8},{10,11... | collective-permute-start | bytes 245768 | tf_op jit(solution)/shard_map/ppermute | solution.py:562
  36.3 2.0 %collective-permute-start.17 = (bf16[160,256]{1,0:T(8,128)(2,1)S(1)}, bf16[160,256]{1,0:T(8,128)(2,1)S(1)}, u32[]{:S(2)}, u32[]{:S(2)}) collective-permute-start(bf16[160,256]{1,0:T(8,128)(2,1)S(1)} %collective-permute-done.15.refs_4_), channel_id=1, source_target_pairs={{0,1},{1,0},{2,3},{3,2},{4,5},{5,4},{6,7},{7,6},{8,9},{9,8},{10,11... | collective-permute-start | bytes 245768 | tf_op jit(solution)/shard_map/ppermute | solution.py:562
  38.3 1.3 %collective-permute-start.13 = (bf16[160,256]{1,0:T(8,128)(2,1)S(1)}, bf16[160,256]{1,0:T(8,128)(2,1)S(1)}, u32[]{:S(2)}, u32[]{:S(2)}) collective-permute-start(bf16[160,256]{1,0:T(8,128)(2,1)S(1)} %collective-permute-done.10.refs_2_), channel_id=1, source_target_pairs={{0,1},{1,0},{2,3},{3,2},{4,5},{5,4},{6,7},{7,6},{8,9},{9,8},{10,11... | collective-permute-start | bytes 245768 | tf_op jit(solution)/shard_map/ppermute | solution.py:562

commit v15 on v13

--- a/solution.py
+++ b/solution.py
@@ -242,7 +242,9 @@
 MAIN = 16
 QUARTERS = 4
 SEND_ROWS = 2 * QUARTERS * MAIN + 16
-BACK_ROWS = QUARTERS * MAIN + 16
+MAIN_ROWS = QUARTERS * MAIN
+BACK_ROWS = MAIN_ROWS + 16
+DOUBLE_ROWS = 2 * MAIN_ROWS + 24
 
 
 def copies_of(experts):
@@ -260,10 +262,6 @@
         step = jnp.where(jnp.right_shift(row, 1) == d + 1, step + base, step)
     step = jnp.where(row < 2, row, step)
     return jnp.bitwise_xor(step, lax.axis_index("expert"))
-
-
-def chunk_views(refs, rows):
-    return [(refs[0], 0), (refs[1], 0)] + [(ref, part * rows) for ref in refs[2:] for part in (0, 1)]
 
 
 def mask(condition):
@@ -368,7 +366,7 @@
     experts = len(ORDER)
     recv_refs = [refs[ORDER.index(c)] for c in range(experts)]
     gate_ref, up_ref, down_ref = refs[experts : experts + 3]
-    back_views = chunk_views(refs[experts + 3 : -5], BACK_ROWS)
+    back_refs = refs[experts + 3 : -5]
     x_ref, s_ref, dg_ref, du_ref, hid_ref = refs[-5:]
     width = refs[0].shape[1]
     main_rows = experts * MAIN
@@ -424,14 +422,21 @@
         mine = jnp.logical_and(jnp.bitwise_and(inner, 3) == q, inner < 8)
         place = mask(jnp.logical_and(mine, tcol == source))
         spread += jnp.dot(place, grad[main_rows:, cols], preferred_element_type=F32)
-        for i, (ref, first) in enumerate(back_views):
-            low = first + q * MAIN
+        for i in range(experts):
+            single = i < 2
+            low = q * MAIN + (0 if single else (i % 2) * MAIN_ROWS)
+            ref = back_refs[i if single else 1 + i // 2]
             ref[low : low + MAIN, :] = grad[i * MAIN : (i + 1) * MAIN, cols]
-    for i, (ref, first) in enumerate(back_views):
-        low = first + QUARTERS * MAIN
-        ref[low : low + 16, :] = jnp.concatenate(
-            [spread[i * MAIN : i * MAIN + 8], gate_lanes], axis=0
-        ).astype(BF)
+    for n, ref in enumerate(back_refs):
+        if n < 2:
+            ref[MAIN_ROWS:, :] = jnp.concatenate(
+                [spread[n * MAIN : n * MAIN + 8], gate_lanes], axis=0
+            ).astype(BF)
+        else:
+            i = 2 * n - 2
+            both = [spread[c * MAIN : c * MAIN + 8] for c in (i, i + 1)]
+            ref[2 * MAIN_ROWS : 2 * MAIN_ROWS + 16, :] = jnp.concatenate(both, axis=0).astype(BF)
+            ref[2 * MAIN_ROWS + 16 :, :] = gate_lanes.astype(BF)
 
 
 def grads_of(half, x_ref, s_ref, dg_ref, du_ref, hid_ref):
@@ -462,6 +467,14 @@
     for n, out_ref in enumerate((gate_ref, up_ref, down_ref)):
         came = came_ref[n * rows : (n + 1) * rows, :].astype(F32)
         out_ref[...] = (parts[n].astype(BF).astype(F32) + came).astype(BF)
+
+
+def tail_of(ref, part):
+    if part is None:
+        return ref[MAIN_ROWS:, :]
+    both = ref[2 * MAIN_ROWS : 2 * MAIN_ROWS + 16, :].astype(F32)
+    sums = ref[2 * MAIN_ROWS + 16 :, :].astype(F32)
+    return jnp.concatenate([both[8 * part : 8 * part + 8], sums], axis=0).astype(BF)
 
 
 def combine_chunks(chunks, views, ids_ref, slot_ref, gates_ref):
@@ -475,12 +488,13 @@
     wanted = MAIN + jnp.right_shift(inner, 2)
     last = jnp.where(jnp.logical_and(slot16 == wanted, inner < 8), 1.0, 0.0)
     quarter = jnp.bitwise_and(inner, 3)
-    tails = [ref[first + BACK_ROWS - 16 : first + BACK_ROWS, :] for ref, first in views]
+    tails = [tail_of(*view) for view in views]
+    starts = [(ref, MAIN_ROWS if part else 0) for ref, part in views]
     tail = jnp.concatenate(tails, axis=0)
     totals = []
     for q in range(QUARTERS):
         main = jnp.concatenate(
-            [ref[first + q * MAIN : first + (q + 1) * MAIN, :] for ref, first in views], axis=0
+            [ref[first + q * MAIN : first + (q + 1) * MAIN, :] for ref, first in starts], axis=0
         )
         place = jnp.where(quarter == q, last, 0.0).astype(BF)
         total = lax.dot_general(onehot, main, CONTRACT_ROWS, preferred_element_type=F32)
@@ -505,14 +519,14 @@
 
 def combine_kernel(ids_ref, slot_ref, gates_ref, *refs):
     token_ref, grad_ref = refs[-2:]
-    singles = [(refs[0], 0), (refs[1], 0)]
+    singles = [(refs[0], None), (refs[1], None)]
     kept_refs = refs[2 : 2 + len(BASES)]
     given_refs = refs[2 + len(BASES) : -2]
     views = dict(enumerate(singles))
     for d, ref in enumerate(kept_refs):
         views[2 + 2 * d] = (ref, 0)
     for d, ref in enumerate(given_refs):
-        views[LAST + 2 + 2 * d] = (ref, BACK_ROWS)
+        views[LAST + 2 + 2 * d] = (ref, 1)
     chunks = sorted(views)
     totals, by_choice = combine_chunks(
         chunks, [views[c] for c in chunks], ids_ref, slot_ref, gates_ref
@@ -524,25 +538,39 @@
 
 
 def combine_last_kernel(
-    ids_ref, slot_ref, gates_ref, given_ref, token_sum_ref, grad_sum_ref, token_ref, grad_ref
+    ids_ref,
+    slot_ref,
+    gates_ref,
+    given_ref,
+    token_sum_ref,
+    grad_sum_ref,
+    token_hbm,
+    grad_ref,
+    token_ref,
+    sems,
 ):
-    totals, by_choice = combine_chunks(
-        [LAST], [(given_ref, BACK_ROWS)], ids_ref, slot_ref, gates_ref
-    )
+    totals, by_choice = combine_chunks([LAST], [(given_ref, 1)], ids_ref, slot_ref, gates_ref)
     width = totals[0].shape[1]
+    stores = []
     for q, total in enumerate(totals):
         cols = slice(q * width, (q + 1) * width)
         token_ref[:, cols] = (token_sum_ref[:, cols] + total).astype(BF)
+        stores.append(
+            pltpu.make_async_copy(token_ref.at[:, cols], token_hbm.at[:, cols], sems.at[q])
+        )
+        stores[q].start()
     grad_ref[...] = (grad_sum_ref[...] + by_choice).astype(BF)
-
-
-def local_call(kernel, outs, arrays, name, flops, moved, space=pltpu.VMEM, scratch=(), limit=16):
+    for store in stores:
+        store.wait()
+
+
+def local_call(kernel, outs, arrays, name, flops, moved, space=pltpu.VMEM, scratch=(), limit=16, first=None):
     vmem = pl.BlockSpec(memory_space=pltpu.VMEM)
     return pl.pallas_call(
         kernel,
         out_shape=[jax.ShapeDtypeStruct(shape, kind) for shape, kind in outs],
         in_specs=[pl.BlockSpec(memory_space=space)] * len(arrays),
-        out_specs=[vmem] * len(outs),
+        out_specs=[pl.BlockSpec(memory_space=first or pltpu.VMEM)] + [vmem] * (len(outs) - 1),
         scratch_shapes=list(scratch),
         compiler_params=pltpu.CompilerParams(vmem_limit_bytes=limit * MIB),
         cost_estimate=pl.CostEstimate(flops=flops, bytes_accessed=moved, transcendentals=0),
@@ -617,7 +645,7 @@
     outs = local_call(
         expert_kernel,
         [((BACK_ROWS, width), BF)] * 2
-        + [((2 * BACK_ROWS, width), BF)] * count
+        + [((DOUBLE_ROWS, width), BF)] * count
         + [((served, model_width), BF)] * 2
         + [((served, hidden_width), BF)] * 3,
         [held, *(recv[c] for c in ORDER[1:]), gate_proj[0], up_proj[0], down_proj[0]],
@@ -662,6 +690,8 @@
         "combine_last",
         1,
         1,
+        scratch=[pltpu.VMEM((token_count, model_width), BF), pltpu.SemaphoreType.DMA((QUARTERS,))],
+        first=pltpu.HBM,
     )
     return (token_grad, gate_grad.T, shares[0][None], shares[1][None], shares[2][None])
 

time: 39.7 us -> 40.1 us (1.010)
  Pallas kernels: 7.43 us -> 7.97 us
    pallas_call x7, Pallas kernels: 7.43 us -> 7.97 us  [local_call(): pl.pallas_call(kernel, out_shape=[jax.ShapeDtypeStruct(shape, kind) for s...]
where the time goes in v15:
time: 40.1 us; the launch traced here: 39.9 us
  starting transfers between devices  21.1 us (53%)
  waiting for transfers between devices  9.17 us (23%)
  Pallas kernels  7.97 us (20%)
  local copies, waits for them, and re-layouts  0.91 us (2%)
  between operations  0.77 us (2%)
    ppermute x9, starting transfers between devices, to_step(): return lax.ppermute(chunk, ('expert', 'replica'), pairs)  15 us
    ppermute x9, waiting for transfers between devices, to_step(): return lax.ppermute(chunk, ('expert', 'replica'), pairs)  8.41 us
    pallas_call x7, Pallas kernels, local_call(): pl.pallas_call(kernel, out_shape=[jax.ShapeDtypeStruct(shape, kind) for s...  7.97 us
    ppermute x2, starting transfers between devices, to_step(): return lax.ppermute(chunk, 'expert', [(i, i ^ 1) for i in range(experts)])  3.56 us
    ppermute x7, starting transfers between devices, to_twin(): return lax.ppermute(chunk, 'replica', [(0, 1), (1, 0)])  2.51 us
    unnamed x14, local copies, waits for them, and re-layouts  0.91 us
  transfers between devices with their start and end apart: 18, of which 6 were waited for; matrix products, arithmetic and copies ran while one was open for 0% of the time, Pallas kernels for 4%

profile of v15, /device:TPU:0, one launch (start us, length us, event | category | flops | bytes accessed | tf_op | source)
XLA Modules:
  0.0 39.9 jit_solution(10507394213405299399)
XLA Ops:
  0.6 0.0 copy-start
  0.6 0.0 copy-start.1
  0.7 0.0 copy-start.2
  0.7 2.5 %route.1 = (bf16[144,256]{1,0:T(8,128)(2,1)}, bf16[144,256]{1,0:T(8,128)(2,1)}, bf16[144,256]{1,0:T(8,128)(2,1)}, bf16[144,256]{1,0:T(8,128)(2,1)}, bf16[144,256...) custom-call(s32[8]{0:T(128)} %plan_hbm.1, ...), custom_call_target="tpu_custom_call" | custom-call | flops 8000000000 | bytes 1114112 | tf_op jit(solution)/shard_map/route/pallas_call | solution.py:569
  3.1 0.5 %collective-permute-start.2 = (bf16[144,256]{1,0:T(8,128)(2,1)}, bf16[144,256]{1,0:T(8,128)(2,1)S(1)}, u32[]{:S(2)}, u32[]{:S(2)}) collective-permute-start(bf16[144,256]{1,0:T(8,128)(2,1)} %get-tuple-element.46), channel_id=1, source_target_pairs={{0,1},{1,0},{2,3},{3,2},{4,5},{5,4},{6,7},{7,6},{8,9},{9,8},{10,11... | collective-permute-start | bytes 221192 | tf_op jit(solution)/shard_map/ppermute | solution.py:590
  3.7 0.1 collective-permute-start.3
  3.7 0.4 %collective-permute-start.4 = (bf16[144,256]{1,0:T(8,128)(2,1)}, bf16[144,256]{1,0:T(8,128)(2,1)S(1)}, u32[]{:S(2)}, u32[]{:S(2)}) collective-permute-start(bf16[144,256]{1,0:T(8,128)(2,1)} %get-tuple-element.48), channel_id=1, source_target_pairs={{0,1},{1,0},{2,3},{3,2},{4,5},{5,4},{6,7},{7,6},{8,9},{9,8},{10,11... | collective-permute-start | bytes 221192 | tf_op jit(solution)/shard_map/ppermute | solution.py:590
  4.2 2.6 %collective-permute-start = (bf16[144,256]{1,0:T(8,128)(2,1)}, bf16[144,256]{1,0:T(8,128)(2,1)S(1)}, u32[]{:S(2)}, u32[]{:S(2)}) collective-permute-start(bf16[144,256]{1,0:T(8,128)(2,1)} %get-tuple-element.44), channel_id=1, source_target_pairs={{0,2},{2,0},{4,6},{6,4},{8,10},{10,8},{12,14},{14,12},{1,3},{3,1},... | collective-permute-start | bytes 221192 | tf_op jit(solution)/shard_map/ppermute | solution.py:584
  6.7 2.6 %collective-permute-start.1 = (bf16[144,256]{1,0:T(8,128)(2,1)}, bf16[144,256]{1,0:T(8,128)(2,1)S(1)}, u32[]{:S(2)}, u32[]{:S(2)}) collective-permute-start(bf16[144,256]{1,0:T(8,128)(2,1)} %get-tuple-element.45), channel_id=1, source_target_pairs={{0,8},{1,11},{2,10},{3,9},{4,12},{5,15},{6,14},{7,13},{8,0},{9,3},... | collective-permute-start | bytes 221192 | tf_op jit(solution)/shard_map/ppermute | solution.py:586
  9.3 0.0 collective-permute-done.2
  9.3 1.6 %collective-permute-start.6 = (bf16[144,256]{1,0:T(8,128)(2,1)}, bf16[144,256]{1,0:T(8,128)(2,1)S(1)}, u32[]{:S(2)}, u32[]{:S(2)}) collective-permute-start(bf16[144,256]{1,0:T(8,128)(2,1)} %get-tuple-element.51), channel_id=1, source_target_pairs={{0,4},{1,7},{2,6},{3,5},{4,0},{5,3},{6,2},{7,1},{8,12},{9,15},{10,... | collective-permute-start | bytes 221192 | tf_op jit(solution)/shard_map/ppermute | solution.py:586
  10.9 0.0 collective-permute-done.3
  10.9 0.0 collective-permute-done.4
  10.9 0.2 collective-permute-start.5
  11.1 1.7 %collective-permute-start.7 = (bf16[144,256]{1,0:T(8,128)(2,1)S(1)}, bf16[144,256]{1,0:T(8,128)(2,1)S(1)}, u32[]{:S(2)}, u32[]{:S(2)}) collective-permute-start(bf16[144,256]{1,0:T(8,128)(2,1)S(1)} %collective-permute-done.2), channel_id=1, source_target_pairs={{0,8},{1,11},{2,10},{3,9},{4,12},{5,15},{6,14},{7,13},{8,0},{9,3},... | collective-permute-start | bytes 221192 | tf_op jit(solution)/shard_map/ppermute | solution.py:586
  12.8 0.0 collective-permute-done.refs_1_
  12.8 2.5 %collective-permute-start.8 = (bf16[144,256]{1,0:T(8,128)(2,1)S(1)}, bf16[144,256]{1,0:T(8,128)(2,1)S(1)}, u32[]{:S(2)}, u32[]{:S(2)}) collective-permute-start(bf16[144,256]{1,0:T(8,128)(2,1)S(1)} %collective-permute-done.4), channel_id=1, source_target_pairs={{0,4},{1,7},{2,6},{3,5},{4,0},{5,3},{6,2},{7,1},{8,12},{9,15},{10,... | collective-permute-start | bytes 221192 | tf_op jit(solution)/shard_map/ppermute | solution.py:586
  15.3 0.0 collective-permute-done.1.refs_2_
  15.3 2.0 %collective-permute-start.9 = (bf16[144,256]{1,0:T(8,128)(2,1)S(1)}, bf16[144,256]{1,0:T(8,128)(2,1)S(1)}, u32[]{:S(2)}, u32[]{:S(2)}) collective-permute-start(bf16[144,256]{1,0:T(8,128)(2,1)S(1)} %collective-permute-done.3), channel_id=1, source_target_pairs={{0,12},{1,15},{2,14},{3,13},{4,8},{5,11},{6,10},{7,9},{8,4},{9,7},... | collective-permute-start | bytes 221192 | tf_op jit(solution)/shard_map/ppermute | solution.py:586
  17.4 0.9 %copy-done.3 = bf16[144,256]{1,0:T(8,128)(2,1)S(1)} copy-done((bf16[144,256]{1,0:T(8,128)(2,1)S(1)}, bf16[144,256]{1,0:T(8,128)(2,1)}, u32[]{:S(2)}) %copy-start.3) | copy-done | bytes 73752
  18.2 0.0 collective-permute-done.6.refs_4_
  18.3 0.0 collective-permute-done.5.refs_3_
  18.3 2.0 %collective-permute-done.7.refs_5_ = bf16[144,256]{1,0:T(8,128)(2,1)S(1)} collective-permute-done((bf16[144,256]{1,0:T(8,128)(2,1)S(1)}, bf16[144,256]{1,0:T(8,128)(2,1)S(1)}, u32[]{:S(2)}, u32[]{:S(2)}) %collective-permute-start.7) | collective-permute-done | bytes 73760 | tf_op jit(solution)/shard_map/ppermute | solution.py:586
  20.3 0.0 collective-permute-done.8.refs_6_
  20.3 1.7 %collective-permute-done.9.refs_7_ = bf16[144,256]{1,0:T(8,128)(2,1)S(1)} collective-permute-done((bf16[144,256]{1,0:T(8,128)(2,1)S(1)}, bf16[144,256]{1,0:T(8,128)(2,1)S(1)}, u32[]{:S(2)}, u32[]{:S(2)}) %collective-permute-start.9) | collective-permute-done | bytes 73760 | tf_op jit(solution)/shard_map/ppermute | solution.py:586
  22.0 0.0 copy-done.1
  22.0 1.5 %expert_rows.1 = (bf16[80,256]{1,0:T(8,128)(2,1)S(1)}, bf16[80,256]{1,0:T(8,128)(2,1)S(1)}, bf16[152,256]{1,0:T(8,128)(2,1)S(1)}, bf16[152,256]{1,0:T(8,128)(2,1...) custom-call(bf16[144,256]{1,0:T(8,128)(2,1)S(1)} %hold.1.refs_0_, ...), custom_call_target="tpu_custom_call" | custom-call | flops 566231040 | bytes 2359296 | tf_op jit(solution)/shard_map/expert_rows/pallas_call | solution.py:569
  23.5 0.6 %other_half.1 = bf16[1536,384]{1,0:T(8,128)(2,1)S(1)} custom-call(bf16[144,1024]{1,0:T(8,128)(2,1)S(1)} %get-tuple-element.57.x_ref, bf16[144,1024]{1,0:T(8,128)(2,1)S(1)} %get-tuple-element.58.s_ref, bf16[144,384]{1,0:T(8,128)(2,1)S(1)} %get-tuple-element.59.dg_ref, bf16[144,384]{1,0:T(8,128)(2,1)S(1)} %get-tuple-element.60.du_ref, ...), custom_call_target="tpu_custom_call" | custom-call | flops 1 | bytes 1 | tf_op jit(solution)/shard_map/other_half/pallas_call | solution.py:569
  24.2 0.0 copy-start.4
  24.2 0.8 %collective-permute-start.12 = (bf16[1536,384]{1,0:T(8,128)(2,1)S(1)}, bf16[1536,384]{1,0:T(8,128)(2,1)S(1)}, u32[]{:S(2)}, u32[]{:S(2)}) collective-permute-start(bf16[1536,384]{1,0:T(8,128)(2,1)S(1)} %other_half.1), channel_id=1, source_target_pairs={{0,1},{1,0},{2,3},{3,2},{4,5},{5,4},{6,7},{7,6},{8,9},{9,8},{10,11... | collective-permute-start | bytes 3538952 | tf_op jit(solution)/shard_map/ppermute | solution.py:590
  25.0 3.0 %collective-permute-start.14 = (bf16[152,256]{1,0:T(8,128)(2,1)S(1)}, bf16[152,256]{1,0:T(8,128)(2,1)S(1)}, u32[]{:S(2)}, u32[]{:S(2)}) collective-permute-start(bf16[152,256]{1,0:T(8,128)(2,1)S(1)} %get-tuple-element.68), channel_id=1, source_target_pairs={{0,12},{1,15},{2,14},{3,13},{4,8},{5,11},{6,10},{7,9},{8,4},{9,7},... | collective-permute-start | bytes 233480 | tf_op jit(solution)/shard_map/ppermute | solution.py:586
  28.0 1.2 %collective-permute-start.15 = (bf16[152,256]{1,0:T(8,128)(2,1)S(1)}, bf16[152,256]{1,0:T(8,128)(2,1)S(1)}, u32[]{:S(2)}, u32[]{:S(2)}) collective-permute-start(bf16[152,256]{1,0:T(8,128)(2,1)S(1)} %get-tuple-element.69), channel_id=1, source_target_pairs={{0,4},{1,7},{2,6},{3,5},{4,0},{5,3},{6,2},{7,1},{8,12},{9,15},{10,... | collective-permute-start | bytes 233480 | tf_op jit(solution)/shard_map/ppermute | solution.py:586
  29.3 0.1 collective-permute-start.10
  29.4 1.0 %collective-permute-start.11 = (bf16[80,256]{1,0:T(8,128)(2,1)S(1)}, bf16[80,256]{1,0:T(8,128)(2,1)S(1)}, u32[]{:S(2)}, u32[]{:S(2)}) collective-permute-start(bf16[80,256]{1,0:T(8,128)(2,1)S(1)} %get-tuple-element.56), channel_id=1, source_target_pairs={{0,2},{2,0},{4,6},{6,4},{8,10},{10,8},{12,14},{14,12},{1,3},{3,1},... | collective-permute-start | bytes 122888 | tf_op jit(solution)/shard_map/ppermute | solution.py:584
  30.4 1.4 %collective-permute-done.14.refs_3_ = bf16[152,256]{1,0:T(8,128)(2,1)S(1)} collective-permute-done((bf16[152,256]{1,0:T(8,128)(2,1)S(1)}, bf16[152,256]{1,0:T(8,128)(2,1)S(1)}, u32[]{:S(2)}, u32[]{:S(2)}) %collective-permute-start.14) | collective-permute-done | bytes 77856 | tf_op jit(solution)/shard_map/ppermute | solution.py:586
  31.8 0.0 collective-permute-start.16
  31.8 1.5 %collective-permute-done.15.refs_4_ = bf16[152,256]{1,0:T(8,128)(2,1)S(1)} collective-permute-done((bf16[152,256]{1,0:T(8,128)(2,1)S(1)}, bf16[152,256]{1,0:T(8,128)(2,1)S(1)}, u32[]{:S(2)}, u32[]{:S(2)}) %collective-permute-start.15) | collective-permute-done | bytes 77856 | tf_op jit(solution)/shard_map/ppermute | solution.py:586
  33.4 0.6 %collective-permute-start.17 = (bf16[152,256]{1,0:T(8,128)(2,1)S(1)}, bf16[152,256]{1,0:T(8,128)(2,1)S(1)}, u32[]{:S(2)}, u32[]{:S(2)}) collective-permute-start(bf16[152,256]{1,0:T(8,128)(2,1)S(1)} %collective-permute-done.15.refs_4_), channel_id=1, source_target_pairs={{0,1},{1,0},{2,3},{3,2},{4,5},{5,4},{6,7},{7,6},{8,9},{9,8},{10,11... | collective-permute-start | bytes 233480 | tf_op jit(solution)/shard_map/ppermute | solution.py:590
  33.9 0.0 collective-permute-done.12.came_ref
  33.9 1.4 %own_half.1 = (bf16[512,384]{1,0:T(8,128)(2,1)}, bf16[512,384]{1,0:T(8,128)(2,1)}, bf16[512,384]{1,0:T(8,128)(2,1)}) custom-call(bf16[144,1024]{1,0:T(8,128)(2,1)S(1)} %get-tuple-element.57.x_ref, bf16[144,1024]{1,0:T(8,128)(2,1)S(1)} %get-tuple-element.58.s_ref, bf16[144,384]{1,0:T(8,128)(2,1)S(1)} %get-tuple-element.59.dg_ref, ...), custom_call_target="tpu_custom_call" | custom-call | flops 1 | bytes 1 | tf_op jit(solution)/shard_map/own_half/pallas_call | solution.py:569
  35.3 0.0 collective-permute-done.11.refs_1_
  35.3 1.7 %collective-permute-done.10.refs_2_ = bf16[152,256]{1,0:T(8,128)(2,1)S(1)} collective-permute-done((bf16[152,256]{1,0:T(8,128)(2,1)S(1)}, bf16[152,256]{1,0:T(8,128)(2,1)S(1)}, u32[]{:S(2)}, u32[]{:S(2)}) %collective-permute-start.10) | collective-permute-done | bytes 77856 | tf_op jit(solution)/shard_map/ppermute | solution.py:586
  37.0 0.1 collective-permute-start.13
  37.1 0.0 collective-permute-done.16.refs_5_
  37.1 0.0 collective-permute-done.17.refs_6_
  37.2 0.4 combine.1
  37.6 0.7 %collective-permute-done.13.given_ref = bf16[152,256]{1,0:T(8,128)(2,1)S(1)} collective-permute-done((bf16[152,256]{1,0:T(8,128)(2,1)S(1)}, bf16[152,256]{1,0:T(8,128)(2,1)S(1)}, u32[]{:S(2)}, u32[]{:S(2)}) %collective-permute-start.13) | collective-permute-done | bytes 77856 | tf_op jit(solution)/shard_map/ppermute | solution.py:590
  38.3 1.6 %combine_last.1 = (bf16[128,1024]{1,0:T(8,128)(2,1)}, bf16[8,128]{1,0:T(8,128)(2,1)}) custom-call(s32[8,128]{1,0:T(8,128)S(1)} %bitcast.15, s32[8,128]{1,0:T(8,128)S(1)} %copy-done.5, f32[8,128]{1,0:T(8,128)S(1)} %copy-done.6, bf16[152,256]{1,0:T(8,128)(2,1)S(1)} %collective-permute-done.13.given_ref, f32[128,1024]{1,0:T(8,128)S(1)} %get-tuple-element.70.token_sum_ref, ...), custom_call_target="tpu_custom_call" | custom-call | flops 1 | bytes 1 | tf_op jit(solution)/shard_map/combine_last/pallas_call | solution.py:569
  (9 shorter events, 0.0 us)
Async XLA Ops:
  0.6 21.4 %copy-start = (bf16[1,1024,384]{2,1,0:T(8,128)(2,1)S(1)}, bf16[1,1024,384]{2,1,0:T(8,128)(2,1)}, u32[]{:S(2)}) copy-start(bf16[1,1024,384]{2,1,0:T(8,128)(2,1)} %param.15) | copy-start | bytes 2359300
  0.6 21.4 %copy-start.1 = (bf16[1,1024,384]{2,1,0:T(8,128)(2,1)S(1)}, bf16[1,1024,384]{2,1,0:T(8,128)(2,1)}, u32[]{:S(2)}) copy-start(bf16[1,1024,384]{2,1,0:T(8,128)(2,1)} %param.16) | copy-start | bytes 2359300
  0.7 21.4 %copy-start.2 = (bf16[1,1024,384]{2,1,0:T(8,128)(2,1)S(1)}, bf16[1,1024,384]{2,1,0:T(8,128)(2,1)}, u32[]{:S(2)}) copy-start(bf16[1,1024,384]{2,1,0:T(8,128)(2,1)} %param.17) | copy-start | bytes 2359300
  3.1 6.2 %collective-permute-start.2 = (bf16[144,256]{1,0:T(8,128)(2,1)}, bf16[144,256]{1,0:T(8,128)(2,1)S(1)}, u32[]{:S(2)}, u32[]{:S(2)}) collective-permute-start(bf16[144,256]{1,0:T(8,128)(2,1)} %get-tuple-element.46), channel_id=1, source_target_pairs={{0,1},{1,0},{2,3},{3,2},{4,5},{5,4},{6,7},{7,6},{8,9},{9,8},{10,11... | collective-permute-start | bytes 221192 | tf_op jit(solution)/shard_map/ppermute | solution.py:590
  3.7 7.2 %collective-permute-start.3 = (bf16[144,256]{1,0:T(8,128)(2,1)}, bf16[144,256]{1,0:T(8,128)(2,1)S(1)}, u32[]{:S(2)}, u32[]{:S(2)}) collective-permute-start(bf16[144,256]{1,0:T(8,128)(2,1)} %get-tuple-element.47), channel_id=1, source_target_pairs={{0,1},{1,0},{2,3},{3,2},{4,5},{5,4},{6,7},{7,6},{8,9},{9,8},{10,11... | collective-permute-start | bytes 221192 | tf_op jit(solution)/shard_map/ppermute | solution.py:590
  3.7 7.2 %collective-permute-start.4 = (bf16[144,256]{1,0:T(8,128)(2,1)}, bf16[144,256]{1,0:T(8,128)(2,1)S(1)}, u32[]{:S(2)}, u32[]{:S(2)}) collective-permute-start(bf16[144,256]{1,0:T(8,128)(2,1)} %get-tuple-element.48), channel_id=1, source_target_pairs={{0,1},{1,0},{2,3},{3,2},{4,5},{5,4},{6,7},{7,6},{8,9},{9,8},{10,11... | collective-permute-start | bytes 221192 | tf_op jit(solution)/shard_map/ppermute | solution.py:590
  4.2 8.7 %collective-permute-start = (bf16[144,256]{1,0:T(8,128)(2,1)}, bf16[144,256]{1,0:T(8,128)(2,1)S(1)}, u32[]{:S(2)}, u32[]{:S(2)}) collective-permute-start(bf16[144,256]{1,0:T(8,128)(2,1)} %get-tuple-element.44), channel_id=1, source_target_pairs={{0,2},{2,0},{4,6},{6,4},{8,10},{10,8},{12,14},{14,12},{1,3},{3,1},... | collective-permute-start | bytes 221192 | tf_op jit(solution)/shard_map/ppermute | solution.py:584
  6.7 8.6 %collective-permute-start.1 = (bf16[144,256]{1,0:T(8,128)(2,1)}, bf16[144,256]{1,0:T(8,128)(2,1)S(1)}, u32[]{:S(2)}, u32[]{:S(2)}) collective-permute-start(bf16[144,256]{1,0:T(8,128)(2,1)} %get-tuple-element.45), channel_id=1, source_target_pairs={{0,8},{1,11},{2,10},{3,9},{4,12},{5,15},{6,14},{7,13},{8,0},{9,3},... | collective-permute-start | bytes 221192 | tf_op jit(solution)/shard_map/ppermute | solution.py:586
  9.3 8.9 %collective-permute-start.6 = (bf16[144,256]{1,0:T(8,128)(2,1)}, bf16[144,256]{1,0:T(8,128)(2,1)S(1)}, u32[]{:S(2)}, u32[]{:S(2)}) collective-permute-start(bf16[144,256]{1,0:T(8,128)(2,1)} %get-tuple-element.51), channel_id=1, source_target_pairs={{0,4},{1,7},{2,6},{3,5},{4,0},{5,3},{6,2},{7,1},{8,12},{9,15},{10,... | collective-permute-start | bytes 221192 | tf_op jit(solution)/shard_map/ppermute | solution.py:586
  10.9 7.3 %collective-permute-start.5 = (bf16[144,256]{1,0:T(8,128)(2,1)}, bf16[144,256]{1,0:T(8,128)(2,1)S(1)}, u32[]{:S(2)}, u32[]{:S(2)}) collective-permute-start(bf16[144,256]{1,0:T(8,128)(2,1)} %get-tuple-element.50), channel_id=1, source_target_pairs={{0,12},{1,15},{2,14},{3,13},{4,8},{5,11},{6,10},{7,9},{8,4},{9,7},... | collective-permute-start | bytes 221192 | tf_op jit(solution)/shard_map/ppermute | solution.py:586
  11.1 9.1 %collective-permute-start.7 = (bf16[144,256]{1,0:T(8,128)(2,1)S(1)}, bf16[144,256]{1,0:T(8,128)(2,1)S(1)}, u32[]{:S(2)}, u32[]{:S(2)}) collective-permute-start(bf16[144,256]{1,0:T(8,128)(2,1)S(1)} %collective-permute-done.2), channel_id=1, source_target_pairs={{0,8},{1,11},{2,10},{3,9},{4,12},{5,15},{6,14},{7,13},{8,0},{9,3},... | collective-permute-start | bytes 221192 | tf_op jit(solution)/shard_map/ppermute | solution.py:586
  12.8 7.5 %collective-permute-start.8 = (bf16[144,256]{1,0:T(8,128)(2,1)S(1)}, bf16[144,256]{1,0:T(8,128)(2,1)S(1)}, u32[]{:S(2)}, u32[]{:S(2)}) collective-permute-start(bf16[144,256]{1,0:T(8,128)(2,1)S(1)} %collective-permute-done.4), channel_id=1, source_target_pairs={{0,4},{1,7},{2,6},{3,5},{4,0},{5,3},{6,2},{7,1},{8,12},{9,15},{10,... | collective-permute-start | bytes 221192 | tf_op jit(solution)/shard_map/ppermute | solution.py:586
  15.3 6.7 %collective-permute-start.9 = (bf16[144,256]{1,0:T(8,128)(2,1)S(1)}, bf16[144,256]{1,0:T(8,128)(2,1)S(1)}, u32[]{:S(2)}, u32[]{:S(2)}) collective-permute-start(bf16[144,256]{1,0:T(8,128)(2,1)S(1)} %collective-permute-done.3), channel_id=1, source_target_pairs={{0,12},{1,15},{2,14},{3,13},{4,8},{5,11},{6,10},{7,9},{8,4},{9,7},... | collective-permute-start | bytes 221192 | tf_op jit(solution)/shard_map/ppermute | solution.py:586
  17.4 0.9 %copy-start.3 = (bf16[144,256]{1,0:T(8,128)(2,1)S(1)}, bf16[144,256]{1,0:T(8,128)(2,1)}, u32[]{:S(2)}) copy-start(bf16[144,256]{1,0:T(8,128)(2,1)} %get-tuple-element.43.source_ref) | copy-start | bytes 221188
  24.2 13.0 %copy-start.4 = (s32[128,8]{0,1:T(8,128)S(1)}, s32[128,8]{0,1:T(8,128)}, u32[]{:S(2)}) copy-start(s32[128,8]{0,1:T(8,128)} %param.11) | copy-start | bytes 12292
  24.2 13.0 %copy-start.5 = (s32[8,128]{1,0:T(8,128)S(1)}, s32[8,128]{1,0:T(8,128)}, u32[]{:S(2)}) copy-start(s32[8,128]{1,0:T(8,128)} %get-tuple-element.41.slot_ref) | copy-start | bytes 12292
  24.2 13.0 %copy-start.6 = (f32[8,128]{1,0:T(8,128)S(1)}, f32[8,128]{1,0:T(8,128)}, u32[]{:S(2)}) copy-start(f32[8,128]{1,0:T(8,128)} %get-tuple-element.42.gates_ref) | copy-start | bytes 12292
  24.2 9.7 %collective-permute-start.12 = (bf16[1536,384]{1,0:T(8,128)(2,1)S(1)}, bf16[1536,384]{1,0:T(8,128)(2,1)S(1)}, u32[]{:S(2)}, u32[]{:S(2)}) collective-permute-start(bf16[1536,384]{1,0:T(8,128)(2,1)S(1)} %other_half.1), channel_id=1, source_target_pairs={{0,1},{1,0},{2,3},{3,2},{4,5},{5,4},{6,7},{7,6},{8,9},{9,8},{10,11... | collective-permute-start | bytes 3538952 | tf_op jit(solution)/shard_map/ppermute | solution.py:590
  25.0 6.8 %collective-permute-start.14 = (bf16[152,256]{1,0:T(8,128)(2,1)S(1)}, bf16[152,256]{1,0:T(8,128)(2,1)S(1)}, u32[]{:S(2)}, u32[]{:S(2)}) collective-permute-start(bf16[152,256]{1,0:T(8,128)(2,1)S(1)} %get-tuple-element.68), channel_id=1, source_target_pairs={{0,12},{1,15},{2,14},{3,13},{4,8},{5,11},{6,10},{7,9},{8,4},{9,7},... | collective-permute-start | bytes 233480 | tf_op jit(solution)/shard_map/ppermute | solution.py:586
  28.0 5.3 %collective-permute-start.15 = (bf16[152,256]{1,0:T(8,128)(2,1)S(1)}, bf16[152,256]{1,0:T(8,128)(2,1)S(1)}, u32[]{:S(2)}, u32[]{:S(2)}) collective-permute-start(bf16[152,256]{1,0:T(8,128)(2,1)S(1)} %get-tuple-element.69), channel_id=1, source_target_pairs={{0,4},{1,7},{2,6},{3,5},{4,0},{5,3},{6,2},{7,1},{8,12},{9,15},{10,... | collective-permute-start | bytes 233480 | tf_op jit(solution)/shard_map/ppermute | solution.py:586
  29.3 7.8 %collective-permute-start.10 = (bf16[152,256]{1,0:T(8,128)(2,1)S(1)}, bf16[152,256]{1,0:T(8,128)(2,1)S(1)}, u32[]{:S(2)}, u32[]{:S(2)}) collective-permute-start(bf16[152,256]{1,0:T(8,128)(2,1)S(1)} %get-tuple-element.55), channel_id=1, source_target_pairs={{0,8},{1,11},{2,10},{3,9},{4,12},{5,15},{6,14},{7,13},{8,0},{9,3},... | collective-permute-start | bytes 233480 | tf_op jit(solution)/shard_map/ppermute | solution.py:586
  29.4 5.9 %collective-permute-start.11 = (bf16[80,256]{1,0:T(8,128)(2,1)S(1)}, bf16[80,256]{1,0:T(8,128)(2,1)S(1)}, u32[]{:S(2)}, u32[]{:S(2)}) collective-permute-start(bf16[80,256]{1,0:T(8,128)(2,1)S(1)} %get-tuple-element.56), channel_id=1, source_target_pairs={{0,2},{2,0},{4,6},{6,4},{8,10},{10,8},{12,14},{14,12},{1,3},{3,1},... | collective-permute-start | bytes 122888 | tf_op jit(solution)/shard_map/ppermute | solution.py:584
  31.8 5.3 %collective-permute-start.16 = (bf16[152,256]{1,0:T(8,128)(2,1)S(1)}, bf16[152,256]{1,0:T(8,128)(2,1)S(1)}, u32[]{:S(2)}, u32[]{:S(2)}) collective-permute-start(bf16[152,256]{1,0:T(8,128)(2,1)S(1)} %collective-permute-done.14.refs_3_), channel_id=1, source_target_pairs={{0,1},{1,0},{2,3},{3,2},{4,5},{5,4},{6,7},{7,6},{8,9},{9,8},{10,11... | collective-permute-start | bytes 233480 | tf_op jit(solution)/shard_map/ppermute | solution.py:590
  33.4 3.8 %collective-permute-start.17 = (bf16[152,256]{1,0:T(8,128)(2,1)S(1)}, bf16[152,256]{1,0:T(8,128)(2,1)S(1)}, u32[]{:S(2)}, u32[]{:S(2)}) collective-permute-start(bf16[152,256]{1,0:T(8,128)(2,1)S(1)} %collective-permute-done.15.refs_4_), channel_id=1, source_target_pairs={{0,1},{1,0},{2,3},{3,2},{4,5},{5,4},{6,7},{7,6},{8,9},{9,8},{10,11... | collective-permute-start | bytes 233480 | tf_op jit(solution)/shard_map/ppermute | solution.py:590
  37.0 1.3 %collective-permute-start.13 = (bf16[152,256]{1,0:T(8,128)(2,1)S(1)}, bf16[152,256]{1,0:T(8,128)(2,1)S(1)}, u32[]{:S(2)}, u32[]{:S(2)}) collective-permute-start(bf16[152,256]{1,0:T(8,128)(2,1)S(1)} %collective-permute-done.10.refs_2_), channel_id=1, source_target_pairs={{0,1},{1,0},{2,3},{3,2},{4,5},{5,4},{6,7},{7,6},{8,9},{9,8},{10,11... | collective-permute-start | bytes 233480 | tf_op jit(solution)/shard_map/ppermute | solution.py:590

commit v16 on v15

--- a/solution.py
+++ b/solution.py
@@ -538,39 +538,23 @@
 
 
 def combine_last_kernel(
-    ids_ref,
-    slot_ref,
-    gates_ref,
-    given_ref,
-    token_sum_ref,
-    grad_sum_ref,
-    token_hbm,
-    grad_ref,
-    token_ref,
-    sems,
+    ids_ref, slot_ref, gates_ref, given_ref, token_sum_ref, grad_sum_ref, token_ref, grad_ref
 ):
     totals, by_choice = combine_chunks([LAST], [(given_ref, 1)], ids_ref, slot_ref, gates_ref)
     width = totals[0].shape[1]
-    stores = []
     for q, total in enumerate(totals):
         cols = slice(q * width, (q + 1) * width)
         token_ref[:, cols] = (token_sum_ref[:, cols] + total).astype(BF)
-        stores.append(
-            pltpu.make_async_copy(token_ref.at[:, cols], token_hbm.at[:, cols], sems.at[q])
-        )
-        stores[q].start()
     grad_ref[...] = (grad_sum_ref[...] + by_choice).astype(BF)
-    for store in stores:
-        store.wait()
-
-
-def local_call(kernel, outs, arrays, name, flops, moved, space=pltpu.VMEM, scratch=(), limit=16, first=None):
+
+
+def local_call(kernel, outs, arrays, name, flops, moved, space=pltpu.VMEM, scratch=(), limit=16):
     vmem = pl.BlockSpec(memory_space=pltpu.VMEM)
     return pl.pallas_call(
         kernel,
         out_shape=[jax.ShapeDtypeStruct(shape, kind) for shape, kind in outs],
         in_specs=[pl.BlockSpec(memory_space=space)] * len(arrays),
-        out_specs=[pl.BlockSpec(memory_space=first or pltpu.VMEM)] + [vmem] * (len(outs) - 1),
+        out_specs=[vmem] * len(outs),
         scratch_shapes=list(scratch),
         compiler_params=pltpu.CompilerParams(vmem_limit_bytes=limit * MIB),
         cost_estimate=pl.CostEstimate(flops=flops, bytes_accessed=moved, transcendentals=0),
@@ -690,8 +674,6 @@
         "combine_last",
         1,
         1,
-        scratch=[pltpu.VMEM((token_count, model_width), BF), pltpu.SemaphoreType.DMA((QUARTERS,))],
-        first=pltpu.HBM,
     )
     return (token_grad, gate_grad.T, shares[0][None], shares[1][None], shares[2][None])
 

time: 40.1 us -> 39.5 us (0.985)
  Pallas kernels: 7.97 us -> 7.43 us
    pallas_call x7, Pallas kernels: 7.97 us -> 7.43 us  [local_call(): pl.pallas_call(kernel, out_shape=[jax.ShapeDtypeStruct(shape, kind) for s...]
  transfers between devices with their start and end apart: 18 -> 18, of which waited for: 6 -> 6; matrix products, arithmetic and copies ran while one was open for 0% -> 0% of each run, Pallas kernels for 4% -> 5%
where the time goes in v16:
time: 39.5 us; the launch traced here: 39.3 us
  starting transfers between devices  21.1 us (53%)
  waiting for transfers between devices  9.17 us (23%)
  Pallas kernels  7.43 us (19%)
  local copies, waits for them, and re-layouts  0.91 us (2%)
  between operations  0.77 us (2%)
    ppermute x9, starting transfers between devices, to_step(): return lax.ppermute(chunk, ('expert', 'replica'), pairs)  15 us
    ppermute x9, waiting for transfers between devices, to_step(): return lax.ppermute(chunk, ('expert', 'replica'), pairs)  8.41 us
    pallas_call x7, Pallas kernels, local_call(): pl.pallas_call(kernel, out_shape=[jax.ShapeDtypeStruct(shape, kind) for s...  7.43 us
    ppermute x2, starting transfers between devices, to_step(): return lax.ppermute(chunk, 'expert', [(i, i ^ 1) for i in range(experts)])  3.56 us
    ppermute x7, starting transfers between devices, to_twin(): return lax.ppermute(chunk, 'replica', [(0, 1), (1, 0)])  2.51 us
    unnamed x14, local copies, waits for them, and re-layouts  0.91 us
  transfers between devices with their start and end apart: 18, of which 6 were waited for; matrix products, arithmetic and copies ran while one was open for 0% of the time, Pallas kernels for 5%

profile of v16, /device:TPU:0, one launch (start us, length us, event | category | flops | bytes accessed | tf_op | source)
XLA Modules:
  0.0 39.3 jit_solution(10055918792306548016)
XLA Ops:
  0.6 0.0 copy-start
  0.6 0.0 copy-start.1
  0.7 0.0 copy-start.2
  0.7 2.5 %route.1 = (bf16[144,256]{1,0:T(8,128)(2,1)}, bf16[144,256]{1,0:T(8,128)(2,1)}, bf16[144,256]{1,0:T(8,128)(2,1)}, bf16[144,256]{1,0:T(8,128)(2,1)}, bf16[144,256...) custom-call(s32[8]{0:T(128)} %plan_hbm.1, ...), custom_call_target="tpu_custom_call" | custom-call | flops 8000000000 | bytes 1114112 | tf_op jit(solution)/shard_map/route/pallas_call | solution.py:553
  3.1 0.5 %collective-permute-start.2 = (bf16[144,256]{1,0:T(8,128)(2,1)}, bf16[144,256]{1,0:T(8,128)(2,1)S(1)}, u32[]{:S(2)}, u32[]{:S(2)}) collective-permute-start(bf16[144,256]{1,0:T(8,128)(2,1)} %get-tuple-element.46), channel_id=1, source_target_pairs={{0,1},{1,0},{2,3},{3,2},{4,5},{5,4},{6,7},{7,6},{8,9},{9,8},{10,11... | collective-permute-start | bytes 221192 | tf_op jit(solution)/shard_map/ppermute | solution.py:574
  3.7 0.1 collective-permute-start.3
  3.7 0.4 %collective-permute-start.4 = (bf16[144,256]{1,0:T(8,128)(2,1)}, bf16[144,256]{1,0:T(8,128)(2,1)S(1)}, u32[]{:S(2)}, u32[]{:S(2)}) collective-permute-start(bf16[144,256]{1,0:T(8,128)(2,1)} %get-tuple-element.48), channel_id=1, source_target_pairs={{0,1},{1,0},{2,3},{3,2},{4,5},{5,4},{6,7},{7,6},{8,9},{9,8},{10,11... | collective-permute-start | bytes 221192 | tf_op jit(solution)/shard_map/ppermute | solution.py:574
  4.2 2.6 %collective-permute-start = (bf16[144,256]{1,0:T(8,128)(2,1)}, bf16[144,256]{1,0:T(8,128)(2,1)S(1)}, u32[]{:S(2)}, u32[]{:S(2)}) collective-permute-start(bf16[144,256]{1,0:T(8,128)(2,1)} %get-tuple-element.44), channel_id=1, source_target_pairs={{0,2},{2,0},{4,6},{6,4},{8,10},{10,8},{12,14},{14,12},{1,3},{3,1},... | collective-permute-start | bytes 221192 | tf_op jit(solution)/shard_map/ppermute | solution.py:568
  6.7 2.6 %collective-permute-start.1 = (bf16[144,256]{1,0:T(8,128)(2,1)}, bf16[144,256]{1,0:T(8,128)(2,1)S(1)}, u32[]{:S(2)}, u32[]{:S(2)}) collective-permute-start(bf16[144,256]{1,0:T(8,128)(2,1)} %get-tuple-element.45), channel_id=1, source_target_pairs={{0,8},{1,11},{2,10},{3,9},{4,12},{5,15},{6,14},{7,13},{8,0},{9,3},... | collective-permute-start | bytes 221192 | tf_op jit(solution)/shard_map/ppermute | solution.py:570
  9.3 0.0 collective-permute-done.2
  9.3 1.6 %collective-permute-start.6 = (bf16[144,256]{1,0:T(8,128)(2,1)}, bf16[144,256]{1,0:T(8,128)(2,1)S(1)}, u32[]{:S(2)}, u32[]{:S(2)}) collective-permute-start(bf16[144,256]{1,0:T(8,128)(2,1)} %get-tuple-element.51), channel_id=1, source_target_pairs={{0,4},{1,7},{2,6},{3,5},{4,0},{5,3},{6,2},{7,1},{8,12},{9,15},{10,... | collective-permute-start | bytes 221192 | tf_op jit(solution)/shard_map/ppermute | solution.py:570
  10.9 0.0 collective-permute-done.3
  10.9 0.0 collective-permute-done.4
  10.9 0.2 collective-permute-start.5
  11.1 1.7 %collective-permute-start.7 = (bf16[144,256]{1,0:T(8,128)(2,1)S(1)}, bf16[144,256]{1,0:T(8,128)(2,1)S(1)}, u32[]{:S(2)}, u32[]{:S(2)}) collective-permute-start(bf16[144,256]{1,0:T(8,128)(2,1)S(1)} %collective-permute-done.2), channel_id=1, source_target_pairs={{0,8},{1,11},{2,10},{3,9},{4,12},{5,15},{6,14},{7,13},{8,0},{9,3},... | collective-permute-start | bytes 221192 | tf_op jit(solution)/shard_map/ppermute | solution.py:570
  12.8 0.0 collective-permute-done.refs_1_
  12.8 2.5 %collective-permute-start.8 = (bf16[144,256]{1,0:T(8,128)(2,1)S(1)}, bf16[144,256]{1,0:T(8,128)(2,1)S(1)}, u32[]{:S(2)}, u32[]{:S(2)}) collective-permute-start(bf16[144,256]{1,0:T(8,128)(2,1)S(1)} %collective-permute-done.4), channel_id=1, source_target_pairs={{0,4},{1,7},{2,6},{3,5},{4,0},{5,3},{6,2},{7,1},{8,12},{9,15},{10,... | collective-permute-start | bytes 221192 | tf_op jit(solution)/shard_map/ppermute | solution.py:570
  15.3 0.0 collective-permute-done.1.refs_2_
  15.3 2.0 %collective-permute-start.9 = (bf16[144,256]{1,0:T(8,128)(2,1)S(1)}, bf16[144,256]{1,0:T(8,128)(2,1)S(1)}, u32[]{:S(2)}, u32[]{:S(2)}) collective-permute-start(bf16[144,256]{1,0:T(8,128)(2,1)S(1)} %collective-permute-done.3), channel_id=1, source_target_pairs={{0,12},{1,15},{2,14},{3,13},{4,8},{5,11},{6,10},{7,9},{8,4},{9,7},... | collective-permute-start | bytes 221192 | tf_op jit(solution)/shard_map/ppermute | solution.py:570
  17.4 0.9 %copy-done.3 = bf16[144,256]{1,0:T(8,128)(2,1)S(1)} copy-done((bf16[144,256]{1,0:T(8,128)(2,1)S(1)}, bf16[144,256]{1,0:T(8,128)(2,1)}, u32[]{:S(2)}) %copy-start.3) | copy-done | bytes 73752
  18.2 0.0 collective-permute-done.6.refs_4_
  18.3 0.0 collective-permute-done.5.refs_3_
  18.3 2.0 %collective-permute-done.7.refs_5_ = bf16[144,256]{1,0:T(8,128)(2,1)S(1)} collective-permute-done((bf16[144,256]{1,0:T(8,128)(2,1)S(1)}, bf16[144,256]{1,0:T(8,128)(2,1)S(1)}, u32[]{:S(2)}, u32[]{:S(2)}) %collective-permute-start.7) | collective-permute-done | bytes 73760 | tf_op jit(solution)/shard_map/ppermute | solution.py:570
  20.3 0.0 collective-permute-done.8.refs_6_
  20.3 1.7 %collective-permute-done.9.refs_7_ = bf16[144,256]{1,0:T(8,128)(2,1)S(1)} collective-permute-done((bf16[144,256]{1,0:T(8,128)(2,1)S(1)}, bf16[144,256]{1,0:T(8,128)(2,1)S(1)}, u32[]{:S(2)}, u32[]{:S(2)}) %collective-permute-start.9) | collective-permute-done | bytes 73760 | tf_op jit(solution)/shard_map/ppermute | solution.py:570
  22.0 0.0 copy-done.2
  22.0 1.5 %expert_rows.1 = (bf16[80,256]{1,0:T(8,128)(2,1)S(1)}, bf16[80,256]{1,0:T(8,128)(2,1)S(1)}, bf16[152,256]{1,0:T(8,128)(2,1)S(1)}, bf16[152,256]{1,0:T(8,128)(2,1...) custom-call(bf16[144,256]{1,0:T(8,128)(2,1)S(1)} %hold.1.refs_0_, ...), custom_call_target="tpu_custom_call" | custom-call | flops 566231040 | bytes 2359296 | tf_op jit(solution)/shard_map/expert_rows/pallas_call | solution.py:553
  23.5 0.6 %other_half.1 = bf16[1536,384]{1,0:T(8,128)(2,1)S(1)} custom-call(bf16[144,1024]{1,0:T(8,128)(2,1)S(1)} %get-tuple-element.57.x_ref, bf16[144,1024]{1,0:T(8,128)(2,1)S(1)} %get-tuple-element.58.s_ref, bf16[144,384]{1,0:T(8,128)(2,1)S(1)} %get-tuple-element.59.dg_ref, bf16[144,384]{1,0:T(8,128)(2,1)S(1)} %get-tuple-element.60.du_ref, ...), custom_call_target="tpu_custom_call" | custom-call | flops 1 | bytes 1 | tf_op jit(solution)/shard_map/other_half/pallas_call | solution.py:553
  24.2 0.0 copy-start.4
  24.2 0.8 %collective-permute-start.12 = (bf16[1536,384]{1,0:T(8,128)(2,1)S(1)}, bf16[1536,384]{1,0:T(8,128)(2,1)S(1)}, u32[]{:S(2)}, u32[]{:S(2)}) collective-permute-start(bf16[1536,384]{1,0:T(8,128)(2,1)S(1)} %other_half.1), channel_id=1, source_target_pairs={{0,1},{1,0},{2,3},{3,2},{4,5},{5,4},{6,7},{7,6},{8,9},{9,8},{10,11... | collective-permute-start | bytes 3538952 | tf_op jit(solution)/shard_map/ppermute | solution.py:574
  25.0 3.0 %collective-permute-start.14 = (bf16[152,256]{1,0:T(8,128)(2,1)S(1)}, bf16[152,256]{1,0:T(8,128)(2,1)S(1)}, u32[]{:S(2)}, u32[]{:S(2)}) collective-permute-start(bf16[152,256]{1,0:T(8,128)(2,1)S(1)} %get-tuple-element.68), channel_id=1, source_target_pairs={{0,12},{1,15},{2,14},{3,13},{4,8},{5,11},{6,10},{7,9},{8,4},{9,7},... | collective-permute-start | bytes 233480 | tf_op jit(solution)/shard_map/ppermute | solution.py:570
  28.0 1.2 %collective-permute-start.15 = (bf16[152,256]{1,0:T(8,128)(2,1)S(1)}, bf16[152,256]{1,0:T(8,128)(2,1)S(1)}, u32[]{:S(2)}, u32[]{:S(2)}) collective-permute-start(bf16[152,256]{1,0:T(8,128)(2,1)S(1)} %get-tuple-element.69), channel_id=1, source_target_pairs={{0,4},{1,7},{2,6},{3,5},{4,0},{5,3},{6,2},{7,1},{8,12},{9,15},{10,... | collective-permute-start | bytes 233480 | tf_op jit(solution)/shard_map/ppermute | solution.py:570
  29.3 0.1 collective-permute-start.10
  29.4 1.0 %collective-permute-start.11 = (bf16[80,256]{1,0:T(8,128)(2,1)S(1)}, bf16[80,256]{1,0:T(8,128)(2,1)S(1)}, u32[]{:S(2)}, u32[]{:S(2)}) collective-permute-start(bf16[80,256]{1,0:T(8,128)(2,1)S(1)} %get-tuple-element.56), channel_id=1, source_target_pairs={{0,2},{2,0},{4,6},{6,4},{8,10},{10,8},{12,14},{14,12},{1,3},{3,1},... | collective-permute-start | bytes 122888 | tf_op jit(solution)/shard_map/ppermute | solution.py:568
  30.4 1.4 %collective-permute-done.14.refs_3_ = bf16[152,256]{1,0:T(8,128)(2,1)S(1)} collective-permute-done((bf16[152,256]{1,0:T(8,128)(2,1)S(1)}, bf16[152,256]{1,0:T(8,128)(2,1)S(1)}, u32[]{:S(2)}, u32[]{:S(2)}) %collective-permute-start.14) | collective-permute-done | bytes 77856 | tf_op jit(solution)/shard_map/ppermute | solution.py:570
  31.8 0.0 collective-permute-start.16
  31.8 1.5 %collective-permute-done.15.refs_4_ = bf16[152,256]{1,0:T(8,128)(2,1)S(1)} collective-permute-done((bf16[152,256]{1,0:T(8,128)(2,1)S(1)}, bf16[152,256]{1,0:T(8,128)(2,1)S(1)}, u32[]{:S(2)}, u32[]{:S(2)}) %collective-permute-start.15) | collective-permute-done | bytes 77856 | tf_op jit(solution)/shard_map/ppermute | solution.py:570
  33.4 0.6 %collective-permute-start.17 = (bf16[152,256]{1,0:T(8,128)(2,1)S(1)}, bf16[152,256]{1,0:T(8,128)(2,1)S(1)}, u32[]{:S(2)}, u32[]{:S(2)}) collective-permute-start(bf16[152,256]{1,0:T(8,128)(2,1)S(1)} %collective-permute-done.15.refs_4_), channel_id=1, source_target_pairs={{0,1},{1,0},{2,3},{3,2},{4,5},{5,4},{6,7},{7,6},{8,9},{9,8},{10,11... | collective-permute-start | bytes 233480 | tf_op jit(solution)/shard_map/ppermute | solution.py:574
  33.9 0.0 collective-permute-done.12.came_ref
  33.9 1.4 %own_half.1 = (bf16[512,384]{1,0:T(8,128)(2,1)}, bf16[512,384]{1,0:T(8,128)(2,1)}, bf16[512,384]{1,0:T(8,128)(2,1)}) custom-call(bf16[144,1024]{1,0:T(8,128)(2,1)S(1)} %get-tuple-element.57.x_ref, bf16[144,1024]{1,0:T(8,128)(2,1)S(1)} %get-tuple-element.58.s_ref, bf16[144,384]{1,0:T(8,128)(2,1)S(1)} %get-tuple-element.59.dg_ref, ...), custom_call_target="tpu_custom_call" | custom-call | flops 1 | bytes 1 | tf_op jit(solution)/shard_map/own_half/pallas_call | solution.py:553
  35.3 0.0 collective-permute-done.11.refs_1_
  35.3 1.7 %collective-permute-done.10.refs_2_ = bf16[152,256]{1,0:T(8,128)(2,1)S(1)} collective-permute-done((bf16[152,256]{1,0:T(8,128)(2,1)S(1)}, bf16[152,256]{1,0:T(8,128)(2,1)S(1)}, u32[]{:S(2)}, u32[]{:S(2)}) %collective-permute-start.10) | collective-permute-done | bytes 77856 | tf_op jit(solution)/shard_map/ppermute | solution.py:570
  37.0 0.1 collective-permute-start.13
  37.1 0.0 collective-permute-done.16.refs_5_
  37.1 0.0 collective-permute-done.17.refs_6_
  37.2 0.4 combine.1
  37.6 0.7 %collective-permute-done.13.given_ref = bf16[152,256]{1,0:T(8,128)(2,1)S(1)} collective-permute-done((bf16[152,256]{1,0:T(8,128)(2,1)S(1)}, bf16[152,256]{1,0:T(8,128)(2,1)S(1)}, u32[]{:S(2)}, u32[]{:S(2)}) %collective-permute-start.13) | collective-permute-done | bytes 77856 | tf_op jit(solution)/shard_map/ppermute | solution.py:574
  38.3 1.0 %combine_last.1 = (bf16[128,1024]{1,0:T(8,128)(2,1)}, bf16[8,128]{1,0:T(8,128)(2,1)}) custom-call(s32[8,128]{1,0:T(8,128)S(1)} %bitcast.15, s32[8,128]{1,0:T(8,128)S(1)} %copy-done.5, f32[8,128]{1,0:T(8,128)S(1)} %copy-done.6, bf16[152,256]{1,0:T(8,128)(2,1)S(1)} %collective-permute-done.13.given_ref, f32[128,1024]{1,0:T(8,128)S(1)} %get-tuple-element.70.token_sum_ref, ...), custom_call_target="tpu_custom_call" | custom-call | flops 1 | bytes 1 | tf_op jit(solution)/shard_map/combine_last/pallas_call | solution.py:553
  (9 shorter events, 0.0 us)
Async XLA Ops:
  0.6 21.4 %copy-start = (bf16[1,1024,384]{2,1,0:T(8,128)(2,1)S(1)}, bf16[1,1024,384]{2,1,0:T(8,128)(2,1)}, u32[]{:S(2)}) copy-start(bf16[1,1024,384]{2,1,0:T(8,128)(2,1)} %param.15) | copy-start | bytes 2359300
  0.6 21.4 %copy-start.1 = (bf16[1,1024,384]{2,1,0:T(8,128)(2,1)S(1)}, bf16[1,1024,384]{2,1,0:T(8,128)(2,1)}, u32[]{:S(2)}) copy-start(bf16[1,1024,384]{2,1,0:T(8,128)(2,1)} %param.16) | copy-start | bytes 2359300
  0.7 21.4 %copy-start.2 = (bf16[1,1024,384]{2,1,0:T(8,128)(2,1)S(1)}, bf16[1,1024,384]{2,1,0:T(8,128)(2,1)}, u32[]{:S(2)}) copy-start(bf16[1,1024,384]{2,1,0:T(8,128)(2,1)} %param.17) | copy-start | bytes 2359300
  3.1 6.2 %collective-permute-start.2 = (bf16[144,256]{1,0:T(8,128)(2,1)}, bf16[144,256]{1,0:T(8,128)(2,1)S(1)}, u32[]{:S(2)}, u32[]{:S(2)}) collective-permute-start(bf16[144,256]{1,0:T(8,128)(2,1)} %get-tuple-element.46), channel_id=1, source_target_pairs={{0,1},{1,0},{2,3},{3,2},{4,5},{5,4},{6,7},{7,6},{8,9},{9,8},{10,11... | collective-permute-start | bytes 221192 | tf_op jit(solution)/shard_map/ppermute | solution.py:574
  3.7 7.2 %collective-permute-start.3 = (bf16[144,256]{1,0:T(8,128)(2,1)}, bf16[144,256]{1,0:T(8,128)(2,1)S(1)}, u32[]{:S(2)}, u32[]{:S(2)}) collective-permute-start(bf16[144,256]{1,0:T(8,128)(2,1)} %get-tuple-element.47), channel_id=1, source_target_pairs={{0,1},{1,0},{2,3},{3,2},{4,5},{5,4},{6,7},{7,6},{8,9},{9,8},{10,11... | collective-permute-start | bytes 221192 | tf_op jit(solution)/shard_map/ppermute | solution.py:574
  3.7 7.2 %collective-permute-start.4 = (bf16[144,256]{1,0:T(8,128)(2,1)}, bf16[144,256]{1,0:T(8,128)(2,1)S(1)}, u32[]{:S(2)}, u32[]{:S(2)}) collective-permute-start(bf16[144,256]{1,0:T(8,128)(2,1)} %get-tuple-element.48), channel_id=1, source_target_pairs={{0,1},{1,0},{2,3},{3,2},{4,5},{5,4},{6,7},{7,6},{8,9},{9,8},{10,11... | collective-permute-start | bytes 221192 | tf_op jit(solution)/shard_map/ppermute | solution.py:574
  4.2 8.7 %collective-permute-start = (bf16[144,256]{1,0:T(8,128)(2,1)}, bf16[144,256]{1,0:T(8,128)(2,1)S(1)}, u32[]{:S(2)}, u32[]{:S(2)}) collective-permute-start(bf16[144,256]{1,0:T(8,128)(2,1)} %get-tuple-element.44), channel_id=1, source_target_pairs={{0,2},{2,0},{4,6},{6,4},{8,10},{10,8},{12,14},{14,12},{1,3},{3,1},... | collective-permute-start | bytes 221192 | tf_op jit(solution)/shard_map/ppermute | solution.py:568
  6.7 8.6 %collective-permute-start.1 = (bf16[144,256]{1,0:T(8,128)(2,1)}, bf16[144,256]{1,0:T(8,128)(2,1)S(1)}, u32[]{:S(2)}, u32[]{:S(2)}) collective-permute-start(bf16[144,256]{1,0:T(8,128)(2,1)} %get-tuple-element.45), channel_id=1, source_target_pairs={{0,8},{1,11},{2,10},{3,9},{4,12},{5,15},{6,14},{7,13},{8,0},{9,3},... | collective-permute-start | bytes 221192 | tf_op jit(solution)/shard_map/ppermute | solution.py:570
  9.3 8.9 %collective-permute-start.6 = (bf16[144,256]{1,0:T(8,128)(2,1)}, bf16[144,256]{1,0:T(8,128)(2,1)S(1)}, u32[]{:S(2)}, u32[]{:S(2)}) collective-permute-start(bf16[144,256]{1,0:T(8,128)(2,1)} %get-tuple-element.51), channel_id=1, source_target_pairs={{0,4},{1,7},{2,6},{3,5},{4,0},{5,3},{6,2},{7,1},{8,12},{9,15},{10,... | collective-permute-start | bytes 221192 | tf_op jit(solution)/shard_map/ppermute | solution.py:570
  10.9 7.3 %collective-permute-start.5 = (bf16[144,256]{1,0:T(8,128)(2,1)}, bf16[144,256]{1,0:T(8,128)(2,1)S(1)}, u32[]{:S(2)}, u32[]{:S(2)}) collective-permute-start(bf16[144,256]{1,0:T(8,128)(2,1)} %get-tuple-element.50), channel_id=1, source_target_pairs={{0,12},{1,15},{2,14},{3,13},{4,8},{5,11},{6,10},{7,9},{8,4},{9,7},... | collective-permute-start | bytes 221192 | tf_op jit(solution)/shard_map/ppermute | solution.py:570
  11.1 9.1 %collective-permute-start.7 = (bf16[144,256]{1,0:T(8,128)(2,1)S(1)}, bf16[144,256]{1,0:T(8,128)(2,1)S(1)}, u32[]{:S(2)}, u32[]{:S(2)}) collective-permute-start(bf16[144,256]{1,0:T(8,128)(2,1)S(1)} %collective-permute-done.2), channel_id=1, source_target_pairs={{0,8},{1,11},{2,10},{3,9},{4,12},{5,15},{6,14},{7,13},{8,0},{9,3},... | collective-permute-start | bytes 221192 | tf_op jit(solution)/shard_map/ppermute | solution.py:570
  12.8 7.5 %collective-permute-start.8 = (bf16[144,256]{1,0:T(8,128)(2,1)S(1)}, bf16[144,256]{1,0:T(8,128)(2,1)S(1)}, u32[]{:S(2)}, u32[]{:S(2)}) collective-permute-start(bf16[144,256]{1,0:T(8,128)(2,1)S(1)} %collective-permute-done.4), channel_id=1, source_target_pairs={{0,4},{1,7},{2,6},{3,5},{4,0},{5,3},{6,2},{7,1},{8,12},{9,15},{10,... | collective-permute-start | bytes 221192 | tf_op jit(solution)/shard_map/ppermute | solution.py:570
  15.3 6.7 %collective-permute-start.9 = (bf16[144,256]{1,0:T(8,128)(2,1)S(1)}, bf16[144,256]{1,0:T(8,128)(2,1)S(1)}, u32[]{:S(2)}, u32[]{:S(2)}) collective-permute-start(bf16[144,256]{1,0:T(8,128)(2,1)S(1)} %collective-permute-done.3), channel_id=1, source_target_pairs={{0,12},{1,15},{2,14},{3,13},{4,8},{5,11},{6,10},{7,9},{8,4},{9,7},... | collective-permute-start | bytes 221192 | tf_op jit(solution)/shard_map/ppermute | solution.py:570
  17.4 0.9 %copy-start.3 = (bf16[144,256]{1,0:T(8,128)(2,1)S(1)}, bf16[144,256]{1,0:T(8,128)(2,1)}, u32[]{:S(2)}) copy-start(bf16[144,256]{1,0:T(8,128)(2,1)} %get-tuple-element.43.source_ref) | copy-start | bytes 221188
  24.2 13.0 %copy-start.4 = (s32[128,8]{0,1:T(8,128)S(1)}, s32[128,8]{0,1:T(8,128)}, u32[]{:S(2)}) copy-start(s32[128,8]{0,1:T(8,128)} %param.11) | copy-start | bytes 12292
  24.2 13.0 %copy-start.5 = (s32[8,128]{1,0:T(8,128)S(1)}, s32[8,128]{1,0:T(8,128)}, u32[]{:S(2)}) copy-start(s32[8,128]{1,0:T(8,128)} %get-tuple-element.41.slot_ref) | copy-start | bytes 12292
  24.2 13.0 %copy-start.6 = (f32[8,128]{1,0:T(8,128)S(1)}, f32[8,128]{1,0:T(8,128)}, u32[]{:S(2)}) copy-start(f32[8,128]{1,0:T(8,128)} %get-tuple-element.42.gates_ref) | copy-start | bytes 12292
  24.2 9.7 %collective-permute-start.12 = (bf16[1536,384]{1,0:T(8,128)(2,1)S(1)}, bf16[1536,384]{1,0:T(8,128)(2,1)S(1)}, u32[]{:S(2)}, u32[]{:S(2)}) collective-permute-start(bf16[1536,384]{1,0:T(8,128)(2,1)S(1)} %other_half.1), channel_id=1, source_target_pairs={{0,1},{1,0},{2,3},{3,2},{4,5},{5,4},{6,7},{7,6},{8,9},{9,8},{10,11... | collective-permute-start | bytes 3538952 | tf_op jit(solution)/shard_map/ppermute | solution.py:574
  25.0 6.8 %collective-permute-start.14 = (bf16[152,256]{1,0:T(8,128)(2,1)S(1)}, bf16[152,256]{1,0:T(8,128)(2,1)S(1)}, u32[]{:S(2)}, u32[]{:S(2)}) collective-permute-start(bf16[152,256]{1,0:T(8,128)(2,1)S(1)} %get-tuple-element.68), channel_id=1, source_target_pairs={{0,12},{1,15},{2,14},{3,13},{4,8},{5,11},{6,10},{7,9},{8,4},{9,7},... | collective-permute-start | bytes 233480 | tf_op jit(solution)/shard_map/ppermute | solution.py:570
  28.0 5.3 %collective-permute-start.15 = (bf16[152,256]{1,0:T(8,128)(2,1)S(1)}, bf16[152,256]{1,0:T(8,128)(2,1)S(1)}, u32[]{:S(2)}, u32[]{:S(2)}) collective-permute-start(bf16[152,256]{1,0:T(8,128)(2,1)S(1)} %get-tuple-element.69), channel_id=1, source_target_pairs={{0,4},{1,7},{2,6},{3,5},{4,0},{5,3},{6,2},{7,1},{8,12},{9,15},{10,... | collective-permute-start | bytes 233480 | tf_op jit(solution)/shard_map/ppermute | solution.py:570
  29.3 7.8 %collective-permute-start.10 = (bf16[152,256]{1,0:T(8,128)(2,1)S(1)}, bf16[152,256]{1,0:T(8,128)(2,1)S(1)}, u32[]{:S(2)}, u32[]{:S(2)}) collective-permute-start(bf16[152,256]{1,0:T(8,128)(2,1)S(1)} %get-tuple-element.55), channel_id=1, source_target_pairs={{0,8},{1,11},{2,10},{3,9},{4,12},{5,15},{6,14},{7,13},{8,0},{9,3},... | collective-permute-start | bytes 233480 | tf_op jit(solution)/shard_map/ppermute | solution.py:570
  29.4 5.9 %collective-permute-start.11 = (bf16[80,256]{1,0:T(8,128)(2,1)S(1)}, bf16[80,256]{1,0:T(8,128)(2,1)S(1)}, u32[]{:S(2)}, u32[]{:S(2)}) collective-permute-start(bf16[80,256]{1,0:T(8,128)(2,1)S(1)} %get-tuple-element.56), channel_id=1, source_target_pairs={{0,2},{2,0},{4,6},{6,4},{8,10},{10,8},{12,14},{14,12},{1,3},{3,1},... | collective-permute-start | bytes 122888 | tf_op jit(solution)/shard_map/ppermute | solution.py:568
  31.8 5.3 %collective-permute-start.16 = (bf16[152,256]{1,0:T(8,128)(2,1)S(1)}, bf16[152,256]{1,0:T(8,128)(2,1)S(1)}, u32[]{:S(2)}, u32[]{:S(2)}) collective-permute-start(bf16[152,256]{1,0:T(8,128)(2,1)S(1)} %collective-permute-done.14.refs_3_), channel_id=1, source_target_pairs={{0,1},{1,0},{2,3},{3,2},{4,5},{5,4},{6,7},{7,6},{8,9},{9,8},{10,11... | collective-permute-start | bytes 233480 | tf_op jit(solution)/shard_map/ppermute | solution.py:574
  33.4 3.8 %collective-permute-start.17 = (bf16[152,256]{1,0:T(8,128)(2,1)S(1)}, bf16[152,256]{1,0:T(8,128)(2,1)S(1)}, u32[]{:S(2)}, u32[]{:S(2)}) collective-permute-start(bf16[152,256]{1,0:T(8,128)(2,1)S(1)} %collective-permute-done.15.refs_4_), channel_id=1, source_target_pairs={{0,1},{1,0},{2,3},{3,2},{4,5},{5,4},{6,7},{7,6},{8,9},{9,8},{10,11... | collective-permute-start | bytes 233480 | tf_op jit(solution)/shard_map/ppermute | solution.py:574
  37.0 1.3 %collective-permute-start.13 = (bf16[152,256]{1,0:T(8,128)(2,1)S(1)}, bf16[152,256]{1,0:T(8,128)(2,1)S(1)}, u32[]{:S(2)}, u32[]{:S(2)}) collective-permute-start(bf16[152,256]{1,0:T(8,128)(2,1)S(1)} %collective-permute-done.10.refs_2_), channel_id=1, source_target_pairs={{0,1},{1,0},{2,3},{3,2},{4,5},{5,4},{6,7},{7,6},{8,9},{9,8},{10,11... | collective-permute-start | bytes 233480 | tf_op jit(solution)/shard_map/ppermute | solution.py:574

commit v17 on v16

--- a/solution.py
+++ b/solution.py
@@ -237,7 +237,7 @@
 MIB = 1024 * 1024
 
 BASES = (4, 6, 2)
-ORDER = (0, 1, 2, 4, 6, 3, 7, 5)
+ORDER = (0, 1, 2, 4, 3, 6, 7, 5)
 LONG = 8 * 10**9
 MAIN = 16
 QUARTERS = 4
@@ -619,11 +619,14 @@
     )
     recv = list(chunks)
     recv[1] = to_step(chunks[1], 1)
+    recv[2] = to_step(chunks[2], 4)
     twin = [to_twin(chunks[c]) for c in (3, 5, 7)]
-    twin, mine = lax.optimization_barrier((twin, chunks[4]))
-    for d, base in enumerate(BASES):
-        recv[2 + 2 * d] = to_step(mine if base == 6 else chunks[2 + 2 * d], base)
-        recv[3 + 2 * d] = to_step(twin[d], base)
+    twin, near = lax.optimization_barrier((twin, chunks[6]))
+    recv[4] = to_step(chunks[4], 6)
+    recv[6] = to_step(near, 2)
+    recv[3] = to_step(twin[0], 4)
+    recv[5] = to_step(twin[1], 6)
+    recv[7] = to_step(twin[2], 2)
     (held,) = local_call(hold_kernel, [(recv[0].shape, BF)], [recv[0]], "hold", 1, 1)
     matmul = 2 * served * model_width * hidden_width
     outs = local_call(

time: 39.5 us -> 40.6 us (1.028)
  starting transfers between devices: 21.1 us -> 23.7 us
  waiting for transfers between devices: 9.17 us -> 7.62 us
    ppermute x9, starting transfers between devices: 15 us -> 18.2 us  [to_step(): return lax.ppermute(chunk, ('expert', 'replica'), pairs)]
    ppermute x9, waiting for transfers between devices: 8.41 us -> 6.98 us  [to_step(): return lax.ppermute(chunk, ('expert', 'replica'), pairs)]
    ppermute x7, starting transfers between devices: 2.51 us -> 1.76 us  [to_twin(): return lax.ppermute(chunk, 'replica', [(0, 1), (1, 0)])]
  transfers between devices with their start and end apart: 18 -> 18, of which waited for: 6 -> 4; matrix products, arithmetic and copies ran while one was open for 0% -> 0% of each run, Pallas kernels for 5% -> 4%
where the time goes in v17:
time: 40.6 us; the launch traced here: 40.4 us
  starting transfers between devices  23.7 us (58%)
  waiting for transfers between devices  7.62 us (19%)
  Pallas kernels  7.44 us (18%)
  local copies, waits for them, and re-layouts  0.91 us (2%)
  between operations  0.79 us (2%)
    ppermute x9, starting transfers between devices, to_step(): return lax.ppermute(chunk, ('expert', 'replica'), pairs)  18.2 us
    pallas_call x7, Pallas kernels, local_call(): pl.pallas_call(kernel, out_shape=[jax.ShapeDtypeStruct(shape, kind) for s...  7.44 us
    ppermute x9, waiting for transfers between devices, to_step(): return lax.ppermute(chunk, ('expert', 'replica'), pairs)  6.98 us
    ppermute x2, starting transfers between devices, to_step(): return lax.ppermute(chunk, 'expert', [(i, i ^ 1) for i in range(experts)])  3.71 us
    ppermute x7, starting transfers between devices, to_twin(): return lax.ppermute(chunk, 'replica', [(0, 1), (1, 0)])  1.76 us
    unnamed x14, local copies, waits for them, and re-layouts  0.91 us
  transfers between devices with their start and end apart: 18, of which 4 were waited for; matrix products, arithmetic and copies ran while one was open for 0% of the time, Pallas kernels for 4%

profile of v17, /device:TPU:0, one launch (start us, length us, event | category | flops | bytes accessed | tf_op | source)
XLA Modules:
  0.0 40.4 jit_solution(10843885248605418936)
XLA Ops:
  0.7 2.5 %route.1 = (bf16[144,256]{1,0:T(8,128)(2,1)}, bf16[144,256]{1,0:T(8,128)(2,1)}, bf16[144,256]{1,0:T(8,128)(2,1)}, bf16[144,256]{1,0:T(8,128)(2,1)}, bf16[144,256...) custom-call(s32[8]{0:T(128)} %plan_hbm.1, ...), custom_call_target="tpu_custom_call" | custom-call | flops 8000000000 | bytes 1114112 | tf_op jit(solution)/shard_map/route/pallas_call | solution.py:553
  3.1 0.5 %collective-permute-start.3 = (bf16[144,256]{1,0:T(8,128)(2,1)}, bf16[144,256]{1,0:T(8,128)(2,1)S(1)}, u32[]{:S(2)}, u32[]{:S(2)}) collective-permute-start(bf16[144,256]{1,0:T(8,128)(2,1)} %get-tuple-element.47), channel_id=1, source_target_pairs={{0,1},{1,0},{2,3},{3,2},{4,5},{5,4},{6,7},{7,6},{8,9},{9,8},{10,11... | collective-permute-start | bytes 221192 | tf_op jit(solution)/shard_map/ppermute | solution.py:574
  3.7 0.1 collective-permute-start.4
  3.7 0.4 %collective-permute-start.5 = (bf16[144,256]{1,0:T(8,128)(2,1)}, bf16[144,256]{1,0:T(8,128)(2,1)S(1)}, u32[]{:S(2)}, u32[]{:S(2)}) collective-permute-start(bf16[144,256]{1,0:T(8,128)(2,1)} %get-tuple-element.49), channel_id=1, source_target_pairs={{0,1},{1,0},{2,3},{3,2},{4,5},{5,4},{6,7},{7,6},{8,9},{9,8},{10,11... | collective-permute-start | bytes 221192 | tf_op jit(solution)/shard_map/ppermute | solution.py:574
  4.2 2.6 %collective-permute-start = (bf16[144,256]{1,0:T(8,128)(2,1)}, bf16[144,256]{1,0:T(8,128)(2,1)S(1)}, u32[]{:S(2)}, u32[]{:S(2)}) collective-permute-start(bf16[144,256]{1,0:T(8,128)(2,1)} %get-tuple-element.44), channel_id=1, source_target_pairs={{0,2},{2,0},{4,6},{6,4},{8,10},{10,8},{12,14},{14,12},{1,3},{3,1},... | collective-permute-start | bytes 221192 | tf_op jit(solution)/shard_map/ppermute | solution.py:568
  6.7 2.6 %collective-permute-start.1 = (bf16[144,256]{1,0:T(8,128)(2,1)}, bf16[144,256]{1,0:T(8,128)(2,1)S(1)}, u32[]{:S(2)}, u32[]{:S(2)}) collective-permute-start(bf16[144,256]{1,0:T(8,128)(2,1)} %get-tuple-element.45), channel_id=1, source_target_pairs={{0,8},{1,11},{2,10},{3,9},{4,12},{5,15},{6,14},{7,13},{8,0},{9,3},... | collective-permute-start | bytes 221192 | tf_op jit(solution)/shard_map/ppermute | solution.py:570
  9.3 0.0 collective-permute-done.3
  9.3 1.3 %collective-permute-start.2 = (bf16[144,256]{1,0:T(8,128)(2,1)}, bf16[144,256]{1,0:T(8,128)(2,1)S(1)}, u32[]{:S(2)}, u32[]{:S(2)}) collective-permute-start(bf16[144,256]{1,0:T(8,128)(2,1)} %get-tuple-element.46), channel_id=1, source_target_pairs={{0,12},{1,15},{2,14},{3,13},{4,8},{5,11},{6,10},{7,9},{8,4},{9,7},... | collective-permute-start | bytes 221192 | tf_op jit(solution)/shard_map/ppermute | solution.py:570
  10.7 0.0 collective-permute-done.4
  10.7 0.0 collective-permute-done.5
  10.7 1.7 %collective-permute-start.6 = (bf16[144,256]{1,0:T(8,128)(2,1)S(1)}, bf16[144,256]{1,0:T(8,128)(2,1)S(1)}, u32[]{:S(2)}, u32[]{:S(2)}) collective-permute-start(bf16[144,256]{1,0:T(8,128)(2,1)S(1)} %collective-permute-done.3), channel_id=1, source_target_pairs={{0,8},{1,11},{2,10},{3,9},{4,12},{5,15},{6,14},{7,13},{8,0},{9,3},... | collective-permute-start | bytes 221192 | tf_op jit(solution)/shard_map/ppermute | solution.py:570
  12.4 1.3 %collective-permute-start.7 = (bf16[144,256]{1,0:T(8,128)(2,1)}, bf16[144,256]{1,0:T(8,128)(2,1)S(1)}, u32[]{:S(2)}, u32[]{:S(2)}) collective-permute-start(bf16[144,256]{1,0:T(8,128)(2,1)} %get-tuple-element.52), channel_id=1, source_target_pairs={{0,4},{1,7},{2,6},{3,5},{4,0},{5,3},{6,2},{7,1},{8,12},{9,15},{10,... | collective-permute-start | bytes 221192 | tf_op jit(solution)/shard_map/ppermute | solution.py:570
  13.7 0.0 collective-permute-done.refs_1_
  13.7 0.7 %collective-permute-start.8 = (bf16[144,256]{1,0:T(8,128)(2,1)S(1)}, bf16[144,256]{1,0:T(8,128)(2,1)S(1)}, u32[]{:S(2)}, u32[]{:S(2)}) collective-permute-start(bf16[144,256]{1,0:T(8,128)(2,1)S(1)} %collective-permute-done.5), channel_id=1, source_target_pairs={{0,4},{1,7},{2,6},{3,5},{4,0},{5,3},{6,2},{7,1},{8,12},{9,15},{10,... | collective-permute-start | bytes 221192 | tf_op jit(solution)/shard_map/ppermute | solution.py:570
  14.4 0.0 collective-permute-done.1.refs_2_
  14.4 6.1 %collective-permute-start.9 = (bf16[144,256]{1,0:T(8,128)(2,1)S(1)}, bf16[144,256]{1,0:T(8,128)(2,1)S(1)}, u32[]{:S(2)}, u32[]{:S(2)}) collective-permute-start(bf16[144,256]{1,0:T(8,128)(2,1)S(1)} %collective-permute-done.4), channel_id=1, source_target_pairs={{0,12},{1,15},{2,14},{3,13},{4,8},{5,11},{6,10},{7,9},{8,4},{9,7},... | collective-permute-start | bytes 221192 | tf_op jit(solution)/shard_map/ppermute | solution.py:570
  20.5 0.9 %copy-done.3 = bf16[144,256]{1,0:T(8,128)(2,1)S(1)} copy-done((bf16[144,256]{1,0:T(8,128)(2,1)S(1)}, bf16[144,256]{1,0:T(8,128)(2,1)}, u32[]{:S(2)}) %copy-start.3) | copy-done | bytes 73752
  21.4 0.0 collective-permute-done.2.refs_3_
  21.4 0.0 collective-permute-done.6.refs_4_
  21.4 0.0 collective-permute-done.7.refs_5_
  21.4 0.0 collective-permute-done.8.refs_6_
  21.4 2.2 %collective-permute-done.9.refs_7_ = bf16[144,256]{1,0:T(8,128)(2,1)S(1)} collective-permute-done((bf16[144,256]{1,0:T(8,128)(2,1)S(1)}, bf16[144,256]{1,0:T(8,128)(2,1)S(1)}, u32[]{:S(2)}, u32[]{:S(2)}) %collective-permute-start.9) | collective-permute-done | bytes 73760 | tf_op jit(solution)/shard_map/ppermute | solution.py:570
  23.6 0.0 copy-done
  23.7 0.0 copy-done.2
  23.7 1.5 %expert_rows.1 = (bf16[80,256]{1,0:T(8,128)(2,1)S(1)}, bf16[80,256]{1,0:T(8,128)(2,1)S(1)}, bf16[152,256]{1,0:T(8,128)(2,1)S(1)}, bf16[152,256]{1,0:T(8,128)(2,1...) custom-call(bf16[144,256]{1,0:T(8,128)(2,1)S(1)} %hold.1.refs_0_, ...), custom_call_target="tpu_custom_call" | custom-call | flops 566231040 | bytes 2359296 | tf_op jit(solution)/shard_map/expert_rows/pallas_call | solution.py:553
  25.2 0.6 %other_half.1 = bf16[1536,384]{1,0:T(8,128)(2,1)S(1)} custom-call(bf16[144,1024]{1,0:T(8,128)(2,1)S(1)} %get-tuple-element.57.x_ref, bf16[144,1024]{1,0:T(8,128)(2,1)S(1)} %get-tuple-element.58.s_ref, bf16[144,384]{1,0:T(8,128)(2,1)S(1)} %get-tuple-element.59.dg_ref, bf16[144,384]{1,0:T(8,128)(2,1)S(1)} %get-tuple-element.60.du_ref, ...), custom_call_target="tpu_custom_call" | custom-call | flops 1 | bytes 1 | tf_op jit(solution)/shard_map/other_half/pallas_call | solution.py:553
  25.8 0.0 copy-start.4
  25.8 0.0 copy-start.5
  25.8 0.0 copy-start.6
  25.9 0.1 collective-permute-start.12
  25.9 3.9 %collective-permute-start.14 = (bf16[152,256]{1,0:T(8,128)(2,1)S(1)}, bf16[152,256]{1,0:T(8,128)(2,1)S(1)}, u32[]{:S(2)}, u32[]{:S(2)}) collective-permute-start(bf16[152,256]{1,0:T(8,128)(2,1)S(1)} %get-tuple-element.68), channel_id=1, source_target_pairs={{0,12},{1,15},{2,14},{3,13},{4,8},{5,11},{6,10},{7,9},{8,4},{9,7},... | collective-permute-start | bytes 233480 | tf_op jit(solution)/shard_map/ppermute | solution.py:570
  29.8 0.0 collective-permute-start.15
  29.8 0.6 %collective-permute-start.10 = (bf16[152,256]{1,0:T(8,128)(2,1)S(1)}, bf16[152,256]{1,0:T(8,128)(2,1)S(1)}, u32[]{:S(2)}, u32[]{:S(2)}) collective-permute-start(bf16[152,256]{1,0:T(8,128)(2,1)S(1)} %get-tuple-element.55), channel_id=1, source_target_pairs={{0,8},{1,11},{2,10},{3,9},{4,12},{5,15},{6,14},{7,13},{8,0},{9,3},... | collective-permute-start | bytes 233480 | tf_op jit(solution)/shard_map/ppermute | solution.py:570
  30.4 1.1 %collective-permute-start.11 = (bf16[80,256]{1,0:T(8,128)(2,1)S(1)}, bf16[80,256]{1,0:T(8,128)(2,1)S(1)}, u32[]{:S(2)}, u32[]{:S(2)}) collective-permute-start(bf16[80,256]{1,0:T(8,128)(2,1)S(1)} %get-tuple-element.56), channel_id=1, source_target_pairs={{0,2},{2,0},{4,6},{6,4},{8,10},{10,8},{12,14},{14,12},{1,3},{3,1},... | collective-permute-start | bytes 122888 | tf_op jit(solution)/shard_map/ppermute | solution.py:568
  31.5 1.4 %collective-permute-done.14.refs_3_ = bf16[152,256]{1,0:T(8,128)(2,1)S(1)} collective-permute-done((bf16[152,256]{1,0:T(8,128)(2,1)S(1)}, bf16[152,256]{1,0:T(8,128)(2,1)S(1)}, u32[]{:S(2)}, u32[]{:S(2)}) %collective-permute-start.14) | collective-permute-done | bytes 77856 | tf_op jit(solution)/shard_map/ppermute | solution.py:570
  32.9 0.1 collective-permute-start.16
  33.1 3.4 %collective-permute-done.15.refs_4_ = bf16[152,256]{1,0:T(8,128)(2,1)S(1)} collective-permute-done((bf16[152,256]{1,0:T(8,128)(2,1)S(1)}, bf16[152,256]{1,0:T(8,128)(2,1)S(1)}, u32[]{:S(2)}, u32[]{:S(2)}) %collective-permute-start.15) | collective-permute-done | bytes 77856 | tf_op jit(solution)/shard_map/ppermute | solution.py:570
  36.5 0.3 collective-permute-start.17
  36.7 0.0 collective-permute-done.12.came_ref
  36.7 1.4 %own_half.1 = (bf16[512,384]{1,0:T(8,128)(2,1)}, bf16[512,384]{1,0:T(8,128)(2,1)}, bf16[512,384]{1,0:T(8,128)(2,1)}) custom-call(bf16[144,1024]{1,0:T(8,128)(2,1)S(1)} %get-tuple-element.57.x_ref, bf16[144,1024]{1,0:T(8,128)(2,1)S(1)} %get-tuple-element.58.s_ref, bf16[144,384]{1,0:T(8,128)(2,1)S(1)} %get-tuple-element.59.dg_ref, ...), custom_call_target="tpu_custom_call" | custom-call | flops 1 | bytes 1 | tf_op jit(solution)/shard_map/own_half/pallas_call | solution.py:553
  38.1 0.0 collective-permute-done.11.refs_1_
  38.1 0.0 collective-permute-done.10.refs_2_
  38.1 0.2 collective-permute-start.13
  38.4 0.0 collective-permute-done.16.refs_5_
  38.4 0.0 collective-permute-done.17.refs_6_
  38.4 0.4 combine.1
  38.8 0.6 %collective-permute-done.13.given_ref = bf16[152,256]{1,0:T(8,128)(2,1)S(1)} collective-permute-done((bf16[152,256]{1,0:T(8,128)(2,1)S(1)}, bf16[152,256]{1,0:T(8,128)(2,1)S(1)}, u32[]{:S(2)}, u32[]{:S(2)}) %collective-permute-start.13) | collective-permute-done | bytes 77856 | tf_op jit(solution)/shard_map/ppermute | solution.py:574
  39.4 1.0 %combine_last.1 = (bf16[128,1024]{1,0:T(8,128)(2,1)}, bf16[8,128]{1,0:T(8,128)(2,1)}) custom-call(s32[8,128]{1,0:T(8,128)S(1)} %bitcast.15, s32[8,128]{1,0:T(8,128)S(1)} %copy-done.5, f32[8,128]{1,0:T(8,128)S(1)} %copy-done.6, bf16[152,256]{1,0:T(8,128)(2,1)S(1)} %collective-permute-done.13.given_ref, f32[128,1024]{1,0:T(8,128)S(1)} %get-tuple-element.70.token_sum_ref, ...), custom_call_target="tpu_custom_call" | custom-call | flops 1 | bytes 1 | tf_op jit(solution)/shard_map/combine_last/pallas_call | solution.py:553
  (9 shorter events, 0.0 us)
Async XLA Ops:
  0.6 23.0 %copy-start = (bf16[1,1024,384]{2,1,0:T(8,128)(2,1)S(1)}, bf16[1,1024,384]{2,1,0:T(8,128)(2,1)}, u32[]{:S(2)}) copy-start(bf16[1,1024,384]{2,1,0:T(8,128)(2,1)} %param.15) | copy-start | bytes 2359300
  0.6 23.0 %copy-start.1 = (bf16[1,1024,384]{2,1,0:T(8,128)(2,1)S(1)}, bf16[1,1024,384]{2,1,0:T(8,128)(2,1)}, u32[]{:S(2)}) copy-start(bf16[1,1024,384]{2,1,0:T(8,128)(2,1)} %param.16) | copy-start | bytes 2359300
  0.7 23.0 %copy-start.2 = (bf16[1,1024,384]{2,1,0:T(8,128)(2,1)S(1)}, bf16[1,1024,384]{2,1,0:T(8,128)(2,1)}, u32[]{:S(2)}) copy-start(bf16[1,1024,384]{2,1,0:T(8,128)(2,1)} %param.17) | copy-start | bytes 2359300
  3.1 6.2 %collective-permute-start.3 = (bf16[144,256]{1,0:T(8,128)(2,1)}, bf16[144,256]{1,0:T(8,128)(2,1)S(1)}, u32[]{:S(2)}, u32[]{:S(2)}) collective-permute-start(bf16[144,256]{1,0:T(8,128)(2,1)} %get-tuple-element.47), channel_id=1, source_target_pairs={{0,1},{1,0},{2,3},{3,2},{4,5},{5,4},{6,7},{7,6},{8,9},{9,8},{10,11... | collective-permute-start | bytes 221192 | tf_op jit(solution)/shard_map/ppermute | solution.py:574
  3.7 7.0 %collective-permute-start.4 = (bf16[144,256]{1,0:T(8,128)(2,1)}, bf16[144,256]{1,0:T(8,128)(2,1)S(1)}, u32[]{:S(2)}, u32[]{:S(2)}) collective-permute-start(bf16[144,256]{1,0:T(8,128)(2,1)} %get-tuple-element.48), channel_id=1, source_target_pairs={{0,1},{1,0},{2,3},{3,2},{4,5},{5,4},{6,7},{7,6},{8,9},{9,8},{10,11... | collective-permute-start | bytes 221192 | tf_op jit(solution)/shard_map/ppermute | solution.py:574
  3.7 6.9 %collective-permute-start.5 = (bf16[144,256]{1,0:T(8,128)(2,1)}, bf16[144,256]{1,0:T(8,128)(2,1)S(1)}, u32[]{:S(2)}, u32[]{:S(2)}) collective-permute-start(bf16[144,256]{1,0:T(8,128)(2,1)} %get-tuple-element.49), channel_id=1, source_target_pairs={{0,1},{1,0},{2,3},{3,2},{4,5},{5,4},{6,7},{7,6},{8,9},{9,8},{10,11... | collective-permute-start | bytes 221192 | tf_op jit(solution)/shard_map/ppermute | solution.py:574
  4.2 9.6 %collective-permute-start = (bf16[144,256]{1,0:T(8,128)(2,1)}, bf16[144,256]{1,0:T(8,128)(2,1)S(1)}, u32[]{:S(2)}, u32[]{:S(2)}) collective-permute-start(bf16[144,256]{1,0:T(8,128)(2,1)} %get-tuple-element.44), channel_id=1, source_target_pairs={{0,2},{2,0},{4,6},{6,4},{8,10},{10,8},{12,14},{14,12},{1,3},{3,1},... | collective-permute-start | bytes 221192 | tf_op jit(solution)/shard_map/ppermute | solution.py:568
  6.7 7.7 %collective-permute-start.1 = (bf16[144,256]{1,0:T(8,128)(2,1)}, bf16[144,256]{1,0:T(8,128)(2,1)S(1)}, u32[]{:S(2)}, u32[]{:S(2)}) collective-permute-start(bf16[144,256]{1,0:T(8,128)(2,1)} %get-tuple-element.45), channel_id=1, source_target_pairs={{0,8},{1,11},{2,10},{3,9},{4,12},{5,15},{6,14},{7,13},{8,0},{9,3},... | collective-permute-start | bytes 221192 | tf_op jit(solution)/shard_map/ppermute | solution.py:570
  9.3 12.1 %collective-permute-start.2 = (bf16[144,256]{1,0:T(8,128)(2,1)}, bf16[144,256]{1,0:T(8,128)(2,1)S(1)}, u32[]{:S(2)}, u32[]{:S(2)}) collective-permute-start(bf16[144,256]{1,0:T(8,128)(2,1)} %get-tuple-element.46), channel_id=1, source_target_pairs={{0,12},{1,15},{2,14},{3,13},{4,8},{5,11},{6,10},{7,9},{8,4},{9,7},... | collective-permute-start | bytes 221192 | tf_op jit(solution)/shard_map/ppermute | solution.py:570
  10.7 10.7 %collective-permute-start.6 = (bf16[144,256]{1,0:T(8,128)(2,1)S(1)}, bf16[144,256]{1,0:T(8,128)(2,1)S(1)}, u32[]{:S(2)}, u32[]{:S(2)}) collective-permute-start(bf16[144,256]{1,0:T(8,128)(2,1)S(1)} %collective-permute-done.3), channel_id=1, source_target_pairs={{0,8},{1,11},{2,10},{3,9},{4,12},{5,15},{6,14},{7,13},{8,0},{9,3},... | collective-permute-start | bytes 221192 | tf_op jit(solution)/shard_map/ppermute | solution.py:570
  12.4 9.0 %collective-permute-start.7 = (bf16[144,256]{1,0:T(8,128)(2,1)}, bf16[144,256]{1,0:T(8,128)(2,1)S(1)}, u32[]{:S(2)}, u32[]{:S(2)}) collective-permute-start(bf16[144,256]{1,0:T(8,128)(2,1)} %get-tuple-element.52), channel_id=1, source_target_pairs={{0,4},{1,7},{2,6},{3,5},{4,0},{5,3},{6,2},{7,1},{8,12},{9,15},{10,... | collective-permute-start | bytes 221192 | tf_op jit(solution)/shard_map/ppermute | solution.py:570
  13.7 7.7 %collective-permute-start.8 = (bf16[144,256]{1,0:T(8,128)(2,1)S(1)}, bf16[144,256]{1,0:T(8,128)(2,1)S(1)}, u32[]{:S(2)}, u32[]{:S(2)}) collective-permute-start(bf16[144,256]{1,0:T(8,128)(2,1)S(1)} %collective-permute-done.5), channel_id=1, source_target_pairs={{0,4},{1,7},{2,6},{3,5},{4,0},{5,3},{6,2},{7,1},{8,12},{9,15},{10,... | collective-permute-start | bytes 221192 | tf_op jit(solution)/shard_map/ppermute | solution.py:570
  14.4 9.2 %collective-permute-start.9 = (bf16[144,256]{1,0:T(8,128)(2,1)S(1)}, bf16[144,256]{1,0:T(8,128)(2,1)S(1)}, u32[]{:S(2)}, u32[]{:S(2)}) collective-permute-start(bf16[144,256]{1,0:T(8,128)(2,1)S(1)} %collective-permute-done.4), channel_id=1, source_target_pairs={{0,12},{1,15},{2,14},{3,13},{4,8},{5,11},{6,10},{7,9},{8,4},{9,7},... | collective-permute-start | bytes 221192 | tf_op jit(solution)/shard_map/ppermute | solution.py:570
  20.5 0.9 %copy-start.3 = (bf16[144,256]{1,0:T(8,128)(2,1)S(1)}, bf16[144,256]{1,0:T(8,128)(2,1)}, u32[]{:S(2)}) copy-start(bf16[144,256]{1,0:T(8,128)(2,1)} %get-tuple-element.43.source_ref) | copy-start | bytes 221188
  25.8 12.5 %copy-start.4 = (s32[128,8]{0,1:T(8,128)S(1)}, s32[128,8]{0,1:T(8,128)}, u32[]{:S(2)}) copy-start(s32[128,8]{0,1:T(8,128)} %param.11) | copy-start | bytes 12292
  25.8 12.5 %copy-start.5 = (s32[8,128]{1,0:T(8,128)S(1)}, s32[8,128]{1,0:T(8,128)}, u32[]{:S(2)}) copy-start(s32[8,128]{1,0:T(8,128)} %get-tuple-element.41.slot_ref) | copy-start | bytes 12292
  25.8 12.5 %copy-start.6 = (f32[8,128]{1,0:T(8,128)S(1)}, f32[8,128]{1,0:T(8,128)}, u32[]{:S(2)}) copy-start(f32[8,128]{1,0:T(8,128)} %get-tuple-element.42.gates_ref) | copy-start | bytes 12292
  25.9 10.9 %collective-permute-start.12 = (bf16[1536,384]{1,0:T(8,128)(2,1)S(1)}, bf16[1536,384]{1,0:T(8,128)(2,1)S(1)}, u32[]{:S(2)}, u32[]{:S(2)}) collective-permute-start(bf16[1536,384]{1,0:T(8,128)(2,1)S(1)} %other_half.1), channel_id=1, source_target_pairs={{0,1},{1,0},{2,3},{3,2},{4,5},{5,4},{6,7},{7,6},{8,9},{9,8},{10,11... | collective-permute-start | bytes 3538952 | tf_op jit(solution)/shard_map/ppermute | solution.py:574
  25.9 7.0 %collective-permute-start.14 = (bf16[152,256]{1,0:T(8,128)(2,1)S(1)}, bf16[152,256]{1,0:T(8,128)(2,1)S(1)}, u32[]{:S(2)}, u32[]{:S(2)}) collective-permute-start(bf16[152,256]{1,0:T(8,128)(2,1)S(1)} %get-tuple-element.68), channel_id=1, source_target_pairs={{0,12},{1,15},{2,14},{3,13},{4,8},{5,11},{6,10},{7,9},{8,4},{9,7},... | collective-permute-start | bytes 233480 | tf_op jit(solution)/shard_map/ppermute | solution.py:570
  29.8 6.6 %collective-permute-start.15 = (bf16[152,256]{1,0:T(8,128)(2,1)S(1)}, bf16[152,256]{1,0:T(8,128)(2,1)S(1)}, u32[]{:S(2)}, u32[]{:S(2)}) collective-permute-start(bf16[152,256]{1,0:T(8,128)(2,1)S(1)} %get-tuple-element.69), channel_id=1, source_target_pairs={{0,4},{1,7},{2,6},{3,5},{4,0},{5,3},{6,2},{7,1},{8,12},{9,15},{10,... | collective-permute-start | bytes 233480 | tf_op jit(solution)/shard_map/ppermute | solution.py:570
  29.8 8.3 %collective-permute-start.10 = (bf16[152,256]{1,0:T(8,128)(2,1)S(1)}, bf16[152,256]{1,0:T(8,128)(2,1)S(1)}, u32[]{:S(2)}, u32[]{:S(2)}) collective-permute-start(bf16[152,256]{1,0:T(8,128)(2,1)S(1)} %get-tuple-element.55), channel_id=1, source_target_pairs={{0,8},{1,11},{2,10},{3,9},{4,12},{5,15},{6,14},{7,13},{8,0},{9,3},... | collective-permute-start | bytes 233480 | tf_op jit(solution)/shard_map/ppermute | solution.py:570
  30.4 7.7 %collective-permute-start.11 = (bf16[80,256]{1,0:T(8,128)(2,1)S(1)}, bf16[80,256]{1,0:T(8,128)(2,1)S(1)}, u32[]{:S(2)}, u32[]{:S(2)}) collective-permute-start(bf16[80,256]{1,0:T(8,128)(2,1)S(1)} %get-tuple-element.56), channel_id=1, source_target_pairs={{0,2},{2,0},{4,6},{6,4},{8,10},{10,8},{12,14},{14,12},{1,3},{3,1},... | collective-permute-start | bytes 122888 | tf_op jit(solution)/shard_map/ppermute | solution.py:568
  32.9 5.4 %collective-permute-start.16 = (bf16[152,256]{1,0:T(8,128)(2,1)S(1)}, bf16[152,256]{1,0:T(8,128)(2,1)S(1)}, u32[]{:S(2)}, u32[]{:S(2)}) collective-permute-start(bf16[152,256]{1,0:T(8,128)(2,1)S(1)} %collective-permute-done.14.refs_3_), channel_id=1, source_target_pairs={{0,1},{1,0},{2,3},{3,2},{4,5},{5,4},{6,7},{7,6},{8,9},{9,8},{10,11... | collective-permute-start | bytes 233480 | tf_op jit(solution)/shard_map/ppermute | solution.py:574
  36.5 1.9 %collective-permute-start.17 = (bf16[152,256]{1,0:T(8,128)(2,1)S(1)}, bf16[152,256]{1,0:T(8,128)(2,1)S(1)}, u32[]{:S(2)}, u32[]{:S(2)}) collective-permute-start(bf16[152,256]{1,0:T(8,128)(2,1)S(1)} %collective-permute-done.15.refs_4_), channel_id=1, source_target_pairs={{0,1},{1,0},{2,3},{3,2},{4,5},{5,4},{6,7},{7,6},{8,9},{9,8},{10,11... | collective-permute-start | bytes 233480 | tf_op jit(solution)/shard_map/ppermute | solution.py:574
  38.1 1.3 %collective-permute-start.13 = (bf16[152,256]{1,0:T(8,128)(2,1)S(1)}, bf16[152,256]{1,0:T(8,128)(2,1)S(1)}, u32[]{:S(2)}, u32[]{:S(2)}) collective-permute-start(bf16[152,256]{1,0:T(8,128)(2,1)S(1)} %collective-permute-done.10.refs_2_), channel_id=1, source_target_pairs={{0,1},{1,0},{2,3},{3,2},{4,5},{5,4},{6,7},{7,6},{8,9},{9,8},{10,11... | collective-permute-start | bytes 233480 | tf_op jit(solution)/shard_map/ppermute | solution.py:574
